TPU v7x, 32 devices: a whole 2x2x4 slice. The times are simulated.
32 devices in a mesh: rows: 2 (over core), batch: 16 (over z, y, x).
Axes of the slice: x: 2, y: 2, z: 4, core: 2. Of those that a mesh axis runs over, the one named last changes fastest.
Arguments:
- images: bfloat16 [32, 56, 56, 256], P('batch', 'rows'), may hold values from -6 to 6
- w_1a: bfloat16 [256, 128], replicated, may hold values from -0.375 to 0.375
- w_1b: bfloat16 [3, 3, 128, 128], replicated, may hold values from -0.1875 to 0.1875
- w_1c: bfloat16 [128, 512], replicated, may hold values from -0.5 to 0.5
- w_1p: bfloat16 [256, 512], replicated, may hold values from -0.375 to 0.375
- w_2a: bfloat16 [512, 128], replicated, may hold values from -0.25 to 0.25
- w_2b: bfloat16 [3, 3, 128, 128], replicated, may hold values from -0.1875 to 0.1875
- w_2c: bfloat16 [128, 512], replicated, may hold values from -0.5 to 0.5
- norm_1a: float32 [2, 3, 128], replicated, may hold values from 0.5 to 1.5
- norm_1b: float32 [2, 3, 128], replicated, may hold values from 0.5 to 1.5
- norm_1c: float32 [2, 3, 512], replicated, may hold values from 0.5 to 1.5
- norm_1p: float32 [2, 3, 512], replicated, may hold values from 0.5 to 1.5
- norm_2a: float32 [2, 3, 128], replicated, may hold values from 0.5 to 1.5
- norm_2b: float32 [2, 3, 128], replicated, may hold values from 0.5 to 1.5
- norm_2c: float32 [2, 3, 512], replicated, may hold values from 0.5 to 1.5
- cotangent: bfloat16 [32, 28, 28, 512], P(('batch', 'rows')), may hold values from -6 to 6
- group: int32 [32], P('batch'), may hold values from 0 to 2, as said below
- width: int32 [3], replicated, may hold values from 2 to 4
- gate: int32 [3], replicated, may hold values from 0 to 4, as said below
Outputs:
- result: bfloat16 [32, 28, 28, 512], P(('batch', 'rows'))
- grad_images: bfloat16 [32, 56, 56, 256], P('batch', 'rows')
- grad_w_1a: float32 [256, 128], replicated
- grad_w_1b: float32 [3, 3, 128, 128], replicated
- grad_w_1c: float32 [128, 512], replicated
- grad_w_1p: float32 [256, 512], replicated
- grad_w_2a: float32 [512, 128], replicated
- grad_w_2b: float32 [3, 3, 128, 128], replicated
- grad_w_2c: float32 [128, 512], replicated
- grad_norm_1a: float32 [2, 3, 128], replicated
- grad_norm_1b: float32 [2, 3, 128], replicated
- grad_norm_1c: float32 [2, 3, 512], replicated
- grad_norm_1p: float32 [2, 3, 512], replicated
- grad_norm_2a: float32 [2, 3, 128], replicated
- grad_norm_2b: float32 [2, 3, 128], replicated
- grad_norm_2c: float32 [2, 3, 512], replicated
Inputs may be any that keep to these rules, and one draw needn't show every extreme that they name: Every group holds at least one image. One group has gate 0, one has gate 4, the third 1 to 3.
All inputs are finite; a program needn't handle non-finite values.
Results may differ from a plain program's by a relative error of at most 0.015.
Values may be sent and summed in bfloat16 or wider, within the bound.
No kernel may reach another device: no remote copies, remote signals or barrier semaphores. Data moves between devices by JAX's collectives and lax.ppermute only.
A program may use at most 128 MiB of HBM per device.

v0:
```python
import functools

import jax
import jax.numpy as jnp
from jax import lax
from jax.experimental import pallas as pl
from jax.experimental.pallas import tpu as pltpu
from jax.sharding import PartitionSpec as P

EPSILON = 1e-05
F32 = jnp.float32
BF16 = jnp.bfloat16
AXES = ("rows", "batch")
VMEM_LIMIT = 40 * 1024 * 1024
LANES = 128
COLS = 32


def full(memory=pltpu.VMEM):
    return pl.BlockSpec(memory_space=memory)


def stage(kernel, outs, scratch=(), flops=0, smem=(0,)):
    def call(*args):
        return pl.pallas_call(
            kernel,
            out_shape=tuple(jax.ShapeDtypeStruct(s, d) for s, d in outs),
            in_specs=[full(pltpu.SMEM if i in smem else pltpu.VMEM) for i in range(len(args))],
            out_specs=tuple(full() for _ in outs),
            scratch_shapes=list(scratch),
            compiler_params=pltpu.CompilerParams(vmem_limit_bytes=VMEM_LIMIT),
            cost_estimate=pl.CostEstimate(
                flops=flops, bytes_accessed=4 * 1024 * 1024, transcendentals=0
            ),
            name=kernel.func.__name__ if isinstance(kernel, functools.partial) else kernel.__name__,
        )(*args)

    return call


def sigmoid(v):
    return 0.5 * jnp.tanh(0.5 * v) + 0.5


def fold(x):
    return (x[0:8] + x[8:16]) + (x[16:24] + x[24:32])


def row(total, stat):
    blocks = total.shape[0]
    pieces = [total[j : j + 1, LANES * stat : LANES * (stat + 1)] for j in range(blocks)]
    return pieces[0] if blocks == 1 else jnp.concatenate(pieces, axis=1)


def spread(out_ref, rows):
    blocks = out_ref.shape[1]
    for stat, values in enumerate(rows):
        for j in range(blocks):
            piece = values[:, LANES * j : LANES * (j + 1)]
            out_ref[:, j : j + 1, LANES * stat : LANES * (stat + 1)] = jnp.broadcast_to(
                piece[None], (out_ref.shape[0], 1, LANES)
            )


def group_sum(got_ref, labels, label):
    same = (labels == label).astype(F32)
    stats = got_ref.shape[2] // LANES
    parts = [
        jnp.sum(got_ref[:, :, LANES * s : LANES * (s + 1)] * same, axis=0) for s in range(stats)
    ]
    return jnp.concatenate(parts, axis=1) if stats > 1 else parts[0]


def group_count(labels, label):
    return jnp.sum((labels == label).astype(F32), axis=0)


def tiled(values, channels):
    return jnp.concatenate([values] * (channels // LANES), axis=1) if channels > LANES else values


def moments(first, second, pixels):
    mean = first / pixels
    return mean, lax.rsqrt(second / pixels - mean * mean + EPSILON)


def gain_of(norm_ref, group):
    return norm_ref[0, pl.ds(group, 1), :]


def shift_of(norm_ref, group):
    return norm_ref[1, pl.ds(group, 1), :]


def valid_cols(channels):
    return lax.broadcasted_iota(jnp.int32, (COLS, channels), 0) < COLS - 4


def chan_mask(limit, channels):
    return lax.broadcasted_iota(jnp.int32, (1, channels), 1) < limit


def flat(x):
    return x.reshape(x.shape[0] * x.shape[1], x.shape[2])


def mm(a, b):
    return jnp.dot(a, b, preferred_element_type=F32)


def mm_nt(a, b):
    return lax.dot_general(a, b, (((1,), (1,)), ((), ())), preferred_element_type=F32)


def mm_tn(a, b):
    return lax.dot_general(a, b, (((0,), (0,)), ((), ())), preferred_element_type=F32)


def zeros8(channels):
    return jnp.zeros((8, channels), F32)


def down(x):
    return jnp.sum(x, axis=0, keepdims=True)


OWN, OTHER, HALF, LIMIT, GATE = range(5)


def prepare(w1b, w2b, w_cur, w_up, b_even, b_odd, b_same):
    n = LANES
    for k, (y, x) in enumerate(((1, 1), (1, 2), (1, 0), (2, 1), (2, 2), (2, 0))):
        w_cur[n * k : n * (k + 1), :] = w1b[y, x]
    for k, (y, x) in enumerate(((0, 1), (0, 2), (0, 0))):
        w_up[n * k : n * (k + 1), :] = w1b[y, x]
    nothing = jnp.zeros((n, n), BF16)
    b_even[0:n, 0:n] = w1b[1, 1]
    b_even[0:n, n : 2 * n] = nothing
    b_even[n : 2 * n, 0:n] = w1b[1, 2]
    b_even[n : 2 * n, n : 2 * n] = w1b[1, 0]
    for k, top in ((0, 2), (1, 0)):
        b_odd[0:n, 2 * n * k : 2 * n * k + n] = w1b[top, 1]
        b_odd[0:n, 2 * n * k + n : 2 * n * (k + 1)] = nothing
        b_odd[n : 2 * n, 2 * n * k : 2 * n * k + n] = w1b[top, 2]
        b_odd[n : 2 * n, 2 * n * k + n : 2 * n * (k + 1)] = w1b[top, 0]
    for y in range(3):
        for x in range(3):
            b_same[y, :, n * x : n * (x + 1)] = w2b[y, x]


def widen(source, x_pad):
    rows, cols, chans = source.shape
    gap = x_pad.shape[1] - cols

    def put(i, carry):
        x_pad[i, 0:cols, :] = source[i]
        x_pad[i, cols : cols + gap, :] = jnp.zeros((gap, chans), BF16)
        return carry

    lax.fori_loop(0, rows, put, 0, unroll=4)


def first_project(x_pad, w, z):
    rows = x_pad.shape[0]
    step = rows // 4
    sums, squares = zeros8(LANES), zeros8(LANES)
    for c in range(4):
        values = mm(flat(x_pad[step * c : step * (c + 1)]), w[...])
        z[step * c : step * (c + 1)] = values.reshape(step, x_pad.shape[1], LANES)
        parts = values.reshape(-1, 8, LANES)
        sums = sums + jnp.sum(parts, axis=0)
        squares = squares + jnp.sum(parts * parts, axis=0)
    return sums, squares


def f1_own(scal, images, w, x_pad, z, part):
    widen(images.at[scal[HALF]], x_pad)
    sums, squares = first_project(x_pad, w, z)
    part[0] = sums
    part[1] = squares


def f1_other(scal, received, w, part, x_pad, z, send):
    widen(received, x_pad)
    sums, squares = first_project(x_pad, w, z)
    label = jnp.full((1, LANES), scal[OWN].astype(F32))
    spread(send, [down(sums + part[0]), down(squares + part[1]), label])


def f1_strided(scal, x_own, x_oth, w, xee, z, stats, wide):
    half = scal[HALF]
    rows = x_own.shape[0] // 2
    for k, x_pad in enumerate((x_own, x_oth)):
        first = rows * (half if k == 0 else 1 - half)

        def put(i, carry, x_pad=x_pad, first=first):
            for b in range(wide.shape[0]):
                lanes = slice(LANES * b, LANES * (b + 1))
                wide[b] = x_pad[2 * i, :, lanes].astype(F32)
                xee[first + i, :, lanes] = wide[b, pl.ds(0, COLS, stride=2), :].astype(BF16)
            return carry

        lax.fori_loop(0, rows, put, 0, unroll=2)
    total = 2 * rows
    step = total // 7
    chans = z.shape[2]
    sums, squares = zeros8(chans), zeros8(chans)
    for c in range(7):
        values = mm(flat(xee[step * c : step * (c + 1)]), w[...])
        z[step * c : step * (c + 1)] = values.reshape(step, COLS, chans)
        parts = values.reshape(-1, 8, chans)
        sums = sums + jnp.sum(parts, axis=0)
        squares = squares + jnp.sum(parts * parts, axis=0)
    stats[0] = down(sums)
    stats[1] = down(squares)


def scale_shift(got, labels, scal, norm, pixels, slot=0):
    label = scal[OWN].astype(F32)
    total = group_sum(got, labels, label)
    chans = norm.shape[2]
    count = tiled(group_count(labels, label), chans) * pixels
    mean, rstd = moments(row(total, 2 * slot), row(total, 2 * slot + 1), count)
    gain, shift = gain_of(norm, scal[OWN]), shift_of(norm, scal[OWN])
    return mean, rstd, gain, shift, count


def conv_stats(z, pieces, send):
    keep = valid_cols(LANES)[None]
    rows = z.shape[0]
    step = rows // 4
    sums, squares = zeros8(LANES), zeros8(LANES)
    for c in range(4):
        values = None
        for source, first, lane, weight in pieces:
            term = mm(flat(source[first + step * c : first + step * (c + 1), :, lane:]), weight)
            values = term if values is None else values + term
        values = jnp.where(keep, values.reshape(step, COLS, LANES), 0.0)
        z[step * c : step * (c + 1)] = values
        parts = values.reshape(-1, 8, LANES)
        sums = sums + jnp.sum(parts, axis=0)
        squares = squares + jnp.sum(parts * parts, axis=0)
    spread(send, [down(sums), down(squares)])


def f2(scal, got, z_own, z_oth, norm, w_cur, w_up, xs, z, send, labels, keeps):
    marks = got[:, :, 2 * LANES : 3 * LANES]
    labels[...] = marks
    rows = xs.shape[0] - 1
    pixels = 4.0 * rows * (COLS - 4)
    mean, rstd, gain, shift, _ = scale_shift(got, marks, scal, norm, pixels)
    keeps[0:1, :] = mean
    keeps[1:2, :] = rstd
    other = scal[OTHER].astype(F32)
    total = group_sum(got, marks, other)
    count = group_count(marks, other) * pixels
    mean_2, rstd_2 = moments(row(total, 0), row(total, 1), count)
    keeps[2:3, :] = mean_2
    keeps[3:4, :] = rstd_2
    scale = rstd * gain
    bias = shift - mean * scale
    keep = valid_cols(LANES) & chan_mask(scal[LIMIT], LANES)
    half = scal[HALF]
    xs[0] = jnp.zeros(xs.shape[1:], BF16)
    n = LANES
    for k, zz in enumerate((z_own, z_oth)):
        first = 1 + (rows // 2) * (half if k == 0 else 1 - half)

        def put(i, carry, zz=zz, first=first):
            lane = 0
            for a in (0, 1):
                for b in (0, 1):
                    v = zz[2 * i + a, pl.ds(b, COLS, stride=2), :] * scale + bias
                    act = jnp.where(keep, v * sigmoid(v), 0.0)
                    xs[first + i, :, lane : lane + n] = act.astype(BF16)
                    lane += n
                    if b == 1:
                        moved = pltpu.roll(act, 1, 0)
                        xs[first + i, :, lane : lane + n] = moved.astype(BF16)
                        lane += n
            return carry

        lax.fori_loop(0, rows // 2, put, 0, unroll=2)
    conv_stats(z, ((xs, 1, 0, w_cur[...]), (xs, 0, 3 * n, w_up[...])), send)


def expand(act, w, z, send, extra=()):
    rows, chans = z.shape[0], z.shape[2]
    step = rows // 7
    sums, squares = zeros8(chans), zeros8(chans)
    for c in range(7):
        values = mm(flat(act[step * c : step * (c + 1)]), w[...])
        z[step * c : step * (c + 1)] = values.reshape(step, COLS, chans)
        parts = values.reshape(-1, 8, chans)
        sums = sums + jnp.sum(parts, axis=0)
        squares = squares + jnp.sum(parts * parts, axis=0)
    spread(send, [down(sums), down(squares), *extra])


def activate(scal, got, labels, z_in, norm, act, keeps):
    rows = z_in.shape[0]
    pixels = 1.0 * rows * (COLS - 4)
    mean, rstd, gain, shift, _ = scale_shift(got, labels[...], scal, norm, pixels)
    keeps[0:1, :] = mean
    keeps[1:2, :] = rstd
    scale = rstd * gain
    bias = shift - mean * scale
    keep = valid_cols(LANES) & chan_mask(scal[LIMIT], LANES)

    def put(i, carry):
        v = z_in[i] * scale + bias
        act[i] = jnp.where(keep, v * sigmoid(v), 0.0).astype(BF16)
        return carry

    lax.fori_loop(0, rows, put, 0, unroll=4)


def f3(scal, got, labels, z_in, norm, w, stats_p, act, z, send, keeps):
    activate(scal, got, labels, z_in, norm, act, keeps)
    expand(act, w, z, send, (stats_p[0], stats_p[1]))


def f4(scal, got, labels, zc, zp, norm_c, norm_p, w, joined, slope, z, send, keeps):
    rows, chans = zc.shape[0], zc.shape[2]
    pixels = 1.0 * rows * (COLS - 4)
    label = scal[OWN].astype(F32)
    marks = labels[...]
    total = group_sum(got, marks, label)
    count = tiled(group_count(marks, label), chans) * pixels
    mean_c, rstd_c = moments(row(total, 0), row(total, 1), count)
    mean_p, rstd_p = moments(row(total, 2), row(total, 3), count)
    for k, v in enumerate((mean_c, rstd_c, mean_p, rstd_p)):
        keeps[k : k + 1, :] = v
    group = scal[OWN]
    scale_c = rstd_c * gain_of(norm_c, group)
    scale_p = rstd_p * gain_of(norm_p, group)
    bias = (shift_of(norm_c, group) - mean_c * scale_c) + (
        shift_of(norm_p, group) - mean_p * scale_p
    )
    keep = valid_cols(chans)

    def put(i, carry):
        v = zc[i] * scale_c + zp[i] * scale_p + bias
        s = sigmoid(v)
        joined[i] = jnp.where(keep, v * s, 0.0).astype(BF16)
        slope[i] = s * (1.0 + v * (1.0 - s))
        return carry

    lax.fori_loop(0, rows, put, 0, unroll=2)
    step = rows // 4
    sums, squares = zeros8(LANES), zeros8(LANES)
    for c in range(4):
        values = mm(flat(joined[step * c : step * (c + 1)]), w[...])
        z[step * c : step * (c + 1)] = values.reshape(step, COLS, LANES)
        parts = values.reshape(-1, 8, LANES)
        sums = sums + jnp.sum(parts, axis=0)
        squares = squares + jnp.sum(parts * parts, axis=0)
    spread(send, [down(sums), down(squares)])


def f5(scal, got, labels, z_in, norm, w, x3, z, send, keeps):
    rows = z_in.shape[0]
    pixels = 1.0 * rows * (COLS - 4)
    mean, rstd, gain, shift, _ = scale_shift(got, labels[...], scal, norm, pixels)
    keeps[0:1, :] = mean
    keeps[1:2, :] = rstd
    scale = rstd * gain
    bias = shift - mean * scale
    keep = valid_cols(LANES) & chan_mask(scal[LIMIT], LANES)
    x3[0] = jnp.zeros(x3.shape[1:], BF16)
    x3[rows + 1] = jnp.zeros(x3.shape[1:], BF16)
    n = LANES

    def put(i, carry):
        v = z_in[i] * scale + bias
        act = jnp.where(keep, v * sigmoid(v), 0.0)
        x3[i + 1, :, 0:n] = pltpu.roll(act, 1, 0).astype(BF16)
        x3[i + 1, :, n : 2 * n] = act.astype(BF16)
        x3[i + 1, :, 2 * n : 3 * n] = pltpu.roll(act, COLS - 1, 0).astype(BF16)
        return carry

    lax.fori_loop(0, rows, put, 0, unroll=2)
    conv_stats(z, tuple((x3, y, 0, w[y]) for y in range(3)), send)


def f6(scal, got, labels, z_in, norm, w, act, z, send, keeps):
    activate(scal, got, labels, z_in, norm, act, keeps)
    expand(act, w, z, send)


def b7(scal, got, labels, joined, z, norm, cot, result, grad_pre, send, keeps):
    rows, chans = z.shape[0], z.shape[2]
    cols = COLS - 4
    pixels = 1.0 * rows * cols
    mean, rstd, gain, shift, _ = scale_shift(got, labels[...], scal, norm, pixels)
    keeps[0:1, :] = mean
    keeps[1:2, :] = rstd
    gate = 0.25 * scal[GATE].astype(F32)
    scale = rstd * gain * gate
    bias = (shift - mean * rstd * gain) * gate

    def put(i, carry):
        sums, products = carry
        zz = z[i, 0:cols, :]
        v = joined[i, 0:cols, :].astype(F32) + zz * scale + bias
        s = sigmoid(v)
        result[i] = (v * s).astype(BF16)
        g = cot[i].astype(F32) * (s * (1.0 + v * (1.0 - s)))
        grad_pre[i, 0:cols, :] = g
        grad_pre[i, cols:COLS, :] = jnp.zeros((COLS - cols, chans), F32)
        return sums + down(g), products + down(g * (zz - mean))

    start = jnp.zeros((1, chans), F32)
    sums, products = lax.fori_loop(0, rows, put, (start, start), unroll=2)
    spread(send, [sums * gate, products * rstd * gate])


def backward_norm(scal, got, labels, norm, keeps, pixels, grad_norm, slots=(0, 1)):
    marks = labels[...]
    chans = norm.shape[2]
    own_shift = jnp.zeros((1, chans), F32)
    own_gain = jnp.zeros((1, chans), F32)
    group = scal[OWN]
    for g in range(norm.shape[1]):
        total = group_sum(got, marks, float(g))
        shift_sum, gain_sum = row(total, slots[0]), row(total, slots[1])
        grad_norm[0, g : g + 1, :] = gain_sum
        grad_norm[1, g : g + 1, :] = shift_sum
        mine = group == g
        own_shift = jnp.where(mine, shift_sum, own_shift)
        own_gain = jnp.where(mine, gain_sum, own_gain)
    count = tiled(group_count(marks, group.astype(F32)), chans) * pixels
    mean, rstd = keeps[0:1, :], keeps[1:2, :]
    a = rstd * gain_of(norm, group)
    return mean, a, -(a * rstd) * own_gain / count, -a * own_shift / count


def slope_sums(scal, d, z_in, norm, keeps, dout, send):
    rows = z_in.shape[0]
    mean, rstd = keeps[0:1, :], keeps[1:2, :]
    group = scal[OWN]
    scale = rstd * gain_of(norm, group)
    bias = shift_of(norm, group) - mean * scale
    keep = valid_cols(LANES) & chan_mask(scal[LIMIT], LANES)

    def put(i, carry):
        sums, products = carry
        zz = z_in[i]
        v = zz * scale + bias
        s = sigmoid(v)
        g = jnp.where(keep, d[i] * (s * (1.0 + v * (1.0 - s))), 0.0)
        dout[i] = g
        return sums + fold(g), products + fold(g * (zz - mean))

    sums, products = lax.fori_loop(
        0, rows, put, (zeros8(LANES), zeros8(LANES)), unroll=4
    )
    spread(send, [down(sums), down(products) * rstd])


def b8(
    scal, got, labels, grad_pre, z, norm, keeps, w, z_in, norm_in, keeps_in,
    dz, dout, send, grad_norm, d,
):
    rows, chans = z.shape[0], z.shape[2]
    pixels = 1.0 * rows * (COLS - 4)
    mean, a, b, c = backward_norm(scal, got, labels, norm, keeps, pixels, grad_norm)
    a = a * (0.25 * scal[GATE].astype(F32))
    keep = valid_cols(chans)

    def put(i, carry):
        v = a * grad_pre[i] + b * (z[i] - mean) + c
        dz[i] = jnp.where(keep, v, 0.0).astype(BF16)
        return carry

    lax.fori_loop(0, rows, put, 0, unroll=2)
    d[...] = mm_nt(flat(dz[...]), w[...]).reshape(d.shape)
    slope_sums(scal, d, z_in, norm_in, keeps_in, dout, send)


def b9(
    scal, got, labels, dout_in, z, norm, keeps, b_same, z_in, norm_in, keeps_in,
    dz, dout, send, grad_norm, d3, d,
):
    rows = z.shape[0]
    pixels = 1.0 * rows * (COLS - 4)
    mean, a, b, c = backward_norm(scal, got, labels, norm, keeps, pixels, grad_norm)
    keep = valid_cols(LANES)
    n = LANES
    d3[0] = jnp.zeros(d3.shape[1:], BF16)
    d3[rows + 1] = jnp.zeros(d3.shape[1:], BF16)

    def put(i, carry):
        v = a * dout_in[i] + b * (z[i] - mean) + c
        v = jnp.where(keep, v, 0.0)
        d3[i + 1, :, 0:n] = pltpu.roll(v, COLS - 1, 0).astype(BF16)
        low = v.astype(BF16)
        d3[i + 1, :, n : 2 * n] = low
        dz[i] = low
        d3[i + 1, :, 2 * n : 3 * n] = pltpu.roll(v, 1, 0).astype(BF16)
        return carry

    lax.fori_loop(0, rows, put, 0, unroll=2)
    step = rows // 4
    for k in range(4):
        value = None
        for y in range(3):
            first = 2 - y + step * k
            term = mm_nt(flat(d3[first : first + step]), b_same[y])
            value = term if value is None else value + term
        d[step * k : step * (k + 1)] = value.reshape(step, COLS, LANES)
    slope_sums(scal, d, z_in, norm_in, keeps_in, dout, send)


def b10(
    scal, got, labels, dout_in, z, norm, keeps, w, grad_pre, slope, zc, zp, keeps_cp,
    dz, grad_pre_2, send, grad_norm, d,
):
    rows, chans = zc.shape[0], zc.shape[2]
    pixels = 1.0 * rows * (COLS - 4)
    mean, a, b, c = backward_norm(scal, got, labels, norm, keeps, pixels, grad_norm)
    keep = valid_cols(LANES)

    def put(i, carry):
        v = a * dout_in[i] + b * (z[i] - mean) + c
        dz[i] = jnp.where(keep, v, 0.0).astype(BF16)
        return carry

    lax.fori_loop(0, rows, put, 0, unroll=4)
    d[...] = mm_nt(flat(dz[...]), w[...]).reshape(d.shape)
    mean_c, rstd_c, mean_p, rstd_p = (keeps_cp[k : k + 1, :] for k in range(4))

    def sum_up(i, carry):
        sums, prod_c, prod_p = carry
        g = (grad_pre[i] + d[i]).astype(BF16).astype(F32) * slope[i]
        grad_pre_2[i] = g
        return (
            sums + fold(g),
            prod_c + fold(g * (zc[i] - mean_c)),
            prod_p + fold(g * (zp[i] - mean_p)),
        )

    start = zeros8(chans)
    sums, prod_c, prod_p = lax.fori_loop(0, rows, sum_up, (start, start, start), unroll=2)
    spread(send, [down(sums), down(prod_c) * rstd_c, down(prod_p) * rstd_p])


def b11(
    scal, got, labels, grad_pre_2, zc, zp, norm_c, norm_p, keeps_cp, w, z_in, norm_in, keeps_in,
    dz_c, dz_p, dout, send, grad_norm_c, grad_norm_p, d,
):
    rows, chans = zc.shape[0], zc.shape[2]
    pixels = 1.0 * rows * (COLS - 4)
    mean_c, a_c, b_c, c_c = backward_norm(
        scal, got, labels, norm_c, keeps_cp.at[0:2], pixels, grad_norm_c, (0, 1)
    )
    mean_p, a_p, b_p, c_p = backward_norm(
        scal, got, labels, norm_p, keeps_cp.at[2:4], pixels, grad_norm_p, (0, 2)
    )
    keep = valid_cols(chans)

    def put(i, carry):
        g = grad_pre_2[i]
        v = a_c * g + b_c * (zc[i] - mean_c) + c_c
        dz_c[i] = jnp.where(keep, v, 0.0).astype(BF16)
        v = a_p * g + b_p * (zp[i] - mean_p) + c_p
        dz_p[i] = jnp.where(keep, v, 0.0).astype(BF16)
        return carry

    lax.fori_loop(0, rows, put, 0, unroll=2)
    d[...] = mm_nt(flat(dz_c[...]), w[...]).reshape(d.shape)
    slope_sums(scal, d, z_in, norm_in, keeps_in, dout, send)


def b12(
    scal, got, labels, dout_in, z, norm, keeps, b_even, b_odd, z_own, z_oth, norm_in, keeps_in,
    dz, dn_own, dn_oth, send, grad_norm, d2, de, do, wide,
):
    rows = z.shape[0]
    pixels = 1.0 * rows * (COLS - 4)
    mean, a, b, c = backward_norm(scal, got, labels, norm, keeps, pixels, grad_norm)
    keep = valid_cols(LANES)
    n = LANES
    d2[rows] = jnp.zeros(d2.shape[1:], BF16)

    def put(i, carry):
        v = a * dout_in[i] + b * (z[i] - mean) + c
        v = jnp.where(keep, v, 0.0)
        low = v.astype(BF16)
        dz[i] = low
        d2[i, :, 0:n] = low
        d2[i, :, n : 2 * n] = pltpu.roll(v, COLS - 1, 0).astype(BF16)
        return carry

    lax.fori_loop(0, rows, put, 0, unroll=4)
    step = rows // 4
    for k in range(4):
        here = flat(d2[step * k : step * (k + 1)])
        below = flat(d2[step * k + 1 : step * (k + 1) + 1])
        de[step * k : step * (k + 1)] = mm_nt(here, b_even[...]).reshape(step, COLS, 2 * n)
        odd = mm_nt(here, b_odd[:, 0 : 2 * n]) + mm_nt(below, b_odd[:, 2 * n : 4 * n])
        do[step * k : step * (k + 1)] = odd.reshape(step, COLS, 2 * n)
    mean_1, rstd_1 = keeps_in[0:1, :], keeps_in[1:2, :]
    group = scal[OWN]
    scale = rstd_1 * gain_of(norm_in, group)
    bias = shift_of(norm_in, group) - mean_1 * scale
    keep = valid_cols(LANES) & chan_mask(scal[LIMIT], LANES)
    half = scal[HALF]
    totals = (zeros8(n), zeros8(n))
    for k, (zz, dn) in enumerate(((z_own, dn_own), (z_oth, dn_oth))):
        first = (rows // 2) * (half if k == 0 else 1 - half)

        def emit(i, carry, zz=zz, dn=dn, first=first):
            sums, products = carry
            for ra in (0, 1):
                planes = (de, do)[ra]
                for cb in (0, 1):
                    zv = zz[2 * i + ra, pl.ds(cb, COLS, stride=2), :]
                    v = zv * scale + bias
                    s = sigmoid(v)
                    g = planes[first + i, :, n * cb : n * (cb + 1)]
                    g = jnp.where(keep, g * (s * (1.0 + v * (1.0 - s))), 0.0)
                    sums = sums + fold(g)
                    products = products + fold(g * (zv - mean_1))
                    wide[ra, pl.ds(cb, COLS, stride=2), :] = g
                dn[2 * i + ra] = wide[ra].astype(BF16)
            return sums, products

        totals = lax.fori_loop(0, rows // 2, emit, totals, unroll=2)
    spread(send, [down(totals[0]), down(totals[1]) * rstd_1])


def b13(
    scal, got, labels, norm, keeps, images, w, z_own, dn_own, dn_oth, gs_own, gs_oth,
    grad, grad_norm, x_pad, z_oth, dz, wide,
):
    rows, cols = images.shape[1], images.shape[2]
    half = scal[HALF]
    pixels = 2.0 * rows * cols
    marks = labels[...]
    widen(images.at[1 - half], x_pad)
    for c in range(4):
        step = rows // 4
        values = mm(flat(x_pad[step * c : step * (c + 1)]), w[...])
        z_oth[step * c : step * (c + 1)] = values.reshape(step, x_pad.shape[1], LANES)
    totals = []
    for g in range(norm.shape[1]):
        total = group_sum(got, marks, float(g))
        totals.append((row(total, 0), row(total, 1)))
        grad_norm[0, g : g + 1, :] = totals[g][1]
        grad_norm[1, g : g + 1, :] = totals[g][0]
    keep = lax.broadcasted_iota(jnp.int32, (x_pad.shape[1], LANES), 0) < cols
    for k, (z, dn, gs) in enumerate(((z_own, dn_own, gs_own), (z_oth, dn_oth, gs_oth))):
        group = scal[OWN if k == 0 else OTHER]
        shift_sum, gain_sum = totals[0]
        for g in range(1, norm.shape[1]):
            shift_sum = jnp.where(group == g, totals[g][0], shift_sum)
            gain_sum = jnp.where(group == g, totals[g][1], gain_sum)
        count = group_count(marks, group.astype(F32)) * pixels
        mean, rstd = keeps[2 * k : 2 * k + 1, :], keeps[2 * k + 1 : 2 * k + 2, :]
        a = rstd * gain_of(norm, group)
        b = -(a * rstd) * gain_sum / count
        c = -a * shift_sum / count

        def put(i, carry, z=z, dn=dn, mean=mean, a=a, b=b, c=c):
            v = a * dn[i].astype(F32) + b * (z[i] - mean) + c
            dz[i] = jnp.where(keep, v, 0.0).astype(BF16)
            return carry

        lax.fori_loop(0, rows, put, 0, unroll=2)
        step = rows // 4
        for q in range(4):
            low = flat(dz[step * q : step * (q + 1)])
            for p in range(wide.shape[0]):
                values = mm_nt(low, w[LANES * p : LANES * (p + 1), :])
                wide[p, step * q : step * (q + 1)] = values.reshape(step, -1, LANES)
        place = half if k == 0 else 1 - half

        def emit(i, carry, gs=gs, place=place):
            even = pl.ds(0, COLS, stride=2)
            for p in range(wide.shape[0]):
                lanes = slice(LANES * p, LANES * (p + 1))
                wide[p, 2 * i, even, :] = wide[p, 2 * i, even, :] + gs[i, :, lanes].astype(F32)
                grad[place, 2 * i, :, lanes] = wide[p, 2 * i, 0:cols, :].astype(BF16)
                grad[place, 2 * i + 1, :, lanes] = wide[p, 2 * i + 1, 0:cols, :].astype(BF16)
            return carry

        lax.fori_loop(0, rows // 2, emit, 0, unroll=2)


def g_2c(act, dz, out):
    out[...] = mm_tn(flat(act[...]), flat(dz[...]))


def g_2b(x3, dz, out):
    rows = dz.shape[0]
    low = flat(dz[...])
    for y in range(3):
        got = mm_tn(flat(x3[y : y + rows]), low)
        out[y] = got.reshape(3, LANES, LANES)


def g_2a(joined, dz, out):
    out[...] = mm_tn(flat(joined[...]), flat(dz[...]))


def g_1(scal, act, dz_c, xee, dz_p, w_p, out_c, out_p, gs_own, gs_oth):
    out_c[...] = mm_tn(flat(act[...]), flat(dz_c[...]))
    out_p[...] = mm_tn(flat(xee[...]), flat(dz_p[...]))
    half = scal[HALF]
    rows = gs_own.shape[0]
    for k, gs in enumerate((gs_own, gs_oth)):
        first = rows * (half if k == 0 else 1 - half)
        got = mm_nt(flat(dz_p[pl.ds(first, rows)]), w_p[...])
        gs[...] = got.reshape(gs.shape).astype(BF16)


def g_1b(xs, dz, out):
    rows = dz.shape[0]
    low = flat(dz[...])
    n = LANES
    cur = mm_tn(flat(xs[1 : rows + 1]), low)
    for k, (y, x) in enumerate(((1, 1), (1, 2), (1, 0), (2, 1), (2, 2), (2, 0))):
        out[y, x] = cur[n * k : n * (k + 1)]
    up = mm_tn(flat(xs[0:rows, :, 3 * n : 6 * n]), low)
    for k, (y, x) in enumerate(((0, 1), (0, 2), (0, 0))):
        out[y, x] = up[n * k : n * (k + 1)]


def g_1a(scal, got, labels, norm, keeps, z_own, z_oth, dn_own, dn_oth, x_own, x_oth, out, dz):
    rows = z_own.shape[0]
    cols = 2 * (COLS - 4)
    pixels = 2.0 * rows * cols
    marks = labels[...]
    group = scal[OWN]
    total = group_sum(got, marks, group.astype(F32))
    count = group_count(marks, group.astype(F32)) * pixels
    mean, rstd = keeps[0:1, :], keeps[1:2, :]
    a = rstd * gain_of(norm, group)
    b = -(a * rstd) * row(total, 1) / count
    c = -a * row(total, 0) / count
    keep = lax.broadcasted_iota(jnp.int32, (z_own.shape[1], LANES), 0) < cols
    value = None
    for z, dn, x in ((z_own, dn_own, x_own), (z_oth, dn_oth, x_oth)):

        def put(i, carry, z=z, dn=dn):
            v = a * dn[i].astype(F32) + b * (z[i] - mean) + c
            dz[i] = jnp.where(keep, v, 0.0).astype(BF16)
            return carry

        lax.fori_loop(0, rows, put, 0, unroll=2)
        term = mm_tn(flat(x[...]), flat(dz[...]))
        value = term if value is None else value + term
    out[...] = value


def gather(send):
    return lax.all_to_all(send, AXES, 0, 0)


def reduce_weights(grads, devices):
    shapes = [g.shape for g in grads]
    sizes = [g.size for g in grads]
    total = sum(sizes)
    unit = devices * 16 * LANES
    padded = -(-total // unit) * unit
    one = jnp.concatenate(
        [g.astype(BF16).reshape(-1) for g in grads] + [jnp.zeros((padded - total,), BF16)]
    )
    parts = one.reshape(devices, padded // devices // LANES, LANES)
    mine = jnp.sum(lax.all_to_all(parts, AXES, 0, 0).astype(F32), axis=0).astype(BF16)
    everyone = lax.all_to_all(jnp.broadcast_to(mine[None], parts.shape), AXES, 0, 0)
    flat_sum = everyone.reshape(-1)
    outs, at = [], 0
    for shape, size in zip(shapes, sizes):
        outs.append(flat_sum[at : at + size].astype(F32).reshape(shape))
        at += size
    return outs


def swap(block):
    return lax.ppermute(block, "rows", [(0, 1), (1, 0)])


def body(
    images, w_1a, w_1b, w_1c, w_1p, w_2a, w_2b, w_2c,
    norm_1a, norm_1b, norm_1c, norm_1p, norm_2a, norm_2b, norm_2c,
    cotangent, group, width, gate,
):
    devices = lax.axis_size("rows") * lax.axis_size("batch")
    half = lax.axis_index("rows")
    own = jnp.take(group, half)
    other = jnp.take(group, 1 - half)
    inner, outer, inputs = w_1a.shape[1], w_1c.shape[1], w_1a.shape[0]
    scal = jnp.stack(
        [own, other, half.astype(jnp.int32), inner // 4 * jnp.take(width, own), jnp.take(gate, own)]
        + [jnp.int32(0)] * 3
    ).astype(jnp.int32)
    rows = cotangent.shape[1]
    cols_in = 2 * COLS
    n, m = LANES, devices

    def send(stats, channels=LANES):
        return ((m, channels // LANES, stats * LANES), F32)

    def maps(channels, dtype=F32):
        return ((rows, COLS, channels), dtype)

    def scratch(channels, dtype=F32):
        return pltpu.VMEM((rows, COLS, channels), dtype)

    def params(*arrays):
        return [((2, a.shape[1], a.shape[2]), F32) for a in arrays]

    def mean_scale(channels, count=1):
        return ((2 * count, channels), F32)

    received = swap(lax.dynamic_index_in_dim(images, 1 - half, 0, keepdims=False))
    w_cur, w_up, b_even, b_odd, b_same = stage(
        prepare,
        [((6 * n, n), BF16), ((3 * n, n), BF16), ((2 * n, 2 * n), BF16), ((2 * n, 4 * n), BF16),
         ((3, n, 3 * n), BF16)],
        smem=(),
    )(w_1b, w_2b)
    wide_in = ((rows, cols_in, inputs), BF16)
    wide_z = ((rows, cols_in, n), F32)
    x_own, z_own, part = stage(f1_own, [wide_in, wide_z, ((2, 8, n), F32)])(scal, images, w_1a)
    x_oth, z_oth, s1 = stage(f1_other, [wide_in, wide_z, send(3)])(scal, received, w_1a, part)
    g1 = gather(s1)
    xee, z_1p, stats_1p = stage(
        f1_strided,
        [maps(inputs, BF16), maps(outer), ((2, 1, outer), F32)],
        [pltpu.VMEM((inputs // n, cols_in, n), F32)],
    )(scal, x_own, x_oth, w_1p)
    xs, z_1b, s2, labels, k_1a = stage(
        f2,
        [((rows + 1, COLS, 6 * n), BF16), maps(n), send(2), ((m, 1, n), F32), mean_scale(n, 2)],
    )(scal, g1, z_own, z_oth, norm_1a, w_cur, w_up)
    g2 = gather(s2)
    act_1b, z_1c, s3, k_1b = stage(
        f3, [maps(n, BF16), maps(outer), send(4, outer), mean_scale(n)]
    )(scal, g2, labels, z_1b, norm_1b, w_1c, stats_1p)
    g3 = gather(s3)
    joined, slope, z_2a, s4, k_cp = stage(
        f4, [maps(outer, BF16), maps(outer), maps(n), send(2), mean_scale(outer, 2)]
    )(scal, g3, labels, z_1c, z_1p, norm_1c, norm_1p, w_2a)
    g4 = gather(s4)
    x3, z_2b, s5, k_2a = stage(
        f5, [((rows + 2, COLS, 3 * n), BF16), maps(n), send(2), mean_scale(n)]
    )(scal, g4, labels, z_2a, norm_2a, w_2b.reshape(3, 3 * n, n))
    g5 = gather(s5)
    act_2b, z_2c, s6, k_2b = stage(
        f6, [maps(n, BF16), maps(outer), send(2, outer), mean_scale(n)]
    )(scal, g5, labels, z_2b, norm_2b, w_2c)
    g6 = gather(s6)
    result, grad_pre, s7, k_2c = stage(
        b7, [(cotangent.shape[1:], BF16), maps(outer), send(2, outer), mean_scale(outer)]
    )(scal, g6, labels, joined, z_2c, norm_2c, cotangent[0])
    g7 = gather(s7)
    dz_2c, dout_2b, s8, grad_norm_2c = stage(
        b8, [maps(outer, BF16), maps(n), send(2), *params(norm_2c)], [scratch(n)]
    )(scal, g7, labels, grad_pre, z_2c, norm_2c, k_2c, w_2c, z_2b, norm_2b, k_2b)
    g8 = gather(s8)
    (grad_w_2c,) = stage(g_2c, [(w_2c.shape, F32)], smem=())(act_2b, dz_2c)
    dz_2b, dout_2a, s9, grad_norm_2b = stage(
        b9, [maps(n, BF16), maps(n), send(2), *params(norm_2b)],
        [pltpu.VMEM((rows + 2, COLS, 3 * n), BF16), scratch(n)],
    )(scal, g8, labels, dout_2b, z_2b, norm_2b, k_2b, b_same, z_2a, norm_2a, k_2a)
    g9 = gather(s9)
    (grad_w_2b,) = stage(g_2b, [(w_2b.shape, F32)], smem=())(x3, dz_2b)
    dz_2a, grad_pre_2, s10, grad_norm_2a = stage(
        b10, [maps(n, BF16), maps(outer), send(3, outer), *params(norm_2a)], [scratch(outer)]
    )(scal, g9, labels, dout_2a, z_2a, norm_2a, k_2a, w_2a, grad_pre, slope, z_1c, z_1p, k_cp)
    g10 = gather(s10)
    (grad_w_2a,) = stage(g_2a, [(w_2a.shape, F32)], smem=())(joined, dz_2a)
    dz_1c, dz_1p, dout_1b, s11, grad_norm_1c, grad_norm_1p = stage(
        b11, [maps(outer, BF16), maps(outer, BF16), maps(n), send(2), *params(norm_1c, norm_1p)],
        [scratch(n)],
    )(scal, g10, labels, grad_pre_2, z_1c, z_1p, norm_1c, norm_1p, k_cp, w_1c, z_1b, norm_1b, k_1b)
    g11 = gather(s11)
    half_map = ((rows // 2, COLS, inputs), BF16)
    grad_w_1c, grad_w_1p, gs_own, gs_send = stage(
        g_1, [(w_1c.shape, F32), (w_1p.shape, F32), half_map, half_map]
    )(scal, act_1b, dz_1c, xee, dz_1p, w_1p)
    gs_oth = swap(gs_send)
    half_in = ((rows, cols_in, n), BF16)
    dz_1b, dn_own, dn_send, s12, grad_norm_1b = stage(
        b12, [maps(n, BF16), half_in, half_in, send(2), *params(norm_1b)],
        [pltpu.VMEM((rows + 1, COLS, 2 * n), BF16), scratch(2 * n), scratch(2 * n),
         pltpu.VMEM((2, cols_in, n), F32)],
    )(scal, g11, labels, dout_1b, z_1b, norm_1b, k_1b, b_even, b_odd, z_own, z_oth, norm_1a, k_1a)
    dn_oth = swap(dn_send)
    g12 = gather(s12)
    (grad_w_1b,) = stage(g_1b, [(w_1b.shape, F32)], smem=())(xs, dz_1b)
    grad_images, grad_norm_1a = stage(
        b13, [(images.shape, BF16), *params(norm_1a)],
        [pltpu.VMEM(wide_in[0], BF16), pltpu.VMEM(wide_z[0], F32), pltpu.VMEM(half_in[0], BF16),
         pltpu.VMEM((inputs // n, rows, cols_in, n), F32)],
    )(scal, g12, labels, norm_1a, k_1a, images, w_1a, z_own, dn_own, dn_oth, gs_own, gs_oth)
    (grad_w_1a,) = stage(g_1a, [(w_1a.shape, F32)], [pltpu.VMEM(half_in[0], BF16)])(
        scal, g12, labels, norm_1a, k_1a, z_own, z_oth, dn_own, dn_send, x_own, x_oth
    )
    totals = reduce_weights(
        (grad_w_1a, grad_w_1b, grad_w_1c, grad_w_1p, grad_w_2a, grad_w_2b, grad_w_2c), devices
    )
    return (
        result[None], grad_images, *totals,
        grad_norm_1a, grad_norm_1b, grad_norm_1c, grad_norm_1p,
        grad_norm_2a, grad_norm_2b, grad_norm_2c,
    )


def solution(mesh):
    return jax.shard_map(
        body,
        mesh=mesh,
        in_specs=(
            P("batch", "rows", None, None),
            *[P()] * 14,
            P(("batch", "rows"), None, None, None),
            P("batch"),
            P(),
            P(),
        ),
        out_specs=(
            P(("batch", "rows"), None, None, None),
            P("batch", "rows", None, None),
            *[P()] * 14,
        ),
        check_vma=False,
    )
```

profile of v0, /device:TPU:0, one launch (start us, length us, event | category | flops | bytes accessed | tf_op | source)
XLA Modules:
  0.0 306.1 jit_solution(16791134802759984060)
XLA Ops:
  0.7 2.2 dynamic-slice_bitcast_fusion
  9.9 2.3 f1_other.1
  12.2 7.0 %all-to-all-start = ((f32[32,1,384]{2,1,0:T(1,128)}), f32[32,1,384]{2,1,0:T(1,128)S(1)}, u32[]{:S(2)}, u32[]{:S(2)}) async-start(f32[32,1,384]{2,1,0:T(1,128)} %get-tuple-element.86), calls=%async_computation | async-start | bytes 98304 | tf_op jit(solution)/shard_map/all_to_all | solution.py:758
  22.7 3.7 %all-to-all-done.got = f32[32,1,384]{2,1,0:T(1,128)S(1)} async-done(((f32[32,1,384]{2,1,0:T(1,128)}), f32[32,1,384]{2,1,0:T(1,128)S(1)}, u32[]{:S(2)}, u32[]{:S(2)}) %all-to-all-start) | async-done | bytes 49184 | tf_op jit(solution)/shard_map/all_to_all | solution.py:758
  29.7 2.1 f2.1
  34.0 3.3 %all-to-all-start.1 = ((f32[32,1,256]{2,1,0:T(1,128)}), f32[32,1,256]{2,1,0:T(1,128)}, u32[]{:S(2)}, u32[]{:S(2)}) async-start(f32[32,1,256]{2,1,0:T(1,128)} %copy-done.98), calls=%async_computation.1 | async-start | bytes 65536 | tf_op jit(solution)/shard_map/all_to_all | solution.py:758
  50.1 4.0 %all-to-all-start.2 = ((f32[32,4,512]{2,1,0:T(4,128)}), f32[32,4,512]{2,1,0:T(4,128)S(1)}, u32[]{:S(2)}, u32[]{:S(2)}) async-start(f32[32,4,512]{2,1,0:T(4,128)} %copy-done.70), calls=%async_computation.2 | async-start | bytes 524288 | tf_op jit(solution)/shard_map/all_to_all | solution.py:758
  55.5 9.8 %all-to-all-done.2.got = f32[32,4,512]{2,1,0:T(4,128)S(1)} async-done(((f32[32,4,512]{2,1,0:T(4,128)}), f32[32,4,512]{2,1,0:T(4,128)S(1)}, u32[]{:S(2)}, u32[]{:S(2)}) %all-to-all-start.2) | async-done | bytes 262176 | tf_op jit(solution)/shard_map/all_to_all | solution.py:758
  67.7 2.6 f4.1
  73.8 2.6 all-to-all-start.3
  76.4 7.2 %all-to-all-done.3.got = f32[32,1,256]{2,1,0:T(1,128)S(1)} async-done(((f32[32,1,256]{2,1,0:T(1,128)}), f32[32,1,256]{2,1,0:T(1,128)S(1)}, u32[]{:S(2)}, u32[]{:S(2)}) %all-to-all-start.3) | async-done | bytes 32800 | tf_op jit(solution)/shard_map/all_to_all | solution.py:758
  89.7 2.6 all-to-all-start.4
  93.0 6.5 %all-to-all-done.4.got = f32[32,1,256]{2,1,0:T(1,128)S(1)} async-done(((f32[32,1,256]{2,1,0:T(1,128)}), f32[32,1,256]{2,1,0:T(1,128)S(1)}, u32[]{:S(2)}, u32[]{:S(2)}) %all-to-all-start.4) | async-done | bytes 32800 | tf_op jit(solution)/shard_map/all_to_all | solution.py:758
  104.3 2.6 all-to-all-start.5
  107.6 7.2 %all-to-all-done.5.got = f32[32,4,256]{2,1,0:T(4,128)S(1)} async-done(((f32[32,4,256]{2,1,0:T(4,128)}), f32[32,4,256]{2,1,0:T(4,128)S(1)}, u32[]{:S(2)}, u32[]{:S(2)}) %all-to-all-start.5) | async-done | bytes 131104 | tf_op jit(solution)/shard_map/all_to_all | solution.py:758
  118.6 3.0 b7.1
  121.7 9.8 %all_to_all.70.got = f32[32,4,256]{2,1,0:T(4,128)S(1)} all-to-all(f32[32,4,256]{2,1,0:T(4,128)S(1)} %get-tuple-element.108), channel_id=1, replica_groups=mesh['rows'=2,'batch'=16] {'rows','batch'}, dimensions={0} | all-to-all | bytes 262144 | tf_op jit(solution)/shard_map/all_to_all | solution.py:758
  134.1 9.2 %all_to_all.71.got = f32[32,1,256]{2,1,0:T(1,128)S(1)} all-to-all(f32[32,1,256]{2,1,0:T(1,128)S(1)} %get-tuple-element.112), channel_id=1, replica_groups=mesh['rows'=2,'batch'=16] {'rows','batch'}, dimensions={0} | all-to-all | bytes 65536 | tf_op jit(solution)/shard_map/all_to_all | solution.py:758
  146.1 8.9 %all_to_all.72.got = f32[32,1,256]{2,1,0:T(1,128)S(1)} all-to-all(f32[32,1,256]{2,1,0:T(1,128)S(1)} %get-tuple-element.116), channel_id=1, replica_groups=mesh['rows'=2,'batch'=16] {'rows','batch'}, dimensions={0} | all-to-all | bytes 65536 | tf_op jit(solution)/shard_map/all_to_all | solution.py:758
  155.0 2.8 b10.1
  160.4 2.8 all-to-all-start.9
  169.2 3.6 %all-to-all-done.9.got = f32[32,4,384]{2,1,0:T(4,128)S(1)} async-done(((f32[32,4,384]{2,1,0:T(4,128)}), f32[32,4,384]{2,1,0:T(4,128)S(1)}, u32[]{:S(2)}, u32[]{:S(2)}) %all-to-all-start.9) | async-done | bytes 196640 | tf_op jit(solution)/shard_map/all_to_all | solution.py:758
  178.3 2.5 b11.1
  185.2 2.6 all-to-all-start.10
  196.4 3.5 %b12.1 = (bf16[28,32,128]{2,1,0:T(8,128)(2,1)S(1)}, bf16[28,64,128]{2,1,0:T(8,128)(2,1)S(1)}, bf16[28,64,128]{2,1,0:T(8,128)(2,1)S(1)}, f32[32,1,256]{2,1,0:T(1,128)}, f32[2,3,128]{2,1,0:T(4,128)S(1)}) custom-call(s32[8]{0:T(128)S(1)} %stack.23.scal, f32[32,1,256]{2,1,0:T(1,128)S(1)} %all-to-all-done.10.got, f32[32,1,128]{2,1,0:T(1,128)S(1)} %get-tuple-element.92.labels, ...), custom_call_target="tpu_custom_call" | custom-call | bytes 4194304 | tf_op jit(solution)/shard_map/b12/pallas_call | solution.py:25
  202.1 5.8 %all-to-all-start.11 = ((f32[32,1,256]{2,1,0:T(1,128)}), f32[32,1,256]{2,1,0:T(1,128)S(1)}, u32[]{:S(2)}, u32[]{:S(2)}) async-start(f32[32,1,256]{2,1,0:T(1,128)} %get-tuple-element.128), calls=%async_computation.11 | async-start | bytes 65536 | tf_op jit(solution)/shard_map/all_to_all | solution.py:758
  212.7 2.5 all-to-all-done.11.got
  220.3 36.8 %all_to_all.73 = bf16[32,160,128]{2,1,0:T(8,128)(2,1)S(1)} all-to-all(bf16[32,160,128]{2,1,0:T(8,128)(2,1)S(1)} %bitcast.34), channel_id=1, replica_groups=mesh['rows'=2,'batch'=16] {'rows','batch'}, dimensions={0} | all-to-all | bytes 2621440 | tf_op jit(solution)/shard_map/all_to_all | solution.py:771
  258.7 3.6 %all-to-all-start.13 = ((bf16[32,160,128]{2,1,0:T(8,128)(2,1)}), bf16[32,160,128]{2,1,0:T(8,128)(2,1)}, u32[]{:S(2)}, u32[]{:S(2)}) async-start(bf16[32,160,128]{2,1,0:T(8,128)(2,1)} %broadcast_in_dim.25), calls=%async_computation.13 | async-start | bytes 2621440 | tf_op jit(solution)/shard_map/all_to_all | solution.py:772
  266.4 3.9 %b13.1 = (bf16[2,28,56,256]{3,2,1,0:T(8,128)(2,1)}, f32[2,3,128]{2,1,0:T(4,128)S(1)}) custom-call(s32[8]{0:T(128)S(1)} %stack.23.scal, f32[32,1,256]{2,1,0:T(1,128)S(1)} %all-to-all-done.11.got, f32[32,1,128]{2,1,0:T(1,128)S(1)} %get-tuple-element.92.labels, f32[2,3,128]{2,1,0:T(4,128)S(1)} %copy.61.norm.norm_in, f32[4,128]{1,0:T(4,128)S(1)} %copy-done.101, ...), custom_call_target="tpu_custom_call" | custom-call | bytes 4194304 | tf_op jit(solution)/shard_map/b13/pallas_call | solution.py:25
  270.9 25.0 %all-to-all-done.13 = bf16[32,160,128]{2,1,0:T(8,128)(2,1)} async-done(((bf16[32,160,128]{2,1,0:T(8,128)(2,1)}), bf16[32,160,128]{2,1,0:T(8,128)(2,1)}, u32[]{:S(2)}, u32[]{:S(2)}) %all-to-all-start.13) | async-done | bytes 1310752 | tf_op jit(solution)/shard_map/all_to_all | solution.py:772
  299.1 2.5 slice.33
  (329 shorter events, 107.6 us)
Async XLA Ops:
  2.9 7.0 %collective-permute-start = (bf16[28,56,256]{2,1,0:T(8,128)(2,1)}, bf16[28,56,256]{2,1,0:T(8,128)(2,1)}, u32[]{:S(2)}, u32[]{:S(2)}) collective-permute-start(bf16[28,56,256]{2,1,0:T(8,128)(2,1)} %dynamic-slice_bitcast_fusion), channel_id=1, source_target_pairs={{0,16},{16,0},{1,17},{17,1},{2,18},{18,2},{3,19},{19,3},{4,20},{20... | collective-permute-start | bytes 2408456 | tf_op jit(solution)/shard_map/ppermute | solution.py:782
  12.2 19.5 %copy-start.6 = (f32[28,64,128]{2,1,0:T(8,128)}, f32[28,64,128]{2,1,0:T(8,128)S(1)}, u32[]{:S(2)}) copy-start(f32[28,64,128]{2,1,0:T(8,128)S(1)} %get-tuple-element.88.z_oth) | copy-start | bytes 2752516
  12.2 19.6 %copy-start.19 = (bf16[28,64,256]{2,1,0:T(8,128)(2,1)}, bf16[28,64,256]{2,1,0:T(8,128)(2,1)S(1)}, u32[]{:S(2)}) copy-start(bf16[28,64,256]{2,1,0:T(8,128)(2,1)S(1)} %get-tuple-element.95.x_oth) | copy-start | bytes 2752516
  12.2 14.2 %all-to-all-start = ((f32[32,1,384]{2,1,0:T(1,128)}), f32[32,1,384]{2,1,0:T(1,128)S(1)}, u32[]{:S(2)}, u32[]{:S(2)}) async-start(f32[32,1,384]{2,1,0:T(1,128)} %get-tuple-element.86), calls=%async_computation | async-start | bytes 98304 | tf_op jit(solution)/shard_map/all_to_all | solution.py:758
  19.2 18.1 %copy-start.127 = (f32[2,3,128]{2,0,1:T(2,128)S(1)}, f32[2,3,128]{2,0,1:T(2,128)}, u32[]{:S(2)}) copy-start(f32[2,3,128]{2,0,1:T(2,128)} %param.28) | copy-start | bytes 9220
  34.0 12.9 %copy-start.11 = (f32[28,32,128]{2,1,0:T(8,128)}, f32[28,32,128]{2,1,0:T(8,128)S(1)}, u32[]{:S(2)}) copy-start(f32[28,32,128]{2,1,0:T(8,128)S(1)} %get-tuple-element.93.z_in.z) | copy-start | bytes 1376260
  34.0 10.5 %all-to-all-start.1 = ((f32[32,1,256]{2,1,0:T(1,128)}), f32[32,1,256]{2,1,0:T(1,128)}, u32[]{:S(2)}, u32[]{:S(2)}) async-start(f32[32,1,256]{2,1,0:T(1,128)} %copy-done.98), calls=%async_computation.1 | async-start | bytes 65536 | tf_op jit(solution)/shard_map/all_to_all | solution.py:758
  50.1 15.2 %all-to-all-start.2 = ((f32[32,4,512]{2,1,0:T(4,128)}), f32[32,4,512]{2,1,0:T(4,128)S(1)}, u32[]{:S(2)}, u32[]{:S(2)}) async-start(f32[32,4,512]{2,1,0:T(4,128)} %copy-done.70), calls=%async_computation.2 | async-start | bytes 524288 | tf_op jit(solution)/shard_map/all_to_all | solution.py:758
  55.5 14.8 %copy-start.87 = (f32[2,3,512]{2,1,0:T(4,128)}, f32[2,3,512]{2,1,0:T(4,128)S(1)}, u32[]{:S(2)}) copy-start(f32[2,3,512]{2,1,0:T(4,128)S(1)} %copy.64.norm_p) | copy-start | bytes 36868
  73.8 9.8 %all-to-all-start.3 = ((f32[32,1,256]{2,1,0:T(1,128)}), f32[32,1,256]{2,1,0:T(1,128)S(1)}, u32[]{:S(2)}, u32[]{:S(2)}) async-start(f32[32,1,256]{2,1,0:T(1,128)} %get-tuple-element.100), calls=%async_computation.3 | async-start | bytes 65536 | tf_op jit(solution)/shard_map/all_to_all | solution.py:758
  89.7 9.8 %all-to-all-start.4 = ((f32[32,1,256]{2,1,0:T(1,128)}), f32[32,1,256]{2,1,0:T(1,128)S(1)}, u32[]{:S(2)}, u32[]{:S(2)}) async-start(f32[32,1,256]{2,1,0:T(1,128)} %copy-done.99), calls=%async_computation.4 | async-start | bytes 65536 | tf_op jit(solution)/shard_map/all_to_all | solution.py:758
  104.3 27.2 %copy-start.113 = (f32[2,128]{1,0:T(2,128)}, f32[2,128]{1,0:T(2,128)S(1)}, u32[]{:S(2)}) copy-start(f32[2,128]{1,0:T(2,128)S(1)} %get-tuple-element.111.keeps_in.keeps) | copy-start | bytes 3076
  104.3 10.5 %all-to-all-start.5 = ((f32[32,4,256]{2,1,0:T(4,128)}), f32[32,4,256]{2,1,0:T(4,128)S(1)}, u32[]{:S(2)}, u32[]{:S(2)}) async-start(f32[32,4,256]{2,1,0:T(4,128)} %get-tuple-element.104), calls=%async_computation.5 | async-start | bytes 262144 | tf_op jit(solution)/shard_map/all_to_all | solution.py:758
  118.6 12.9 %copy-start.10 = (f32[28,32,512]{2,1,0:T(8,128)S(1)}, f32[28,32,512]{2,1,0:T(8,128)}, u32[]{:S(2)}) copy-start(f32[28,32,512]{2,1,0:T(8,128)} %copy-done.8) | copy-start | bytes 5505028
  118.6 12.9 %copy-start.54 = (bf16[128,512]{1,0:T(8,128)(2,1)S(1)}, bf16[128,512]{1,0:T(8,128)(2,1)}, u32[]{:S(2)}) copy-start(bf16[128,512]{1,0:T(8,128)(2,1)} %w.16) | copy-start | bytes 393220
  131.5 11.8 %copy-start.15 = (f32[28,32,128]{2,1,0:T(8,128)S(1)}, f32[28,32,128]{2,1,0:T(8,128)}, u32[]{:S(2)}) copy-start(f32[28,32,128]{2,1,0:T(8,128)} %copy-done.13) | copy-start | bytes 1376260
  131.5 11.8 %copy-start.64 = (bf16[3,128,384]{2,1,0:T(8,128)(2,1)S(1)}, bf16[3,128,384]{2,1,0:T(8,128)(2,1)}, u32[]{:S(2)}) copy-start(bf16[3,128,384]{2,1,0:T(8,128)(2,1)} %copy-done.63) | copy-start | bytes 884740
  131.5 11.8 %copy-start.112 = (f32[2,128]{1,0:T(2,128)S(1)}, f32[2,128]{1,0:T(2,128)}, u32[]{:S(2)}) copy-start(f32[2,128]{1,0:T(2,128)} %copy-done.111) | copy-start | bytes 3076
  131.5 23.5 %copy-start.26 = (f32[28,32,512]{2,1,0:T(8,128)S(1)}, f32[28,32,512]{2,1,0:T(8,128)}, u32[]{:S(2)}) copy-start(f32[28,32,512]{2,1,0:T(8,128)} %copy-done.25) | copy-start | bytes 5505028
  131.5 23.4 %copy-start.52 = (bf16[512,128]{1,0:T(8,128)(2,1)S(1)}, bf16[512,128]{1,0:T(8,128)(2,1)}, u32[]{:S(2)}) copy-start(bf16[512,128]{1,0:T(8,128)(2,1)} %w.17) | copy-start | bytes 393220
  134.1 23.7 %copy-start.38 = (bf16[28,32,512]{2,1,0:T(8,128)(2,1)}, bf16[28,32,512]{2,1,0:T(8,128)(2,1)S(1)}, u32[]{:S(2)}) copy-start(bf16[28,32,512]{2,1,0:T(8,128)(2,1)S(1)} %get-tuple-element.146.dz) | copy-start | bytes 2752516
  134.1 20.9 %copy-start.2 = (f32[28,32,512]{2,1,0:T(8,128)S(1)}, f32[28,32,512]{2,1,0:T(8,128)}, u32[]{:S(2)}) copy-start(f32[28,32,512]{2,1,0:T(8,128)} %copy-done) | copy-start | bytes 5505028
  134.1 20.9 %copy-start.96 = (f32[4,512]{1,0:T(4,128)S(1)}, f32[4,512]{1,0:T(4,128)}, u32[]{:S(2)}) copy-start(f32[4,512]{1,0:T(4,128)} %copy-done.95) | copy-start | bytes 24580
  146.1 11.8 %copy-start.75 = (bf16[28,32,128]{2,1,0:T(8,128)(2,1)}, bf16[28,32,128]{2,1,0:T(8,128)(2,1)S(1)}, u32[]{:S(2)}) copy-start(bf16[28,32,128]{2,1,0:T(8,128)(2,1)S(1)} %get-tuple-element.144.dz) | copy-start | bytes 688132
  146.1 11.8 %copy-start.115 = (f32[2,3,128]{2,1,0:T(4,128)}, f32[2,3,128]{2,1,0:T(4,128)S(1)}, u32[]{:S(2)}) copy-start(f32[2,3,128]{2,1,0:T(4,128)S(1)} %get-tuple-element.228) | copy-start | bytes 9220
  160.4 12.4 %all-to-all-start.9 = ((f32[32,4,384]{2,1,0:T(4,128)}), f32[32,4,384]{2,1,0:T(4,128)S(1)}, u32[]{:S(2)}, u32[]{:S(2)}) async-start(f32[32,4,384]{2,1,0:T(4,128)} %get-tuple-element.120), calls=%async_computation.9 | async-start | bytes 393216 | tf_op jit(solution)/shard_map/all_to_all | solution.py:758
  185.2 11.2 %all-to-all-start.10 = ((f32[32,1,256]{2,1,0:T(1,128)}), f32[32,1,256]{2,1,0:T(1,128)S(1)}, u32[]{:S(2)}, u32[]{:S(2)}) async-start(f32[32,1,256]{2,1,0:T(1,128)} %copy-done.97), calls=%async_computation.10 | async-start | bytes 65536 | tf_op jit(solution)/shard_map/all_to_all | solution.py:758
  196.4 11.6 %copy-start.69 = (f32[128,512]{1,0:T(8,128)S(1)}, f32[128,512]{1,0:T(8,128)}, u32[]{:S(2)}) copy-start(f32[128,512]{1,0:T(8,128)} %copy-done.68) | copy-start | bytes 786436
  202.1 13.0 %all-to-all-start.11 = ((f32[32,1,256]{2,1,0:T(1,128)}), f32[32,1,256]{2,1,0:T(1,128)S(1)}, u32[]{:S(2)}, u32[]{:S(2)}) async-start(f32[32,1,256]{2,1,0:T(1,128)} %get-tuple-element.128), calls=%async_computation.11 | async-start | bytes 65536 | tf_op jit(solution)/shard_map/all_to_all | solution.py:758
  258.7 37.3 %all-to-all-start.13 = ((bf16[32,160,128]{2,1,0:T(8,128)(2,1)}), bf16[32,160,128]{2,1,0:T(8,128)(2,1)}, u32[]{:S(2)}, u32[]{:S(2)}) async-start(bf16[32,160,128]{2,1,0:T(8,128)(2,1)} %broadcast_in_dim.25), calls=%async_computation.13 | async-start | bytes 2621440 | tf_op jit(solution)/shard_map/all_to_all | solution.py:772
  262.2 4.2 %collective-permute-start.1 = (bf16[28,64,128]{2,1,0:T(8,128)(2,1)}, bf16[28,64,128]{2,1,0:T(8,128)(2,1)S(1)}, u32[]{:S(2)}, u32[]{:S(2)}) collective-permute-start(bf16[28,64,128]{2,1,0:T(8,128)(2,1)} %copy-done.59), channel_id=1, source_target_pairs={{0,16},{16,0},{1,17},{17,1},{2,18},{18,2},{3,19},{19,3},{4,20},{20... | collective-permute-start | bytes 1376264 | tf_op jit(solution)/shard_map/ppermute | solution.py:782
  262.3 4.0 %collective-permute-start.2 = (bf16[14,32,256]{2,1,0:T(8,128)(2,1)}, bf16[14,32,256]{2,1,0:T(8,128)(2,1)S(1)}, u32[]{:S(2)}, u32[]{:S(2)}) collective-permute-start(bf16[14,32,256]{2,1,0:T(8,128)(2,1)} %copy-done.121), channel_id=1, source_target_pairs={{0,16},{16,0},{1,17},{17,1},{2,18},{18,2},{3,19},{19,3},{4,20},{20... | collective-permute-start | bytes 688136 | tf_op jit(solution)/shard_map/ppermute | solution.py:782
  (113 other events, 277.0 us)
where the time goes:
time: 308 us; the launch traced here: 306 us
  local copies, waits for them, and re-layouts  83.4 us (27%)
  waiting for transfers between devices  67.3 us (22%)
  blocking collectives  64.7 us (21%)
  Pallas kernels  39.7 us (13%)
  starting transfers between devices  37.6 us (12%)
  other arithmetic  9.07 us (3%)
  between operations  4.28 us (1%)
    unnamed x285, local copies, waits for them, and re-layouts  74.5 us
    all_to_all x9, waiting for transfers between devices, gather(): return lax.all_to_all(send, AXES, 0, 0)  42.3 us
    pallas_call x22, Pallas kernels, call(): pl.pallas_call(kernel, out_shape=tuple((jax.ShapeDtypeStruct(s, d) for s,...  39.7 us
    all_to_all x1, blocking collectives, reduce_weights(): lax.all_to_all(parts, AXES, 0, 0).astype(F32)  36.8 us
    all_to_all x9, starting transfers between devices, gather(): return lax.all_to_all(send, AXES, 0, 0)  33.1 us
    all_to_all x3, blocking collectives, gather(): return lax.all_to_all(send, AXES, 0, 0)  27.9 us
    all_to_all x1, waiting for transfers between devices, reduce_weights(): lax.all_to_all(jnp.broadcast_to(mine[None], parts.shape), AXES, 0, 0)  25 us
    convert_element_type x6, other arithmetic, reduce_weights(): outs.append(flat_sum[at:at + size].astype(F32).reshape(shape))  6.56 us
  transfers between devices with their start and end apart: 13, of which 9 were waited for; matrix products, arithmetic and copies ran while one was open for 4% of the time, Pallas kernels for 3%

commit v1 on v0

--- a/solution.py
+++ b/solution.py
@@ -1,5 +1,3 @@
-import functools
-
 import jax
 import jax.numpy as jnp
 from jax import lax
@@ -11,7 +9,7 @@
 F32 = jnp.float32
 BF16 = jnp.bfloat16
 AXES = ("rows", "batch")
-VMEM_LIMIT = 40 * 1024 * 1024
+VMEM_LIMIT = 14 * 1024 * 1024
 LANES = 128
 COLS = 32
 
@@ -20,19 +18,21 @@
     return pl.BlockSpec(memory_space=memory)
 
 
-def stage(kernel, outs, scratch=(), flops=0, smem=(0,)):
+def stage(kernel, outs, scratch=(), flops=0, smem=(0,), smem_out=()):
     def call(*args):
         return pl.pallas_call(
             kernel,
             out_shape=tuple(jax.ShapeDtypeStruct(s, d) for s, d in outs),
             in_specs=[full(pltpu.SMEM if i in smem else pltpu.VMEM) for i in range(len(args))],
-            out_specs=tuple(full() for _ in outs),
+            out_specs=tuple(
+                full(pltpu.SMEM if i in smem_out else pltpu.VMEM) for i in range(len(outs))
+            ),
             scratch_shapes=list(scratch),
             compiler_params=pltpu.CompilerParams(vmem_limit_bytes=VMEM_LIMIT),
             cost_estimate=pl.CostEstimate(
                 flops=flops, bytes_accessed=4 * 1024 * 1024, transcendentals=0
             ),
-            name=kernel.func.__name__ if isinstance(kernel, functools.partial) else kernel.__name__,
+            name=kernel.__name__,
         )(*args)
 
     return call
@@ -85,11 +85,11 @@
 
 
 def gain_of(norm_ref, group):
-    return norm_ref[0, pl.ds(group, 1), :]
+    return norm_ref[group, 0:1, :]
 
 
 def shift_of(norm_ref, group):
-    return norm_ref[1, pl.ds(group, 1), :]
+    return norm_ref[group, 1:2, :]
 
 
 def valid_cols(channels):
@@ -160,31 +160,37 @@
     lax.fori_loop(0, rows, put, 0, unroll=4)
 
 
-def first_project(x_pad, w, z):
+def first_project(x_pad, w, z, stats=True):
     rows = x_pad.shape[0]
     step = rows // 4
     sums, squares = zeros8(LANES), zeros8(LANES)
     for c in range(4):
         values = mm(flat(x_pad[step * c : step * (c + 1)]), w[...])
         z[step * c : step * (c + 1)] = values.reshape(step, x_pad.shape[1], LANES)
-        parts = values.reshape(-1, 8, LANES)
-        sums = sums + jnp.sum(parts, axis=0)
-        squares = squares + jnp.sum(parts * parts, axis=0)
+        if stats:
+            parts = values.reshape(-1, 8, LANES)
+            sums = sums + jnp.sum(parts, axis=0)
+            squares = squares + jnp.sum(parts * parts, axis=0)
     return sums, squares
 
 
-def f1_own(scal, images, w, x_pad, z, part):
-    widen(images.at[scal[HALF]], x_pad)
-    sums, squares = first_project(x_pad, w, z)
-    part[0] = sums
-    part[1] = squares
-
-
-def f1_other(scal, received, w, part, x_pad, z, send):
-    widen(received, x_pad)
-    sums, squares = first_project(x_pad, w, z)
-    label = jnp.full((1, LANES), scal[OWN].astype(F32))
-    spread(send, [down(sums + part[0]), down(squares + part[1]), label])
+def f1(half_ref, group, width, gate, images, w, scal, x_own, x_for, z_own, z_for, send):
+    half = half_ref[0]
+    own, other = group[half], group[1 - half]
+    scal[OWN] = own
+    scal[OTHER] = other
+    scal[HALF] = half
+    scal[LIMIT] = w.shape[1] // 4 * width[own]
+    scal[GATE] = gate[own]
+    for k in range(GATE + 1, scal.shape[0]):
+        scal[k] = 0
+    widen(images.at[half], x_own)
+    widen(images.at[1 - half], x_for)
+    rows = []
+    for x_pad, z in ((x_own, z_own), (x_for, z_for)):
+        sums, squares = first_project(x_pad, w, z)
+        rows += [down(sums), down(squares)]
+    spread(send, [*rows, jnp.full((1, LANES), (own + 4 * other).astype(F32))])
 
 
 def f1_strided(scal, x_own, x_oth, w, xee, z, stats, wide):
@@ -243,20 +249,30 @@
     spread(send, [down(sums), down(squares)])
 
 
-def f2(scal, got, z_own, z_oth, norm, w_cur, w_up, xs, z, send, labels, keeps):
-    marks = got[:, :, 2 * LANES : 3 * LANES]
+def f2(scal, got, z_own, x_oth, w, norm, w_cur, w_up, xs, z, send, labels, keeps, z_oth):
+    codes = got[:, :, 4 * LANES : 5 * LANES]
+    others = jnp.floor(0.25 * codes)
+    marks = codes - 4.0 * others
     labels[...] = marks
     rows = xs.shape[0] - 1
     pixels = 4.0 * rows * (COLS - 4)
-    mean, rstd, gain, shift, _ = scale_shift(got, marks, scal, norm, pixels)
-    keeps[0:1, :] = mean
-    keeps[1:2, :] = rstd
-    other = scal[OTHER].astype(F32)
-    total = group_sum(got, marks, other)
-    count = group_count(marks, other) * pixels
-    mean_2, rstd_2 = moments(row(total, 0), row(total, 1), count)
-    keeps[2:3, :] = mean_2
-    keeps[3:4, :] = rstd_2
+    first_project(x_oth, w, z_oth, False)
+    for k, slot in enumerate((OWN, OTHER)):
+        label = scal[slot].astype(F32)
+        mine, theirs = (marks == label).astype(F32), (others == label).astype(F32)
+        totals = [
+            jnp.sum(
+                got[:, :, LANES * s : LANES * (s + 1)] * mine
+                + got[:, :, LANES * (s + 2) : LANES * (s + 3)] * theirs,
+                axis=0,
+            )
+            for s in (0, 1)
+        ]
+        mean, rstd = moments(*totals, group_count(marks, label) * pixels)
+        keeps[2 * k : 2 * k + 1, :] = mean
+        keeps[2 * k + 1 : 2 * k + 2, :] = rstd
+    mean, rstd = keeps[0:1, :], keeps[1:2, :]
+    gain, shift = gain_of(norm, scal[OWN]), shift_of(norm, scal[OWN])
     scale = rstd * gain
     bias = shift - mean * scale
     keep = valid_cols(LANES) & chan_mask(scal[LIMIT], LANES)
@@ -421,11 +437,11 @@
     own_shift = jnp.zeros((1, chans), F32)
     own_gain = jnp.zeros((1, chans), F32)
     group = scal[OWN]
-    for g in range(norm.shape[1]):
+    for g in range(norm.shape[0]):
         total = group_sum(got, marks, float(g))
         shift_sum, gain_sum = row(total, slots[0]), row(total, slots[1])
-        grad_norm[0, g : g + 1, :] = gain_sum
-        grad_norm[1, g : g + 1, :] = shift_sum
+        grad_norm[g, 0:1, :] = gain_sum
+        grad_norm[g, 1:2, :] = shift_sum
         mine = group == g
         own_shift = jnp.where(mine, shift_sum, own_shift)
         own_gain = jnp.where(mine, gain_sum, own_gain)
@@ -631,29 +647,24 @@
 
 
 def b13(
-    scal, got, labels, norm, keeps, images, w, z_own, dn_own, dn_oth, gs_own, gs_oth,
-    grad, grad_norm, x_pad, z_oth, dz, wide,
+    scal, got, labels, norm, keeps, w, z_own, z_for, dn_own, dn_for, gs_own, gs_for,
+    grad, grad_norm, dz, wide,
 ):
-    rows, cols = images.shape[1], images.shape[2]
+    rows, cols = grad.shape[1], grad.shape[2]
     half = scal[HALF]
     pixels = 2.0 * rows * cols
     marks = labels[...]
-    widen(images.at[1 - half], x_pad)
-    for c in range(4):
-        step = rows // 4
-        values = mm(flat(x_pad[step * c : step * (c + 1)]), w[...])
-        z_oth[step * c : step * (c + 1)] = values.reshape(step, x_pad.shape[1], LANES)
     totals = []
-    for g in range(norm.shape[1]):
+    for g in range(norm.shape[0]):
         total = group_sum(got, marks, float(g))
         totals.append((row(total, 0), row(total, 1)))
-        grad_norm[0, g : g + 1, :] = totals[g][1]
-        grad_norm[1, g : g + 1, :] = totals[g][0]
-    keep = lax.broadcasted_iota(jnp.int32, (x_pad.shape[1], LANES), 0) < cols
-    for k, (z, dn, gs) in enumerate(((z_own, dn_own, gs_own), (z_oth, dn_oth, gs_oth))):
+        grad_norm[g, 0:1, :] = totals[g][1]
+        grad_norm[g, 1:2, :] = totals[g][0]
+    keep = lax.broadcasted_iota(jnp.int32, (z_own.shape[1], LANES), 0) < cols
+    for k, (z, dn, gs) in enumerate(((z_own, dn_own, gs_own), (z_for, dn_for, gs_for))):
         group = scal[OWN if k == 0 else OTHER]
         shift_sum, gain_sum = totals[0]
-        for g in range(1, norm.shape[1]):
+        for g in range(1, norm.shape[0]):
             shift_sum = jnp.where(group == g, totals[g][0], shift_sum)
             gain_sum = jnp.where(group == g, totals[g][1], gain_sum)
         count = group_count(marks, group.astype(F32)) * pixels
@@ -688,30 +699,38 @@
         lax.fori_loop(0, rows // 2, emit, 0, unroll=2)
 
 
-def g_2c(act, dz, out):
-    out[...] = mm_tn(flat(act[...]), flat(dz[...]))
-
-
-def g_2b(x3, dz, out):
-    rows = dz.shape[0]
-    low = flat(dz[...])
+def put_rows(out, at, value):
+    for j in range(value.shape[1] // LANES):
+        out[at : at + value.shape[0], :] = value[:, LANES * j : LANES * (j + 1)].astype(BF16)
+        at += value.shape[0]
+    return at
+
+
+def take_rows(source, at, out):
+    rows = out.shape[0]
+    for j in range(out.shape[1] // LANES):
+        out[:, LANES * j : LANES * (j + 1)] = source(at, rows)
+        at += rows
+    return at
+
+
+def g_most(
+    scal, act_2b, dz_2c, x3, dz_2b, joined, dz_2a, act_1b, dz_1c, xee, dz_1p, w_1p,
+    out, gs_own, gs_oth,
+):
+    rows = dz_2b.shape[0]
+    at = put_rows(out, 0, mm_tn(flat(act_2b[...]), flat(dz_2c[...])))
+    low = flat(dz_2b[...])
     for y in range(3):
-        got = mm_tn(flat(x3[y : y + rows]), low)
-        out[y] = got.reshape(3, LANES, LANES)
-
-
-def g_2a(joined, dz, out):
-    out[...] = mm_tn(flat(joined[...]), flat(dz[...]))
-
-
-def g_1(scal, act, dz_c, xee, dz_p, w_p, out_c, out_p, gs_own, gs_oth):
-    out_c[...] = mm_tn(flat(act[...]), flat(dz_c[...]))
-    out_p[...] = mm_tn(flat(xee[...]), flat(dz_p[...]))
+        at = put_rows(out, at, mm_tn(flat(x3[y : y + rows]), low))
+    at = put_rows(out, at, mm_tn(flat(joined[...]), flat(dz_2a[...])))
+    at = put_rows(out, at, mm_tn(flat(act_1b[...]), flat(dz_1c[...])))
+    put_rows(out, at, mm_tn(flat(xee[...]), flat(dz_1p[...])))
     half = scal[HALF]
-    rows = gs_own.shape[0]
+    count = gs_own.shape[0]
     for k, gs in enumerate((gs_own, gs_oth)):
-        first = rows * (half if k == 0 else 1 - half)
-        got = mm_nt(flat(dz_p[pl.ds(first, rows)]), w_p[...])
+        first = count * (half if k == 0 else 1 - half)
+        got = mm_nt(flat(dz_1p[pl.ds(first, count)]), w_1p[...])
         gs[...] = got.reshape(gs.shape).astype(BF16)
 
 
@@ -721,13 +740,16 @@
     n = LANES
     cur = mm_tn(flat(xs[1 : rows + 1]), low)
     for k, (y, x) in enumerate(((1, 1), (1, 2), (1, 0), (2, 1), (2, 2), (2, 0))):
-        out[y, x] = cur[n * k : n * (k + 1)]
+        put_rows(out, n * (3 * y + x), cur[n * k : n * (k + 1)])
     up = mm_tn(flat(xs[0:rows, :, 3 * n : 6 * n]), low)
     for k, (y, x) in enumerate(((0, 1), (0, 2), (0, 0))):
-        out[y, x] = up[n * k : n * (k + 1)]
-
-
-def g_1a(scal, got, labels, norm, keeps, z_own, z_oth, dn_own, dn_oth, x_own, x_oth, out, dz):
+        put_rows(out, n * (3 * y + x), up[n * k : n * (k + 1)])
+
+
+def g_1a(
+    scal, got, labels, norm, keeps, z_own, z_oth, dn_own, dn_oth, x_own, x_oth, most, grad_1b,
+    kept, sent, dz, packed,
+):
     rows = z_own.shape[0]
     cols = 2 * (COLS - 4)
     pixels = 2.0 * rows * cols
@@ -751,31 +773,50 @@
         lax.fori_loop(0, rows, put, 0, unroll=2)
         term = mm_tn(flat(x[...]), flat(dz[...]))
         value = term if value is None else value + term
-    out[...] = value
+    at = put_rows(packed, 0, value)
+    packed[at : at + grad_1b.shape[0], :] = grad_1b[...]
+    at += grad_1b.shape[0]
+    packed[at : at + most.shape[0], :] = most[...]
+    at += most.shape[0]
+    if at < packed.shape[0]:
+        packed[at:, :] = jnp.zeros((packed.shape[0] - at, LANES), BF16)
+    half = scal[HALF]
+    size = kept.shape[0] * kept.shape[1]
+    for out, place in ((kept, half), (sent, 1 - half)):
+        out[...] = packed[pl.ds(pl.multiple_of(size * place, 16), size), :].reshape(out.shape)
+
+
+def add_pair(kept, received, out):
+    out[...] = (kept[...].astype(F32) + received[...].astype(F32)).astype(BF16)
+
+
+def add_all(parts, out):
+    half = parts.shape[0] // 2
+    for k in (0, 1):
+        total = jnp.sum(parts[half * k : half * (k + 1)].astype(F32), axis=0).astype(BF16)
+        out[half * k : half * (k + 1)] = jnp.broadcast_to(total[None], (half, *total.shape))
+
+
+def unpack(scal, own, other, w_1a, w_1b, w_2c, w_2b, w_2a, w_1c, w_1p, packed):
+    half = scal[HALF]
+    size = own.shape[0]
+    for part, place in ((own, half), (other, 1 - half)):
+        packed[pl.ds(pl.multiple_of(size * place, 16), size), :] = part[...]
+
+    def source(at, rows):
+        return packed[at : at + rows, :].astype(F32)
+
+    at = 0
+    for out in (w_1a, w_1b, w_2c, w_2b, w_2a, w_1c, w_1p):
+        at = take_rows(source, at, out)
 
 
 def gather(send):
     return lax.all_to_all(send, AXES, 0, 0)
 
 
-def reduce_weights(grads, devices):
-    shapes = [g.shape for g in grads]
-    sizes = [g.size for g in grads]
-    total = sum(sizes)
-    unit = devices * 16 * LANES
-    padded = -(-total // unit) * unit
-    one = jnp.concatenate(
-        [g.astype(BF16).reshape(-1) for g in grads] + [jnp.zeros((padded - total,), BF16)]
-    )
-    parts = one.reshape(devices, padded // devices // LANES, LANES)
-    mine = jnp.sum(lax.all_to_all(parts, AXES, 0, 0).astype(F32), axis=0).astype(BF16)
-    everyone = lax.all_to_all(jnp.broadcast_to(mine[None], parts.shape), AXES, 0, 0)
-    flat_sum = everyone.reshape(-1)
-    outs, at = [], 0
-    for shape, size in zip(shapes, sizes):
-        outs.append(flat_sum[at : at + size].astype(F32).reshape(shape))
-        at += size
-    return outs
+def tie(*values):
+    return lax.optimization_barrier(values)
 
 
 def swap(block):
@@ -788,14 +829,12 @@
     cotangent, group, width, gate,
 ):
     devices = lax.axis_size("rows") * lax.axis_size("batch")
-    half = lax.axis_index("rows")
-    own = jnp.take(group, half)
-    other = jnp.take(group, 1 - half)
-    inner, outer, inputs = w_1a.shape[1], w_1c.shape[1], w_1a.shape[0]
-    scal = jnp.stack(
-        [own, other, half.astype(jnp.int32), inner // 4 * jnp.take(width, own), jnp.take(gate, own)]
-        + [jnp.int32(0)] * 3
-    ).astype(jnp.int32)
+    half = lax.axis_index("rows").astype(jnp.int32).reshape(1)
+    norms = (norm_1a, norm_1b, norm_1c, norm_1p, norm_2a, norm_2b, norm_2c)
+    norm_1a, norm_1b, norm_1c, norm_1p, norm_2a, norm_2b, norm_2c = (
+        v.transpose(1, 0, 2) for v in norms
+    )
+    outer, inputs = w_1c.shape[1], w_1a.shape[0]
     rows = cotangent.shape[1]
     cols_in = 2 * COLS
     n, m = LANES, devices
@@ -810,32 +849,37 @@
         return pltpu.VMEM((rows, COLS, channels), dtype)
 
     def params(*arrays):
-        return [((2, a.shape[1], a.shape[2]), F32) for a in arrays]
+        return [(a.shape, F32) for a in arrays]
 
     def mean_scale(channels, count=1):
         return ((2 * count, channels), F32)
 
-    received = swap(lax.dynamic_index_in_dim(images, 1 - half, 0, keepdims=False))
+    wide_in = ((rows, cols_in, inputs), BF16)
+    wide_z = ((rows, cols_in, n), F32)
+    scal, x_own, x_for, z_own, z_for, s1 = stage(
+        f1, [((8,), jnp.int32), wide_in, wide_in, wide_z, wide_z, send(5)],
+        smem=(0, 1, 2, 3), smem_out=(0,),
+    )(half, group, width, gate, images, w_1a)
+    x_oth = swap(x_for)
+    g1 = gather(s1)
     w_cur, w_up, b_even, b_odd, b_same = stage(
         prepare,
         [((6 * n, n), BF16), ((3 * n, n), BF16), ((2 * n, 2 * n), BF16), ((2 * n, 4 * n), BF16),
          ((3, n, 3 * n), BF16)],
         smem=(),
     )(w_1b, w_2b)
-    wide_in = ((rows, cols_in, inputs), BF16)
-    wide_z = ((rows, cols_in, n), F32)
-    x_own, z_own, part = stage(f1_own, [wide_in, wide_z, ((2, 8, n), F32)])(scal, images, w_1a)
-    x_oth, z_oth, s1 = stage(f1_other, [wide_in, wide_z, send(3)])(scal, received, w_1a, part)
-    g1 = gather(s1)
+    g1, w_cur, w_up = tie(g1, w_cur, w_up)
+    xs, z_1b, s2, labels, k_1a, z_oth = stage(
+        f2,
+        [((rows + 1, COLS, 6 * n), BF16), maps(n), send(2), ((m, 1, n), F32), mean_scale(n, 2),
+         wide_z],
+    )(scal, g1, z_own, x_oth, w_1a, norm_1a, w_cur, w_up)
     xee, z_1p, stats_1p = stage(
         f1_strided,
         [maps(inputs, BF16), maps(outer), ((2, 1, outer), F32)],
         [pltpu.VMEM((inputs // n, cols_in, n), F32)],
     )(scal, x_own, x_oth, w_1p)
-    xs, z_1b, s2, labels, k_1a = stage(
-        f2,
-        [((rows + 1, COLS, 6 * n), BF16), maps(n), send(2), ((m, 1, n), F32), mean_scale(n, 2)],
-    )(scal, g1, z_own, z_oth, norm_1a, w_cur, w_up)
+    s2, xee, z_1p, stats_1p = tie(s2, xee, z_1p, stats_1p)
     g2 = gather(s2)
     act_1b, z_1c, s3, k_1b = stage(
         f3, [maps(n, BF16), maps(outer), send(4, outer), mean_scale(n)]
@@ -861,52 +905,65 @@
         b8, [maps(outer, BF16), maps(n), send(2), *params(norm_2c)], [scratch(n)]
     )(scal, g7, labels, grad_pre, z_2c, norm_2c, k_2c, w_2c, z_2b, norm_2b, k_2b)
     g8 = gather(s8)
-    (grad_w_2c,) = stage(g_2c, [(w_2c.shape, F32)], smem=())(act_2b, dz_2c)
     dz_2b, dout_2a, s9, grad_norm_2b = stage(
         b9, [maps(n, BF16), maps(n), send(2), *params(norm_2b)],
         [pltpu.VMEM((rows + 2, COLS, 3 * n), BF16), scratch(n)],
     )(scal, g8, labels, dout_2b, z_2b, norm_2b, k_2b, b_same, z_2a, norm_2a, k_2a)
     g9 = gather(s9)
-    (grad_w_2b,) = stage(g_2b, [(w_2b.shape, F32)], smem=())(x3, dz_2b)
     dz_2a, grad_pre_2, s10, grad_norm_2a = stage(
         b10, [maps(n, BF16), maps(outer), send(3, outer), *params(norm_2a)], [scratch(outer)]
     )(scal, g9, labels, dout_2a, z_2a, norm_2a, k_2a, w_2a, grad_pre, slope, z_1c, z_1p, k_cp)
     g10 = gather(s10)
-    (grad_w_2a,) = stage(g_2a, [(w_2a.shape, F32)], smem=())(joined, dz_2a)
     dz_1c, dz_1p, dout_1b, s11, grad_norm_1c, grad_norm_1p = stage(
         b11, [maps(outer, BF16), maps(outer, BF16), maps(n), send(2), *params(norm_1c, norm_1p)],
         [scratch(n)],
     )(scal, g10, labels, grad_pre_2, z_1c, z_1p, norm_1c, norm_1p, k_cp, w_1c, z_1b, norm_1b, k_1b)
+    half_map = ((rows // 2, COLS, inputs), BF16)
+    most_rows = sum(v.size for v in (w_2c, w_2b, w_2a, w_1c, w_1p)) // n
+    most, gs_own, gs_send = stage(g_most, [((most_rows, n), BF16), half_map, half_map])(
+        scal, act_2b, dz_2c, x3, dz_2b, joined, dz_2a, act_1b, dz_1c, xee, dz_1p, w_1p
+    )
+    s11, most, gs_own, gs_send = tie(s11, most, gs_own, gs_send)
+    gs_for = swap(gs_send)
     g11 = gather(s11)
-    half_map = ((rows // 2, COLS, inputs), BF16)
-    grad_w_1c, grad_w_1p, gs_own, gs_send = stage(
-        g_1, [(w_1c.shape, F32), (w_1p.shape, F32), half_map, half_map]
-    )(scal, act_1b, dz_1c, xee, dz_1p, w_1p)
-    gs_oth = swap(gs_send)
     half_in = ((rows, cols_in, n), BF16)
     dz_1b, dn_own, dn_send, s12, grad_norm_1b = stage(
         b12, [maps(n, BF16), half_in, half_in, send(2), *params(norm_1b)],
         [pltpu.VMEM((rows + 1, COLS, 2 * n), BF16), scratch(2 * n), scratch(2 * n),
          pltpu.VMEM((2, cols_in, n), F32)],
     )(scal, g11, labels, dout_1b, z_1b, norm_1b, k_1b, b_even, b_odd, z_own, z_oth, norm_1a, k_1a)
-    dn_oth = swap(dn_send)
+    (grad_1b,) = stage(g_1b, [((w_1b.size // n, n), BF16)], smem=())(xs, dz_1b)
+    s12, grad_1b, dn_own, dn_send = tie(s12, grad_1b, dn_own, dn_send)
+    dn_for = swap(dn_send)
     g12 = gather(s12)
-    (grad_w_1b,) = stage(g_1b, [(w_1b.shape, F32)], smem=())(xs, dz_1b)
+    all_rows = most_rows + (w_1b.size + w_1a.size) // n
+    unit = 2 * devices * 16
+    piece = -(-all_rows // unit) * 16
+    share = ((devices, piece, n), BF16)
+    kept, sent = stage(
+        g_1a, [share, share],
+        [pltpu.VMEM(half_in[0], BF16), pltpu.VMEM((2 * devices * piece, n), BF16)],
+    )(scal, g12, labels, norm_1a, k_1a, z_own, z_oth, dn_own, dn_send, x_own, x_oth, most, grad_1b)
+    (pair,) = stage(add_pair, [share], smem=())(kept, swap(sent))
+    (mine,) = stage(add_all, [share], smem=())(gather(pair))
     grad_images, grad_norm_1a = stage(
         b13, [(images.shape, BF16), *params(norm_1a)],
-        [pltpu.VMEM(wide_in[0], BF16), pltpu.VMEM(wide_z[0], F32), pltpu.VMEM(half_in[0], BF16),
-         pltpu.VMEM((inputs // n, rows, cols_in, n), F32)],
-    )(scal, g12, labels, norm_1a, k_1a, images, w_1a, z_own, dn_own, dn_oth, gs_own, gs_oth)
-    (grad_w_1a,) = stage(g_1a, [(w_1a.shape, F32)], [pltpu.VMEM(half_in[0], BF16)])(
-        scal, g12, labels, norm_1a, k_1a, z_own, z_oth, dn_own, dn_send, x_own, x_oth
-    )
-    totals = reduce_weights(
-        (grad_w_1a, grad_w_1b, grad_w_1c, grad_w_1p, grad_w_2a, grad_w_2b, grad_w_2c), devices
+        [pltpu.VMEM(half_in[0], BF16), pltpu.VMEM((inputs // n, rows, cols_in, n), F32)],
+    )(scal, g12, labels, norm_1a, k_1a, w_1a, z_own, z_for, dn_own, dn_for, gs_own, gs_for)
+    part = gather(mine).reshape(devices * piece, n)
+    totals = stage(
+        unpack,
+        [(v.shape, F32) for v in (w_1a, w_1b.reshape(-1, n), w_2c, w_2b.reshape(-1, n), w_2a, w_1c, w_1p)],
+        [pltpu.VMEM((2 * devices * piece, n), BF16)],
+    )(scal, part, swap(part))
+    t_1a, t_1b, t_2c, t_2b, t_2a, t_1c, t_1p = totals
+    grads = (
+        grad_norm_1a, grad_norm_1b, grad_norm_1c, grad_norm_1p,
+        grad_norm_2a, grad_norm_2b, grad_norm_2c,
     )
     return (
-        result[None], grad_images, *totals,
-        grad_norm_1a, grad_norm_1b, grad_norm_1c, grad_norm_1p,
-        grad_norm_2a, grad_norm_2b, grad_norm_2c,
+        result[None], grad_images, t_1a, t_1b.reshape(w_1b.shape), t_1c, t_1p, t_2a,
+        t_2b.reshape(w_2b.shape), t_2c, *[v.transpose(1, 0, 2) for v in grads],
     )
 
 

time: 308 us -> 217 us (0.70)
  blocking collectives: 64.7 us -> 151 us
  local copies, waits for them, and re-layouts: 83.4 us -> 9.57 us
  waiting for transfers between devices: 67.3 us -> 7.65 us
  starting transfers between devices: 37.6 us -> 8 us
  other arithmetic: 9.07 us -> 0 us
  between operations: 4.28 us -> 0.96 us
    all_to_all x3 -> x13, blocking collectives: 27.9 us -> 151 us  [gather(): return lax.all_to_all(send, AXES, 0, 0)]
    unnamed x285 -> x64, local copies, waits for them, and re-layouts: 74.5 us -> 9.57 us
    all_to_all x9 -> x1, waiting for transfers between devices: 42.3 us -> 2.99 us  [gather(): return lax.all_to_all(send, AXES, 0, 0)]
    all_to_all x1 -> x0, blocking collectives: 36.8 us -> none  [reduce_weights(): lax.all_to_all(parts, AXES, 0, 0).astype(F32)]
    all_to_all x9 -> x1, starting transfers between devices: 33.1 us -> 6.96 us  [gather(): return lax.all_to_all(send, AXES, 0, 0)]
    all_to_all x1 -> x0, waiting for transfers between devices: 25 us -> none  [reduce_weights(): lax.all_to_all(jnp.broadcast_to(mine[None], parts.shape), AXES, 0, 0)]
    convert_element_type x8 -> x0, other arithmetic: 8.08 us -> none  [the longest x6 6.56 us: reduce_weights(): outs.append(flat_sum[at:at + size].astype(F32).reshape(shape))]
    ppermute x3 -> x5, waiting for transfers between devices: 0.01 us -> 4.66 us  [swap(): return lax.ppermute(block, 'rows', [(0, 1), (1, 0)])]
  transfers between devices with their start and end apart: 13 -> 6, of which waited for: 9 -> 3; matrix products, arithmetic and copies ran while one was open for 4% -> 0% of each run, Pallas kernels for 3% -> 2%
where the time goes in v1:
time: 217 us
  blocking collectives  151 us (70%)
  Pallas kernels  40.1 us (18%)
  local copies, waits for them, and re-layouts  9.57 us (4%)
  starting transfers between devices  8 us (4%)
  waiting for transfers between devices  7.65 us (4%)
    all_to_all x13, blocking collectives, gather(): return lax.all_to_all(send, AXES, 0, 0)  151 us
    pallas_call x21, Pallas kernels, call(): pl.pallas_call(kernel, out_shape=tuple((jax.ShapeDtypeStruct(s, d) for s,...  40.1 us
    unnamed x64, local copies, waits for them, and re-layouts  9.57 us
    all_to_all x1, starting transfers between devices, gather(): return lax.all_to_all(send, AXES, 0, 0)  6.96 us
    ppermute x5, waiting for transfers between devices, swap(): return lax.ppermute(block, 'rows', [(0, 1), (1, 0)])  4.66 us
  transfers between devices with their start and end apart: 6, of which 3 were waited for; matrix products, arithmetic and copies ran while one was open for 0% of the time, Pallas kernels for 2%

profile of v1, /device:TPU:0, one launch (start us, length us, event | category | flops | bytes accessed | tf_op | source)
XLA Modules:
  0.0 216.8 jit_solution(16313130451146679249)
XLA Ops:
  0.7 1.4 copy-done
  4.9 2.0 f1.1
  8.3 7.0 %all-to-all-start = ((f32[32,1,640]{2,1,0:T(1,128)}), f32[32,1,640]{2,1,0:T(1,128)S(1)}, u32[]{:S(2)}, u32[]{:S(2)}) async-start(f32[32,1,640]{2,1,0:T(1,128)} %get-tuple-element.110), calls=%async_computation | async-start | bytes 163840 | tf_op jit(solution)/shard_map/all_to_all | solution.py:815
  19.8 3.0 %all-to-all-done.got = f32[32,1,640]{2,1,0:T(1,128)S(1)} async-done(((f32[32,1,640]{2,1,0:T(1,128)}), f32[32,1,640]{2,1,0:T(1,128)S(1)}, u32[]{:S(2)}, u32[]{:S(2)}) %all-to-all-start) | async-done | bytes 81952 | tf_op jit(solution)/shard_map/all_to_all | solution.py:815
  24.1 2.4 %f2.1 = (bf16[29,32,768]{2,1,0:T(8,128)(2,1)S(1)}, f32[28,32,128]{2,1,0:T(8,128)S(1)}, f32[32,1,256]{2,1,0:T(1,128)S(1)}, f32[32,1,128]{2,1,0:T(1,128)S(1)}, f32...) custom-call(s32[8]{0:T(128)S(1)} %get-tuple-element.109.scal, f32[32,1,640]{2,1,0:T(1,128)S(1)} %all-to-all-done.got, ...), custom_call_target="tpu_custom_call" | custom-call | bytes 4194304 | tf_op jit(solution)/shard_map/f2/pallas_call | solution.py:23
  26.6 9.9 %all_to_all.70.got = f32[32,1,256]{2,1,0:T(1,128)S(1)} all-to-all(f32[32,1,256]{2,1,0:T(1,128)S(1)} %get-tuple-element.123), channel_id=1, replica_groups=mesh['rows'=2,'batch'=16] {'rows','batch'}, dimensions={0} | all-to-all | bytes 65536 | tf_op jit(solution)/shard_map/all_to_all | solution.py:815
  37.7 12.9 %all_to_all.71.got = f32[32,4,512]{2,1,0:T(4,128)S(1)} all-to-all(f32[32,4,512]{2,1,0:T(4,128)S(1)} %get-tuple-element.127), channel_id=1, replica_groups=mesh['rows'=2,'batch'=16] {'rows','batch'}, dimensions={0} | all-to-all | bytes 524288 | tf_op jit(solution)/shard_map/all_to_all | solution.py:815
  50.7 2.0 f4.1
  52.7 9.0 %all_to_all.72.got = f32[32,1,256]{2,1,0:T(1,128)S(1)} all-to-all(f32[32,1,256]{2,1,0:T(1,128)S(1)} %get-tuple-element.130), channel_id=1, replica_groups=mesh['rows'=2,'batch'=16] {'rows','batch'}, dimensions={0} | all-to-all | bytes 65536 | tf_op jit(solution)/shard_map/all_to_all | solution.py:815
  61.7 1.7 f5.1
  63.4 8.9 %all_to_all.73.got = f32[32,1,256]{2,1,0:T(1,128)S(1)} all-to-all(f32[32,1,256]{2,1,0:T(1,128)S(1)} %get-tuple-element.132), channel_id=1, replica_groups=mesh['rows'=2,'batch'=16] {'rows','batch'}, dimensions={0} | all-to-all | bytes 65536 | tf_op jit(solution)/shard_map/all_to_all | solution.py:815
  73.6 9.6 %all_to_all.74.got = f32[32,4,256]{2,1,0:T(4,128)S(1)} all-to-all(f32[32,4,256]{2,1,0:T(4,128)S(1)} %get-tuple-element.134), channel_id=1, replica_groups=mesh['rows'=2,'batch'=16] {'rows','batch'}, dimensions={0} | all-to-all | bytes 262144 | tf_op jit(solution)/shard_map/all_to_all | solution.py:815
  83.2 3.0 %b7.1 = (bf16[28,28,512]{2,1,0:T(8,128)(2,1)}, f32[28,32,512]{2,1,0:T(8,128)S(1)}, f32[32,4,256]{2,1,0:T(4,128)S(1)}, f32[2,512]{1,0:T(2,128)S(1)}) custom-call(s32[8]{0:T(128)S(1)} %get-tuple-element.109.scal, f32[32,4,256]{2,1,0:T(4,128)S(1)} %all_to_all.74.got, f32[32,1,128]{2,1,0:T(1,128)S(1)} %get-tuple-element.124.labels, ...), custom_call_target="tpu_custom_call" | custom-call | bytes 4194304 | tf_op jit(solution)/shard_map/b7/pallas_call | solution.py:23
  86.2 9.8 %all_to_all.75.got = f32[32,4,256]{2,1,0:T(4,128)S(1)} all-to-all(f32[32,4,256]{2,1,0:T(4,128)S(1)} %get-tuple-element.138), channel_id=1, replica_groups=mesh['rows'=2,'batch'=16] {'rows','batch'}, dimensions={0} | all-to-all | bytes 262144 | tf_op jit(solution)/shard_map/all_to_all | solution.py:815
  96.0 2.5 %b8.1 = (bf16[28,32,512]{2,1,0:T(8,128)(2,1)S(1)}, f32[28,32,128]{2,1,0:T(8,128)S(1)}, f32[32,1,256]{2,1,0:T(1,128)S(1)}, f32[3,2,512]{2,1,0:T(2,128)}) custom-call(s32[8]{0:T(128)S(1)} %get-tuple-element.109.scal, f32[32,4,256]{2,1,0:T(4,128)S(1)} %all_to_all.75.got, f32[32,1,128]{2,1,0:T(1,128)S(1)} %get-tuple-element.124.labels, ...), custom_call_target="tpu_custom_call" | custom-call | bytes 4194304 | tf_op jit(solution)/shard_map/b8/pallas_call | solution.py:23
  98.5 9.2 %all_to_all.76.got = f32[32,1,256]{2,1,0:T(1,128)S(1)} all-to-all(f32[32,1,256]{2,1,0:T(1,128)S(1)} %get-tuple-element.142), channel_id=1, replica_groups=mesh['rows'=2,'batch'=16] {'rows','batch'}, dimensions={0} | all-to-all | bytes 65536 | tf_op jit(solution)/shard_map/all_to_all | solution.py:815
  107.7 2.5 %b9.1 = (bf16[28,32,128]{2,1,0:T(8,128)(2,1)S(1)}, f32[28,32,128]{2,1,0:T(8,128)S(1)}, f32[32,1,256]{2,1,0:T(1,128)S(1)}, f32[3,2,128]{2,1,0:T(2,128)}) custom-call(s32[8]{0:T(128)S(1)} %get-tuple-element.109.scal, f32[32,1,256]{2,1,0:T(1,128)S(1)} %all_to_all.76.got, f32[32,1,128]{2,1,0:T(1,128)S(1)} %get-tuple-element.124.labels, ...), custom_call_target="tpu_custom_call" | custom-call | bytes 4194304 | tf_op jit(solution)/shard_map/b9/pallas_call | solution.py:23
  110.3 8.9 %all_to_all.77.got = f32[32,1,256]{2,1,0:T(1,128)S(1)} all-to-all(f32[32,1,256]{2,1,0:T(1,128)S(1)} %get-tuple-element.146), channel_id=1, replica_groups=mesh['rows'=2,'batch'=16] {'rows','batch'}, dimensions={0} | all-to-all | bytes 65536 | tf_op jit(solution)/shard_map/all_to_all | solution.py:815
  119.2 2.6 %b10.1 = (bf16[28,32,128]{2,1,0:T(8,128)(2,1)S(1)}, f32[28,32,512]{2,1,0:T(8,128)S(1)}, f32[32,4,384]{2,1,0:T(4,128)S(1)}, f32[3,2,128]{2,1,0:T(2,128)}) custom-call(s32[8]{0:T(128)S(1)} %get-tuple-element.109.scal, f32[32,1,256]{2,1,0:T(1,128)S(1)} %all_to_all.77.got, f32[32,1,128]{2,1,0:T(1,128)S(1)} %get-tuple-element.124.labels, ...), custom_call_target="tpu_custom_call" | custom-call | bytes 4194304 | tf_op jit(solution)/shard_map/b10/pallas_call | solution.py:23
  121.8 11.5 %all_to_all.78.got = f32[32,4,384]{2,1,0:T(4,128)S(1)} all-to-all(f32[32,4,384]{2,1,0:T(4,128)S(1)} %get-tuple-element.150), channel_id=1, replica_groups=mesh['rows'=2,'batch'=16] {'rows','batch'}, dimensions={0} | all-to-all | bytes 393216 | tf_op jit(solution)/shard_map/all_to_all | solution.py:815
  133.3 3.0 %b11.1 = (bf16[28,32,512]{2,1,0:T(8,128)(2,1)S(1)}, bf16[28,32,512]{2,1,0:T(8,128)(2,1)S(1)}, f32[28,32,128]{2,1,0:T(8,128)S(1)}, f32[32,1,256]{2,1,0:T(1,128)S(...) custom-call(s32[8]{0:T(128)S(1)} %get-tuple-element.109.scal, f32[32,4,384]{2,1,0:T(4,128)S(1)} %all_to_all.78.got, ...), custom_call_target="tpu_custom_call" | custom-call | bytes 4194304 | tf_op jit(solution)/shard_map/b11/pallas_call | solution.py:23
  136.3 2.3 %g_most.1 = (bf16[3712,128]{1,0:T(8,128)(2,1)S(1)}, bf16[14,32,256]{2,1,0:T(8,128)(2,1)S(1)}, bf16[14,32,256]{2,1,0:T(8,128)(2,1)S(1)}) custom-call(s32[8]{0:T(128)S(1)} %get-tuple-element.109.scal, bf16[28,32,128]{2,1,0:T(8,128)(2,1)S(1)} %get-tuple-element.154.act_2b, bf16[28,32,512]{2,1,0:T(8,128)(2,1)S(1)} %get-tuple-element.155.dz_2c, ...), custom_call_target="tpu_custom_call" | custom-call | bytes 4194304 | tf_op jit(solution)/shard_map/g_most/pallas_call | solution.py:23
  138.6 9.1 %all_to_all.79.got = f32[32,1,256]{2,1,0:T(1,128)S(1)} all-to-all(f32[32,1,256]{2,1,0:T(1,128)S(1)} %get-tuple-element.166), channel_id=1, replica_groups=mesh['rows'=2,'batch'=16] {'rows','batch'}, dimensions={0} | all-to-all | bytes 65536 | tf_op jit(solution)/shard_map/all_to_all | solution.py:815
  147.7 3.3 %b12.1 = (bf16[28,32,128]{2,1,0:T(8,128)(2,1)S(1)}, bf16[28,64,128]{2,1,0:T(8,128)(2,1)S(1)}, bf16[28,64,128]{2,1,0:T(8,128)(2,1)S(1)}, f32[32,1,256]{2,1,0:T(1,128)S(1)}, f32[3,2,128]{2,1,0:T(2,128)}) custom-call(s32[8]{0:T(128)S(1)} %get-tuple-element.109.scal, f32[32,1,256]{2,1,0:T(1,128)S(1)} %all_to_all.79.got, ...), custom_call_target="tpu_custom_call" | custom-call | bytes 4194304 | tf_op jit(solution)/shard_map/b12/pallas_call | solution.py:23
  151.8 8.9 %all_to_all.80.got = f32[32,1,256]{2,1,0:T(1,128)S(1)} all-to-all(f32[32,1,256]{2,1,0:T(1,128)S(1)} %get-tuple-element.177), channel_id=1, replica_groups=mesh['rows'=2,'batch'=16] {'rows','batch'}, dimensions={0} | all-to-all | bytes 65536 | tf_op jit(solution)/shard_map/all_to_all | solution.py:815
  160.7 2.0 g_1a.1
  162.7 2.1 collective-permute-done.3.received
  165.0 21.5 %all_to_all.81.parts = bf16[32,80,128]{2,1,0:T(8,128)(2,1)S(1)} all-to-all(bf16[32,80,128]{2,1,0:T(8,128)(2,1)S(1)} %add_pair.1), channel_id=1, replica_groups=mesh['rows'=2,'batch'=16] {'rows','batch'}, dimensions={0} | all-to-all | bytes 1310720 | tf_op jit(solution)/shard_map/all_to_all | solution.py:815
  186.6 21.4 %all_to_all.82 = bf16[32,80,128]{2,1,0:T(8,128)(2,1)S(1)} all-to-all(bf16[32,80,128]{2,1,0:T(8,128)(2,1)S(1)} %add_all.1), channel_id=1, replica_groups=mesh['rows'=2,'batch'=16] {'rows','batch'}, dimensions={0} | all-to-all | bytes 1310720 | tf_op jit(solution)/shard_map/all_to_all | solution.py:815
  208.5 2.6 %collective-permute-done.2.gs_for = bf16[14,32,256]{2,1,0:T(8,128)(2,1)S(1)} collective-permute-done((bf16[14,32,256]{2,1,0:T(8,128)(2,1)S(1)}, bf16[14,32,256]{2,1,0:T(8,128)(2,1)S(1)}, u32[]{:S(2)}, u32[]{:S(2)}) %collective-permute-start.2) | collective-permute-done | bytes 229408 | tf_op jit(solution)/shard_map/ppermute | solution.py:823
  211.1 3.6 %b13.1 = (bf16[2,28,56,256]{3,2,1,0:T(8,128)(2,1)}, f32[3,2,128]{2,1,0:T(2,128)}) custom-call(s32[8]{0:T(128)S(1)} %get-tuple-element.109.scal, f32[32,1,256]{2,1,0:T(1,128)S(1)} %all_to_all.80.got, f32[32,1,128]{2,1,0:T(1,128)S(1)} %get-tuple-element.124.labels, f32[3,2,128]{2,1,0:T(2,128)S(1)} %bitcast.34, f32[4,128]{1,0:T(4,128)S(1)} %get-tuple-element.171.keeps_in.keeps, ...), custom_call_target="tpu_custom_call" | custom-call | bytes 4194304 | tf_op jit(solution)/shard_map/b13/pallas_call | solution.py:23
  214.6 2.2 unpack.1
  (78 shorter events, 14.1 us)
Async XLA Ops:
  0.7 1.4 copy-start
  2.1 0.8 copy-start.6
  4.9 10.4 %copy-start.1 = (bf16[3,3,128,128]{3,2,1,0:T(8,128)(2,1)S(1)}, bf16[3,3,128,128]{3,2,1,0:T(8,128)(2,1)}, u32[]{:S(2)}) copy-start(bf16[3,3,128,128]{3,2,1,0:T(8,128)(2,1)} %w2b.1) | copy-start | bytes 884740
  4.9 17.9 %copy-start.2 = (bf16[256,512]{1,0:T(8,128)(2,1)S(1)}, bf16[256,512]{1,0:T(8,128)(2,1)}, u32[]{:S(2)}) copy-start(bf16[256,512]{1,0:T(8,128)(2,1)} %w_1p.1) | copy-start | bytes 786436
  6.9 0.9 copy-start.4
  7.8 16.3 %copy-start.7 = (bf16[256,128]{1,0:T(8,128)(2,1)S(1)}, bf16[256,128]{1,0:T(8,128)(2,1)}, u32[]{:S(2)}) copy-start(bf16[256,128]{1,0:T(8,128)(2,1)} %w.19) | copy-start | bytes 196612
  7.8 16.3 %copy-start.25 = (f32[2,3,128]{2,0,1:T(2,128)S(1)}, f32[2,3,128]{2,0,1:T(2,128)}, u32[]{:S(2)}) copy-start(f32[2,3,128]{2,0,1:T(2,128)} %param.27) | copy-start | bytes 9220
  7.8 14.9 %collective-permute-start = (bf16[28,64,256]{2,1,0:T(8,128)(2,1)}, bf16[28,64,256]{2,1,0:T(8,128)(2,1)S(1)}, u32[]{:S(2)}, u32[]{:S(2)}) collective-permute-start(bf16[28,64,256]{2,1,0:T(8,128)(2,1)} %get-tuple-element.115), channel_id=1, source_target_pairs={{0,16},{16,0},{1,17},{17,1},{2,18},{18,2},{3,19},{19,3},{4,20},{20... | collective-permute-start | bytes 2752520 | tf_op jit(solution)/shard_map/ppermute | solution.py:823
  8.3 14.5 %all-to-all-start = ((f32[32,1,640]{2,1,0:T(1,128)}), f32[32,1,640]{2,1,0:T(1,128)S(1)}, u32[]{:S(2)}, u32[]{:S(2)}) async-start(f32[32,1,640]{2,1,0:T(1,128)} %get-tuple-element.110), calls=%async_computation | async-start | bytes 163840 | tf_op jit(solution)/shard_map/all_to_all | solution.py:815
  15.3 1.0 copy-start.13
  16.4 0.7 copy-start.11
  17.1 0.7 copy-start.14
  22.8 1.4 copy-start.17
  22.8 1.4 copy-start.21
  22.8 13.7 %copy-start.10 = (bf16[128,512]{1,0:T(8,128)(2,1)S(1)}, bf16[128,512]{1,0:T(8,128)(2,1)}, u32[]{:S(2)}) copy-start(bf16[128,512]{1,0:T(8,128)(2,1)} %w.18) | copy-start | bytes 393220
  22.8 13.7 %copy-start.27 = (f32[2,3,128]{2,0,1:T(2,128)S(1)}, f32[2,3,128]{2,0,1:T(2,128)}, u32[]{:S(2)}) copy-start(f32[2,3,128]{2,0,1:T(2,128)} %param.28) | copy-start | bytes 9220
  24.1 26.6 %copy-start.8 = (bf16[512,128]{1,0:T(8,128)(2,1)S(1)}, bf16[512,128]{1,0:T(8,128)(2,1)}, u32[]{:S(2)}) copy-start(bf16[512,128]{1,0:T(8,128)(2,1)} %w.17) | copy-start | bytes 393220
  24.1 26.6 %copy-start.23 = (f32[2,3,512]{2,0,1:T(2,128)S(1)}, f32[2,3,512]{2,0,1:T(2,128)}, u32[]{:S(2)}) copy-start(f32[2,3,512]{2,0,1:T(2,128)} %param.29) | copy-start | bytes 36868
  24.1 26.6 %copy-start.24 = (f32[2,3,512]{2,0,1:T(2,128)S(1)}, f32[2,3,512]{2,0,1:T(2,128)}, u32[]{:S(2)}) copy-start(f32[2,3,512]{2,0,1:T(2,128)} %param.30) | copy-start | bytes 36868
  50.7 11.1 %copy-start.26 = (f32[2,3,128]{2,0,1:T(2,128)S(1)}, f32[2,3,128]{2,0,1:T(2,128)}, u32[]{:S(2)}) copy-start(f32[2,3,128]{2,0,1:T(2,128)} %param.31) | copy-start | bytes 9220
  50.7 21.7 %copy-start.9 = (bf16[128,512]{1,0:T(8,128)(2,1)S(1)}, bf16[128,512]{1,0:T(8,128)(2,1)}, u32[]{:S(2)}) copy-start(bf16[128,512]{1,0:T(8,128)(2,1)} %w.16) | copy-start | bytes 393220
  50.7 21.6 %copy-start.28 = (f32[2,3,128]{2,0,1:T(2,128)S(1)}, f32[2,3,128]{2,0,1:T(2,128)}, u32[]{:S(2)}) copy-start(f32[2,3,128]{2,0,1:T(2,128)} %param.32) | copy-start | bytes 9220
  52.7 30.5 %copy-start.3 = (bf16[1,28,28,512]{3,2,1,0:T(8,128)(2,1)S(1)}, bf16[1,28,28,512]{3,2,1,0:T(8,128)(2,1)}, u32[]{:S(2)}) copy-start(bf16[1,28,28,512]{3,2,1,0:T(8,128)(2,1)} %param.34) | copy-start | bytes 2408452
  52.7 30.5 %copy-start.22 = (f32[2,3,512]{2,0,1:T(2,128)S(1)}, f32[2,3,512]{2,0,1:T(2,128)}, u32[]{:S(2)}) copy-start(f32[2,3,512]{2,0,1:T(2,128)} %param.33) | copy-start | bytes 36868
  96.0 11.7 %copy-start.12 = (bf16[3,128,384]{2,1,0:T(8,128)(2,1)S(1)}, bf16[3,128,384]{2,1,0:T(8,128)(2,1)}, u32[]{:S(2)}) copy-start(bf16[3,128,384]{2,1,0:T(8,128)(2,1)} %copy-done.11) | copy-start | bytes 884740
  136.3 11.4 %copy-start.15 = (bf16[256,512]{1,0:T(8,128)(2,1)S(1)}, bf16[256,512]{1,0:T(8,128)(2,1)}, u32[]{:S(2)}) copy-start(bf16[256,512]{1,0:T(8,128)(2,1)} %copy-done.14) | copy-start | bytes 786436
  136.3 11.4 %copy-start.19 = (bf16[256,256]{1,0:T(8,128)(2,1)S(1)}, bf16[256,256]{1,0:T(8,128)(2,1)}, u32[]{:S(2)}) copy-start(bf16[256,256]{1,0:T(8,128)(2,1)} %copy-done.18) | copy-start | bytes 393220
  162.7 2.2 collective-permute-start.3
  165.0 46.1 %copy-start.5 = (f32[28,64,128]{2,1,0:T(8,128)S(1)}, f32[28,64,128]{2,1,0:T(8,128)}, u32[]{:S(2)}) copy-start(f32[28,64,128]{2,1,0:T(8,128)} %copy-done.4) | copy-start | bytes 2752516
  208.0 6.7 %collective-permute-start.4 = (bf16[2560,128]{1,0:T(8,128)(2,1)S(1)}, bf16[2560,128]{1,0:T(8,128)(2,1)S(1)}, u32[]{:S(2)}, u32[]{:S(2)}) collective-permute-start(bf16[2560,128]{1,0:T(8,128)(2,1)S(1)} %bitcast.21), channel_id=1, source_target_pairs={{0,16},{16,0},{1,17},{17,1},{2,18},{18,2},{3,19},{19,3},{4,20},{20... | collective-permute-start | bytes 1966088 | tf_op jit(solution)/shard_map/ppermute | solution.py:823
  208.0 3.1 %collective-permute-start.1 = (bf16[28,64,128]{2,1,0:T(8,128)(2,1)S(1)}, bf16[28,64,128]{2,1,0:T(8,128)(2,1)S(1)}, u32[]{:S(2)}, u32[]{:S(2)}) collective-permute-start(bf16[28,64,128]{2,1,0:T(8,128)(2,1)S(1)} %get-tuple-element.180.dn_oth), channel_id=1, source_target_pairs={{0,16},{16,0},{1,17},{17,1},{2,18},{18,2},{3,19},{19,3},{4,20},{20... | collective-permute-start | bytes 1376264 | tf_op jit(solution)/shard_map/ppermute | solution.py:823
  208.5 2.6 %collective-permute-start.2 = (bf16[14,32,256]{2,1,0:T(8,128)(2,1)S(1)}, bf16[14,32,256]{2,1,0:T(8,128)(2,1)S(1)}, u32[]{:S(2)}, u32[]{:S(2)}) collective-permute-start(bf16[14,32,256]{2,1,0:T(8,128)(2,1)S(1)} %get-tuple-element.182), channel_id=1, source_target_pairs={{0,16},{16,0},{1,17},{17,1},{2,18},{18,2},{3,19},{19,3},{4,20},{20... | collective-permute-start | bytes 688136 | tf_op jit(solution)/shard_map/ppermute | solution.py:823
  (6 other events, 3.9 us)

commit v2 on v1

--- a/solution.py
+++ b/solution.py
@@ -1,3 +1,5 @@
+import functools
+
 import jax
 import jax.numpy as jnp
 from jax import lax
@@ -18,21 +20,25 @@
     return pl.BlockSpec(memory_space=memory)
 
 
-def stage(kernel, outs, scratch=(), flops=0, smem=(0,), smem_out=()):
+def stage(kernel, outs, scratch=(), smem=(0,), smem_out=(), hbm=()):
+    def place(i):
+        return pltpu.SMEM if i in smem else pltpu.HBM if i in hbm else pltpu.VMEM
+
     def call(*args):
+        args = [
+            pltpu.with_memory_space_constraint(a, pltpu.HBM) if i in hbm else a
+            for i, a in enumerate(args)
+        ]
         return pl.pallas_call(
             kernel,
             out_shape=tuple(jax.ShapeDtypeStruct(s, d) for s, d in outs),
-            in_specs=[full(pltpu.SMEM if i in smem else pltpu.VMEM) for i in range(len(args))],
+            in_specs=[full(place(i)) for i in range(len(args))],
             out_specs=tuple(
                 full(pltpu.SMEM if i in smem_out else pltpu.VMEM) for i in range(len(outs))
             ),
             scratch_shapes=list(scratch),
             compiler_params=pltpu.CompilerParams(vmem_limit_bytes=VMEM_LIMIT),
-            cost_estimate=pl.CostEstimate(
-                flops=flops, bytes_accessed=4 * 1024 * 1024, transcendentals=0
-            ),
-            name=kernel.__name__,
+            name=(kernel.func if isinstance(kernel, functools.partial) else kernel).__name__,
         )(*args)
 
     return call
@@ -174,8 +180,31 @@
     return sums, squares
 
 
-def f1(half_ref, group, width, gate, images, w, scal, x_own, x_for, z_own, z_for, send):
+def f1(
+    half_ref, group_at, width_at, gate_at, images, w_at, scal, x_own, x_for, z_own, z_for, send,
+    group, width, gate, raw, w, sems,
+):
     half = half_ref[0]
+    small = [
+        pltpu.make_async_copy(a, b, sems.at[k])
+        for k, (a, b) in enumerate(((group_at, group), (width_at, width), (gate_at, gate)))
+    ]
+    large = [
+        pltpu.make_async_copy(images.at[place], raw.at[k], sems.at[3 + k])
+        for k, place in enumerate((half, 1 - half))
+    ]
+    weight = pltpu.make_async_copy(w_at, w, sems.at[5])
+    for copy in (weight, *large, *small):
+        copy.start()
+    weight.wait()
+    rows = []
+    for k, (x_pad, z) in enumerate(((x_own, z_own), (x_for, z_for))):
+        large[k].wait()
+        widen(raw.at[k], x_pad)
+        sums, squares = first_project(x_pad, w, z)
+        rows += [down(sums), down(squares)]
+    for copy in small:
+        copy.wait()
     own, other = group[half], group[1 - half]
     scal[OWN] = own
     scal[OTHER] = other
@@ -184,12 +213,6 @@
     scal[GATE] = gate[own]
     for k in range(GATE + 1, scal.shape[0]):
         scal[k] = 0
-    widen(images.at[half], x_own)
-    widen(images.at[1 - half], x_for)
-    rows = []
-    for x_pad, z in ((x_own, z_own), (x_for, z_for)):
-        sums, squares = first_project(x_pad, w, z)
-        rows += [down(sums), down(squares)]
     spread(send, [*rows, jnp.full((1, LANES), (own + 4 * other).astype(F32))])
 
 
@@ -231,7 +254,7 @@
     return mean, rstd, gain, shift, count
 
 
-def conv_stats(z, pieces, send):
+def conv_stats(z, pieces, send, extra=()):
     keep = valid_cols(LANES)[None]
     rows = z.shape[0]
     step = rows // 4
@@ -246,10 +269,13 @@
         parts = values.reshape(-1, 8, LANES)
         sums = sums + jnp.sum(parts, axis=0)
         squares = squares + jnp.sum(parts * parts, axis=0)
-    spread(send, [down(sums), down(squares)])
-
-
-def f2(scal, got, z_own, x_oth, w, norm, w_cur, w_up, xs, z, send, labels, keeps, z_oth):
+    spread(send, [down(sums), down(squares), *extra])
+
+
+def f2(
+    scal, got, z_own, x_own, x_oth, w, norm, w_cur, w_up, stats_p,
+    xs, z, send, labels, keeps, keeps_all, z_oth, x_sum,
+):
     codes = got[:, :, 4 * LANES : 5 * LANES]
     others = jnp.floor(0.25 * codes)
     marks = codes - 4.0 * others
@@ -257,9 +283,8 @@
     rows = xs.shape[0] - 1
     pixels = 4.0 * rows * (COLS - 4)
     first_project(x_oth, w, z_oth, False)
-    for k, slot in enumerate((OWN, OTHER)):
-        label = scal[slot].astype(F32)
-        mine, theirs = (marks == label).astype(F32), (others == label).astype(F32)
+    for g in range(norm.shape[0]):
+        mine, theirs = (marks == float(g)).astype(F32), (others == float(g)).astype(F32)
         totals = [
             jnp.sum(
                 got[:, :, LANES * s : LANES * (s + 1)] * mine
@@ -268,11 +293,17 @@
             )
             for s in (0, 1)
         ]
-        mean, rstd = moments(*totals, group_count(marks, label) * pixels)
-        keeps[2 * k : 2 * k + 1, :] = mean
-        keeps[2 * k + 1 : 2 * k + 2, :] = rstd
+        mean, rstd = moments(*totals, group_count(marks, float(g)) * pixels)
+        keeps_all[2 * g : 2 * g + 1, :] = mean
+        keeps_all[2 * g + 1 : 2 * g + 2, :] = rstd
+    for k, slot in enumerate((OWN, OTHER)):
+        at = 2 * scal[slot]
+        keeps[2 * k : 2 * k + 1, :] = keeps_all[pl.ds(at, 1), :]
+        keeps[2 * k + 1 : 2 * k + 2, :] = keeps_all[pl.ds(at + 1, 1), :]
     mean, rstd = keeps[0:1, :], keeps[1:2, :]
     gain, shift = gain_of(norm, scal[OWN]), shift_of(norm, scal[OWN])
+    ones = jnp.ones((8, x_own.shape[0] * x_own.shape[1]), BF16)
+    x_sum[...] = mm(ones, flat(x_own[...])) + mm(ones, flat(x_oth[...]))
     scale = rstd * gain
     bias = shift - mean * scale
     keep = valid_cols(LANES) & chan_mask(scal[LIMIT], LANES)
@@ -297,7 +328,10 @@
             return carry
 
         lax.fori_loop(0, rows // 2, put, 0, unroll=2)
-    conv_stats(z, ((xs, 1, 0, w_cur[...]), (xs, 0, 3 * n, w_up[...])), send)
+    extra = [x_sum[0:1, n * b : n * (b + 1)] for b in range(x_sum.shape[1] // n)]
+    for k in (0, 1):
+        extra += [stats_p[k, :, n * b : n * (b + 1)] for b in range(stats_p.shape[2] // n)]
+    conv_stats(z, ((xs, 1, 0, w_cur[...]), (xs, 0, 3 * n, w_up[...])), send, extra)
 
 
 def expand(act, w, z, send, extra=()):
@@ -314,6 +348,7 @@
 
 
 def activate(scal, got, labels, z_in, norm, act, keeps):
+    got = got.at[:, :, 0 : 2 * LANES]
     rows = z_in.shape[0]
     pixels = 1.0 * rows * (COLS - 4)
     mean, rstd, gain, shift, _ = scale_shift(got, labels[...], scal, norm, pixels)
@@ -331,12 +366,27 @@
     lax.fori_loop(0, rows, put, 0, unroll=4)
 
 
-def f3(scal, got, labels, z_in, norm, w, stats_p, act, z, send, keeps):
+def f3(scal, got, labels, z_in, norm, w, x_sum, act, z, send, keeps, keeps_p, x_dev):
     activate(scal, got, labels, z_in, norm, act, keeps)
-    expand(act, w, z, send, (stats_p[0], stats_p[1]))
-
-
-def f4(scal, got, labels, zc, zp, norm_c, norm_p, w, joined, slope, z, send, keeps):
+    expand(act, w, z, send)
+    marks = labels[...]
+    label = scal[OWN].astype(F32)
+    inputs, outer = x_sum.shape[1] // LANES, z.shape[2] // LANES
+    total = group_sum(got, marks, label)
+    images = group_count(marks, label)
+    for b in range(inputs):
+        lanes = slice(LANES * b, LANES * (b + 1))
+        x_dev[:, lanes] = x_sum[0:1, lanes] - row(total, 2 + b) / images
+    pixels = images * (1.0 * z.shape[0] * (COLS - 4))
+    for b in range(outer):
+        lanes = slice(LANES * b, LANES * (b + 1))
+        first = 2 + inputs + b
+        mean, rstd = moments(row(total, first), row(total, first + outer), pixels)
+        keeps_p[0:1, lanes] = mean
+        keeps_p[1:2, lanes] = rstd
+
+
+def f4(scal, got, labels, zc, zp, norm_c, norm_p, keeps_p, w, joined, slope, z, send, keeps):
     rows, chans = zc.shape[0], zc.shape[2]
     pixels = 1.0 * rows * (COLS - 4)
     label = scal[OWN].astype(F32)
@@ -344,7 +394,7 @@
     total = group_sum(got, marks, label)
     count = tiled(group_count(marks, label), chans) * pixels
     mean_c, rstd_c = moments(row(total, 0), row(total, 1), count)
-    mean_p, rstd_p = moments(row(total, 2), row(total, 3), count)
+    mean_p, rstd_p = keeps_p[0:1, :], keeps_p[1:2, :]
     for k, v in enumerate((mean_c, rstd_c, mean_p, rstd_p)):
         keeps[k : k + 1, :] = v
     group = scal[OWN]
@@ -374,7 +424,7 @@
     spread(send, [down(sums), down(squares)])
 
 
-def f5(scal, got, labels, z_in, norm, w, x3, z, send, keeps):
+def f5(scal, got, labels, z_in, norm, w, xz, x3, z, send, keeps):
     rows = z_in.shape[0]
     pixels = 1.0 * rows * (COLS - 4)
     mean, rstd, gain, shift, _ = scale_shift(got, labels[...], scal, norm, pixels)
@@ -396,7 +446,12 @@
         return carry
 
     lax.fori_loop(0, rows, put, 0, unroll=2)
-    conv_stats(z, tuple((x3, y, 0, w[y]) for y in range(3)), send)
+    conv_stats(z, tuple((x3, y, 0, w[y]) for y in range(3)), send.at[:, :, 0 : 2 * n])
+    devices = send.shape[0]
+    share = xz.shape[0] // devices
+    pieces = xz[...].reshape(devices, share, n)
+    for q in range(share):
+        send[:, :, n * (2 + q) : n * (3 + q)] = pieces[:, q : q + 1, :]
 
 
 def f6(scal, got, labels, z_in, norm, w, act, z, send, keeps):
@@ -404,7 +459,7 @@
     expand(act, w, z, send)
 
 
-def b7(scal, got, labels, joined, z, norm, cot, result, grad_pre, send, keeps):
+def b7(scal, got, labels, joined, z, norm, cot, result, grad_pre, send, keeps, wide):
     rows, chans = z.shape[0], z.shape[2]
     cols = COLS - 4
     pixels = 1.0 * rows * cols
@@ -415,19 +470,22 @@
     scale = rstd * gain * gate
     bias = (shift - mean * rstd * gain) * gate
 
+    wide[...] = jnp.zeros(wide.shape, F32)
+
     def put(i, carry):
         sums, products = carry
-        zz = z[i, 0:cols, :]
-        v = joined[i, 0:cols, :].astype(F32) + zz * scale + bias
+        wide[0:cols, :] = cot[i].astype(F32)
+        zz = z[i]
+        v = joined[i].astype(F32) + zz * scale + bias
         s = sigmoid(v)
-        result[i] = (v * s).astype(BF16)
-        g = cot[i].astype(F32) * (s * (1.0 + v * (1.0 - s)))
-        grad_pre[i, 0:cols, :] = g
-        grad_pre[i, cols:COLS, :] = jnp.zeros((COLS - cols, chans), F32)
-        return sums + down(g), products + down(g * (zz - mean))
-
-    start = jnp.zeros((1, chans), F32)
+        result[i] = (v * s)[0:cols].astype(BF16)
+        g = wide[...] * (s * (1.0 + v * (1.0 - s)))
+        grad_pre[i] = g
+        return sums + fold(g), products + fold(g * (zz - mean))
+
+    start = zeros8(chans)
     sums, products = lax.fori_loop(0, rows, put, (start, start), unroll=2)
+    sums, products = down(sums), down(products)
     spread(send, [sums * gate, products * rstd * gate])
 
 
@@ -588,10 +646,7 @@
     slope_sums(scal, d, z_in, norm_in, keeps_in, dout, send)
 
 
-def b12(
-    scal, got, labels, dout_in, z, norm, keeps, b_even, b_odd, z_own, z_oth, norm_in, keeps_in,
-    dz, dn_own, dn_oth, send, grad_norm, d2, de, do, wide,
-):
+def b12(scal, got, labels, dout_in, z, norm, keeps, xs, d2, kept, sent, grad_norm, dz, packed):
     rows = z.shape[0]
     pixels = 1.0 * rows * (COLS - 4)
     mean, a, b, c = backward_norm(scal, got, labels, norm, keeps, pixels, grad_norm)
@@ -609,10 +664,27 @@
         return carry
 
     lax.fori_loop(0, rows, put, 0, unroll=4)
-    step = rows // 4
-    for k in range(4):
-        here = flat(d2[step * k : step * (k + 1)])
-        below = flat(d2[step * k + 1 : step * (k + 1) + 1])
+    low = flat(dz[...])
+    cur = mm_tn(flat(xs[1 : rows + 1]), low)
+    for k, (y, x) in enumerate(((1, 1), (1, 2), (1, 0), (2, 1), (2, 2), (2, 0))):
+        put_rows(packed, n * (3 * y + x), cur[n * k : n * (k + 1)])
+    up = mm_tn(flat(xs[0:rows, :, 3 * n : 6 * n]), low)
+    for k, (y, x) in enumerate(((0, 1), (0, 2), (0, 0))):
+        put_rows(packed, n * (3 * y + x), up[n * k : n * (k + 1)])
+    share_out(scal, packed, 9 * n, kept, sent)
+
+
+def b12_images(
+    scal, d2, b_even, b_odd, zz, norm_in, keeps_in, dn, sums_out, de, do, wide, *, own
+):
+    rows = de.shape[0]
+    n = LANES
+    half = scal[HALF]
+    first = rows * (half if own else 1 - half)
+    step = rows // 2
+    for k in range(2):
+        here = flat(d2[pl.ds(first + step * k, step)])
+        below = flat(d2[pl.ds(first + step * k + 1, step)])
         de[step * k : step * (k + 1)] = mm_nt(here, b_even[...]).reshape(step, COLS, 2 * n)
         odd = mm_nt(here, b_odd[:, 0 : 2 * n]) + mm_nt(below, b_odd[:, 2 * n : 4 * n])
         do[step * k : step * (k + 1)] = odd.reshape(step, COLS, 2 * n)
@@ -621,43 +693,38 @@
     scale = rstd_1 * gain_of(norm_in, group)
     bias = shift_of(norm_in, group) - mean_1 * scale
     keep = valid_cols(LANES) & chan_mask(scal[LIMIT], LANES)
-    half = scal[HALF]
-    totals = (zeros8(n), zeros8(n))
-    for k, (zz, dn) in enumerate(((z_own, dn_own), (z_oth, dn_oth))):
-        first = (rows // 2) * (half if k == 0 else 1 - half)
-
-        def emit(i, carry, zz=zz, dn=dn, first=first):
-            sums, products = carry
-            for ra in (0, 1):
-                planes = (de, do)[ra]
-                for cb in (0, 1):
-                    zv = zz[2 * i + ra, pl.ds(cb, COLS, stride=2), :]
-                    v = zv * scale + bias
-                    s = sigmoid(v)
-                    g = planes[first + i, :, n * cb : n * (cb + 1)]
-                    g = jnp.where(keep, g * (s * (1.0 + v * (1.0 - s))), 0.0)
-                    sums = sums + fold(g)
-                    products = products + fold(g * (zv - mean_1))
-                    wide[ra, pl.ds(cb, COLS, stride=2), :] = g
-                dn[2 * i + ra] = wide[ra].astype(BF16)
-            return sums, products
-
-        totals = lax.fori_loop(0, rows // 2, emit, totals, unroll=2)
-    spread(send, [down(totals[0]), down(totals[1]) * rstd_1])
+
+    def emit(i, carry):
+        sums, products = carry
+        for ra in (0, 1):
+            planes = (de, do)[ra]
+            for cb in (0, 1):
+                zv = zz[2 * i + ra, pl.ds(cb, COLS, stride=2), :]
+                v = zv * scale + bias
+                s = sigmoid(v)
+                g = planes[i, :, n * cb : n * (cb + 1)]
+                g = jnp.where(keep, g * (s * (1.0 + v * (1.0 - s))), 0.0)
+                sums = sums + fold(g)
+                products = products + fold(g * (zv - mean_1))
+                wide[ra, pl.ds(cb, COLS, stride=2), :] = g
+            dn[2 * i + ra] = wide[ra].astype(BF16)
+        return sums, products
+
+    totals = lax.fori_loop(0, rows, emit, (zeros8(n), zeros8(n)), unroll=2)
+    sums_out[0:1, :] = down(totals[0])
+    sums_out[1:2, :] = down(totals[1]) * rstd_1
 
 
 def b13(
     scal, got, labels, norm, keeps, w, z_own, z_for, dn_own, dn_for, gs_own, gs_for,
-    grad, grad_norm, dz, wide,
+    grad, grad_norm, dz, wide, *, at,
 ):
     rows, cols = grad.shape[1], grad.shape[2]
     half = scal[HALF]
     pixels = 2.0 * rows * cols
     marks = labels[...]
-    totals = []
+    totals = last_sums(got.at[:, at : at + 4, :], marks, norm.shape[0])
     for g in range(norm.shape[0]):
-        total = group_sum(got, marks, float(g))
-        totals.append((row(total, 0), row(total, 1)))
         grad_norm[g, 0:1, :] = totals[g][1]
         grad_norm[g, 1:2, :] = totals[g][0]
     keep = lax.broadcasted_iota(jnp.int32, (z_own.shape[1], LANES), 0) < cols
@@ -714,18 +781,28 @@
     return at
 
 
+def share_out(scal, packed, used, kept, sent):
+    if used < packed.shape[0]:
+        packed[used:, :] = jnp.zeros((packed.shape[0] - used, LANES), BF16)
+    half = scal[HALF]
+    size = kept.shape[0] * kept.shape[1]
+    for out, place in ((kept, half), (sent, 1 - half)):
+        out[...] = packed[pl.ds(pl.multiple_of(size * place, 16), size), :].reshape(out.shape)
+
+
 def g_most(
     scal, act_2b, dz_2c, x3, dz_2b, joined, dz_2a, act_1b, dz_1c, xee, dz_1p, w_1p,
-    out, gs_own, gs_oth,
+    kept, sent, gs_own, gs_oth, packed,
 ):
     rows = dz_2b.shape[0]
-    at = put_rows(out, 0, mm_tn(flat(act_2b[...]), flat(dz_2c[...])))
+    at = put_rows(packed, 0, mm_tn(flat(act_2b[...]), flat(dz_2c[...])))
     low = flat(dz_2b[...])
     for y in range(3):
-        at = put_rows(out, at, mm_tn(flat(x3[y : y + rows]), low))
-    at = put_rows(out, at, mm_tn(flat(joined[...]), flat(dz_2a[...])))
-    at = put_rows(out, at, mm_tn(flat(act_1b[...]), flat(dz_1c[...])))
-    put_rows(out, at, mm_tn(flat(xee[...]), flat(dz_1p[...])))
+        at = put_rows(packed, at, mm_tn(flat(x3[y : y + rows]), low))
+    at = put_rows(packed, at, mm_tn(flat(joined[...]), flat(dz_2a[...])))
+    at = put_rows(packed, at, mm_tn(flat(act_1b[...]), flat(dz_1c[...])))
+    at = put_rows(packed, at, mm_tn(flat(xee[...]), flat(dz_1p[...])))
+    share_out(scal, packed, at, kept, sent)
     half = scal[HALF]
     count = gs_own.shape[0]
     for k, gs in enumerate((gs_own, gs_oth)):
@@ -734,80 +811,119 @@
         gs[...] = got.reshape(gs.shape).astype(BF16)
 
 
-def g_1b(xs, dz, out):
-    rows = dz.shape[0]
-    low = flat(dz[...])
+def g_xz(keeps, x_own, x_oth, z_own, z_oth, out, low):
+    rows = z_own.shape[0]
+    mean = keeps[0:1, :]
+    value = None
+    for x, z in ((x_own, z_own), (x_oth, z_oth)):
+
+        def put(i, carry, z=z):
+            low[i] = (z[i] - mean).astype(BF16)
+            return carry
+
+        lax.fori_loop(0, rows, put, 0, unroll=4)
+        term = mm_tn(flat(x[...]), flat(low[...]))
+        value = term if value is None else value + term
+    at = value.shape[0]
+    out[0:at, :] = value
+    if at < out.shape[0]:
+        out[at:, :] = jnp.zeros((out.shape[0] - at, LANES), F32)
+
+
+def g_xd(scal, sums_own, sums_oth, norm, keeps, x_dev, x_own, x_oth, dn_own, dn_oth, out, sums, low):
+    rows = dn_own.shape[0]
     n = LANES
-    cur = mm_tn(flat(xs[1 : rows + 1]), low)
-    for k, (y, x) in enumerate(((1, 1), (1, 2), (1, 0), (2, 1), (2, 2), (2, 0))):
-        put_rows(out, n * (3 * y + x), cur[n * k : n * (k + 1)])
-    up = mm_tn(flat(xs[0:rows, :, 3 * n : 6 * n]), low)
-    for k, (y, x) in enumerate(((0, 1), (0, 2), (0, 0))):
-        put_rows(out, n * (3 * y + x), up[n * k : n * (k + 1)])
-
-
-def g_1a(
-    scal, got, labels, norm, keeps, z_own, z_oth, dn_own, dn_oth, x_own, x_oth, most, grad_1b,
-    kept, sent, dz, packed,
-):
-    rows = z_own.shape[0]
-    cols = 2 * (COLS - 4)
-    pixels = 2.0 * rows * cols
+    pixels = 1.0 * (2 * rows) * (2 * (COLS - 4))
+    sums[...] = sums_own[...] + sums_oth[...]
+    a = keeps[1:2, :] * gain_of(norm, scal[OWN])
+    local = sums[0:1, :] / pixels
+    value = None
+    for x, dn in ((x_own, dn_own), (x_oth, dn_oth)):
+
+        def put(i, carry, dn=dn):
+            low[i] = (a * (dn[i].astype(F32) - local)).astype(BF16)
+            return carry
+
+        lax.fori_loop(0, rows, put, 0, unroll=4)
+        term = mm_tn(flat(x[...]), flat(low[...]))
+        value = term if value is None else value + term
+    spread_dev = jnp.broadcast_to(x_dev[...], (8, x_dev.shape[1]))
+    column = jnp.transpose(spread_dev)[:, 0:1]
+    value = value + column * (a * local)
+    at = value.shape[0]
+    out[0:at, :] = value.astype(BF16)
+    if at < out.shape[0]:
+        out[at:, :] = jnp.zeros((out.shape[0] - at, n), BF16)
+
+
+def pack_last(tall, sums, kept, got, kept_1b, got_1b, send, *, stats_at):
+    n = LANES
+    devices = send.shape[0]
+    piece, share = kept.shape[1], tall.shape[0] // devices
+    first = kept.shape[0]
+    second = first + kept_1b.shape[0]
+    send[0:first, 0:piece, :] = (kept[...].astype(F32) + got[...].astype(F32)).astype(BF16)
+    send[first:second, 0:piece, :] = (kept_1b[...].astype(F32) + got_1b[...].astype(F32)).astype(BF16)
+    if second < devices:
+        send[second:, 0:piece, :] = jnp.zeros((devices - second, piece, n), BF16)
+    send[:, piece : piece + share, :] = tall[...].reshape(devices, share, n)
+    high = sums[...].astype(BF16)
+    rest = (sums[...] - high.astype(F32)).astype(BF16)
+    for k, v in enumerate((high, rest)):
+        send[:, stats_at + 2 * k : stats_at + 2 * k + 2, :] = jnp.broadcast_to(v[None], (devices, 2, n))
+
+
+def last_sums(stats, marks, groups):
+    values = stats[:, 0:2, :].astype(F32) + stats[:, 2:4, :].astype(F32)
+    out = []
+    for g in range(groups):
+        total = jnp.sum(values * (marks == float(g)).astype(F32), axis=0)
+        out.append((total[0:1], total[1:2]))
+    return out
+
+
+def add_all(got, labels, norm, keeps_all, xz_got, out, *, at, pixels):
+    devices, n = got.shape[0], LANES
+    half = devices // 2
+    share = xz_got.shape[2] // n - 2
+    piece = out.shape[1] - share
     marks = labels[...]
-    group = scal[OWN]
-    total = group_sum(got, marks, group.astype(F32))
-    count = group_count(marks, group.astype(F32)) * pixels
-    mean, rstd = keeps[0:1, :], keeps[1:2, :]
-    a = rstd * gain_of(norm, group)
-    b = -(a * rstd) * row(total, 1) / count
-    c = -a * row(total, 0) / count
-    keep = lax.broadcasted_iota(jnp.int32, (z_own.shape[1], LANES), 0) < cols
-    value = None
-    for z, dn, x in ((z_own, dn_own, x_own), (z_oth, dn_oth, x_oth)):
-
-        def put(i, carry, z=z, dn=dn):
-            v = a * dn[i].astype(F32) + b * (z[i] - mean) + c
-            dz[i] = jnp.where(keep, v, 0.0).astype(BF16)
-            return carry
-
-        lax.fori_loop(0, rows, put, 0, unroll=2)
-        term = mm_tn(flat(x[...]), flat(dz[...]))
-        value = term if value is None else value + term
-    at = put_rows(packed, 0, value)
-    packed[at : at + grad_1b.shape[0], :] = grad_1b[...]
-    at += grad_1b.shape[0]
-    packed[at : at + most.shape[0], :] = most[...]
-    at += most.shape[0]
-    if at < packed.shape[0]:
-        packed[at:, :] = jnp.zeros((packed.shape[0] - at, LANES), BF16)
+    value = jnp.sum(got[:, piece : piece + share, :].astype(F32), axis=0)
+    sums = last_sums(got.at[:, at : at + 4, :], marks, norm.shape[0])
+    for g in range(norm.shape[0]):
+        rstd = keeps_all[2 * g + 1 : 2 * g + 2, :]
+        count = group_count(marks, float(g)) * pixels
+        b = -(rstd * rstd * gain_of(norm, g)) * sums[g][1] / count
+        same = (marks == float(g)).astype(F32)
+        rows = [
+            jnp.sum(xz_got[:, :, n * (2 + q) : n * (3 + q)] * same, axis=0) for q in range(share)
+        ]
+        value = value + jnp.concatenate(rows, axis=0) * b
+    for k in (0, 1):
+        total = jnp.sum(got[half * k : half * (k + 1), 0:piece, :].astype(F32), axis=0).astype(BF16)
+        out[half * k : half * (k + 1), 0:piece, :] = jnp.broadcast_to(total[None], (half, piece, n))
+    out[:, piece:, :] = jnp.broadcast_to(value.astype(BF16)[None], (devices, share, n))
+
+
+def unpack(scal, own, other, w_1a, w_1b, w_2c, w_2b, w_2a, w_1c, w_1p, tall, packed, packed_1b):
     half = scal[HALF]
-    size = kept.shape[0] * kept.shape[1]
-    for out, place in ((kept, half), (sent, 1 - half)):
-        out[...] = packed[pl.ds(pl.multiple_of(size * place, 16), size), :].reshape(out.shape)
-
-
-def add_pair(kept, received, out):
-    out[...] = (kept[...].astype(F32) + received[...].astype(F32)).astype(BF16)
-
-
-def add_all(parts, out):
-    half = parts.shape[0] // 2
-    for k in (0, 1):
-        total = jnp.sum(parts[half * k : half * (k + 1)].astype(F32), axis=0).astype(BF16)
-        out[half * k : half * (k + 1)] = jnp.broadcast_to(total[None], (half, *total.shape))
-
-
-def unpack(scal, own, other, w_1a, w_1b, w_2c, w_2b, w_2a, w_1c, w_1p, packed):
-    half = scal[HALF]
-    size = own.shape[0]
+    devices = own.shape[0]
+    piece = packed.shape[1]
+    first, second = packed.shape[0] // 2, packed_1b.shape[0] // 2
     for part, place in ((own, half), (other, 1 - half)):
-        packed[pl.ds(pl.multiple_of(size * place, 16), size), :] = part[...]
+        packed[pl.ds(first * place, first)] = part[0:first, 0:piece, :]
+        packed_1b[pl.ds(second * place, second)] = part[first : first + second, 0:piece, :]
+    share = own.shape[1] - piece
+    tall[...] = own[:, piece:, :].astype(F32).reshape(tall.shape)
+    w_1a[...] = tall[0 : w_1a.shape[0], :]
+    flat_1b, rest = flat(packed_1b[...]), flat(packed[...])
+    w_1b[...] = flat_1b[0 : w_1b.shape[0]].astype(F32)
 
     def source(at, rows):
-        return packed[at : at + rows, :].astype(F32)
+        return rest[at : at + rows].astype(F32)
 
     at = 0
-    for out in (w_1a, w_1b, w_2c, w_2b, w_2a, w_1c, w_1p):
+    for out in (w_2c, w_2b, w_2a, w_1c, w_1p):
         at = take_rows(source, at, out)
 
 
@@ -856,49 +972,65 @@
 
     wide_in = ((rows, cols_in, inputs), BF16)
     wide_z = ((rows, cols_in, n), F32)
+    raw = images.shape
     scal, x_own, x_for, z_own, z_for, s1 = stage(
         f1, [((8,), jnp.int32), wide_in, wide_in, wide_z, wide_z, send(5)],
-        smem=(0, 1, 2, 3), smem_out=(0,),
+        [*(pltpu.SMEM(v.shape, jnp.int32) for v in (group, width, gate)),
+         pltpu.VMEM(raw, BF16), pltpu.VMEM(w_1a.shape, BF16), pltpu.SemaphoreType.DMA((6,))],
+        smem=(0,), smem_out=(0,), hbm=(1, 2, 3, 4, 5),
     )(half, group, width, gate, images, w_1a)
-    x_oth = swap(x_for)
-    g1 = gather(s1)
+    s1, v_1b, v_2b = tie(s1, w_1b, w_2b)
     w_cur, w_up, b_even, b_odd, b_same = stage(
         prepare,
         [((6 * n, n), BF16), ((3 * n, n), BF16), ((2 * n, 2 * n), BF16), ((2 * n, 4 * n), BF16),
          ((3, n, 3 * n), BF16)],
         smem=(),
-    )(w_1b, w_2b)
-    g1, w_cur, w_up = tie(g1, w_cur, w_up)
-    xs, z_1b, s2, labels, k_1a, z_oth = stage(
-        f2,
-        [((rows + 1, COLS, 6 * n), BF16), maps(n), send(2), ((m, 1, n), F32), mean_scale(n, 2),
-         wide_z],
-    )(scal, g1, z_own, x_oth, w_1a, norm_1a, w_cur, w_up)
+    )(v_1b, v_2b)
+    s1, x_for, w_cur, w_up, b_even, b_odd, b_same = tie(
+        s1, x_for, w_cur, w_up, b_even, b_odd, b_same
+    )
+    x_oth = swap(x_for)
+    g1 = gather(s1)
+    g1, x_oth = tie(g1, x_oth)
     xee, z_1p, stats_1p = stage(
         f1_strided,
         [maps(inputs, BF16), maps(outer), ((2, 1, outer), F32)],
         [pltpu.VMEM((inputs // n, cols_in, n), F32)],
     )(scal, x_own, x_oth, w_1p)
-    s2, xee, z_1p, stats_1p = tie(s2, xee, z_1p, stats_1p)
+    xs, z_1b, s2, labels, k_1a, k_all, z_oth, x_sum = stage(
+        f2,
+        [((rows + 1, COLS, 6 * n), BF16), maps(n), send(2 + (inputs + 2 * outer) // n),
+         ((m, 1, n), F32), mean_scale(n, 2), mean_scale(n, norm_1a.shape[0]), wide_z,
+         ((8, inputs), F32)],
+    )(scal, g1, z_own, x_own, x_oth, w_1a, norm_1a, w_cur, w_up, stats_1p)
     g2 = gather(s2)
-    act_1b, z_1c, s3, k_1b = stage(
-        f3, [maps(n, BF16), maps(outer), send(4, outer), mean_scale(n)]
-    )(scal, g2, labels, z_1b, norm_1b, w_1c, stats_1p)
+    act_1b, z_1c, s3, k_1b, k_p, x_dev = stage(
+        f3, [maps(n, BF16), maps(outer), send(2, outer), mean_scale(n), mean_scale(outer),
+             ((1, inputs), F32)],
+    )(scal, g2, labels, z_1b, norm_1b, w_1c, x_sum)
     g3 = gather(s3)
     joined, slope, z_2a, s4, k_cp = stage(
         f4, [maps(outer, BF16), maps(outer), maps(n), send(2), mean_scale(outer, 2)]
-    )(scal, g3, labels, z_1c, z_1p, norm_1c, norm_1p, w_2a)
+    )(scal, g3, labels, z_1c, z_1p, norm_1c, norm_1p, k_p, w_2a)
+    share = -(-inputs // devices)
+    half_in = ((rows, cols_in, n), BF16)
+    s4, k_1a = tie(s4, k_1a)
+    (xz,) = stage(g_xz, [((devices * share, n), F32)], [pltpu.VMEM(half_in[0], BF16)], smem=())(
+        k_1a, x_own, x_oth, z_own, z_oth
+    )
+    s4, xz = tie(s4, xz)
     g4 = gather(s4)
     x3, z_2b, s5, k_2a = stage(
-        f5, [((rows + 2, COLS, 3 * n), BF16), maps(n), send(2), mean_scale(n)]
-    )(scal, g4, labels, z_2a, norm_2a, w_2b.reshape(3, 3 * n, n))
+        f5, [((rows + 2, COLS, 3 * n), BF16), maps(n), send(2 + share), mean_scale(n)]
+    )(scal, g4, labels, z_2a, norm_2a, w_2b.reshape(3, 3 * n, n), xz)
     g5 = gather(s5)
     act_2b, z_2c, s6, k_2b = stage(
         f6, [maps(n, BF16), maps(outer), send(2, outer), mean_scale(n)]
     )(scal, g5, labels, z_2b, norm_2b, w_2c)
     g6 = gather(s6)
     result, grad_pre, s7, k_2c = stage(
-        b7, [(cotangent.shape[1:], BF16), maps(outer), send(2, outer), mean_scale(outer)]
+        b7, [(cotangent.shape[1:], BF16), maps(outer), send(2, outer), mean_scale(outer)],
+        [pltpu.VMEM((COLS, outer), F32)],
     )(scal, g6, labels, joined, z_2c, norm_2c, cotangent[0])
     g7 = gather(s7)
     dz_2c, dout_2b, s8, grad_norm_2c = stage(
@@ -920,42 +1052,62 @@
     )(scal, g10, labels, grad_pre_2, z_1c, z_1p, norm_1c, norm_1p, k_cp, w_1c, z_1b, norm_1b, k_1b)
     half_map = ((rows // 2, COLS, inputs), BF16)
     most_rows = sum(v.size for v in (w_2c, w_2b, w_2a, w_1c, w_1p)) // n
-    most, gs_own, gs_send = stage(g_most, [((most_rows, n), BF16), half_map, half_map])(
-        scal, act_2b, dz_2c, x3, dz_2b, joined, dz_2a, act_1b, dz_1c, xee, dz_1p, w_1p
-    )
-    s11, most, gs_own, gs_send = tie(s11, most, gs_own, gs_send)
-    gs_for = swap(gs_send)
-    g11 = gather(s11)
-    half_in = ((rows, cols_in, n), BF16)
-    dz_1b, dn_own, dn_send, s12, grad_norm_1b = stage(
-        b12, [maps(n, BF16), half_in, half_in, send(2), *params(norm_1b)],
-        [pltpu.VMEM((rows + 1, COLS, 2 * n), BF16), scratch(2 * n), scratch(2 * n),
-         pltpu.VMEM((2, cols_in, n), F32)],
-    )(scal, g11, labels, dout_1b, z_1b, norm_1b, k_1b, b_even, b_odd, z_own, z_oth, norm_1a, k_1a)
-    (grad_1b,) = stage(g_1b, [((w_1b.size // n, n), BF16)], smem=())(xs, dz_1b)
-    s12, grad_1b, dn_own, dn_send = tie(s12, grad_1b, dn_own, dn_send)
-    dn_for = swap(dn_send)
+    rows_1b = w_1b.size // n
+    piece = 16
+    while -(-most_rows // (2 * piece)) - (-rows_1b // (2 * piece)) > devices:
+        piece += 16
+    first, second = -(-most_rows // (2 * piece)), -(-rows_1b // (2 * piece))
+    part, part_1b = ((first, piece, n), BF16), ((second, piece, n), BF16)
+    kept, sent, gs_own, gs_send = stage(
+        g_most, [part, part, half_map, half_map], [pltpu.VMEM((2 * first * piece, n), BF16)]
+    )(scal, act_2b, dz_2c, x3, dz_2b, joined, dz_2a, act_1b, dz_1c, xee, dz_1p, w_1p)
+    s11, sent, gs_send = tie(s11, sent, gs_send)
+    g11, sent, gs_send = tie(gather(s11), sent, gs_send)
+    got, gs_for = swap(sent), swap(gs_send)
+    d2, kept_1b, sent_1b, grad_norm_1b = stage(
+        b12, [((rows + 1, COLS, 2 * n), BF16), part_1b, part_1b, *params(norm_1b)],
+        [scratch(n, BF16), pltpu.VMEM((2 * second * piece, n), BF16)],
+    )(scal, g11, labels, dout_1b, z_1b, norm_1b, k_1b, xs)
+    got_1b = swap(sent_1b)
+    sides = []
+    for own, z in ((False, z_oth), (True, z_own)):
+        sides.append(
+            stage(
+                functools.partial(b12_images, own=own), [half_in, ((2, n), F32)],
+                [pltpu.VMEM((rows // 2, COLS, 2 * n), F32), pltpu.VMEM((rows // 2, COLS, 2 * n), F32),
+                 pltpu.VMEM((2, cols_in, n), F32)],
+            )(scal, d2, b_even, b_odd, z, norm_1a, k_1a)
+        )
+        if not own:
+            dn_for = swap(sides[0][0])
+            d2, _ = tie(d2, sides[0][0])
+    (dn_send, sums_send), (dn_own, sums_own) = sides
+    stats_at = piece + -(-share // 8) * 8
+    high = -(-(stats_at + 4) // 16) * 16
+    tall, sums_1a = stage(
+        g_xd, [((devices * share, n), BF16), ((2, n), F32)], [pltpu.VMEM(half_in[0], BF16)]
+    )(scal, sums_own, sums_send, norm_1a, k_1a, x_dev, x_own, x_oth, dn_own, dn_send)
+    tall, gs_for, dn_for = tie(tall, gs_for, dn_for)
+    (s12,) = stage(
+        functools.partial(pack_last, stats_at=stats_at), [((devices, high, n), BF16)], smem=()
+    )(tall, sums_1a, kept, got, kept_1b, got_1b)
     g12 = gather(s12)
-    all_rows = most_rows + (w_1b.size + w_1a.size) // n
-    unit = 2 * devices * 16
-    piece = -(-all_rows // unit) * 16
-    share = ((devices, piece, n), BF16)
-    kept, sent = stage(
-        g_1a, [share, share],
-        [pltpu.VMEM(half_in[0], BF16), pltpu.VMEM((2 * devices * piece, n), BF16)],
-    )(scal, g12, labels, norm_1a, k_1a, z_own, z_oth, dn_own, dn_send, x_own, x_oth, most, grad_1b)
-    (pair,) = stage(add_pair, [share], smem=())(kept, swap(sent))
-    (mine,) = stage(add_all, [share], smem=())(gather(pair))
+    pixels = 4.0 * images.shape[1] * images.shape[1]
+    (mine,) = stage(
+        functools.partial(add_all, at=stats_at, pixels=pixels),
+        [((devices, piece + share, n), BF16)], smem=(),
+    )(g12, labels, norm_1a, k_all, g5)
     grad_images, grad_norm_1a = stage(
-        b13, [(images.shape, BF16), *params(norm_1a)],
+        functools.partial(b13, at=stats_at), [(images.shape, BF16), *params(norm_1a)],
         [pltpu.VMEM(half_in[0], BF16), pltpu.VMEM((inputs // n, rows, cols_in, n), F32)],
     )(scal, g12, labels, norm_1a, k_1a, w_1a, z_own, z_for, dn_own, dn_for, gs_own, gs_for)
-    part = gather(mine).reshape(devices * piece, n)
+    whole = gather(mine)
     totals = stage(
         unpack,
         [(v.shape, F32) for v in (w_1a, w_1b.reshape(-1, n), w_2c, w_2b.reshape(-1, n), w_2a, w_1c, w_1p)],
-        [pltpu.VMEM((2 * devices * piece, n), BF16)],
-    )(scal, part, swap(part))
+        [pltpu.VMEM((devices * share, n), F32), pltpu.VMEM((2 * first, piece, n), BF16),
+         pltpu.VMEM((2 * second, piece, n), BF16)],
+    )(scal, whole, swap(whole))
     t_1a, t_1b, t_2c, t_2b, t_2a, t_1c, t_1p = totals
     grads = (
         grad_norm_1a, grad_norm_1b, grad_norm_1c, grad_norm_1p,

time: 217 us -> 207 us (0.954)
  local copies, waits for them, and re-layouts: 9.57 us -> 0.09 us
  blocking collectives: 151 us -> 160 us
  waiting for transfers between devices: 7.65 us -> 0.02 us
  starting transfers between devices: 8 us -> 1.61 us
  Pallas kernels: 40.1 us -> 43.9 us
    unnamed x64 -> x30, local copies, waits for them, and re-layouts: 9.57 us -> 0.09 us
    all_to_all x13, blocking collectives: 151 us -> 160 us  [gather(): return lax.all_to_all(send, AXES, 0, 0)]
    all_to_all x1 -> x0, starting transfers between devices: 6.96 us -> none  [gather(): return lax.all_to_all(send, AXES, 0, 0)]
    ppermute x5 -> x6, waiting for transfers between devices: 4.66 us -> 0.02 us  [swap(): return lax.ppermute(block, 'rows', [(0, 1), (1, 0)])]
    pallas_call x21 -> x23, Pallas kernels: 40.1 us -> 43.9 us  [call(): pl.pallas_call(kernel, out_shape=tuple((jax.ShapeDtypeStruct(s, d) for s,...]
    all_to_all x1 -> x0, waiting for transfers between devices: 2.99 us -> none  [gather(): return lax.all_to_all(send, AXES, 0, 0)]
  transfers between devices with their start and end apart: 6 -> 6, of which waited for: 3 -> 0; matrix products, arithmetic and copies ran while one was open for 0% -> 0% of each run, Pallas kernels for 2% -> 5%
where the time goes in v2:
time: 207 us; the launch traced here: 206 us
  blocking collectives  160 us (77%)
  Pallas kernels  43.9 us (21%)
    all_to_all x13, blocking collectives, gather(): return lax.all_to_all(send, AXES, 0, 0)  160 us
    pallas_call x23, Pallas kernels, call(): pl.pallas_call(kernel, out_shape=tuple((jax.ShapeDtypeStruct(s, d) for s,...  43.9 us
  transfers between devices with their start and end apart: 6, of which 0 were waited for; matrix products, arithmetic and copies ran while one was open for 0% of the time, Pallas kernels for 5%

profile of v2, /device:TPU:0, one launch (start us, length us, event | category | flops | bytes accessed | tf_op | source)
XLA Modules:
  0.0 206.5 jit_solution(8031234130706746123)
XLA Ops:
  0.7 2.9 %f1.1 = (s32[8]{0:T(128)S(1)}, bf16[28,64,256]{2,1,0:T(8,128)(2,1)S(1)}, bf16[28,64,256]{2,1,0:T(8,128)(2,1)S(1)}, f32[28,64,128]{2,1,0:T(8,128)S(1)}, f32[28,64...) custom-call(s32[1]{0:T(128)} %bitcast.half_ref, s32[2]{0:T(128)} %group_at.1, s32[3]{0:T(128)} %width_at.1, s32[3]{0:T(128)} %gate_at.1, ...), custom_call_target="tpu_custom_call" | custom-call | tf_op jit(solution)/shard_map/f1/pallas_call | solution.py:32
  4.3 14.2 %all_to_all.65.got = f32[32,1,640]{2,1,0:T(1,128)S(1)} all-to-all(f32[32,1,640]{2,1,0:T(1,128)S(1)} %get-tuple-element.139), channel_id=1, replica_groups=mesh['rows'=2,'batch'=16] {'rows','batch'}, dimensions={0} | all-to-all | bytes 163840 | tf_op jit(solution)/shard_map/all_to_all | solution.py:931
  18.5 1.3 f1_strided.1
  19.9 3.1 %f2.1 = (bf16[29,32,768]{2,1,0:T(8,128)(2,1)S(1)}, f32[28,32,128]{2,1,0:T(8,128)S(1)}, f32[32,1,1536]{2,1,0:T(1,128)S(1)}, f32[32,1,128]{2,1,0:T(1,128)S(1)}, f3...) custom-call(s32[8]{0:T(128)S(1)} %get-tuple-element.128.scal, ...), custom_call_target="tpu_custom_call" | custom-call | tf_op jit(solution)/shard_map/f2/pallas_call | solution.py:32
  23.0 11.5 %all_to_all.66.got = f32[32,1,1536]{2,1,0:T(1,128)S(1)} all-to-all(f32[32,1,1536]{2,1,0:T(1,128)S(1)} %get-tuple-element.148), channel_id=1, replica_groups=mesh['rows'=2,'batch'=16] {'rows','batch'}, dimensions={0} | all-to-all | bytes 393216 | tf_op jit(solution)/shard_map/all_to_all | solution.py:931
  34.5 1.4 f3.1
  35.9 9.6 %all_to_all.67.got = f32[32,4,256]{2,1,0:T(4,128)S(1)} all-to-all(f32[32,4,256]{2,1,0:T(4,128)S(1)} %get-tuple-element.152), channel_id=1, replica_groups=mesh['rows'=2,'batch'=16] {'rows','batch'}, dimensions={0} | all-to-all | bytes 262144 | tf_op jit(solution)/shard_map/all_to_all | solution.py:931
  45.6 1.9 f4.1
  48.5 9.1 %all_to_all.68.got = f32[32,1,256]{2,1,0:T(1,128)S(1)} all-to-all(f32[32,1,256]{2,1,0:T(1,128)S(1)} %get-tuple-element.161), channel_id=1, replica_groups=mesh['rows'=2,'batch'=16] {'rows','batch'}, dimensions={0} | all-to-all | bytes 65536 | tf_op jit(solution)/shard_map/all_to_all | solution.py:931
  57.6 1.7 f5.1
  59.3 10.5 %all_to_all.69.got.xz_got = f32[32,1,1280]{2,1,0:T(1,128)S(1)} all-to-all(f32[32,1,1280]{2,1,0:T(1,128)S(1)} %get-tuple-element.164), channel_id=1, replica_groups=mesh['rows'=2,'batch'=16] {'rows','batch'}, dimensions={0} | all-to-all | bytes 327680 | tf_op jit(solution)/shard_map/all_to_all | solution.py:931
  69.8 1.2 f6.1
  71.1 9.6 %all_to_all.70.got = f32[32,4,256]{2,1,0:T(4,128)S(1)} all-to-all(f32[32,4,256]{2,1,0:T(4,128)S(1)} %get-tuple-element.166), channel_id=1, replica_groups=mesh['rows'=2,'batch'=16] {'rows','batch'}, dimensions={0} | all-to-all | bytes 262144 | tf_op jit(solution)/shard_map/all_to_all | solution.py:931
  80.7 3.0 %b7.1 = (bf16[28,28,512]{2,1,0:T(8,128)(2,1)}, f32[28,32,512]{2,1,0:T(8,128)S(1)}, f32[32,4,256]{2,1,0:T(4,128)S(1)}, f32[2,512]{1,0:T(2,128)S(1)}) custom-call(s32[8]{0:T(128)S(1)} %get-tuple-element.128.scal, f32[32,4,256]{2,1,0:T(4,128)S(1)} %all_to_all.70.got, f32[32,1,128]{2,1,0:T(1,128)S(1)} %get-tuple-element.149.labels, ...), custom_call_target="tpu_custom_call" | custom-call | tf_op jit(solution)/shard_map/b7/pallas_call | solution.py:32
  83.7 9.9 %all_to_all.71.got = f32[32,4,256]{2,1,0:T(4,128)S(1)} all-to-all(f32[32,4,256]{2,1,0:T(4,128)S(1)} %get-tuple-element.170), channel_id=1, replica_groups=mesh['rows'=2,'batch'=16] {'rows','batch'}, dimensions={0} | all-to-all | bytes 262144 | tf_op jit(solution)/shard_map/all_to_all | solution.py:931
  93.6 2.5 %b8.1 = (bf16[28,32,512]{2,1,0:T(8,128)(2,1)S(1)}, f32[28,32,128]{2,1,0:T(8,128)S(1)}, f32[32,1,256]{2,1,0:T(1,128)S(1)}, f32[3,2,512]{2,1,0:T(2,128)}) custom-call(s32[8]{0:T(128)S(1)} %get-tuple-element.128.scal, f32[32,4,256]{2,1,0:T(4,128)S(1)} %all_to_all.71.got, f32[32,1,128]{2,1,0:T(1,128)S(1)} %get-tuple-element.149.labels, ...), custom_call_target="tpu_custom_call" | custom-call | tf_op jit(solution)/shard_map/b8/pallas_call | solution.py:32
  96.1 9.2 %all_to_all.72.got = f32[32,1,256]{2,1,0:T(1,128)S(1)} all-to-all(f32[32,1,256]{2,1,0:T(1,128)S(1)} %get-tuple-element.174), channel_id=1, replica_groups=mesh['rows'=2,'batch'=16] {'rows','batch'}, dimensions={0} | all-to-all | bytes 65536 | tf_op jit(solution)/shard_map/all_to_all | solution.py:931
  105.3 2.5 %b9.1 = (bf16[28,32,128]{2,1,0:T(8,128)(2,1)S(1)}, f32[28,32,128]{2,1,0:T(8,128)S(1)}, f32[32,1,256]{2,1,0:T(1,128)S(1)}, f32[3,2,128]{2,1,0:T(2,128)}) custom-call(s32[8]{0:T(128)S(1)} %get-tuple-element.128.scal, f32[32,1,256]{2,1,0:T(1,128)S(1)} %all_to_all.72.got, f32[32,1,128]{2,1,0:T(1,128)S(1)} %get-tuple-element.149.labels, ...), custom_call_target="tpu_custom_call" | custom-call | tf_op jit(solution)/shard_map/b9/pallas_call | solution.py:32
  107.8 8.9 %all_to_all.73.got = f32[32,1,256]{2,1,0:T(1,128)S(1)} all-to-all(f32[32,1,256]{2,1,0:T(1,128)S(1)} %get-tuple-element.178), channel_id=1, replica_groups=mesh['rows'=2,'batch'=16] {'rows','batch'}, dimensions={0} | all-to-all | bytes 65536 | tf_op jit(solution)/shard_map/all_to_all | solution.py:931
  116.7 2.6 %b10.1 = (bf16[28,32,128]{2,1,0:T(8,128)(2,1)S(1)}, f32[28,32,512]{2,1,0:T(8,128)S(1)}, f32[32,4,384]{2,1,0:T(4,128)S(1)}, f32[3,2,128]{2,1,0:T(2,128)}) custom-call(s32[8]{0:T(128)S(1)} %get-tuple-element.128.scal, f32[32,1,256]{2,1,0:T(1,128)S(1)} %all_to_all.73.got, f32[32,1,128]{2,1,0:T(1,128)S(1)} %get-tuple-element.149.labels, ...), custom_call_target="tpu_custom_call" | custom-call | tf_op jit(solution)/shard_map/b10/pallas_call | solution.py:32
  119.3 11.5 %all_to_all.74.got = f32[32,4,384]{2,1,0:T(4,128)S(1)} all-to-all(f32[32,4,384]{2,1,0:T(4,128)S(1)} %get-tuple-element.182), channel_id=1, replica_groups=mesh['rows'=2,'batch'=16] {'rows','batch'}, dimensions={0} | all-to-all | bytes 393216 | tf_op jit(solution)/shard_map/all_to_all | solution.py:931
  130.8 3.0 %b11.1 = (bf16[28,32,512]{2,1,0:T(8,128)(2,1)S(1)}, bf16[28,32,512]{2,1,0:T(8,128)(2,1)S(1)}, f32[28,32,128]{2,1,0:T(8,128)S(1)}, f32[32,1,256]{2,1,0:T(1,128)S(...) custom-call(s32[8]{0:T(128)S(1)} %get-tuple-element.128.scal, f32[32,4,384]{2,1,0:T(4,128)S(1)} %all_to_all.74.got, ...), custom_call_target="tpu_custom_call" | custom-call | tf_op jit(solution)/shard_map/b11/pallas_call | solution.py:32
  133.8 2.3 %g_most.1 = (bf16[24,80,128]{2,1,0:T(8,128)(2,1)S(1)}, bf16[24,80,128]{2,1,0:T(8,128)(2,1)S(1)}, bf16[14,32,256]{2,1,0:T(8,128)(2,1)S(1)}, bf16[14,32,256]{2,1,0:T(8,128)(2,1)S(1)}) custom-call(s32[8]{0:T(128)S(1)} %get-tuple-element.128.scal, bf16[28,32,128]{2,1,0:T(8,128)(2,1)S(1)} %get-tuple-element.186.act_2b, ...), custom_call_target="tpu_custom_call" | custom-call | tf_op jit(solution)/shard_map/g_most/pallas_call | solution.py:32
  136.2 8.9 %all_to_all.75.got = f32[32,1,256]{2,1,0:T(1,128)S(1)} all-to-all(f32[32,1,256]{2,1,0:T(1,128)S(1)} %get-tuple-element.197), channel_id=1, replica_groups=mesh['rows'=2,'batch'=16] {'rows','batch'}, dimensions={0} | all-to-all | bytes 65536 | tf_op jit(solution)/shard_map/all_to_all | solution.py:931
  145.1 2.0 b12.1
  147.1 1.6 b12_images.2
  149.8 1.6 b12_images.3
  151.4 1.7 g_xd.1
  153.3 24.2 %all_to_all.76.got = bf16[32,96,128]{2,1,0:T(8,128)(2,1)S(1)} all-to-all(bf16[32,96,128]{2,1,0:T(8,128)(2,1)S(1)} %pack_last.1), channel_id=1, replica_groups=mesh['rows'=2,'batch'=16] {'rows','batch'}, dimensions={0} | all-to-all | bytes 1572864 | tf_op jit(solution)/shard_map/all_to_all | solution.py:931
  178.1 22.8 %all_to_all.77.own = bf16[32,88,128]{2,1,0:T(8,128)(2,1)S(1)} all-to-all(bf16[32,88,128]{2,1,0:T(8,128)(2,1)S(1)} %add_all.1), channel_id=1, replica_groups=mesh['rows'=2,'batch'=16] {'rows','batch'}, dimensions={0} | all-to-all | bytes 1441792 | tf_op jit(solution)/shard_map/all_to_all | solution.py:931
  200.8 3.5 %b13.1 = (bf16[2,28,56,256]{3,2,1,0:T(8,128)(2,1)}, f32[3,2,128]{2,1,0:T(2,128)}) custom-call(s32[8]{0:T(128)S(1)} %get-tuple-element.128.scal, bf16[32,96,128]{2,1,0:T(8,128)(2,1)S(1)} %all_to_all.76.got, f32[32,1,128]{2,1,0:T(1,128)S(1)} %get-tuple-element.149.labels, f32[3,2,128]{2,1,0:T(2,128)S(1)} %bitcast.27, ...), custom_call_target="tpu_custom_call" | custom-call | tf_op jit(solution)/shard_map/b13/pallas_call | solution.py:32
  204.4 2.1 %unpack.1 = (f32[256,128]{1,0:T(8,128)}, f32[1152,128]{1,0:T(8,128)}, f32[128,512]{1,0:T(8,128)}, f32[1152,128]{1,0:T(8,128)}, f32[512,128]{1,0:T(8,128)}, /*index=5*/f32[128,512]{1,0:T(8,128)}, f32[256,512]{1,0:T(8,128)}) custom-call(s32[8]{0:T(128)S(1)} %get-tuple-element.128.scal, bf16[32,88,128]{2,1,0:T(8,128)(2,1)S(1)} %all_to_all.77.own, ...), custom_call_target="tpu_custom_call" | custom-call | tf_op jit(solution)/shard_map/unpack/pallas_call | solution.py:32
  (46 shorter events, 3.6 us)
Async XLA Ops:
  0.6 2.9 %copy-start = (bf16[3,3,128,128]{3,2,1,0:T(8,128)(2,1)S(1)}, bf16[3,3,128,128]{3,2,1,0:T(8,128)(2,1)}, u32[]{:S(2)}) copy-start(bf16[3,3,128,128]{3,2,1,0:T(8,128)(2,1)} %w2b) | copy-start | bytes 884740
  0.7 2.9 %copy-start.7 = (bf16[3,3,128,128]{3,2,1,0:T(8,128)(2,1)S(1)}, bf16[3,3,128,128]{3,2,1,0:T(8,128)(2,1)}, u32[]{:S(2)}) copy-start(bf16[3,3,128,128]{3,2,1,0:T(8,128)(2,1)} %w1b) | copy-start | bytes 884740
  0.7 17.9 %copy-start.1 = (bf16[256,512]{1,0:T(8,128)(2,1)S(1)}, bf16[256,512]{1,0:T(8,128)(2,1)}, u32[]{:S(2)}) copy-start(bf16[256,512]{1,0:T(8,128)(2,1)} %w_1p.1) | copy-start | bytes 786436
  3.6 16.3 %copy-start.3 = (bf16[256,128]{1,0:T(8,128)(2,1)S(1)}, bf16[256,128]{1,0:T(8,128)(2,1)}, u32[]{:S(2)}) copy-start(bf16[256,128]{1,0:T(8,128)(2,1)} %w.17) | copy-start | bytes 196612
  3.6 16.3 %copy-start.8 = (f32[2,3,128]{2,0,1:T(2,128)S(1)}, f32[2,3,128]{2,0,1:T(2,128)}, u32[]{:S(2)}) copy-start(f32[2,3,128]{2,0,1:T(2,128)} %param.27) | copy-start | bytes 9220
  3.8 14.8 %collective-permute-start = (bf16[28,64,256]{2,1,0:T(8,128)(2,1)S(1)}, bf16[28,64,256]{2,1,0:T(8,128)(2,1)S(1)}, u32[]{:S(2)}, u32[]{:S(2)}) collective-permute-start(bf16[28,64,256]{2,1,0:T(8,128)(2,1)S(1)} %get-tuple-element.140), channel_id=1, source_target_pairs={{0,16},{16,0},{1,17},{17,1},{2,18},{18,2},{3,19},{19,3},{4,20},{20... | collective-permute-start | bytes 2752520 | tf_op jit(solution)/shard_map/ppermute | solution.py:939
  19.8 14.7 %copy-start.6 = (bf16[128,512]{1,0:T(8,128)(2,1)S(1)}, bf16[128,512]{1,0:T(8,128)(2,1)}, u32[]{:S(2)}) copy-start(bf16[128,512]{1,0:T(8,128)(2,1)} %w.16) | copy-start | bytes 393220
  19.8 14.7 %copy-start.13 = (f32[2,3,128]{2,0,1:T(2,128)S(1)}, f32[2,3,128]{2,0,1:T(2,128)}, u32[]{:S(2)}) copy-start(f32[2,3,128]{2,0,1:T(2,128)} %param.28) | copy-start | bytes 9220
  19.9 25.7 %copy-start.4 = (bf16[512,128]{1,0:T(8,128)(2,1)S(1)}, bf16[512,128]{1,0:T(8,128)(2,1)}, u32[]{:S(2)}) copy-start(bf16[512,128]{1,0:T(8,128)(2,1)} %w.15) | copy-start | bytes 393220
  19.9 25.7 %copy-start.10 = (f32[2,3,512]{2,0,1:T(2,128)S(1)}, f32[2,3,512]{2,0,1:T(2,128)}, u32[]{:S(2)}) copy-start(f32[2,3,512]{2,0,1:T(2,128)} %param.29) | copy-start | bytes 36868
  19.9 25.7 %copy-start.11 = (f32[2,3,512]{2,0,1:T(2,128)S(1)}, f32[2,3,512]{2,0,1:T(2,128)}, u32[]{:S(2)}) copy-start(f32[2,3,512]{2,0,1:T(2,128)} %param.30) | copy-start | bytes 36868
  47.5 10.1 %copy-start.12 = (f32[2,3,128]{2,0,1:T(2,128)S(1)}, f32[2,3,128]{2,0,1:T(2,128)}, u32[]{:S(2)}) copy-start(f32[2,3,128]{2,0,1:T(2,128)} %param.31) | copy-start | bytes 9220
  47.5 22.3 %copy-start.5 = (bf16[128,512]{1,0:T(8,128)(2,1)S(1)}, bf16[128,512]{1,0:T(8,128)(2,1)}, u32[]{:S(2)}) copy-start(bf16[128,512]{1,0:T(8,128)(2,1)} %w.14) | copy-start | bytes 393220
  47.5 22.3 %copy-start.14 = (f32[2,3,128]{2,0,1:T(2,128)S(1)}, f32[2,3,128]{2,0,1:T(2,128)}, u32[]{:S(2)}) copy-start(f32[2,3,128]{2,0,1:T(2,128)} %param.32) | copy-start | bytes 9220
  48.5 32.2 %copy-start.2 = (bf16[1,28,28,512]{3,2,1,0:T(8,128)(2,1)S(1)}, bf16[1,28,28,512]{3,2,1,0:T(8,128)(2,1)}, u32[]{:S(2)}) copy-start(bf16[1,28,28,512]{3,2,1,0:T(8,128)(2,1)} %param.34) | copy-start | bytes 2408452
  48.5 32.2 %copy-start.9 = (f32[2,3,512]{2,0,1:T(2,128)S(1)}, f32[2,3,512]{2,0,1:T(2,128)}, u32[]{:S(2)}) copy-start(f32[2,3,512]{2,0,1:T(2,128)} %param.33) | copy-start | bytes 36868
  145.1 8.0 %collective-permute-start.3 = (bf16[24,80,128]{2,1,0:T(8,128)(2,1)S(1)}, bf16[24,80,128]{2,1,0:T(8,128)(2,1)S(1)}, u32[]{:S(2)}, u32[]{:S(2)}) collective-permute-start(bf16[24,80,128]{2,1,0:T(8,128)(2,1)S(1)} %get-tuple-element.217), channel_id=1, source_target_pairs={{0,16},{16,0},{1,17},{17,1},{2,18},{18,2},{3,19},{19,3},{4,20},{20... | collective-permute-start | bytes 1474568 | tf_op jit(solution)/shard_map/ppermute | solution.py:939
  148.7 4.4 %collective-permute-start.2 = (bf16[28,64,128]{2,1,0:T(8,128)(2,1)S(1)}, bf16[28,64,128]{2,1,0:T(8,128)(2,1)S(1)}, u32[]{:S(2)}, u32[]{:S(2)}) collective-permute-start(bf16[28,64,128]{2,1,0:T(8,128)(2,1)S(1)} %get-tuple-element.206.dn_oth), channel_id=1, source_target_pairs={{0,16},{16,0},{1,17},{17,1},{2,18},{18,2},{3,19},{19,3},{4,20},{20... | collective-permute-start | bytes 1376264 | tf_op jit(solution)/shard_map/ppermute | solution.py:939
  149.3 3.8 %collective-permute-start.1 = (bf16[14,32,256]{2,1,0:T(8,128)(2,1)S(1)}, bf16[14,32,256]{2,1,0:T(8,128)(2,1)S(1)}, u32[]{:S(2)}, u32[]{:S(2)}) collective-permute-start(bf16[14,32,256]{2,1,0:T(8,128)(2,1)S(1)} %get-tuple-element.213), channel_id=1, source_target_pairs={{0,16},{16,0},{1,17},{17,1},{2,18},{18,2},{3,19},{19,3},{4,20},{20... | collective-permute-start | bytes 688136 | tf_op jit(solution)/shard_map/ppermute | solution.py:939
  149.3 3.7 %collective-permute-start.4 = (bf16[8,80,128]{2,1,0:T(8,128)(2,1)S(1)}, bf16[8,80,128]{2,1,0:T(8,128)(2,1)S(1)}, u32[]{:S(2)}, u32[]{:S(2)}) collective-permute-start(bf16[8,80,128]{2,1,0:T(8,128)(2,1)S(1)} %get-tuple-element.219), channel_id=1, source_target_pairs={{0,16},{16,0},{1,17},{17,1},{2,18},{18,2},{3,19},{19,3},{4,20},{20... | collective-permute-start | bytes 491528 | tf_op jit(solution)/shard_map/ppermute | solution.py:939
  200.8 3.5 %collective-permute-start.5 = (bf16[32,88,128]{2,1,0:T(8,128)(2,1)S(1)}, bf16[32,88,128]{2,1,0:T(8,128)(2,1)S(1)}, u32[]{:S(2)}, u32[]{:S(2)}) collective-permute-start(bf16[32,88,128]{2,1,0:T(8,128)(2,1)S(1)} %all_to_all.77.own), channel_id=1, source_target_pairs={{0,16},{16,0},{1,17},{17,1},{2,18},{18,2},{3,19},{19,3},{4,20},{20... | collective-permute-start | bytes 2162696 | tf_op jit(solution)/shard_map/ppermute | solution.py:939

commit v3 on v2

v3 whole, which is shorter than its diff:
```python
import functools

import jax
import jax.numpy as jnp
from jax import lax
from jax.experimental import pallas as pl
from jax.experimental.pallas import tpu as pltpu
from jax.sharding import PartitionSpec as P

EPSILON = 1e-05
F32 = jnp.float32
BF16 = jnp.bfloat16
AXES = ("rows", "batch")
VMEM_LIMIT = 14 * 1024 * 1024
LANES = 128
COLS = 32


def full(memory=pltpu.VMEM):
    return pl.BlockSpec(memory_space=memory)


def stage(kernel, outs, scratch=(), hbm=(), hbm_out=()):
    def place(i, outside):
        return pltpu.HBM if i in outside else pltpu.VMEM

    def call(*args):
        args = [
            pltpu.with_memory_space_constraint(a, pltpu.HBM) if i in hbm else a
            for i, a in enumerate(args)
        ]
        return pl.pallas_call(
            kernel,
            out_shape=tuple(jax.ShapeDtypeStruct(s, d) for s, d in outs),
            in_specs=[full(place(i, hbm)) for i in range(len(args))],
            out_specs=tuple(
                full(place(i, hbm_out)) for i in range(len(outs))
            ),
            scratch_shapes=list(scratch),
            compiler_params=pltpu.CompilerParams(vmem_limit_bytes=VMEM_LIMIT),
            name=(kernel.func if isinstance(kernel, functools.partial) else kernel).__name__,
        )(*args)

    return call


def silu_of_half(u):
    return u + u * jnp.tanh(u)


def slope_of_half(u):
    t = jnp.tanh(u)
    return (0.5 + 0.5 * t) * (1.0 + u - u * t)


def fold(x):
    return (x[0:8] + x[8:16]) + (x[16:24] + x[24:32])


def row(total, stat):
    blocks = total.shape[0]
    pieces = [total[j : j + 1, LANES * stat : LANES * (stat + 1)] for j in range(blocks)]
    return pieces[0] if blocks == 1 else jnp.concatenate(pieces, axis=1)


def spread(out_ref, rows):
    blocks = out_ref.shape[1]
    for stat, values in enumerate(rows):
        for j in range(blocks):
            piece = values[:, LANES * j : LANES * (j + 1)]
            out_ref[:, j : j + 1, LANES * stat : LANES * (stat + 1)] = jnp.broadcast_to(
                piece[None], (out_ref.shape[0], 1, LANES)
            )


def group_sum(got_ref, labels, label):
    same = (labels == label).astype(F32)
    stats = got_ref.shape[2] // LANES
    parts = [
        jnp.sum(got_ref[:, :, LANES * s : LANES * (s + 1)] * same, axis=0) for s in range(stats)
    ]
    return jnp.concatenate(parts, axis=1) if stats > 1 else parts[0]


def group_count(labels, label):
    return jnp.sum((labels == label).astype(F32), axis=0)


def tiled(values, channels):
    return jnp.concatenate([values] * (channels // LANES), axis=1) if channels > LANES else values


def moments(first, second, pixels):
    mean = first / pixels
    return mean, lax.rsqrt(second / pixels - mean * mean + EPSILON)


def own_of(values, label):
    out = values[0]
    label = tiled(label, out.shape[1])
    for g in range(1, len(values)):
        out = jnp.where(label == float(g), values[g], out)
    return out


def gain_of(norm_ref, label):
    return own_of([norm_ref[g, 0:1, :] for g in range(norm_ref.shape[0])], label)


def shift_of(norm_ref, label):
    return own_of([norm_ref[g, 1:2, :] for g in range(norm_ref.shape[0])], label)


def valid_cols(channels):
    return lax.broadcasted_iota(jnp.int32, (COLS, channels), 0) < COLS - 4


def chan_mask(tab):
    return lax.broadcasted_iota(jnp.int32, (1, LANES), 1).astype(F32) < entry(tab, LIMIT)


def flat(x):
    return x.reshape(x.shape[0] * x.shape[1], x.shape[2])


def mm(a, b):
    return jnp.dot(a, b, preferred_element_type=F32)


def mm_nt(a, b):
    return lax.dot_general(a, b, (((1,), (1,)), ((), ())), preferred_element_type=F32)


def mm_tn(a, b):
    return lax.dot_general(a, b, (((0,), (0,)), ((), ())), preferred_element_type=F32)


def mm_side(a, b):
    turned = mm_tn(b, a)
    blocks = [
        jnp.transpose(turned[:, LANES * j : LANES * (j + 1)]) for j in range(a.shape[1] // LANES)
    ]
    return blocks[0] if len(blocks) == 1 else jnp.concatenate(blocks, axis=0)


def zeros8(channels):
    return jnp.zeros((8, channels), F32)


def down(x):
    return jnp.sum(x, axis=0, keepdims=True)


OWN, OTHER, HALF, LIMIT, GATE = range(5)


def entry(tab, k):
    return tab[k : k + 1, :]


def half_of(tab):
    return (jnp.sum(entry(tab, HALF)) * (1.0 / LANES)).astype(jnp.int32)


def prepare(w1b, w2b, w_even, w_odd, w_two, w_last, b_even, b_odd, b_two, b_last):
    n = LANES
    for k, (y, x) in enumerate(((1, 1), (1, 2), (1, 0))):
        w_even[n * k : n * (k + 1), :] = w1b[y, x]
    for k, (low, high) in enumerate((((2, 1), (0, 1)), ((2, 2), (0, 2)), ((2, 0), (0, 0)))):
        w_odd[n * k : n * (k + 1), 0:n] = w1b[low]
        w_odd[n * k : n * (k + 1), n : 2 * n] = w1b[high]
    for x in range(3):
        w_two[n * x : n * (x + 1), 0:n] = w2b[0, x]
        w_two[n * x : n * (x + 1), n : 2 * n] = w2b[1, x]
        w_last[n * x : n * (x + 1), :] = w2b[2, x]
        b_two[0:n, n * x : n * (x + 1)] = w2b[1, x]
        b_two[n : 2 * n, n * x : n * (x + 1)] = w2b[2, x]
        b_last[:, n * x : n * (x + 1)] = w2b[0, x]
    nothing = jnp.zeros((n, n), BF16)
    b_even[0:n, 0:n] = w1b[1, 1]
    b_even[0:n, n : 2 * n] = nothing
    b_even[n : 2 * n, 0:n] = w1b[1, 2]
    b_even[n : 2 * n, n : 2 * n] = w1b[1, 0]
    for k, top in ((0, 2), (1, 0)):
        b_odd[0:n, 2 * n * k : 2 * n * k + n] = w1b[top, 1]
        b_odd[0:n, 2 * n * k + n : 2 * n * (k + 1)] = nothing
        b_odd[n : 2 * n, 2 * n * k : 2 * n * k + n] = w1b[top, 2]
        b_odd[n : 2 * n, 2 * n * k + n : 2 * n * (k + 1)] = w1b[top, 0]


def widen(source, x_pad):
    rows, cols, chans = source.shape
    gap = x_pad.shape[1] - cols

    def put(i, carry):
        x_pad[i, 0:cols, :] = source[i]
        x_pad[i, cols : cols + gap, :] = jnp.zeros((gap, chans), BF16)
        return carry

    lax.fori_loop(0, rows, put, 0, unroll=4)


def first_project(x_pad, w, z, stats=True):
    rows = x_pad.shape[0]
    step = rows // 4
    sums, squares = zeros8(LANES), zeros8(LANES)
    for c in range(4):
        values = mm(flat(x_pad[step * c : step * (c + 1)]), w[...])
        z[step * c : step * (c + 1)] = values.reshape(step, x_pad.shape[1], LANES)
        if stats:
            parts = values.reshape(-1, 8, LANES)
            sums = sums + jnp.sum(parts, axis=0)
            squares = squares + jnp.sum(parts * parts, axis=0)
    return sums, squares


def f1(
    half_at, group_at, width_at, gate_at, images, w_at, tab, x_own, x_for, z_own, z_for, send,
    half_ref, group, width, gate, raw, w, sems,
):
    pairs = (
        (half_at, half_ref), (group_at, group), (width_at, width), (gate_at, gate), (w_at, w),
        (images.at[0], raw.at[0]), (images.at[1], raw.at[1]),
    )
    copies = [pltpu.make_async_copy(a, b, sems.at[k]) for k, (a, b) in enumerate(pairs)]
    for k in (0, 4, 5, 6, 1, 2, 3):
        copies[k].start()
    for copy in copies:
        copy.wait()
    half = half_ref[0]
    rows = []
    for place, x_pad, z in ((half, x_own, z_own), (1 - half, x_for, z_for)):
        widen(raw.at[place], x_pad)
        sums, squares = first_project(x_pad, w, z)
        rows += [down(sums), down(squares)]
    own, other = group[half], group[1 - half]
    values = {
        OWN: own, OTHER: other, HALF: half, LIMIT: w.shape[1] // 4 * width[own], GATE: gate[own]
    }
    tab[...] = jnp.zeros(tab.shape, F32)
    for k, v in values.items():
        tab[k : k + 1, :] = jnp.full((1, LANES), v.astype(F32))
    spread(send, [*rows, jnp.full((1, LANES), (own + 4 * other).astype(F32))])


def f1_strided(tab, x_own, x_oth, w, xee, z, stats, wide):
    half = half_of(tab)
    rows = x_own.shape[0] // 2
    for k, x_pad in enumerate((x_own, x_oth)):
        first = rows * (half if k == 0 else 1 - half)

        def put(i, carry, x_pad=x_pad, first=first):
            for b in range(wide.shape[0]):
                lanes = slice(LANES * b, LANES * (b + 1))
                wide[b] = x_pad[2 * i, :, lanes].astype(F32)
                xee[first + i, :, lanes] = wide[b, pl.ds(0, COLS, stride=2), :].astype(BF16)
            return carry

        lax.fori_loop(0, rows, put, 0, unroll=2)
    total = 2 * rows
    step = total // 7
    chans = z.shape[2]
    squares = zeros8(chans)
    for c in range(7):
        values = mm(flat(xee[step * c : step * (c + 1)]), w[...])
        z[step * c : step * (c + 1)] = values.reshape(step, COLS, chans)
        parts = values.reshape(-1, 8, chans)
        squares = squares + jnp.sum(parts * parts, axis=0)
    ones = jnp.ones((8, total * COLS), BF16)
    stats[:, 0 : w.shape[0]] = mm(ones, flat(xee[...]))[0:1]
    stats[:, w.shape[0] :] = down(squares)


def scale_shift(got, labels, tab, norm, pixels, slot=0):
    label = entry(tab, OWN)
    total = group_sum(got, labels, label)
    chans = norm.shape[2]
    count = tiled(group_count(labels, label), chans) * pixels
    mean, rstd = moments(row(total, 2 * slot), row(total, 2 * slot + 1), count)
    gain, shift = gain_of(norm, entry(tab, OWN)), shift_of(norm, entry(tab, OWN))
    return mean, rstd, gain, shift, count


def conv_stats(z, source, pair, single, send, extra=()):
    keep = valid_cols(LANES)[None]
    rows = z.shape[0]
    step = rows // 4
    (lanes_2, w_2, offsets), (lanes_1, w_1, offset) = pair, single
    sums, squares = zeros8(LANES), zeros8(LANES)
    base = min(offsets)
    for c in range(4):
        at = step * c
        both = mm(flat(source[at + base : at + base + step + 1, :, lanes_2]), w_2)
        values = mm(flat(source[at + offset : at + offset + step, :, lanes_1]), w_1)
        for k, own in enumerate(offsets):
            skip = COLS * (own - base)
            values = values + both[skip : skip + step * COLS, LANES * k : LANES * (k + 1)]
        values = jnp.where(keep, values.reshape(step, COLS, LANES), 0.0)
        z[at : at + step] = values
        parts = values.reshape(-1, 8, LANES)
        sums = sums + jnp.sum(parts, axis=0)
        squares = squares + jnp.sum(parts * parts, axis=0)
    spread(send, [down(sums), down(squares), *extra])


def f2(
    tab, got, z_own, x_own, x_oth, w, norm, w_even, w_odd, stats_p,
    xs, z, send, labels, keeps, keeps_all, z_oth, x_sum,
):
    codes = got[:, :, 4 * LANES : 5 * LANES]
    others = jnp.floor(0.25 * codes)
    marks = codes - 4.0 * others
    labels[...] = marks
    rows = xs.shape[0] - 1
    pixels = 4.0 * rows * (COLS - 4)
    first_project(x_oth, w, z_oth, False)
    for g in range(norm.shape[0]):
        mine, theirs = (marks == float(g)).astype(F32), (others == float(g)).astype(F32)
        totals = [
            jnp.sum(
                got[:, :, LANES * s : LANES * (s + 1)] * mine
                + got[:, :, LANES * (s + 2) : LANES * (s + 3)] * theirs,
                axis=0,
            )
            for s in (0, 1)
        ]
        mean, rstd = moments(*totals, group_count(marks, float(g)) * pixels)
        keeps_all[2 * g : 2 * g + 1, :] = mean
        keeps_all[2 * g + 1 : 2 * g + 2, :] = rstd
    for k, slot in enumerate((OWN, OTHER)):
        for q in (0, 1):
            choices = [keeps_all[2 * g + q : 2 * g + q + 1, :] for g in range(norm.shape[0])]
            keeps[2 * k + q : 2 * k + q + 1, :] = own_of(choices, entry(tab, slot))
    mean, rstd = keeps[0:1, :], keeps[1:2, :]
    gain, shift = gain_of(norm, entry(tab, OWN)), shift_of(norm, entry(tab, OWN))
    ones = jnp.ones((8, x_own.shape[0] * x_own.shape[1]), BF16)
    x_sum[...] = mm(ones, flat(x_own[...])) + mm(ones, flat(x_oth[...]))
    scale = rstd * gain
    bias = 0.5 * (shift - mean * scale)
    scale = 0.5 * scale
    keep = valid_cols(LANES) & chan_mask(tab)
    half = half_of(tab)
    xs[0] = jnp.zeros(xs.shape[1:], BF16)
    n = LANES
    for k, zz in enumerate((z_own, z_oth)):
        first = 1 + (rows // 2) * (half if k == 0 else 1 - half)

        def put(i, carry, zz=zz, first=first):
            lane = 0
            for a in (0, 1):
                for b in (0, 1):
                    u = zz[2 * i + a, pl.ds(b, COLS, stride=2), :] * scale + bias
                    act = jnp.where(keep, silu_of_half(u), 0.0)
                    xs[first + i, :, lane : lane + n] = act.astype(BF16)
                    lane += n
                    if b == 1:
                        moved = pltpu.roll(act, 1, 0)
                        xs[first + i, :, lane : lane + n] = moved.astype(BF16)
                        lane += n
            return carry

        lax.fori_loop(0, rows // 2, put, 0, unroll=2)
    extra = [x_sum[0:1, n * b : n * (b + 1)] for b in range(x_sum.shape[1] // n)]
    extra += [stats_p[:, lanes] for lanes in columns(stats_p.shape[1])]
    pair = (slice(3 * n, 6 * n), w_odd[...], (1, 0))
    conv_stats(z, xs, pair, (slice(0, 3 * n), w_even[...], 1), send, extra)


def expand(act, w, z, send, act_sum):
    rows, chans = z.shape[0], z.shape[2]
    step = rows // 7
    squares = zeros8(chans)
    for c in range(7):
        values = mm(flat(act[step * c : step * (c + 1)]), w[...])
        z[step * c : step * (c + 1)] = values.reshape(step, COLS, chans)
        parts = values.reshape(-1, 8, chans)
        squares = squares + jnp.sum(parts * parts, axis=0)
    squares = down(squares)
    spread(send, [act_sum, *(squares[:, lanes] for lanes in columns(chans))])


def columns(channels):
    return [slice(LANES * j, LANES * (j + 1)) for j in range(channels // LANES)]


def through(sums, w):
    high = sums.astype(BF16)
    rest = sums - high.astype(F32)
    mid = rest.astype(BF16)
    low = (rest - mid.astype(F32)).astype(BF16)
    lines = [v.astype(F32) for v in (high, mid, low)]
    lines.append(jnp.zeros((5, sums.shape[1]), F32))
    return down(mm(jnp.concatenate(lines, axis=0).astype(BF16), w))


def expanded_moments(got, labels, tab, w, pixels):
    label = entry(tab, OWN)
    total = group_sum(got, labels, label)
    chans = w.shape[1]
    count = tiled(group_count(labels, label), chans) * pixels
    return moments(through(total[:, 0:LANES], w[...]), total[:, LANES:], count)


def activate(tab, got, labels, z_in, norm, act, keeps):
    got = got.at[:, :, 0 : 2 * LANES]
    rows = z_in.shape[0]
    pixels = 1.0 * rows * (COLS - 4)
    mean, rstd, gain, shift, _ = scale_shift(got, labels[...], tab, norm, pixels)
    keeps[0:1, :] = mean
    keeps[1:2, :] = rstd
    scale = rstd * gain
    bias = 0.5 * (shift - mean * scale)
    scale = 0.5 * scale
    keep = valid_cols(LANES) & chan_mask(tab)

    def put(i, sums):
        low = jnp.where(keep, silu_of_half(z_in[i] * scale + bias), 0.0).astype(BF16)
        act[i] = low
        return sums + fold(low.astype(F32))

    return down(lax.fori_loop(0, rows, put, zeros8(LANES), unroll=7))


def f3(tab, got, labels, z_in, norm, w, w_p, x_sum, act, z, send, keeps, keeps_p, x_dev):
    sums = activate(tab, got, labels, z_in, norm, act, keeps)
    expand(act, w, z, send, sums)
    marks = labels[...]
    label = entry(tab, OWN)
    inputs, outer = x_sum.shape[1] // LANES, z.shape[2] // LANES
    total = group_sum(got, marks, label)
    images = group_count(marks, label)
    for b in range(inputs):
        lanes = slice(LANES * b, LANES * (b + 1))
        x_dev[:, lanes] = x_sum[0:1, lanes] - row(total, 2 + b) / images
    count = tiled(images, outer * LANES) * (1.0 * z.shape[0] * (COLS - 4))
    first, second = LANES * (2 + inputs), LANES * (2 + 2 * inputs)
    mean, rstd = moments(through(total[:, first:second], w_p[...]), total[:, second:], count)
    keeps_p[0:1, :] = mean
    keeps_p[1:2, :] = rstd


def f4(tab, got, labels, zc, zp, norm_c, norm_p, keeps_p, w_c, w, joined, slope, z, send, keeps):
    rows, chans = zc.shape[0], zc.shape[2]
    pixels = 1.0 * rows * (COLS - 4)
    mean_c, rstd_c = expanded_moments(got, labels[...], tab, w_c, pixels)
    mean_p, rstd_p = keeps_p[0:1, :], keeps_p[1:2, :]
    for k, v in enumerate((mean_c, rstd_c, mean_p, rstd_p)):
        keeps[k : k + 1, :] = v
    group = entry(tab, OWN)
    scale_c = rstd_c * gain_of(norm_c, group)
    scale_p = rstd_p * gain_of(norm_p, group)
    bias = (shift_of(norm_c, group) - mean_c * scale_c) + (
        shift_of(norm_p, group) - mean_p * scale_p
    )
    keep = valid_cols(chans)
    scale_c, scale_p, bias = 0.5 * scale_c, 0.5 * scale_p, 0.5 * bias

    def put(i, carry):
        u = zc[i] * scale_c + zp[i] * scale_p + bias
        t = jnp.tanh(u)
        p = u * t
        joined[i] = jnp.where(keep, u + p, 0.0).astype(BF16)
        slope[i] = (0.5 + 0.5 * t) * (1.0 + u - p)
        return carry

    lax.fori_loop(0, rows, put, 0, unroll=4)
    step = rows // 4
    sums, squares = zeros8(LANES), zeros8(LANES)
    for c in range(4):
        values = mm(flat(joined[step * c : step * (c + 1)]), w[...])
        z[step * c : step * (c + 1)] = values.reshape(step, COLS, LANES)
        parts = values.reshape(-1, 8, LANES)
        sums = sums + jnp.sum(parts, axis=0)
        squares = squares + jnp.sum(parts * parts, axis=0)
    spread(send, [down(sums), down(squares)])


def f5(tab, got, labels, z_in, norm, w_two, w_last, xz, x3, z, send, keeps):
    rows = z_in.shape[0]
    pixels = 1.0 * rows * (COLS - 4)
    mean, rstd, gain, shift, _ = scale_shift(got, labels[...], tab, norm, pixels)
    keeps[0:1, :] = mean
    keeps[1:2, :] = rstd
    scale = rstd * gain
    bias = 0.5 * (shift - mean * scale)
    scale = 0.5 * scale
    keep = valid_cols(LANES) & chan_mask(tab)
    x3[0] = jnp.zeros(x3.shape[1:], BF16)
    x3[rows + 1] = jnp.zeros(x3.shape[1:], BF16)
    n = LANES

    def put(i, carry):
        act = jnp.where(keep, silu_of_half(z_in[i] * scale + bias), 0.0)
        x3[i + 1, :, 0:n] = pltpu.roll(act, 1, 0).astype(BF16)
        x3[i + 1, :, n : 2 * n] = act.astype(BF16)
        x3[i + 1, :, 2 * n : 3 * n] = pltpu.roll(act, COLS - 1, 0).astype(BF16)
        return carry

    lax.fori_loop(0, rows, put, 0, unroll=2)
    lanes = slice(0, 3 * n)
    conv_stats(
        z, x3, (lanes, w_two[...], (0, 1)), (lanes, w_last[...], 2), send.at[:, :, 0 : 2 * n]
    )
    devices = send.shape[0]
    share = xz.shape[0] // devices
    pieces = xz[...].reshape(devices, share, n)
    for q in range(share):
        send[:, :, n * (2 + q) : n * (3 + q)] = pieces[:, q : q + 1, :]


def f6(tab, got, labels, z_in, norm, w, act, z, send, keeps):
    sums = activate(tab, got, labels, z_in, norm, act, keeps)
    expand(act, w, z, send, sums)


def b7(tab, got, labels, joined, z, norm, w, cot, result, grad_pre, send, keeps, wide):
    rows, chans = z.shape[0], z.shape[2]
    cols = COLS - 4
    pixels = 1.0 * rows * cols
    mean, rstd = expanded_moments(got, labels[...], tab, w, pixels)
    gain, shift = gain_of(norm, entry(tab, OWN)), shift_of(norm, entry(tab, OWN))
    keeps[0:1, :] = mean
    keeps[1:2, :] = rstd
    gate = 0.25 * tiled(entry(tab, GATE), chans)
    scale = 0.5 * rstd * gain * gate
    bias = 0.5 * (shift - mean * rstd * gain) * gate
    wide[...] = jnp.zeros(wide.shape, F32)

    def put(i, carry):
        sums, products = carry
        wide[0:cols, :] = cot[i].astype(F32)
        zz = z[i]
        u = 0.5 * joined[i].astype(F32) + zz * scale + bias
        t = jnp.tanh(u)
        p = u * t
        result[i] = (u + p)[0:cols].astype(BF16)
        g = wide[...] * ((0.5 + 0.5 * t) * (1.0 + u - p))
        grad_pre[i] = g
        return sums + fold(g), products + fold(g * (zz - mean))

    start = zeros8(chans)
    sums, products = lax.fori_loop(0, rows, put, (start, start), unroll=2)
    spread(send, [down(sums) * gate, down(products) * rstd * gate])


def backward_norm(tab, got, labels, norm, keeps, pixels, grad_norm, slots=(0, 1)):
    marks = labels[...]
    chans = norm.shape[2]
    own_shift = jnp.zeros((1, chans), F32)
    own_gain = jnp.zeros((1, chans), F32)
    group = entry(tab, OWN)
    for g in range(norm.shape[0]):
        total = group_sum(got, marks, float(g))
        shift_sum, gain_sum = row(total, slots[0]), row(total, slots[1])
        grad_norm[g, 0:1, :] = gain_sum
        grad_norm[g, 1:2, :] = shift_sum
        mine = tiled(group, chans) == float(g)
        own_shift = jnp.where(mine, shift_sum, own_shift)
        own_gain = jnp.where(mine, gain_sum, own_gain)
    count = tiled(group_count(marks, group), chans) * pixels
    mean, rstd = keeps[0:1, :], keeps[1:2, :]
    a = rstd * gain_of(norm, group)
    return mean, a, -(a * rstd) * own_gain / count, -a * own_shift / count


def slope_sums(tab, d, z_in, norm, keeps, dout, send):
    rows = z_in.shape[0]
    mean, rstd = keeps[0:1, :], keeps[1:2, :]
    group = entry(tab, OWN)
    scale = rstd * gain_of(norm, group)
    bias = 0.5 * (shift_of(norm, group) - mean * scale)
    scale = 0.5 * scale
    keep = valid_cols(LANES) & chan_mask(tab)

    def put(i, carry):
        sums, products = carry
        zz = z_in[i]
        g = jnp.where(keep, d[i] * slope_of_half(zz * scale + bias), 0.0)
        dout[i] = g
        return sums + fold(g), products + fold(g * (zz - mean))

    sums, products = lax.fori_loop(
        0, rows, put, (zeros8(LANES), zeros8(LANES)), unroll=4
    )
    spread(send, [down(sums), down(products) * rstd])


def b8(
    tab, got, labels, grad_pre, z, norm, keeps, w, z_in, norm_in, keeps_in,
    dz, dout, send, grad_norm, d,
):
    rows, chans = z.shape[0], z.shape[2]
    pixels = 1.0 * rows * (COLS - 4)
    mean, a, b, c = backward_norm(tab, got, labels, norm, keeps, pixels, grad_norm)
    a = a * (0.25 * tiled(entry(tab, GATE), norm.shape[2]))
    keep = valid_cols(chans)

    def put(i, carry):
        v = a * grad_pre[i] + b * (z[i] - mean) + c
        dz[i] = jnp.where(keep, v, 0.0).astype(BF16)
        return carry

    lax.fori_loop(0, rows, put, 0, unroll=2)
    d[...] = mm_nt(flat(dz[...]), w[...]).reshape(d.shape)
    slope_sums(tab, d, z_in, norm_in, keeps_in, dout, send)


def b9(
    tab, got, labels, dout_in, z, norm, keeps, b_two, b_last, z_in, norm_in, keeps_in,
    dz, dout, send, grad_norm, d3, d,
):
    rows = z.shape[0]
    pixels = 1.0 * rows * (COLS - 4)
    mean, a, b, c = backward_norm(tab, got, labels, norm, keeps, pixels, grad_norm)
    keep = valid_cols(LANES)
    n = LANES
    d3[0] = jnp.zeros(d3.shape[1:], BF16)
    d3[rows + 1] = jnp.zeros(d3.shape[1:], BF16)

    def put(i, carry):
        v = a * dout_in[i] + b * (z[i] - mean) + c
        v = jnp.where(keep, v, 0.0)
        d3[i + 1, :, 0:n] = pltpu.roll(v, COLS - 1, 0).astype(BF16)
        low = v.astype(BF16)
        d3[i + 1, :, n : 2 * n] = low
        dz[i] = low
        d3[i + 1, :, 2 * n : 3 * n] = pltpu.roll(v, 1, 0).astype(BF16)
        return carry

    lax.fori_loop(0, rows, put, 0, unroll=2)
    step = rows // 4
    for k in range(4):
        both = mm_nt(flat(d3[step * k : step * (k + 1) + 1]), b_two[...])
        value = mm_nt(flat(d3[step * k + 2 : step * (k + 1) + 2]), b_last[...])
        value = value + both[COLS:, 0:n] + both[0 : step * COLS, n : 2 * n]
        d[step * k : step * (k + 1)] = value.reshape(step, COLS, LANES)
    slope_sums(tab, d, z_in, norm_in, keeps_in, dout, send)


def b10(
    tab, got, labels, dout_in, z, norm, keeps, w, grad_pre, slope, zc, zp, keeps_cp,
    dz, grad_pre_2, send, grad_norm, d,
):
    rows, chans = zc.shape[0], zc.shape[2]
    pixels = 1.0 * rows * (COLS - 4)
    mean, a, b, c = backward_norm(tab, got, labels, norm, keeps, pixels, grad_norm)
    keep = valid_cols(LANES)

    def put(i, carry):
        v = a * dout_in[i] + b * (z[i] - mean) + c
        dz[i] = jnp.where(keep, v, 0.0).astype(BF16)
        return carry

    lax.fori_loop(0, rows, put, 0, unroll=4)
    d[...] = mm_nt(flat(dz[...]), w[...]).reshape(d.shape)
    mean_c, rstd_c, mean_p, rstd_p = (keeps_cp[k : k + 1, :] for k in range(4))

    def sum_up(i, carry):
        sums, prod_c, prod_p = carry
        g = (grad_pre[i] + d[i]).astype(BF16).astype(F32) * slope[i]
        grad_pre_2[i] = g
        return (
            sums + fold(g),
            prod_c + fold(g * (zc[i] - mean_c)),
            prod_p + fold(g * (zp[i] - mean_p)),
        )

    start = zeros8(chans)
    sums, prod_c, prod_p = lax.fori_loop(0, rows, sum_up, (start, start, start), unroll=2)
    spread(send, [down(sums), down(prod_c) * rstd_c, down(prod_p) * rstd_p])


def b11(
    tab, got, labels, grad_pre_2, zc, zp, norm_c, norm_p, keeps_cp, w, z_in, norm_in, keeps_in,
    dz_c, dz_p, dout, send, grad_norm_c, grad_norm_p, d,
):
    rows, chans = zc.shape[0], zc.shape[2]
    pixels = 1.0 * rows * (COLS - 4)
    mean_c, a_c, b_c, c_c = backward_norm(
        tab, got, labels, norm_c, keeps_cp.at[0:2], pixels, grad_norm_c, (0, 1)
    )
    mean_p, a_p, b_p, c_p = backward_norm(
        tab, got, labels, norm_p, keeps_cp.at[2:4], pixels, grad_norm_p, (0, 2)
    )
    keep = valid_cols(chans)

    def put(i, carry):
        g = grad_pre_2[i]
        v = a_c * g + b_c * (zc[i] - mean_c) + c_c
        dz_c[i] = jnp.where(keep, v, 0.0).astype(BF16)
        v = a_p * g + b_p * (zp[i] - mean_p) + c_p
        dz_p[i] = jnp.where(keep, v, 0.0).astype(BF16)
        return carry

    lax.fori_loop(0, rows, put, 0, unroll=2)
    d[...] = mm_nt(flat(dz_c[...]), w[...]).reshape(d.shape)
    slope_sums(tab, d, z_in, norm_in, keeps_in, dout, send)


def b12(tab, got, labels, dout_in, z, norm, keeps, xs, d2, kept, sent, grad_norm, dz, packed):
    rows = z.shape[0]
    pixels = 1.0 * rows * (COLS - 4)
    mean, a, b, c = backward_norm(tab, got, labels, norm, keeps, pixels, grad_norm)
    keep = valid_cols(LANES)
    n = LANES
    d2[rows] = jnp.zeros(d2.shape[1:], BF16)

    def put(i, carry):
        v = a * dout_in[i] + b * (z[i] - mean) + c
        v = jnp.where(keep, v, 0.0)
        low = v.astype(BF16)
        dz[i] = low
        d2[i, :, 0:n] = low
        d2[i, :, n : 2 * n] = pltpu.roll(v, COLS - 1, 0).astype(BF16)
        return carry

    lax.fori_loop(0, rows, put, 0, unroll=4)
    low = flat(dz[...])
    cur = mm_side(flat(xs[1 : rows + 1]), low)
    for k, (y, x) in enumerate(((1, 1), (1, 2), (1, 0), (2, 1), (2, 2), (2, 0))):
        put_rows(packed, n * (3 * y + x), cur[n * k : n * (k + 1)])
    up = mm_side(flat(xs[0:rows, :, 3 * n : 6 * n]), low)
    for k, (y, x) in enumerate(((0, 1), (0, 2), (0, 0))):
        put_rows(packed, n * (3 * y + x), up[n * k : n * (k + 1)])
    share_out(tab, packed, 9 * n, kept, sent)


def b12_images(
    tab, d2, b_even, b_odd, zz, norm_in, keeps_in, dn, sums_out, de, do, wide, *, own
):
    rows = de.shape[0]
    n = LANES
    half = half_of(tab)
    first = rows * (half if own else 1 - half)
    step = rows // 2
    for k in range(2):
        here = flat(d2[pl.ds(first + step * k, step)])
        below = flat(d2[pl.ds(first + step * k + 1, step)])
        de[step * k : step * (k + 1)] = mm_nt(here, b_even[...]).reshape(step, COLS, 2 * n)
        odd = mm_nt(here, b_odd[:, 0 : 2 * n]) + mm_nt(below, b_odd[:, 2 * n : 4 * n])
        do[step * k : step * (k + 1)] = odd.reshape(step, COLS, 2 * n)
    mean_1, rstd_1 = keeps_in[0:1, :], keeps_in[1:2, :]
    group = entry(tab, OWN)
    scale = rstd_1 * gain_of(norm_in, group)
    bias = 0.5 * (shift_of(norm_in, group) - mean_1 * scale)
    scale = 0.5 * scale
    keep = valid_cols(LANES) & chan_mask(tab)

    def emit(i, carry):
        sums, products = carry
        for ra in (0, 1):
            planes = (de, do)[ra]
            for cb in (0, 1):
                zv = zz[2 * i + ra, pl.ds(cb, COLS, stride=2), :]
                g = planes[i, :, n * cb : n * (cb + 1)] * slope_of_half(zv * scale + bias)
                g = jnp.where(keep, g, 0.0)
                sums = sums + fold(g)
                products = products + fold(g * (zv - mean_1))
                wide[ra, pl.ds(cb, COLS, stride=2), :] = g
            dn[2 * i + ra] = wide[ra].astype(BF16)
        return sums, products

    totals = lax.fori_loop(0, rows, emit, (zeros8(n), zeros8(n)), unroll=2)
    sums_out[0:1, :] = down(totals[0])
    sums_out[1:2, :] = down(totals[1]) * rstd_1


def b13(
    tab, got, labels, norm, keeps, w, z_own, z_for, dn_own, dn_for, gs_own, gs_for, *rest, at, held
):
    finished, outs = rest[:held], rest[held : 2 * held]
    grad, grad_norm, dz, wide, grad_v, norm_v, sems = rest[2 * held :]
    copies = [
        pltpu.make_async_copy(a, b, sems.at[k]) for k, (a, b) in enumerate(zip(finished, outs))
    ]
    for copy in copies:
        copy.start()
    rows, cols = grad.shape[1], grad.shape[2]
    half = half_of(tab)
    pixels = 2.0 * rows * cols
    marks = labels[...]
    totals = last_sums(got.at[:, at : at + 4, :], marks, norm.shape[0])
    for g in range(norm.shape[0]):
        norm_v[g, 0:1, :] = totals[g][1]
        norm_v[g, 1:2, :] = totals[g][0]
    copies.append(pltpu.make_async_copy(norm_v, grad_norm, sems.at[held]))
    copies[-1].start()
    keep = lax.broadcasted_iota(jnp.int32, (z_own.shape[1], LANES), 0) < cols
    for k, (z, dn, gs) in enumerate(((z_own, dn_own, gs_own), (z_for, dn_for, gs_for))):
        group = entry(tab, OWN if k == 0 else OTHER)
        shift_sum = own_of([t[0] for t in totals], group)
        gain_sum = own_of([t[1] for t in totals], group)
        count = group_count(marks, group) * pixels
        mean, rstd = keeps[2 * k : 2 * k + 1, :], keeps[2 * k + 1 : 2 * k + 2, :]
        a = rstd * gain_of(norm, group)
        b = -(a * rstd) * gain_sum / count
        c = -a * shift_sum / count

        def put(i, carry, z=z, dn=dn, mean=mean, a=a, b=b, c=c):
            v = a * dn[i].astype(F32) + b * (z[i] - mean) + c
            dz[i] = jnp.where(keep, v, 0.0).astype(BF16)
            return carry

        lax.fori_loop(0, rows, put, 0, unroll=4)
        place = half if k == 0 else 1 - half
        step = rows // 2
        for q in range(2):
            low = flat(dz[step * q : step * (q + 1)])
            for p in range(wide.shape[0]):
                values = mm_nt(low, w[LANES * p : LANES * (p + 1), :])
                wide[p, step * q : step * (q + 1)] = values.reshape(step, -1, LANES)

            def emit(i, carry, gs=gs, place=place):
                even = pl.ds(0, COLS, stride=2)
                for p in range(wide.shape[0]):
                    lanes = slice(LANES * p, LANES * (p + 1))
                    wide[p, 2 * i, even, :] = wide[p, 2 * i, even, :] + gs[i, :, lanes].astype(F32)
                    grad_v[place, 2 * i, :, lanes] = wide[p, 2 * i, 0:cols, :].astype(BF16)
                    grad_v[place, 2 * i + 1, :, lanes] = wide[p, 2 * i + 1, 0:cols, :].astype(BF16)
                return carry

            lax.fori_loop(step // 2 * q, step // 2 * (q + 1), emit, 0, unroll=True)
            part = pl.ds(step * q, step)
            copies.append(
                pltpu.make_async_copy(
                    grad_v.at[place, part], grad.at[place, part], sems.at[held + 1 + 2 * k + q]
                )
            )
            copies[-1].start()
    for copy in copies:
        copy.wait()


def put_rows(out, at, value):
    for j in range(value.shape[1] // LANES):
        out[at : at + value.shape[0], :] = value[:, LANES * j : LANES * (j + 1)].astype(BF16)
        at += value.shape[0]
    return at


def take_rows(source, at, out):
    rows = out.shape[0]
    for j in range(out.shape[1] // LANES):
        out[:, LANES * j : LANES * (j + 1)] = source(at, rows)
        at += rows
    return at


def share_out(tab, packed, used, kept, sent):
    if used < packed.shape[0]:
        packed[used:, :] = jnp.zeros((packed.shape[0] - used, LANES), BF16)
    half = half_of(tab)
    size = kept.shape[0] * kept.shape[1]
    for out, place in ((kept, half), (sent, 1 - half)):
        out[...] = packed[pl.ds(pl.multiple_of(size * place, 16), size), :].reshape(out.shape)


def g_most(
    tab, act_2b, dz_2c, x3, dz_2b, joined, dz_2a, act_1b, dz_1c, xee, dz_1p, w_1p,
    kept, sent, gs_own, gs_oth, packed,
):
    rows = dz_2b.shape[0]
    at = put_rows(packed, 0, mm_tn(flat(act_2b[...]), flat(dz_2c[...])))
    low = flat(dz_2b[...])
    for y in range(3):
        at = put_rows(packed, at, mm_side(flat(x3[y : y + rows]), low))
    at = put_rows(packed, at, mm_side(flat(joined[...]), flat(dz_2a[...])))
    at = put_rows(packed, at, mm_tn(flat(act_1b[...]), flat(dz_1c[...])))
    at = put_rows(packed, at, mm_tn(flat(xee[...]), flat(dz_1p[...])))
    share_out(tab, packed, at, kept, sent)
    half = half_of(tab)
    count = gs_own.shape[0]
    for k, gs in enumerate((gs_own, gs_oth)):
        first = count * (half if k == 0 else 1 - half)
        got = mm_nt(flat(dz_1p[pl.ds(first, count)]), w_1p[...])
        gs[...] = got.reshape(gs.shape).astype(BF16)


def g_xz(keeps, x_own, x_oth, z_own, z_oth, out, low):
    rows = z_own.shape[0]
    mean = keeps[0:1, :]
    value = None
    for x, z in ((x_own, z_own), (x_oth, z_oth)):

        def put(i, carry, z=z):
            low[i] = (z[i] - mean).astype(BF16)
            return carry

        lax.fori_loop(0, rows, put, 0, unroll=4)
        term = mm_tn(flat(x[...]), flat(low[...]))
        value = term if value is None else value + term
    at = value.shape[0]
    out[0:at, :] = value
    if at < out.shape[0]:
        out[at:, :] = jnp.zeros((out.shape[0] - at, LANES), F32)


def g_xd(tab, sums_own, sums_oth, norm, keeps, x_dev, x_own, x_oth, dn_own, dn_oth, out, sums, low):
    rows = dn_own.shape[0]
    n = LANES
    pixels = 1.0 * (2 * rows) * (2 * (COLS - 4))
    sums[...] = sums_own[...] + sums_oth[...]
    a = keeps[1:2, :] * gain_of(norm, entry(tab, OWN))
    local = sums[0:1, :] / pixels
    value = None
    for x, dn in ((x_own, dn_own), (x_oth, dn_oth)):

        def put(i, carry, dn=dn):
            low[i] = (a * (dn[i].astype(F32) - local)).astype(BF16)
            return carry

        lax.fori_loop(0, rows, put, 0, unroll=4)
        term = mm_tn(flat(x[...]), flat(low[...]))
        value = term if value is None else value + term
    spread_dev = jnp.broadcast_to(x_dev[...], (8, x_dev.shape[1]))
    column = jnp.transpose(spread_dev)[:, 0:1]
    value = value + column * (a * local)
    at = value.shape[0]
    out[0:at, :] = value.astype(BF16)
    if at < out.shape[0]:
        out[at:, :] = jnp.zeros((out.shape[0] - at, n), BF16)


def pack_last(tall, sums, kept, got, kept_1b, got_1b, send, *, stats_at):
    n = LANES
    devices = send.shape[0]
    piece, share = kept.shape[1], tall.shape[0] // devices
    first = kept.shape[0]
    second = first + kept_1b.shape[0]
    send[0:first, 0:piece, :] = (kept[...].astype(F32) + got[...].astype(F32)).astype(BF16)
    send[first:second, 0:piece, :] = (kept_1b[...].astype(F32) + got_1b[...].astype(F32)).astype(BF16)
    if second < devices:
        send[second:, 0:piece, :] = jnp.zeros((devices - second, piece, n), BF16)
    send[:, piece : piece + share, :] = tall[...].reshape(devices, share, n)
    high = sums[...].astype(BF16)
    rest = (sums[...] - high.astype(F32)).astype(BF16)
    for k, v in enumerate((high, rest)):
        send[:, stats_at + 2 * k : stats_at + 2 * k + 2, :] = jnp.broadcast_to(v[None], (devices, 2, n))


def last_sums(stats, marks, groups):
    values = stats[:, 0:2, :].astype(F32) + stats[:, 2:4, :].astype(F32)
    out = []
    for g in range(groups):
        total = jnp.sum(values * (marks == float(g)).astype(F32), axis=0)
        out.append((total[0:1], total[1:2]))
    return out


def add_all(got, labels, norm, keeps_all, xz_got, out, *, at, pixels):
    devices, n = got.shape[0], LANES
    half = devices // 2
    share = xz_got.shape[2] // n - 2
    piece = out.shape[1] - share
    marks = labels[...]
    value = jnp.sum(got[:, piece : piece + share, :].astype(F32), axis=0)
    sums = last_sums(got.at[:, at : at + 4, :], marks, norm.shape[0])
    for g in range(norm.shape[0]):
        rstd = keeps_all[2 * g + 1 : 2 * g + 2, :]
        count = group_count(marks, float(g)) * pixels
        b = -(rstd * rstd * norm[g, 0:1, :]) * sums[g][1] / count
        same = (marks == float(g)).astype(F32)
        rows = [
            jnp.sum(xz_got[:, :, n * (2 + q) : n * (3 + q)] * same, axis=0) for q in range(share)
        ]
        value = value + jnp.concatenate(rows, axis=0) * b
    for k in (0, 1):
        total = jnp.sum(got[half * k : half * (k + 1), 0:piece, :].astype(F32), axis=0).astype(BF16)
        out[half * k : half * (k + 1), 0:piece, :] = jnp.broadcast_to(total[None], (half, piece, n))
    out[:, piece:, :] = jnp.broadcast_to(value.astype(BF16)[None], (devices, share, n))


def unpack(
    tab, own, other, o_1a, o_1b, o_2c, o_2b, o_2a, o_1c, o_1p,
    w_1a, w_1b, w_2c, w_2b, w_2a, w_1c, w_1p, tall, packed, packed_1b, sems,
):
    half = half_of(tab)
    piece = packed.shape[1]
    first, second = packed.shape[0] // 2, packed_1b.shape[0] // 2
    for part, place in ((own, half), (other, 1 - half)):
        packed[pl.ds(first * place, first)] = part[0:first, 0:piece, :]
        packed_1b[pl.ds(second * place, second)] = part[first : first + second, 0:piece, :]
    flat_1b, rest = flat(packed_1b[...]), flat(packed[...])
    copies = []

    def leave(value, out):
        copies.append(pltpu.make_async_copy(value, out, sems.at[len(copies)]))
        copies[-1].start()

    def source(at, rows):
        return rest[at : at + rows].astype(F32)

    at = 0
    for value, out in ((w_2c, o_2c), (w_2b, o_2b), (w_2a, o_2a), (w_1c, o_1c), (w_1p, o_1p)):
        at = take_rows(source, at, value)
        leave(value, out)
    w_1b[...] = flat_1b[0 : w_1b.shape[0]].astype(F32)
    leave(w_1b, o_1b)
    tall[...] = own[:, piece:, :].astype(F32).reshape(tall.shape)
    w_1a[...] = tall[0 : w_1a.shape[0], :]
    leave(w_1a, o_1a)
    for copy in copies:
        copy.wait()


def gather(send):
    return lax.all_to_all(send, AXES, 0, 0)


def tie(*values):
    return lax.optimization_barrier(values)


def swap(block):
    return lax.ppermute(block, "rows", [(0, 1), (1, 0)])


def body(
    images, w_1a, w_1b, w_1c, w_1p, w_2a, w_2b, w_2c,
    norm_1a, norm_1b, norm_1c, norm_1p, norm_2a, norm_2b, norm_2c,
    cotangent, group, width, gate,
):
    devices = lax.axis_size("rows") * lax.axis_size("batch")
    half = lax.axis_index("rows").astype(jnp.int32).reshape(1)
    norms = (norm_1a, norm_1b, norm_1c, norm_1p, norm_2a, norm_2b, norm_2c)
    norm_1a, norm_1b, norm_1c, norm_1p, norm_2a, norm_2b, norm_2c = (
        v.transpose(1, 0, 2) for v in norms
    )
    outer, inputs = w_1c.shape[1], w_1a.shape[0]
    rows = cotangent.shape[1]
    cols_in = 2 * COLS
    n, m = LANES, devices

    def send(stats, channels=LANES):
        return ((m, channels // LANES, stats * LANES), F32)

    def maps(channels, dtype=F32):
        return ((rows, COLS, channels), dtype)

    def scratch(channels, dtype=F32):
        return pltpu.VMEM((rows, COLS, channels), dtype)

    def params(*arrays):
        return [(a.shape, F32) for a in arrays]

    def mean_scale(channels, count=1):
        return ((2 * count, channels), F32)

    wide_in = ((rows, cols_in, inputs), BF16)
    wide_z = ((rows, cols_in, n), F32)
    raw = images.shape
    tab, x_own, x_for, z_own, z_for, s1 = stage(
        f1, [((8, n), F32), wide_in, wide_in, wide_z, wide_z, send(5)],
        [*(pltpu.SMEM(v.shape, jnp.int32) for v in (half, group, width, gate)),
         pltpu.VMEM(raw, BF16), pltpu.VMEM(w_1a.shape, BF16), pltpu.SemaphoreType.DMA((7,))],
        hbm=(0, 1, 2, 3, 4, 5),
    )(half, group, width, gate, images, w_1a)
    s1, v_1b, v_2b = tie(s1, w_1b, w_2b)
    built = stage(
        prepare,
        [(v, BF16) for v in (
            (3 * n, n), (3 * n, 2 * n), (3 * n, 2 * n), (3 * n, n),
            (2 * n, 2 * n), (2 * n, 4 * n), (2 * n, 3 * n), (n, 3 * n),
        )],
    )(v_1b, v_2b)
    s1, x_for, w_even, w_odd, w_two, w_last, b_even, b_odd, b_two, b_last = tie(s1, x_for, *built)
    x_oth = swap(x_for)
    g1 = gather(s1)
    g1, x_oth = tie(g1, x_oth)
    xee, z_1p, stats_1p = stage(
        f1_strided,
        [maps(inputs, BF16), maps(outer), ((1, inputs + outer), F32)],
        [pltpu.VMEM((inputs // n, cols_in, n), F32)],
    )(tab, x_own, x_oth, w_1p)
    xs, z_1b, s2, labels, k_1a, k_all, z_oth, x_sum = stage(
        f2,
        [((rows + 1, COLS, 6 * n), BF16), maps(n), send(2 + (2 * inputs + outer) // n),
         ((m, 1, n), F32), mean_scale(n, 2), mean_scale(n, norm_1a.shape[0]), wide_z,
         ((8, inputs), F32)],
    )(tab, g1, z_own, x_own, x_oth, w_1a, norm_1a, w_even, w_odd, stats_1p)
    g2 = gather(s2)
    act_1b, z_1c, s3, k_1b, k_p, x_dev = stage(
        f3, [maps(n, BF16), maps(outer), send(1 + outer // n), mean_scale(n), mean_scale(outer),
             ((1, inputs), F32)],
    )(tab, g2, labels, z_1b, norm_1b, w_1c, w_1p, x_sum)
    g3 = gather(s3)
    joined, slope, z_2a, s4, k_cp = stage(
        f4, [maps(outer, BF16), maps(outer), maps(n), send(2), mean_scale(outer, 2)]
    )(tab, g3, labels, z_1c, z_1p, norm_1c, norm_1p, k_p, w_1c, w_2a)
    share = -(-inputs // devices)
    half_in = ((rows, cols_in, n), BF16)
    s4, k_1a = tie(s4, k_1a)
    (xz,) = stage(g_xz, [((devices * share, n), F32)], [pltpu.VMEM(half_in[0], BF16)])(
        k_1a, x_own, x_oth, z_own, z_oth
    )
    s4, xz = tie(s4, xz)
    g4 = gather(s4)
    x3, z_2b, s5, k_2a = stage(
        f5, [((rows + 2, COLS, 3 * n), BF16), maps(n), send(2 + share), mean_scale(n)]
    )(tab, g4, labels, z_2a, norm_2a, w_two, w_last, xz)
    g5 = gather(s5)
    act_2b, z_2c, s6, k_2b = stage(
        f6, [maps(n, BF16), maps(outer), send(1 + outer // n), mean_scale(n)]
    )(tab, g5, labels, z_2b, norm_2b, w_2c)
    g6 = gather(s6)
    result, grad_pre, s7, k_2c = stage(
        b7, [(cotangent.shape[1:], BF16), maps(outer), send(2, outer), mean_scale(outer)],
        [pltpu.VMEM((COLS, outer), F32)],
    )(tab, g6, labels, joined, z_2c, norm_2c, w_2c, cotangent[0])
    g7 = gather(s7)
    dz_2c, dout_2b, s8, grad_norm_2c = stage(
        b8, [maps(outer, BF16), maps(n), send(2), *params(norm_2c)], [scratch(n)]
    )(tab, g7, labels, grad_pre, z_2c, norm_2c, k_2c, w_2c, z_2b, norm_2b, k_2b)
    g8 = gather(s8)
    dz_2b, dout_2a, s9, grad_norm_2b = stage(
        b9, [maps(n, BF16), maps(n), send(2), *params(norm_2b)],
        [pltpu.VMEM((rows + 2, COLS, 3 * n), BF16), scratch(n)],
    )(tab, g8, labels, dout_2b, z_2b, norm_2b, k_2b, b_two, b_last, z_2a, norm_2a, k_2a)
    g9 = gather(s9)
    dz_2a, grad_pre_2, s10, grad_norm_2a = stage(
        b10, [maps(n, BF16), maps(outer), send(3, outer), *params(norm_2a)], [scratch(outer)]
    )(tab, g9, labels, dout_2a, z_2a, norm_2a, k_2a, w_2a, grad_pre, slope, z_1c, z_1p, k_cp)
    g10 = gather(s10)
    dz_1c, dz_1p, dout_1b, s11, grad_norm_1c, grad_norm_1p = stage(
        b11, [maps(outer, BF16), maps(outer, BF16), maps(n), send(2), *params(norm_1c, norm_1p)],
        [scratch(n)],
    )(tab, g10, labels, grad_pre_2, z_1c, z_1p, norm_1c, norm_1p, k_cp, w_1c, z_1b, norm_1b, k_1b)
    half_map = ((rows // 2, COLS, inputs), BF16)
    most_rows = sum(v.size for v in (w_2c, w_2b, w_2a, w_1c, w_1p)) // n
    rows_1b = w_1b.size // n
    piece = 16
    while -(-most_rows // (2 * piece)) - (-rows_1b // (2 * piece)) > devices:
        piece += 16
    first, second = -(-most_rows // (2 * piece)), -(-rows_1b // (2 * piece))
    part, part_1b = ((first, piece, n), BF16), ((second, piece, n), BF16)
    kept, sent, gs_own, gs_send = stage(
        g_most, [part, part, half_map, half_map], [pltpu.VMEM((2 * first * piece, n), BF16)]
    )(tab, act_2b, dz_2c, x3, dz_2b, joined, dz_2a, act_1b, dz_1c, xee, dz_1p, w_1p)
    s11, sent, gs_send = tie(s11, sent, gs_send)
    g11, sent, gs_send = tie(gather(s11), sent, gs_send)
    got, gs_for = swap(sent), swap(gs_send)
    d2, kept_1b, sent_1b, grad_norm_1b = stage(
        b12, [((rows + 1, COLS, 2 * n), BF16), part_1b, part_1b, *params(norm_1b)],
        [scratch(n, BF16), pltpu.VMEM((2 * second * piece, n), BF16)],
    )(tab, g11, labels, dout_1b, z_1b, norm_1b, k_1b, xs)
    got_1b = swap(sent_1b)
    sides = []
    for own, z in ((False, z_oth), (True, z_own)):
        sides.append(
            stage(
                functools.partial(b12_images, own=own), [half_in, ((2, n), F32)],
                [pltpu.VMEM((rows // 2, COLS, 2 * n), F32), pltpu.VMEM((rows // 2, COLS, 2 * n), F32),
                 pltpu.VMEM((2, cols_in, n), F32)],
            )(tab, d2, b_even, b_odd, z, norm_1a, k_1a)
        )
        if not own:
            dn_for = swap(sides[0][0])
            d2, _ = tie(d2, sides[0][0])
    (dn_send, sums_send), (dn_own, sums_own) = sides
    stats_at = piece + -(-share // 8) * 8
    high = -(-(stats_at + 4) // 16) * 16
    tall, sums_1a = stage(
        g_xd, [((devices * share, n), BF16), ((2, n), F32)], [pltpu.VMEM(half_in[0], BF16)]
    )(tab, sums_own, sums_send, norm_1a, k_1a, x_dev, x_own, x_oth, dn_own, dn_send)
    tall, gs_for, dn_for = tie(tall, gs_for, dn_for)
    (s12,) = stage(
        functools.partial(pack_last, stats_at=stats_at), [((devices, high, n), BF16)]
    )(tall, sums_1a, kept, got, kept_1b, got_1b)
    g12 = gather(s12)
    pixels = 4.0 * images.shape[1] * images.shape[1]
    (mine,) = stage(
        functools.partial(add_all, at=stats_at, pixels=pixels),
        [((devices, piece + share, n), BF16)],
    )(g12, labels, norm_1a, k_all, g5)
    finished = (
        result, grad_norm_1b, grad_norm_1c, grad_norm_1p, grad_norm_2a, grad_norm_2b, grad_norm_2c
    )
    held = len(finished)
    *finished, grad_images, grad_norm_1a = stage(
        functools.partial(b13, at=stats_at, held=held),
        [*((v.shape, v.dtype) for v in finished), (images.shape, BF16), *params(norm_1a)],
        [pltpu.VMEM(half_in[0], BF16), pltpu.VMEM((inputs // n, rows, cols_in, n), F32),
         pltpu.VMEM(images.shape, BF16), pltpu.VMEM(norm_1a.shape, F32),
         pltpu.SemaphoreType.DMA((held + 5,))],
        hbm_out=range(held + 2),
    )(tab, g12, labels, norm_1a, k_1a, w_1a, z_own, z_for, dn_own, dn_for, gs_own, gs_for, *finished)
    result, grad_norm_1b, grad_norm_1c, grad_norm_1p, grad_norm_2a, grad_norm_2b, grad_norm_2c = finished
    whole = gather(mine)
    weights = (w_1a, w_1b.reshape(-1, n), w_2c, w_2b.reshape(-1, n), w_2a, w_1c, w_1p)
    totals = stage(
        unpack, [(v.shape, F32) for v in weights],
        [*(pltpu.VMEM(v.shape, F32) for v in weights),
         pltpu.VMEM((devices * share, n), F32), pltpu.VMEM((2 * first, piece, n), BF16),
         pltpu.VMEM((2 * second, piece, n), BF16), pltpu.SemaphoreType.DMA((7,))],
        hbm_out=range(7),
    )(tab, whole, swap(whole))
    t_1a, t_1b, t_2c, t_2b, t_2a, t_1c, t_1p = totals
    grads = (
        grad_norm_1a, grad_norm_1b, grad_norm_1c, grad_norm_1p,
        grad_norm_2a, grad_norm_2b, grad_norm_2c,
    )
    return (
        result[None], grad_images, t_1a, t_1b.reshape(w_1b.shape), t_1c, t_1p, t_2a,
        t_2b.reshape(w_2b.shape), t_2c, *[v.transpose(1, 0, 2) for v in grads],
    )


def solution(mesh):
    return jax.shard_map(
        body,
        mesh=mesh,
        in_specs=(
            P("batch", "rows", None, None),
            *[P()] * 14,
            P(("batch", "rows"), None, None, None),
            P("batch"),
            P(),
            P(),
        ),
        out_specs=(
            P(("batch", "rows"), None, None, None),
            P("batch", "rows", None, None),
            *[P()] * 14,
        ),
        check_vma=False,
    )
```

time: 207 us -> 191 us (0.923)
  Pallas kernels: 43.9 us -> 29.9 us
    pallas_call x23, Pallas kernels: 43.9 us -> 29.9 us  [call(): pl.pallas_call(kernel, out_shape=tuple((jax.ShapeDtypeStruct(s, d) for s,...]
    all_to_all x13, blocking collectives: 160 us -> 158 us  [gather(): return lax.all_to_all(send, AXES, 0, 0)]
  transfers between devices with their start and end apart: 6 -> 6, of which waited for: 0 -> 0; matrix products, arithmetic and copies ran while one was open for 0% -> 0% of each run, Pallas kernels for 5% -> 3%
where the time goes in v3:
time: 191 us; the launch traced here: 190 us
  blocking collectives  158 us (83%)
  Pallas kernels  29.9 us (16%)
    all_to_all x13, blocking collectives, gather(): return lax.all_to_all(send, AXES, 0, 0)  158 us
    pallas_call x23, Pallas kernels, call(): pl.pallas_call(kernel, out_shape=tuple((jax.ShapeDtypeStruct(s, d) for s,...  29.9 us
  transfers between devices with their start and end apart: 6, of which 0 were waited for; matrix products, arithmetic and copies ran while one was open for 0% of the time, Pallas kernels for 3%

profile of v3, /device:TPU:0, one launch (start us, length us, event | category | flops | bytes accessed | tf_op | source)
XLA Modules:
  0.0 190.5 jit_solution(13665457134247641768)
XLA Ops:
  0.7 2.5 %f1.1 = (f32[8,128]{1,0:T(8,128)S(1)}, bf16[28,64,256]{2,1,0:T(8,128)(2,1)S(1)}, bf16[28,64,256]{2,1,0:T(8,128)(2,1)S(1)}, f32[28,64,128]{2,1,0:T(8,128)S(1)}, f...) custom-call(s32[1]{0:T(128)} %bitcast.half_at, s32[2]{0:T(128)} %group_at.1, s32[3]{0:T(128)} %width_at.1, s32[3]{0:T(128)} %gate_at.1, ...), custom_call_target="tpu_custom_call" | custom-call | tf_op jit(solution)/shard_map/f1/pallas_call | solution.py:32
  4.0 14.2 %all_to_all.65.got = f32[32,1,640]{2,1,0:T(1,128)S(1)} all-to-all(f32[32,1,640]{2,1,0:T(1,128)S(1)} %get-tuple-element.155), channel_id=1, replica_groups=mesh['rows'=2,'batch'=16] {'rows','batch'}, dimensions={0} | all-to-all | bytes 163840 | tf_op jit(solution)/shard_map/all_to_all | solution.py:1007
  18.2 0.9 f1_strided.1
  19.2 2.5 %f2.1 = (bf16[29,32,768]{2,1,0:T(8,128)(2,1)S(1)}, f32[28,32,128]{2,1,0:T(8,128)S(1)}, f32[32,1,1280]{2,1,0:T(1,128)S(1)}, f32[32,1,128]{2,1,0:T(1,128)S(1)}, f3...) custom-call(f32[8,128]{1,0:T(8,128)S(1)} %get-tuple-element.141.tab, ...), custom_call_target="tpu_custom_call" | custom-call | tf_op jit(solution)/shard_map/f2/pallas_call | solution.py:32
  21.7 10.5 %all_to_all.66.got = f32[32,1,1280]{2,1,0:T(1,128)S(1)} all-to-all(f32[32,1,1280]{2,1,0:T(1,128)S(1)} %get-tuple-element.164), channel_id=1, replica_groups=mesh['rows'=2,'batch'=16] {'rows','batch'}, dimensions={0} | all-to-all | bytes 327680 | tf_op jit(solution)/shard_map/all_to_all | solution.py:1007
  32.2 0.7 f3.1
  32.9 9.2 %all_to_all.67.got = f32[32,1,640]{2,1,0:T(1,128)S(1)} all-to-all(f32[32,1,640]{2,1,0:T(1,128)S(1)} %get-tuple-element.168), channel_id=1, replica_groups=mesh['rows'=2,'batch'=16] {'rows','batch'}, dimensions={0} | all-to-all | bytes 163840 | tf_op jit(solution)/shard_map/all_to_all | solution.py:1007
  42.2 1.4 f4.1
  43.6 0.9 g_xz.1.xz
  44.6 9.0 %all_to_all.68.got = f32[32,1,256]{2,1,0:T(1,128)S(1)} all-to-all(f32[32,1,256]{2,1,0:T(1,128)S(1)} %get-tuple-element.177), channel_id=1, replica_groups=mesh['rows'=2,'batch'=16] {'rows','batch'}, dimensions={0} | all-to-all | bytes 65536 | tf_op jit(solution)/shard_map/all_to_all | solution.py:1007
  53.6 1.1 f5.1
  54.7 10.5 %all_to_all.69.got.xz_got = f32[32,1,1280]{2,1,0:T(1,128)S(1)} all-to-all(f32[32,1,1280]{2,1,0:T(1,128)S(1)} %get-tuple-element.182), channel_id=1, replica_groups=mesh['rows'=2,'batch'=16] {'rows','batch'}, dimensions={0} | all-to-all | bytes 327680 | tf_op jit(solution)/shard_map/all_to_all | solution.py:1007
  65.9 9.2 %all_to_all.70.got = f32[32,1,640]{2,1,0:T(1,128)S(1)} all-to-all(f32[32,1,640]{2,1,0:T(1,128)S(1)} %get-tuple-element.184), channel_id=1, replica_groups=mesh['rows'=2,'batch'=16] {'rows','batch'}, dimensions={0} | all-to-all | bytes 163840 | tf_op jit(solution)/shard_map/all_to_all | solution.py:1007
  75.1 1.8 b7.1
  76.8 9.6 %all_to_all.71.got = f32[32,4,256]{2,1,0:T(4,128)S(1)} all-to-all(f32[32,4,256]{2,1,0:T(4,128)S(1)} %get-tuple-element.187), channel_id=1, replica_groups=mesh['rows'=2,'batch'=16] {'rows','batch'}, dimensions={0} | all-to-all | bytes 262144 | tf_op jit(solution)/shard_map/all_to_all | solution.py:1007
  86.5 1.3 b8.1
  87.8 9.1 %all_to_all.72.got = f32[32,1,256]{2,1,0:T(1,128)S(1)} all-to-all(f32[32,1,256]{2,1,0:T(1,128)S(1)} %get-tuple-element.191), channel_id=1, replica_groups=mesh['rows'=2,'batch'=16] {'rows','batch'}, dimensions={0} | all-to-all | bytes 65536 | tf_op jit(solution)/shard_map/all_to_all | solution.py:1007
  96.9 1.4 b9.1
  98.3 8.9 %all_to_all.73.got = f32[32,1,256]{2,1,0:T(1,128)S(1)} all-to-all(f32[32,1,256]{2,1,0:T(1,128)S(1)} %get-tuple-element.196), channel_id=1, replica_groups=mesh['rows'=2,'batch'=16] {'rows','batch'}, dimensions={0} | all-to-all | bytes 65536 | tf_op jit(solution)/shard_map/all_to_all | solution.py:1007
  107.2 1.7 b10.1
  108.9 11.5 %all_to_all.74.got = f32[32,4,384]{2,1,0:T(4,128)S(1)} all-to-all(f32[32,4,384]{2,1,0:T(4,128)S(1)} %get-tuple-element.200), channel_id=1, replica_groups=mesh['rows'=2,'batch'=16] {'rows','batch'}, dimensions={0} | all-to-all | bytes 393216 | tf_op jit(solution)/shard_map/all_to_all | solution.py:1007
  120.4 1.9 %b11.1 = (bf16[28,32,512]{2,1,0:T(8,128)(2,1)S(1)}, bf16[28,32,512]{2,1,0:T(8,128)(2,1)S(1)}, f32[28,32,128]{2,1,0:T(8,128)S(1)}, f32[32,1,256]{2,1,0:T(1,128)S(...) custom-call(f32[8,128]{1,0:T(8,128)S(1)} %get-tuple-element.141.tab, f32[32,4,384]{2,1,0:T(4,128)S(1)} %all_to_all.74.got, ...), custom_call_target="tpu_custom_call" | custom-call | tf_op jit(solution)/shard_map/b11/pallas_call | solution.py:32
  122.4 1.6 g_most.1
  124.0 8.9 %all_to_all.75.got = f32[32,1,256]{2,1,0:T(1,128)S(1)} all-to-all(f32[32,1,256]{2,1,0:T(1,128)S(1)} %get-tuple-element.215), channel_id=1, replica_groups=mesh['rows'=2,'batch'=16] {'rows','batch'}, dimensions={0} | all-to-all | bytes 65536 | tf_op jit(solution)/shard_map/all_to_all | solution.py:1007
  132.9 1.0 b12.1
  133.9 1.1 b12_images.2
  136.0 1.1 b12_images.3
  137.1 1.1 g_xd.1
  138.5 24.2 %all_to_all.76.got = bf16[32,96,128]{2,1,0:T(8,128)(2,1)S(1)} all-to-all(bf16[32,96,128]{2,1,0:T(8,128)(2,1)S(1)} %pack_last.1), channel_id=1, replica_groups=mesh['rows'=2,'batch'=16] {'rows','batch'}, dimensions={0} | all-to-all | bytes 1572864 | tf_op jit(solution)/shard_map/all_to_all | solution.py:1007
  163.2 22.8 %all_to_all.77.own = bf16[32,88,128]{2,1,0:T(8,128)(2,1)S(1)} all-to-all(bf16[32,88,128]{2,1,0:T(8,128)(2,1)S(1)} %add_all.1), channel_id=1, replica_groups=mesh['rows'=2,'batch'=16] {'rows','batch'}, dimensions={0} | all-to-all | bytes 1441792 | tf_op jit(solution)/shard_map/all_to_all | solution.py:1007
  186.0 2.4 %b13.1 = (bf16[28,28,512]{2,1,0:T(8,128)(2,1)}, f32[3,2,128]{2,1,0:T(2,128)}, f32[3,2,512]{2,1,0:T(2,128)}, f32[3,2,512]{2,1,0:T(2,128)}, f32[3,2,128]{2,1,0:T(2...) custom-call(f32[8,128]{1,0:T(8,128)S(1)} %get-tuple-element.141.tab,, ...), custom_call_target="tpu_custom_call" | custom-call | tf_op jit(solution)/shard_map/b13/pallas_call | solution.py:32
  188.5 1.8 unpack.1
  (46 shorter events, 3.3 us)
Async XLA Ops:
  0.6 2.6 %copy-start.7 = (bf16[3,3,128,128]{3,2,1,0:T(8,128)(2,1)S(1)}, bf16[3,3,128,128]{3,2,1,0:T(8,128)(2,1)}, u32[]{:S(2)}) copy-start(bf16[3,3,128,128]{3,2,1,0:T(8,128)(2,1)} %w2b) | copy-start | bytes 884740
  0.7 2.6 %copy-start.6 = (bf16[3,3,128,128]{3,2,1,0:T(8,128)(2,1)S(1)}, bf16[3,3,128,128]{3,2,1,0:T(8,128)(2,1)}, u32[]{:S(2)}) copy-start(bf16[3,3,128,128]{3,2,1,0:T(8,128)(2,1)} %w1b) | copy-start | bytes 884740
  0.7 17.6 %copy-start = (bf16[256,512]{1,0:T(8,128)(2,1)S(1)}, bf16[256,512]{1,0:T(8,128)(2,1)}, u32[]{:S(2)}) copy-start(bf16[256,512]{1,0:T(8,128)(2,1)} %w_1p.1) | copy-start | bytes 786436
  3.2 15.9 %copy-start.4 = (bf16[256,128]{1,0:T(8,128)(2,1)S(1)}, bf16[256,128]{1,0:T(8,128)(2,1)}, u32[]{:S(2)}) copy-start(bf16[256,128]{1,0:T(8,128)(2,1)} %w.19) | copy-start | bytes 196612
  3.2 15.9 %copy-start.8 = (f32[2,3,128]{2,0,1:T(2,128)S(1)}, f32[2,3,128]{2,0,1:T(2,128)}, u32[]{:S(2)}) copy-start(f32[2,3,128]{2,0,1:T(2,128)} %param.27) | copy-start | bytes 9220
  3.4 14.8 %collective-permute-start = (bf16[28,64,256]{2,1,0:T(8,128)(2,1)S(1)}, bf16[28,64,256]{2,1,0:T(8,128)(2,1)S(1)}, u32[]{:S(2)}, u32[]{:S(2)}) collective-permute-start(bf16[28,64,256]{2,1,0:T(8,128)(2,1)S(1)} %get-tuple-element.156), channel_id=1, source_target_pairs={{0,16},{16,0},{1,17},{17,1},{2,18},{18,2},{3,19},{19,3},{4,20},{20... | collective-permute-start | bytes 2752520 | tf_op jit(solution)/shard_map/ppermute | solution.py:1015
  19.1 13.1 %copy-start.1 = (bf16[128,512]{1,0:T(8,128)(2,1)S(1)}, bf16[128,512]{1,0:T(8,128)(2,1)}, u32[]{:S(2)}) copy-start(bf16[128,512]{1,0:T(8,128)(2,1)} %w.18) | copy-start | bytes 393220
  19.1 13.1 %copy-start.12 = (f32[2,3,128]{2,0,1:T(2,128)S(1)}, f32[2,3,128]{2,0,1:T(2,128)}, u32[]{:S(2)}) copy-start(f32[2,3,128]{2,0,1:T(2,128)} %param.28) | copy-start | bytes 9220
  19.1 23.0 %copy-start.5 = (bf16[512,128]{1,0:T(8,128)(2,1)S(1)}, bf16[512,128]{1,0:T(8,128)(2,1)}, u32[]{:S(2)}) copy-start(bf16[512,128]{1,0:T(8,128)(2,1)} %w.17) | copy-start | bytes 393220
  19.1 23.0 %copy-start.9 = (f32[2,3,512]{2,0,1:T(2,128)S(1)}, f32[2,3,512]{2,0,1:T(2,128)}, u32[]{:S(2)}) copy-start(f32[2,3,512]{2,0,1:T(2,128)} %param.29) | copy-start | bytes 36868
  19.2 23.0 %copy-start.10 = (f32[2,3,512]{2,0,1:T(2,128)S(1)}, f32[2,3,512]{2,0,1:T(2,128)}, u32[]{:S(2)}) copy-start(f32[2,3,512]{2,0,1:T(2,128)} %param.30) | copy-start | bytes 36868
  43.6 10.0 %copy-start.14 = (f32[2,3,128]{2,0,1:T(2,128)S(1)}, f32[2,3,128]{2,0,1:T(2,128)}, u32[]{:S(2)}) copy-start(f32[2,3,128]{2,0,1:T(2,128)} %param.31) | copy-start | bytes 9220
  43.6 21.6 %copy-start.2 = (bf16[128,512]{1,0:T(8,128)(2,1)S(1)}, bf16[128,512]{1,0:T(8,128)(2,1)}, u32[]{:S(2)}) copy-start(bf16[128,512]{1,0:T(8,128)(2,1)} %w.16) | copy-start | bytes 393220
  43.6 21.6 %copy-start.13 = (f32[2,3,128]{2,0,1:T(2,128)S(1)}, f32[2,3,128]{2,0,1:T(2,128)}, u32[]{:S(2)}) copy-start(f32[2,3,128]{2,0,1:T(2,128)} %param.32) | copy-start | bytes 9220
  44.6 30.5 %copy-start.3 = (bf16[1,28,28,512]{3,2,1,0:T(8,128)(2,1)S(1)}, bf16[1,28,28,512]{3,2,1,0:T(8,128)(2,1)}, u32[]{:S(2)}) copy-start(bf16[1,28,28,512]{3,2,1,0:T(8,128)(2,1)} %param.34) | copy-start | bytes 2408452
  44.6 30.5 %copy-start.11 = (f32[2,3,512]{2,0,1:T(2,128)S(1)}, f32[2,3,512]{2,0,1:T(2,128)}, u32[]{:S(2)}) copy-start(f32[2,3,512]{2,0,1:T(2,128)} %param.33) | copy-start | bytes 36868
  132.9 5.4 %collective-permute-start.3 = (bf16[24,80,128]{2,1,0:T(8,128)(2,1)S(1)}, bf16[24,80,128]{2,1,0:T(8,128)(2,1)S(1)}, u32[]{:S(2)}, u32[]{:S(2)}) collective-permute-start(bf16[24,80,128]{2,1,0:T(8,128)(2,1)S(1)} %get-tuple-element.235), channel_id=1, source_target_pairs={{0,16},{16,0},{1,17},{17,1},{2,18},{18,2},{3,19},{19,3},{4,20},{20... | collective-permute-start | bytes 1474568 | tf_op jit(solution)/shard_map/ppermute | solution.py:1015
  135.0 3.3 %collective-permute-start.2 = (bf16[28,64,128]{2,1,0:T(8,128)(2,1)S(1)}, bf16[28,64,128]{2,1,0:T(8,128)(2,1)S(1)}, u32[]{:S(2)}, u32[]{:S(2)}) collective-permute-start(bf16[28,64,128]{2,1,0:T(8,128)(2,1)S(1)} %get-tuple-element.224.dn_oth), channel_id=1, source_target_pairs={{0,16},{16,0},{1,17},{17,1},{2,18},{18,2},{3,19},{19,3},{4,20},{20... | collective-permute-start | bytes 1376264 | tf_op jit(solution)/shard_map/ppermute | solution.py:1015
  135.5 2.7 %collective-permute-start.1 = (bf16[14,32,256]{2,1,0:T(8,128)(2,1)S(1)}, bf16[14,32,256]{2,1,0:T(8,128)(2,1)S(1)}, u32[]{:S(2)}, u32[]{:S(2)}) collective-permute-start(bf16[14,32,256]{2,1,0:T(8,128)(2,1)S(1)} %get-tuple-element.231), channel_id=1, source_target_pairs={{0,16},{16,0},{1,17},{17,1},{2,18},{18,2},{3,19},{19,3},{4,20},{20... | collective-permute-start | bytes 688136 | tf_op jit(solution)/shard_map/ppermute | solution.py:1015
  135.6 2.7 %collective-permute-start.4 = (bf16[8,80,128]{2,1,0:T(8,128)(2,1)S(1)}, bf16[8,80,128]{2,1,0:T(8,128)(2,1)S(1)}, u32[]{:S(2)}, u32[]{:S(2)}) collective-permute-start(bf16[8,80,128]{2,1,0:T(8,128)(2,1)S(1)} %get-tuple-element.237), channel_id=1, source_target_pairs={{0,16},{16,0},{1,17},{17,1},{2,18},{18,2},{3,19},{19,3},{4,20},{20... | collective-permute-start | bytes 491528 | tf_op jit(solution)/shard_map/ppermute | solution.py:1015
  186.0 2.4 %collective-permute-start.5 = (bf16[32,88,128]{2,1,0:T(8,128)(2,1)S(1)}, bf16[32,88,128]{2,1,0:T(8,128)(2,1)S(1)}, u32[]{:S(2)}, u32[]{:S(2)}) collective-permute-start(bf16[32,88,128]{2,1,0:T(8,128)(2,1)S(1)} %all_to_all.77.own), channel_id=1, source_target_pairs={{0,16},{16,0},{1,17},{17,1},{2,18},{18,2},{3,19},{19,3},{4,20},{20... | collective-permute-start | bytes 2162696 | tf_op jit(solution)/shard_map/ppermute | solution.py:1015

commit v4 on v3

--- a/solution.py
+++ b/solution.py
@@ -216,7 +216,7 @@
 
 def f1(
     half_at, group_at, width_at, gate_at, images, w_at, tab, x_own, x_for, z_own, z_for, send,
-    half_ref, group, width, gate, raw, w, sems,
+    half_ref, group, width, gate, raw, w, found, sems,
 ):
     pairs = (
         (half_at, half_ref), (group_at, group), (width_at, width), (gate_at, gate), (w_at, w),
@@ -225,14 +225,29 @@
     copies = [pltpu.make_async_copy(a, b, sems.at[k]) for k, (a, b) in enumerate(pairs)]
     for k in (0, 4, 5, 6, 1, 2, 3):
         copies[k].start()
-    for copy in copies:
-        copy.wait()
+    for k in (0, 4, 5):
+        copies[k].wait()
     half = half_ref[0]
-    rows = []
-    for place, x_pad, z in ((half, x_own, z_own), (1 - half, x_for, z_for)):
-        widen(raw.at[place], x_pad)
-        sums, squares = first_project(x_pad, w, z)
-        rows += [down(sums), down(squares)]
+    sides = ((x_own, z_own), (x_for, z_for))
+
+    def one(k):
+        for place in (0, 1):
+
+            @pl.when(half == place)
+            def _():
+                x_pad, z = sides[k] if place == 0 else sides[1 - k]
+                widen(raw.at[k], x_pad)
+                sums, squares = first_project(x_pad, w, z)
+                at = 2 * (k if place == 0 else 1 - k)
+                found[at : at + 1, :] = down(sums)
+                found[at + 1 : at + 2, :] = down(squares)
+
+    one(0)
+    copies[6].wait()
+    one(1)
+    for k in (1, 2, 3):
+        copies[k].wait()
+    rows = [found[k : k + 1, :] for k in range(4)]
     own, other = group[half], group[1 - half]
     values = {
         OWN: own, OTHER: other, HALF: half, LIMIT: w.shape[1] // 4 * width[own], GATE: gate[own]
@@ -304,8 +319,8 @@
 
 
 def f2(
-    tab, got, z_own, x_own, x_oth, w, norm, w_even, w_odd, stats_p,
-    xs, z, send, labels, keeps, keeps_all, z_oth, x_sum,
+    tab, got, z_own, x_oth, w, norm, w_even, w_odd, stats_p,
+    xs, z, send, labels, keeps, keeps_all, z_oth,
 ):
     codes = got[:, :, 4 * LANES : 5 * LANES]
     others = jnp.floor(0.25 * codes)
@@ -333,8 +348,6 @@
             keeps[2 * k + q : 2 * k + q + 1, :] = own_of(choices, entry(tab, slot))
     mean, rstd = keeps[0:1, :], keeps[1:2, :]
     gain, shift = gain_of(norm, entry(tab, OWN)), shift_of(norm, entry(tab, OWN))
-    ones = jnp.ones((8, x_own.shape[0] * x_own.shape[1]), BF16)
-    x_sum[...] = mm(ones, flat(x_own[...])) + mm(ones, flat(x_oth[...]))
     scale = rstd * gain
     bias = 0.5 * (shift - mean * scale)
     scale = 0.5 * scale
@@ -360,8 +373,7 @@
             return carry
 
         lax.fori_loop(0, rows // 2, put, 0, unroll=2)
-    extra = [x_sum[0:1, n * b : n * (b + 1)] for b in range(x_sum.shape[1] // n)]
-    extra += [stats_p[:, lanes] for lanes in columns(stats_p.shape[1])]
+    extra = [stats_p[:, lanes] for lanes in columns(stats_p.shape[1])]
     pair = (slice(3 * n, 6 * n), w_odd[...], (1, 0))
     conv_stats(z, xs, pair, (slice(0, 3 * n), w_even[...], 1), send, extra)
 
@@ -379,6 +391,10 @@
     spread(send, [act_sum, *(squares[:, lanes] for lanes in columns(chans))])
 
 
+def join(pieces):
+    return pieces[0] if len(pieces) == 1 else jnp.concatenate(pieces, axis=1)
+
+
 def columns(channels):
     return [slice(LANES * j, LANES * (j + 1)) for j in range(channels // LANES)]
 
@@ -421,19 +437,14 @@
     return down(lax.fori_loop(0, rows, put, zeros8(LANES), unroll=7))
 
 
-def f3(tab, got, labels, z_in, norm, w, w_p, x_sum, act, z, send, keeps, keeps_p, x_dev):
+def f3(tab, got, labels, z_in, norm, w, w_p, act, z, send, keeps, keeps_p):
     sums = activate(tab, got, labels, z_in, norm, act, keeps)
     expand(act, w, z, send, sums)
-    marks = labels[...]
-    label = entry(tab, OWN)
-    inputs, outer = x_sum.shape[1] // LANES, z.shape[2] // LANES
+    marks, label = labels[...], entry(tab, OWN)
     total = group_sum(got, marks, label)
-    images = group_count(marks, label)
-    for b in range(inputs):
-        lanes = slice(LANES * b, LANES * (b + 1))
-        x_dev[:, lanes] = x_sum[0:1, lanes] - row(total, 2 + b) / images
-    count = tiled(images, outer * LANES) * (1.0 * z.shape[0] * (COLS - 4))
-    first, second = LANES * (2 + inputs), LANES * (2 + 2 * inputs)
+    outer, first = z.shape[2], 2 * LANES
+    second = first + w_p.shape[0]
+    count = tiled(group_count(marks, label), outer) * (1.0 * z.shape[0] * (COLS - 4))
     mean, rstd = moments(through(total[:, first:second], w_p[...]), total[:, second:], count)
     keeps_p[0:1, :] = mean
     keeps_p[1:2, :] = rstd
@@ -475,6 +486,16 @@
     spread(send, [down(sums), down(squares)])
 
 
+def put_shares(xz, send, part):
+    n, devices = LANES, send.shape[0]
+    share = xz.shape[0] // devices
+    pieces = xz[...].reshape(devices, share, n)
+    first = (share + 1) // 2 * part
+    for q in range(first, (share + 1) // 2 if part == 0 else share):
+        at = n * (2 + q - first)
+        send[:, :, at : at + n] = pieces[:, q : q + 1, :]
+
+
 def f5(tab, got, labels, z_in, norm, w_two, w_last, xz, x3, z, send, keeps):
     rows = z_in.shape[0]
     pixels = 1.0 * rows * (COLS - 4)
@@ -501,11 +522,7 @@
     conv_stats(
         z, x3, (lanes, w_two[...], (0, 1)), (lanes, w_last[...], 2), send.at[:, :, 0 : 2 * n]
     )
-    devices = send.shape[0]
-    share = xz.shape[0] // devices
-    pieces = xz[...].reshape(devices, share, n)
-    for q in range(share):
-        send[:, :, n * (2 + q) : n * (3 + q)] = pieces[:, q : q + 1, :]
+    put_shares(xz, send, 0)
 
 
 def f6(tab, got, labels, z_in, norm, w, act, z, send, keeps):
@@ -543,15 +560,15 @@
     spread(send, [down(sums) * gate, down(products) * rstd * gate])
 
 
-def backward_norm(tab, got, labels, norm, keeps, pixels, grad_norm, slots=(0, 1)):
+def backward_norm(tab, got, labels, norm, keeps, pixels, grad_norm):
     marks = labels[...]
     chans = norm.shape[2]
     own_shift = jnp.zeros((1, chans), F32)
     own_gain = jnp.zeros((1, chans), F32)
     group = entry(tab, OWN)
     for g in range(norm.shape[0]):
-        total = group_sum(got, marks, float(g))
-        shift_sum, gain_sum = row(total, slots[0]), row(total, slots[1])
+        total = group_sum(got.at[:, :, 0 : 2 * LANES], marks, float(g))
+        shift_sum, gain_sum = row(total, 0), row(total, 1)
         grad_norm[g, 0:1, :] = gain_sum
         grad_norm[g, 1:2, :] = shift_sum
         mine = tiled(group, chans) == float(g)
@@ -586,7 +603,7 @@
 
 
 def b8(
-    tab, got, labels, grad_pre, z, norm, keeps, w, z_in, norm_in, keeps_in,
+    tab, got, labels, grad_pre, z, norm, keeps, w, z_in, norm_in, keeps_in, xz,
     dz, dout, send, grad_norm, d,
 ):
     rows, chans = z.shape[0], z.shape[2]
@@ -602,11 +619,12 @@
 
     lax.fori_loop(0, rows, put, 0, unroll=2)
     d[...] = mm_nt(flat(dz[...]), w[...]).reshape(d.shape)
-    slope_sums(tab, d, z_in, norm_in, keeps_in, dout, send)
+    slope_sums(tab, d, z_in, norm_in, keeps_in, dout, send.at[:, :, 0 : 2 * LANES])
+    put_shares(xz, send, 1)
 
 
 def b9(
-    tab, got, labels, dout_in, z, norm, keeps, b_two, b_last, z_in, norm_in, keeps_in,
+    tab, got, labels, dout_in, z, norm, keeps, b_two, b_last, z_in, norm_in, keeps_in, x_sum,
     dz, dout, send, grad_norm, d3, d,
 ):
     rows = z.shape[0]
@@ -634,12 +652,14 @@
         value = mm_nt(flat(d3[step * k + 2 : step * (k + 1) + 2]), b_last[...])
         value = value + both[COLS:, 0:n] + both[0 : step * COLS, n : 2 * n]
         d[step * k : step * (k + 1)] = value.reshape(step, COLS, LANES)
-    slope_sums(tab, d, z_in, norm_in, keeps_in, dout, send)
+    slope_sums(tab, d, z_in, norm_in, keeps_in, dout, send.at[:, :, 0 : 2 * n])
+    turned = join([jnp.transpose(x_sum[lanes, :])[0:1] for lanes in columns(x_sum.shape[0])])
+    spread(send.at[:, :, 2 * n :], [turned[:, lanes] for lanes in columns(x_sum.shape[0])])
 
 
 def b10(
     tab, got, labels, dout_in, z, norm, keeps, w, grad_pre, slope, zc, zp, keeps_cp,
-    dz, grad_pre_2, send, grad_norm, d,
+    dz, grad_pre_2, send, grad_norm, sums_p, d,
 ):
     rows, chans = zc.shape[0], zc.shape[2]
     pixels = 1.0 * rows * (COLS - 4)
@@ -667,34 +687,49 @@
 
     start = zeros8(chans)
     sums, prod_c, prod_p = lax.fori_loop(0, rows, sum_up, (start, start, start), unroll=2)
-    spread(send, [down(sums), down(prod_c) * rstd_c, down(prod_p) * rstd_p])
+    spread(send, [down(sums), down(prod_c) * rstd_c])
+    sums_p[0:1, :] = down(sums)
+    sums_p[1:2, :] = down(prod_p) * rstd_p
 
 
 def b11(
-    tab, got, labels, grad_pre_2, zc, zp, norm_c, norm_p, keeps_cp, w, z_in, norm_in, keeps_in,
-    dz_c, dz_p, dout, send, grad_norm_c, grad_norm_p, d,
+    tab, got, labels, grad_pre_2, zc, norm, keeps, w, z_in, norm_in, keeps_in, sums_p,
+    dz, dout, send, grad_norm, d,
 ):
-    rows, chans = zc.shape[0], zc.shape[2]
-    pixels = 1.0 * rows * (COLS - 4)
-    mean_c, a_c, b_c, c_c = backward_norm(
-        tab, got, labels, norm_c, keeps_cp.at[0:2], pixels, grad_norm_c, (0, 1)
-    )
-    mean_p, a_p, b_p, c_p = backward_norm(
-        tab, got, labels, norm_p, keeps_cp.at[2:4], pixels, grad_norm_p, (0, 2)
-    )
-    keep = valid_cols(chans)
+    pixels = 1.0 * zc.shape[0] * (COLS - 4)
+    mean, a, b, c = backward_norm(tab, got, labels, norm, keeps.at[0:2], pixels, grad_norm)
+    normed_grad(dz, grad_pre_2, zc, mean, a, b, c)
+    d[...] = mm_nt(flat(dz[...]), w[...]).reshape(d.shape)
+    slope_sums(tab, d, z_in, norm_in, keeps_in, dout, send.at[:, :, 0 : 2 * LANES])
+    products = sums_p[1:2, :]
+    spread(send.at[:, :, 2 * LANES :], [products[:, lanes] for lanes in columns(zc.shape[2])])
+
+
+def normed_grad(dz, dout, z, mean, a, b, c):
+    keep = valid_cols(z.shape[2])
 
     def put(i, carry):
-        g = grad_pre_2[i]
-        v = a_c * g + b_c * (zc[i] - mean_c) + c_c
-        dz_c[i] = jnp.where(keep, v, 0.0).astype(BF16)
-        v = a_p * g + b_p * (zp[i] - mean_p) + c_p
-        dz_p[i] = jnp.where(keep, v, 0.0).astype(BF16)
+        v = a * dout[i] + b * (z[i] - mean) + c
+        dz[i] = jnp.where(keep, v, 0.0).astype(BF16)
         return carry
 
-    lax.fori_loop(0, rows, put, 0, unroll=2)
-    d[...] = mm_nt(flat(dz_c[...]), w[...]).reshape(d.shape)
-    slope_sums(tab, d, z_in, norm_in, keeps_in, dout, send)
+    lax.fori_loop(0, z.shape[0], put, 0, unroll=2)
+
+
+def joined_norm(tab, got_c, got_p, labels, norm, keeps, pixels, grad_norm):
+    marks, group, chans = labels[...], entry(tab, OWN), norm.shape[2]
+    sums = []
+    for g in range(norm.shape[0]):
+        shift_sum = row(group_sum(got_c.at[:, :, 0:LANES], marks, float(g)), 0)
+        gain_sum = group_sum(got_p.at[:, :, 2 * LANES :], marks, float(g))
+        grad_norm[g, 0:1, :] = gain_sum
+        grad_norm[g, 1:2, :] = shift_sum
+        sums.append((gain_sum, shift_sum))
+    count = tiled(group_count(marks, group), chans) * pixels
+    own_gain, own_shift = (own_of([v[k] for v in sums], group) for k in (0, 1))
+    mean, rstd = keeps[0:1, :], keeps[1:2, :]
+    a = rstd * gain_of(norm, group)
+    return mean, a, -(a * rstd) * own_gain / count, -a * own_shift / count
 
 
 def b12(tab, got, labels, dout_in, z, norm, keeps, xs, d2, kept, sent, grad_norm, dz, packed):
@@ -856,46 +891,55 @@
 
 
 def g_most(
-    tab, act_2b, dz_2c, x3, dz_2b, joined, dz_2a, act_1b, dz_1c, xee, dz_1p, w_1p,
-    kept, sent, gs_own, gs_oth, packed,
+    tab, act_2b, dz_2c, x3, dz_2b, joined, dz_2a, act_1b, dz_1c, xee, w_p,
+    got_c, got_p, labels, norm, keeps, grad_pre_2, zp,
+    kept, sent, gs_own, gs_oth, grad_norm, packed, dz_p,
 ):
     rows = dz_2b.shape[0]
+    pixels = 1.0 * rows * (COLS - 4)
+    coefs = joined_norm(tab, got_c, got_p, labels, norm, keeps.at[2:4], pixels, grad_norm)
+    normed_grad(dz_p, grad_pre_2, zp, *coefs)
     at = put_rows(packed, 0, mm_tn(flat(act_2b[...]), flat(dz_2c[...])))
     low = flat(dz_2b[...])
     for y in range(3):
         at = put_rows(packed, at, mm_side(flat(x3[y : y + rows]), low))
     at = put_rows(packed, at, mm_side(flat(joined[...]), flat(dz_2a[...])))
     at = put_rows(packed, at, mm_tn(flat(act_1b[...]), flat(dz_1c[...])))
-    at = put_rows(packed, at, mm_tn(flat(xee[...]), flat(dz_1p[...])))
+    at = put_rows(packed, at, mm_tn(flat(xee[...]), flat(dz_p[...])))
     share_out(tab, packed, at, kept, sent)
     half = half_of(tab)
     count = gs_own.shape[0]
     for k, gs in enumerate((gs_own, gs_oth)):
         first = count * (half if k == 0 else 1 - half)
-        got = mm_nt(flat(dz_1p[pl.ds(first, count)]), w_1p[...])
+        got = mm_nt(flat(dz_p[pl.ds(first, count)]), w_p[...])
         gs[...] = got.reshape(gs.shape).astype(BF16)
 
 
-def g_xz(keeps, x_own, x_oth, z_own, z_oth, out, low):
-    rows = z_own.shape[0]
+def g_xz(keeps, x_own, x_oth, z_own, z_oth, out, x_sum, low):
+    rows, n = z_own.shape[0], LANES
     mean = keeps[0:1, :]
+    low[:, :, n : 2 * n] = jnp.ones((rows, z_own.shape[1], n), BF16)
     value = None
     for x, z in ((x_own, z_own), (x_oth, z_oth)):
 
         def put(i, carry, z=z):
-            low[i] = (z[i] - mean).astype(BF16)
+            low[i, :, 0:n] = (z[i] - mean).astype(BF16)
             return carry
 
         lax.fori_loop(0, rows, put, 0, unroll=4)
         term = mm_tn(flat(x[...]), flat(low[...]))
         value = term if value is None else value + term
     at = value.shape[0]
-    out[0:at, :] = value
+    out[0:at, :] = value[:, 0:n]
     if at < out.shape[0]:
-        out[at:, :] = jnp.zeros((out.shape[0] - at, LANES), F32)
-
-
-def g_xd(tab, sums_own, sums_oth, norm, keeps, x_dev, x_own, x_oth, dn_own, dn_oth, out, sums, low):
+        out[at:, :] = jnp.zeros((out.shape[0] - at, n), F32)
+    x_sum[...] = value[:, n : 2 * n]
+
+
+def g_xd(
+    tab, sums_own, sums_oth, norm, keeps, x_sum, got_x, labels, x_own, x_oth, dn_own, dn_oth,
+    out, sums, low,
+):
     rows = dn_own.shape[0]
     n = LANES
     pixels = 1.0 * (2 * rows) * (2 * (COLS - 4))
@@ -912,9 +956,14 @@
         lax.fori_loop(0, rows, put, 0, unroll=4)
         term = mm_tn(flat(x[...]), flat(low[...]))
         value = term if value is None else value + term
-    spread_dev = jnp.broadcast_to(x_dev[...], (8, x_dev.shape[1]))
-    column = jnp.transpose(spread_dev)[:, 0:1]
-    value = value + column * (a * local)
+    marks, label = labels[...], entry(tab, OWN)
+    total = group_sum(got_x.at[:, :, 2 * n :], marks, label)
+    total = total / tiled(group_count(marks, label), total.shape[1])
+    total = jnp.broadcast_to(total, (8, total.shape[1]))
+    means = jnp.concatenate(
+        [jnp.transpose(total[:, lanes])[:, 0:1] for lanes in columns(total.shape[1])], axis=0
+    )
+    value = value + (x_sum[...] - means) * (a * local)
     at = value.shape[0]
     out[0:at, :] = value.astype(BF16)
     if at < out.shape[0]:
@@ -947,10 +996,11 @@
     return out
 
 
-def add_all(got, labels, norm, keeps_all, xz_got, out, *, at, pixels):
+def add_all(got, labels, norm, keeps_all, got_a, got_b, out, *, at, pixels):
     devices, n = got.shape[0], LANES
     half = devices // 2
-    share = xz_got.shape[2] // n - 2
+    split = got_a.shape[2] // n - 2
+    share = split + got_b.shape[2] // n - 2
     piece = out.shape[1] - share
     marks = labels[...]
     value = jnp.sum(got[:, piece : piece + share, :].astype(F32), axis=0)
@@ -961,7 +1011,9 @@
         b = -(rstd * rstd * norm[g, 0:1, :]) * sums[g][1] / count
         same = (marks == float(g)).astype(F32)
         rows = [
-            jnp.sum(xz_got[:, :, n * (2 + q) : n * (3 + q)] * same, axis=0) for q in range(share)
+            jnp.sum(source[:, :, n * (2 + q) : n * (3 + q)] * same, axis=0)
+            for source, count_q in ((got_a, split), (got_b, share - split))
+            for q in range(count_q)
         ]
         value = value + jnp.concatenate(rows, axis=0) * b
     for k in (0, 1):
@@ -972,33 +1024,47 @@
 
 def unpack(
     tab, own, other, o_1a, o_1b, o_2c, o_2b, o_2a, o_1c, o_1p,
-    w_1a, w_1b, w_2c, w_2b, w_2a, w_1c, w_1p, tall, packed, packed_1b, sems,
+    w_1a, w_1b, w_2c, w_2b, w_2a, w_1c, w_1p, tall, sems, *, first, second, piece,
 ):
     half = half_of(tab)
-    piece = packed.shape[1]
-    first, second = packed.shape[0] // 2, packed_1b.shape[0] // 2
-    for part, place in ((own, half), (other, 1 - half)):
-        packed[pl.ds(first * place, first)] = part[0:first, 0:piece, :]
-        packed_1b[pl.ds(second * place, second)] = part[first : first + second, 0:piece, :]
-    flat_1b, rest = flat(packed_1b[...]), flat(packed[...])
     copies = []
 
     def leave(value, out):
         copies.append(pltpu.make_async_copy(value, out, sems.at[len(copies)]))
-        copies[-1].start()
-
-    def source(at, rows):
-        return rest[at : at + rows].astype(F32)
-
-    at = 0
-    for value, out in ((w_2c, o_2c), (w_2b, o_2b), (w_2a, o_2a), (w_1c, o_1c), (w_1p, o_1p)):
-        at = take_rows(source, at, value)
-        leave(value, out)
-    w_1b[...] = flat_1b[0 : w_1b.shape[0]].astype(F32)
-    leave(w_1b, o_1b)
+        return copies[-1]
+
+    weights = ((w_2c, o_2c), (w_2b, o_2b), (w_2a, o_2a), (w_1c, o_1c), (w_1p, o_1p))
+    leaving = [leave(*v) for v in (*weights, (w_1b, o_1b), (w_1a, o_1a))]
+    for place in (0, 1):
+
+        @pl.when(half == place)
+        def _():
+            halves = (own, other) if place == 0 else (other, own)
+            most = [flat(v[0:first, 0:piece, :]) for v in halves]
+            last = [flat(v[first : first + second, 0:piece, :]) for v in halves]
+            size = first * piece
+
+            def source(at, rows):
+                pieces = []
+                if at < size:
+                    pieces.append(most[0][at : min(at + rows, size)])
+                if at + rows > size:
+                    pieces.append(most[1][max(at - size, 0) : at + rows - size])
+                pieces = [v.astype(F32) for v in pieces]
+                return pieces[0] if len(pieces) == 1 else jnp.concatenate(pieces, axis=0)
+
+            at = 0
+            for k, (value, _) in enumerate(weights):
+                at = take_rows(source, at, value)
+                leaving[k].start()
+            size = second * piece
+            w_1b[0:size] = last[0].astype(F32)
+            w_1b[size:] = last[1][0 : w_1b.shape[0] - size].astype(F32)
+            leaving[5].start()
+
     tall[...] = own[:, piece:, :].astype(F32).reshape(tall.shape)
     w_1a[...] = tall[0 : w_1a.shape[0], :]
-    leave(w_1a, o_1a)
+    leaving[6].start()
     for copy in copies:
         copy.wait()
 
@@ -1052,7 +1118,8 @@
     tab, x_own, x_for, z_own, z_for, s1 = stage(
         f1, [((8, n), F32), wide_in, wide_in, wide_z, wide_z, send(5)],
         [*(pltpu.SMEM(v.shape, jnp.int32) for v in (half, group, width, gate)),
-         pltpu.VMEM(raw, BF16), pltpu.VMEM(w_1a.shape, BF16), pltpu.SemaphoreType.DMA((7,))],
+         pltpu.VMEM(raw, BF16), pltpu.VMEM(w_1a.shape, BF16), pltpu.VMEM((8, n), F32),
+         pltpu.SemaphoreType.DMA((7,))],
         hbm=(0, 1, 2, 3, 4, 5),
     )(half, group, width, gate, images, w_1a)
     s1, v_1b, v_2b = tie(s1, w_1b, w_2b)
@@ -1072,17 +1139,15 @@
         [maps(inputs, BF16), maps(outer), ((1, inputs + outer), F32)],
         [pltpu.VMEM((inputs // n, cols_in, n), F32)],
     )(tab, x_own, x_oth, w_1p)
-    xs, z_1b, s2, labels, k_1a, k_all, z_oth, x_sum = stage(
+    xs, z_1b, s2, labels, k_1a, k_all, z_oth = stage(
         f2,
-        [((rows + 1, COLS, 6 * n), BF16), maps(n), send(2 + (2 * inputs + outer) // n),
-         ((m, 1, n), F32), mean_scale(n, 2), mean_scale(n, norm_1a.shape[0]), wide_z,
-         ((8, inputs), F32)],
-    )(tab, g1, z_own, x_own, x_oth, w_1a, norm_1a, w_even, w_odd, stats_1p)
+        [((rows + 1, COLS, 6 * n), BF16), maps(n), send(2 + (inputs + outer) // n),
+         ((m, 1, n), F32), mean_scale(n, 2), mean_scale(n, norm_1a.shape[0]), wide_z],
+    )(tab, g1, z_own, x_oth, w_1a, norm_1a, w_even, w_odd, stats_1p)
     g2 = gather(s2)
-    act_1b, z_1c, s3, k_1b, k_p, x_dev = stage(
-        f3, [maps(n, BF16), maps(outer), send(1 + outer // n), mean_scale(n), mean_scale(outer),
-             ((1, inputs), F32)],
-    )(tab, g2, labels, z_1b, norm_1b, w_1c, w_1p, x_sum)
+    act_1b, z_1c, s3, k_1b, k_p = stage(
+        f3, [maps(n, BF16), maps(outer), send(1 + outer // n), mean_scale(n), mean_scale(outer)]
+    )(tab, g2, labels, z_1b, norm_1b, w_1c, w_1p)
     g3 = gather(s3)
     joined, slope, z_2a, s4, k_cp = stage(
         f4, [maps(outer, BF16), maps(outer), maps(n), send(2), mean_scale(outer, 2)]
@@ -1090,13 +1155,14 @@
     share = -(-inputs // devices)
     half_in = ((rows, cols_in, n), BF16)
     s4, k_1a = tie(s4, k_1a)
-    (xz,) = stage(g_xz, [((devices * share, n), F32)], [pltpu.VMEM(half_in[0], BF16)])(
-        k_1a, x_own, x_oth, z_own, z_oth
-    )
-    s4, xz = tie(s4, xz)
+    xz, x_sum = stage(
+        g_xz, [((devices * share, n), F32), ((inputs, n), F32)],
+        [pltpu.VMEM((rows, cols_in, 2 * n), BF16)],
+    )(k_1a, x_own, x_oth, z_own, z_oth)
+    s4, xz, x_sum = tie(s4, xz, x_sum)
     g4 = gather(s4)
     x3, z_2b, s5, k_2a = stage(
-        f5, [((rows + 2, COLS, 3 * n), BF16), maps(n), send(2 + share), mean_scale(n)]
+        f5, [((rows + 2, COLS, 3 * n), BF16), maps(n), send(2 + (share + 1) // 2), mean_scale(n)]
     )(tab, g4, labels, z_2a, norm_2a, w_two, w_last, xz)
     g5 = gather(s5)
     act_2b, z_2c, s6, k_2b = stage(
@@ -1109,22 +1175,24 @@
     )(tab, g6, labels, joined, z_2c, norm_2c, w_2c, cotangent[0])
     g7 = gather(s7)
     dz_2c, dout_2b, s8, grad_norm_2c = stage(
-        b8, [maps(outer, BF16), maps(n), send(2), *params(norm_2c)], [scratch(n)]
-    )(tab, g7, labels, grad_pre, z_2c, norm_2c, k_2c, w_2c, z_2b, norm_2b, k_2b)
+        b8, [maps(outer, BF16), maps(n), send(2 + share // 2), *params(norm_2c)], [scratch(n)]
+    )(tab, g7, labels, grad_pre, z_2c, norm_2c, k_2c, w_2c, z_2b, norm_2b, k_2b, xz)
     g8 = gather(s8)
     dz_2b, dout_2a, s9, grad_norm_2b = stage(
-        b9, [maps(n, BF16), maps(n), send(2), *params(norm_2b)],
+        b9, [maps(n, BF16), maps(n), send(2 + inputs // n), *params(norm_2b)],
         [pltpu.VMEM((rows + 2, COLS, 3 * n), BF16), scratch(n)],
-    )(tab, g8, labels, dout_2b, z_2b, norm_2b, k_2b, b_two, b_last, z_2a, norm_2a, k_2a)
+    )(tab, g8, labels, dout_2b, z_2b, norm_2b, k_2b, b_two, b_last, z_2a, norm_2a, k_2a, x_sum)
     g9 = gather(s9)
-    dz_2a, grad_pre_2, s10, grad_norm_2a = stage(
-        b10, [maps(n, BF16), maps(outer), send(3, outer), *params(norm_2a)], [scratch(outer)]
+    dz_2a, grad_pre_2, s10, grad_norm_2a, sums_p = stage(
+        b10,
+        [maps(n, BF16), maps(outer), send(2, outer), *params(norm_2a), mean_scale(outer)],
+        [scratch(outer)],
     )(tab, g9, labels, dout_2a, z_2a, norm_2a, k_2a, w_2a, grad_pre, slope, z_1c, z_1p, k_cp)
     g10 = gather(s10)
-    dz_1c, dz_1p, dout_1b, s11, grad_norm_1c, grad_norm_1p = stage(
-        b11, [maps(outer, BF16), maps(outer, BF16), maps(n), send(2), *params(norm_1c, norm_1p)],
-        [scratch(n)],
-    )(tab, g10, labels, grad_pre_2, z_1c, z_1p, norm_1c, norm_1p, k_cp, w_1c, z_1b, norm_1b, k_1b)
+    dz_1c, dout_1b, s11, grad_norm_1c = stage(
+        b11, [maps(outer, BF16), maps(n), send(2 + outer // n), *params(norm_1c)], [scratch(n)]
+    )(tab, g10, labels, grad_pre_2, z_1c, norm_1c, k_cp, w_1c, z_1b, norm_1b, k_1b, sums_p)
+    g11 = gather(s11)
     half_map = ((rows // 2, COLS, inputs), BF16)
     most_rows = sum(v.size for v in (w_2c, w_2b, w_2a, w_1c, w_1p)) // n
     rows_1b = w_1b.size // n
@@ -1133,12 +1201,13 @@
         piece += 16
     first, second = -(-most_rows // (2 * piece)), -(-rows_1b // (2 * piece))
     part, part_1b = ((first, piece, n), BF16), ((second, piece, n), BF16)
-    kept, sent, gs_own, gs_send = stage(
-        g_most, [part, part, half_map, half_map], [pltpu.VMEM((2 * first * piece, n), BF16)]
-    )(tab, act_2b, dz_2c, x3, dz_2b, joined, dz_2a, act_1b, dz_1c, xee, dz_1p, w_1p)
-    s11, sent, gs_send = tie(s11, sent, gs_send)
-    g11, sent, gs_send = tie(gather(s11), sent, gs_send)
+    kept, sent, gs_own, gs_send, grad_norm_1p = stage(
+        g_most, [part, part, half_map, half_map, *params(norm_1p)],
+        [pltpu.VMEM((2 * first * piece, n), BF16), scratch(outer, BF16)],
+    )(tab, act_2b, dz_2c, x3, dz_2b, joined, dz_2a, act_1b, dz_1c, xee, w_1p,
+      g10, g11, labels, norm_1p, k_cp, grad_pre_2, z_1p)
     got, gs_for = swap(sent), swap(gs_send)
+    g11, _ = tie(g11, sent)
     d2, kept_1b, sent_1b, grad_norm_1b = stage(
         b12, [((rows + 1, COLS, 2 * n), BF16), part_1b, part_1b, *params(norm_1b)],
         [scratch(n, BF16), pltpu.VMEM((2 * second * piece, n), BF16)],
@@ -1161,7 +1230,7 @@
     high = -(-(stats_at + 4) // 16) * 16
     tall, sums_1a = stage(
         g_xd, [((devices * share, n), BF16), ((2, n), F32)], [pltpu.VMEM(half_in[0], BF16)]
-    )(tab, sums_own, sums_send, norm_1a, k_1a, x_dev, x_own, x_oth, dn_own, dn_send)
+    )(tab, sums_own, sums_send, norm_1a, k_1a, x_sum, g9, labels, x_own, x_oth, dn_own, dn_send)
     tall, gs_for, dn_for = tie(tall, gs_for, dn_for)
     (s12,) = stage(
         functools.partial(pack_last, stats_at=stats_at), [((devices, high, n), BF16)]
@@ -1171,7 +1240,7 @@
     (mine,) = stage(
         functools.partial(add_all, at=stats_at, pixels=pixels),
         [((devices, piece + share, n), BF16)],
-    )(g12, labels, norm_1a, k_all, g5)
+    )(g12, labels, norm_1a, k_all, g5, g8)
     finished = (
         result, grad_norm_1b, grad_norm_1c, grad_norm_1p, grad_norm_2a, grad_norm_2b, grad_norm_2c
     )
@@ -1188,10 +1257,10 @@
     whole = gather(mine)
     weights = (w_1a, w_1b.reshape(-1, n), w_2c, w_2b.reshape(-1, n), w_2a, w_1c, w_1p)
     totals = stage(
-        unpack, [(v.shape, F32) for v in weights],
+        functools.partial(unpack, first=first, second=second, piece=piece),
+        [(v.shape, F32) for v in weights],
         [*(pltpu.VMEM(v.shape, F32) for v in weights),
-         pltpu.VMEM((devices * share, n), F32), pltpu.VMEM((2 * first, piece, n), BF16),
-         pltpu.VMEM((2 * second, piece, n), BF16), pltpu.SemaphoreType.DMA((7,))],
+         pltpu.VMEM((devices * share, n), F32), pltpu.SemaphoreType.DMA((7,))],
         hbm_out=range(7),
     )(tab, whole, swap(whole))
     t_1a, t_1b, t_2c, t_2b, t_2a, t_1c, t_1p = totals

time: 191 us -> 188 us (0.984)
  blocking collectives: 158 us -> 155 us
    all_to_all x13, blocking collectives: 158 us -> 155 us  [gather(): return lax.all_to_all(send, AXES, 0, 0)]
  transfers between devices with their start and end apart: 6 -> 6, of which waited for: 0 -> 0; matrix products, arithmetic and copies ran while one was open for 0% -> 0% of each run, Pallas kernels for 3% -> 4%
where the time goes in v4:
time: 188 us; the launch traced here: 187 us
  blocking collectives  155 us (82%)
  Pallas kernels  29.1 us (15%)
    all_to_all x13, blocking collectives, gather(): return lax.all_to_all(send, AXES, 0, 0)  155 us
    pallas_call x23, Pallas kernels, call(): pl.pallas_call(kernel, out_shape=tuple((jax.ShapeDtypeStruct(s, d) for s,...  29.1 us
  transfers between devices with their start and end apart: 6, of which 0 were waited for; matrix products, arithmetic and copies ran while one was open for 0% of the time, Pallas kernels for 4%

profile of v4, /device:TPU:0, one launch (start us, length us, event | category | flops | bytes accessed | tf_op | source)
XLA Modules:
  0.0 187.3 jit_solution(3007715539771660709)
XLA Ops:
  0.7 2.3 %f1.1 = (f32[8,128]{1,0:T(8,128)S(1)}, bf16[28,64,256]{2,1,0:T(8,128)(2,1)S(1)}, bf16[28,64,256]{2,1,0:T(8,128)(2,1)S(1)}, f32[28,64,128]{2,1,0:T(8,128)S(1)}, f...) custom-call(s32[1]{0:T(128)} %bitcast.half_at, s32[2]{0:T(128)} %group_at.1, s32[3]{0:T(128)} %width_at.1, s32[3]{0:T(128)} %gate_at.1, ...), custom_call_target="tpu_custom_call" | custom-call | tf_op jit(solution)/shard_map/f1/pallas_call | solution.py:32
  3.8 14.2 %all_to_all.65.got = f32[32,1,640]{2,1,0:T(1,128)S(1)} all-to-all(f32[32,1,640]{2,1,0:T(1,128)S(1)} %get-tuple-element.151), channel_id=1, replica_groups=mesh['rows'=2,'batch'=16] {'rows','batch'}, dimensions={0} | all-to-all | bytes 163840 | tf_op jit(solution)/shard_map/all_to_all | solution.py:1073
  18.0 0.9 f1_strided.1
  19.0 1.9 f2.1
  20.8 9.6 %all_to_all.66.got = f32[32,1,1024]{2,1,0:T(1,128)S(1)} all-to-all(f32[32,1,1024]{2,1,0:T(1,128)S(1)} %get-tuple-element.160), channel_id=1, replica_groups=mesh['rows'=2,'batch'=16] {'rows','batch'}, dimensions={0} | all-to-all | bytes 262144 | tf_op jit(solution)/shard_map/all_to_all | solution.py:1073
  30.5 0.7 f3.1
  31.1 9.4 %all_to_all.67.got = f32[32,1,640]{2,1,0:T(1,128)S(1)} all-to-all(f32[32,1,640]{2,1,0:T(1,128)S(1)} %get-tuple-element.163), channel_id=1, replica_groups=mesh['rows'=2,'batch'=16] {'rows','batch'}, dimensions={0} | all-to-all | bytes 163840 | tf_op jit(solution)/shard_map/all_to_all | solution.py:1073
  40.5 1.4 f4.1
  42.0 1.1 g_xz.1
  43.1 9.0 %all_to_all.68.got = f32[32,1,256]{2,1,0:T(1,128)S(1)} all-to-all(f32[32,1,256]{2,1,0:T(1,128)S(1)} %get-tuple-element.174), channel_id=1, replica_groups=mesh['rows'=2,'batch'=16] {'rows','batch'}, dimensions={0} | all-to-all | bytes 65536 | tf_op jit(solution)/shard_map/all_to_all | solution.py:1073
  52.1 1.1 f5.1
  53.2 9.4 %all_to_all.69.got.got_a = f32[32,1,768]{2,1,0:T(1,128)S(1)} all-to-all(f32[32,1,768]{2,1,0:T(1,128)S(1)} %get-tuple-element.179), channel_id=1, replica_groups=mesh['rows'=2,'batch'=16] {'rows','batch'}, dimensions={0} | all-to-all | bytes 196608 | tf_op jit(solution)/shard_map/all_to_all | solution.py:1073
  63.2 9.2 %all_to_all.70.got = f32[32,1,640]{2,1,0:T(1,128)S(1)} all-to-all(f32[32,1,640]{2,1,0:T(1,128)S(1)} %get-tuple-element.181), channel_id=1, replica_groups=mesh['rows'=2,'batch'=16] {'rows','batch'}, dimensions={0} | all-to-all | bytes 163840 | tf_op jit(solution)/shard_map/all_to_all | solution.py:1073
  72.4 1.8 b7.1
  74.2 9.6 %all_to_all.71.got = f32[32,4,256]{2,1,0:T(4,128)S(1)} all-to-all(f32[32,4,256]{2,1,0:T(4,128)S(1)} %get-tuple-element.184), channel_id=1, replica_groups=mesh['rows'=2,'batch'=16] {'rows','batch'}, dimensions={0} | all-to-all | bytes 262144 | tf_op jit(solution)/shard_map/all_to_all | solution.py:1073
  83.8 1.4 b8.1
  85.2 9.6 %all_to_all.72.got.got_b = f32[32,1,768]{2,1,0:T(1,128)S(1)} all-to-all(f32[32,1,768]{2,1,0:T(1,128)S(1)} %get-tuple-element.188), channel_id=1, replica_groups=mesh['rows'=2,'batch'=16] {'rows','batch'}, dimensions={0} | all-to-all | bytes 196608 | tf_op jit(solution)/shard_map/all_to_all | solution.py:1073
  94.8 1.5 b9.1
  96.2 9.0 %all_to_all.73.got.got_x = f32[32,1,512]{2,1,0:T(1,128)S(1)} all-to-all(f32[32,1,512]{2,1,0:T(1,128)S(1)} %get-tuple-element.194), channel_id=1, replica_groups=mesh['rows'=2,'batch'=16] {'rows','batch'}, dimensions={0} | all-to-all | bytes 131072 | tf_op jit(solution)/shard_map/all_to_all | solution.py:1073
  105.3 1.6 b10.1
  106.9 9.6 %all_to_all.74.got.got_c = f32[32,4,256]{2,1,0:T(4,128)S(1)} all-to-all(f32[32,4,256]{2,1,0:T(4,128)S(1)} %get-tuple-element.198), channel_id=1, replica_groups=mesh['rows'=2,'batch'=16] {'rows','batch'}, dimensions={0} | all-to-all | bytes 262144 | tf_op jit(solution)/shard_map/all_to_all | solution.py:1073
  116.5 1.3 b11.1
  117.9 9.6 %all_to_all.75.got_p.got = f32[32,1,768]{2,1,0:T(1,128)S(1)} all-to-all(f32[32,1,768]{2,1,0:T(1,128)S(1)} %get-tuple-element.202), channel_id=1, replica_groups=mesh['rows'=2,'batch'=16] {'rows','batch'}, dimensions={0} | all-to-all | bytes 196608 | tf_op jit(solution)/shard_map/all_to_all | solution.py:1073
  127.5 2.3 %g_most.1 = (bf16[24,80,128]{2,1,0:T(8,128)(2,1)S(1)}, bf16[24,80,128]{2,1,0:T(8,128)(2,1)S(1)}, bf16[14,32,256]{2,1,0:T(8,128)(2,1)S(1)}, bf16[14,32,256]{2,1,0:T(8,128)(2,1)S(1)}, f32[3,2,512]{2,1,0:T(2,128)S(1)}) custom-call(f32[8,128]{1,0:T(8,128)S(1)} %get-tuple-element.137.tab, bf16[28,32,128]{2,1,0:T(8,128)(2,1)S(1)} %get-tuple-element.203.act_2b, ...), custom_call_target="tpu_custom_call" | custom-call | tf_op jit(solution)/shard_map/g_most/pallas_call | solution.py:32
  129.9 1.0 b12.1
  130.8 1.1 b12_images.2
  133.0 1.1 b12_images.3
  134.1 1.1 g_xd.1
  135.4 24.2 %all_to_all.76.got = bf16[32,96,128]{2,1,0:T(8,128)(2,1)S(1)} all-to-all(bf16[32,96,128]{2,1,0:T(8,128)(2,1)S(1)} %pack_last.1), channel_id=1, replica_groups=mesh['rows'=2,'batch'=16] {'rows','batch'}, dimensions={0} | all-to-all | bytes 1572864 | tf_op jit(solution)/shard_map/all_to_all | solution.py:1073
  160.2 22.8 %all_to_all.77.own = bf16[32,88,128]{2,1,0:T(8,128)(2,1)S(1)} all-to-all(bf16[32,88,128]{2,1,0:T(8,128)(2,1)S(1)} %add_all.1), channel_id=1, replica_groups=mesh['rows'=2,'batch'=16] {'rows','batch'}, dimensions={0} | all-to-all | bytes 1441792 | tf_op jit(solution)/shard_map/all_to_all | solution.py:1073
  183.0 2.4 %b13.1 = (bf16[28,28,512]{2,1,0:T(8,128)(2,1)}, f32[3,2,128]{2,1,0:T(2,128)}, f32[3,2,512]{2,1,0:T(2,128)}, f32[3,2,512]{2,1,0:T(2,128)}, f32[3,2,128]{2,1,0:T(2...) custom-call(f32[8,128]{1,0:T(8,128)S(1)} %get-tuple-element.137.tab,, ...), custom_call_target="tpu_custom_call" | custom-call | tf_op jit(solution)/shard_map/b13/pallas_call | solution.py:32
  185.4 1.7 unpack.1
  (46 shorter events, 3.4 us)
Async XLA Ops:
  0.6 2.4 %copy-start.7 = (bf16[3,3,128,128]{3,2,1,0:T(8,128)(2,1)S(1)}, bf16[3,3,128,128]{3,2,1,0:T(8,128)(2,1)}, u32[]{:S(2)}) copy-start(bf16[3,3,128,128]{3,2,1,0:T(8,128)(2,1)} %w2b) | copy-start | bytes 884740
  0.7 2.4 %copy-start.6 = (bf16[3,3,128,128]{3,2,1,0:T(8,128)(2,1)S(1)}, bf16[3,3,128,128]{3,2,1,0:T(8,128)(2,1)}, u32[]{:S(2)}) copy-start(bf16[3,3,128,128]{3,2,1,0:T(8,128)(2,1)} %w1b) | copy-start | bytes 884740
  0.7 17.4 %copy-start = (bf16[256,512]{1,0:T(8,128)(2,1)S(1)}, bf16[256,512]{1,0:T(8,128)(2,1)}, u32[]{:S(2)}) copy-start(bf16[256,512]{1,0:T(8,128)(2,1)} %w_p.3) | copy-start | bytes 786436
  3.0 15.9 %copy-start.4 = (bf16[256,128]{1,0:T(8,128)(2,1)S(1)}, bf16[256,128]{1,0:T(8,128)(2,1)}, u32[]{:S(2)}) copy-start(bf16[256,128]{1,0:T(8,128)(2,1)} %w.19) | copy-start | bytes 196612
  3.0 15.9 %copy-start.8 = (f32[2,3,128]{2,0,1:T(2,128)S(1)}, f32[2,3,128]{2,0,1:T(2,128)}, u32[]{:S(2)}) copy-start(f32[2,3,128]{2,0,1:T(2,128)} %param.27) | copy-start | bytes 9220
  3.3 14.8 %collective-permute-start = (bf16[28,64,256]{2,1,0:T(8,128)(2,1)S(1)}, bf16[28,64,256]{2,1,0:T(8,128)(2,1)S(1)}, u32[]{:S(2)}, u32[]{:S(2)}) collective-permute-start(bf16[28,64,256]{2,1,0:T(8,128)(2,1)S(1)} %get-tuple-element.152), channel_id=1, source_target_pairs={{0,16},{16,0},{1,17},{17,1},{2,18},{18,2},{3,19},{19,3},{4,20},{20... | collective-permute-start | bytes 2752520 | tf_op jit(solution)/shard_map/ppermute | solution.py:1081
  18.0 12.4 %copy-start.1 = (bf16[128,512]{1,0:T(8,128)(2,1)S(1)}, bf16[128,512]{1,0:T(8,128)(2,1)}, u32[]{:S(2)}) copy-start(bf16[128,512]{1,0:T(8,128)(2,1)} %w.18) | copy-start | bytes 393220
  18.0 12.4 %copy-start.12 = (f32[2,3,128]{2,0,1:T(2,128)S(1)}, f32[2,3,128]{2,0,1:T(2,128)}, u32[]{:S(2)}) copy-start(f32[2,3,128]{2,0,1:T(2,128)} %param.28) | copy-start | bytes 9220
  18.9 21.6 %copy-start.5 = (bf16[512,128]{1,0:T(8,128)(2,1)S(1)}, bf16[512,128]{1,0:T(8,128)(2,1)}, u32[]{:S(2)}) copy-start(bf16[512,128]{1,0:T(8,128)(2,1)} %w.17) | copy-start | bytes 393220
  18.9 21.6 %copy-start.10 = (f32[2,3,512]{2,0,1:T(2,128)S(1)}, f32[2,3,512]{2,0,1:T(2,128)}, u32[]{:S(2)}) copy-start(f32[2,3,512]{2,0,1:T(2,128)} %param.30) | copy-start | bytes 36868
  19.0 21.6 %copy-start.11 = (f32[2,3,512]{2,0,1:T(2,128)S(1)}, f32[2,3,512]{2,0,1:T(2,128)}, u32[]{:S(2)}) copy-start(f32[2,3,512]{2,0,1:T(2,128)} %param.29) | copy-start | bytes 36868
  42.0 10.2 %copy-start.14 = (f32[2,3,128]{2,0,1:T(2,128)S(1)}, f32[2,3,128]{2,0,1:T(2,128)}, u32[]{:S(2)}) copy-start(f32[2,3,128]{2,0,1:T(2,128)} %param.31) | copy-start | bytes 9220
  42.0 20.6 %copy-start.2 = (bf16[128,512]{1,0:T(8,128)(2,1)S(1)}, bf16[128,512]{1,0:T(8,128)(2,1)}, u32[]{:S(2)}) copy-start(bf16[128,512]{1,0:T(8,128)(2,1)} %w.16) | copy-start | bytes 393220
  42.0 20.6 %copy-start.13 = (f32[2,3,128]{2,0,1:T(2,128)S(1)}, f32[2,3,128]{2,0,1:T(2,128)}, u32[]{:S(2)}) copy-start(f32[2,3,128]{2,0,1:T(2,128)} %param.32) | copy-start | bytes 9220
  43.1 29.4 %copy-start.3 = (bf16[1,28,28,512]{3,2,1,0:T(8,128)(2,1)S(1)}, bf16[1,28,28,512]{3,2,1,0:T(8,128)(2,1)}, u32[]{:S(2)}) copy-start(bf16[1,28,28,512]{3,2,1,0:T(8,128)(2,1)} %param.34) | copy-start | bytes 2408452
  43.1 29.3 %copy-start.9 = (f32[2,3,512]{2,0,1:T(2,128)S(1)}, f32[2,3,512]{2,0,1:T(2,128)}, u32[]{:S(2)}) copy-start(f32[2,3,512]{2,0,1:T(2,128)} %param.33) | copy-start | bytes 36868
  129.8 5.5 %collective-permute-start.3 = (bf16[24,80,128]{2,1,0:T(8,128)(2,1)S(1)}, bf16[24,80,128]{2,1,0:T(8,128)(2,1)S(1)}, u32[]{:S(2)}, u32[]{:S(2)}) collective-permute-start(bf16[24,80,128]{2,1,0:T(8,128)(2,1)S(1)} %get-tuple-element.211), channel_id=1, source_target_pairs={{0,16},{16,0},{1,17},{17,1},{2,18},{18,2},{3,19},{19,3},{4,20},{20... | collective-permute-start | bytes 1474568 | tf_op jit(solution)/shard_map/ppermute | solution.py:1081
  131.9 3.3 %collective-permute-start.2 = (bf16[28,64,128]{2,1,0:T(8,128)(2,1)S(1)}, bf16[28,64,128]{2,1,0:T(8,128)(2,1)S(1)}, u32[]{:S(2)}, u32[]{:S(2)}) collective-permute-start(bf16[28,64,128]{2,1,0:T(8,128)(2,1)S(1)} %get-tuple-element.218.dn_oth), channel_id=1, source_target_pairs={{0,16},{16,0},{1,17},{17,1},{2,18},{18,2},{3,19},{19,3},{4,20},{20... | collective-permute-start | bytes 1376264 | tf_op jit(solution)/shard_map/ppermute | solution.py:1081
  132.5 2.7 %collective-permute-start.1 = (bf16[14,32,256]{2,1,0:T(8,128)(2,1)S(1)}, bf16[14,32,256]{2,1,0:T(8,128)(2,1)S(1)}, u32[]{:S(2)}, u32[]{:S(2)}) collective-permute-start(bf16[14,32,256]{2,1,0:T(8,128)(2,1)S(1)} %get-tuple-element.224), channel_id=1, source_target_pairs={{0,16},{16,0},{1,17},{17,1},{2,18},{18,2},{3,19},{19,3},{4,20},{20... | collective-permute-start | bytes 688136 | tf_op jit(solution)/shard_map/ppermute | solution.py:1081
  132.6 2.7 %collective-permute-start.4 = (bf16[8,80,128]{2,1,0:T(8,128)(2,1)S(1)}, bf16[8,80,128]{2,1,0:T(8,128)(2,1)S(1)}, u32[]{:S(2)}, u32[]{:S(2)}) collective-permute-start(bf16[8,80,128]{2,1,0:T(8,128)(2,1)S(1)} %get-tuple-element.229), channel_id=1, source_target_pairs={{0,16},{16,0},{1,17},{17,1},{2,18},{18,2},{3,19},{19,3},{4,20},{20... | collective-permute-start | bytes 491528 | tf_op jit(solution)/shard_map/ppermute | solution.py:1081
  183.0 2.4 %collective-permute-start.5 = (bf16[32,88,128]{2,1,0:T(8,128)(2,1)S(1)}, bf16[32,88,128]{2,1,0:T(8,128)(2,1)S(1)}, u32[]{:S(2)}, u32[]{:S(2)}) collective-permute-start(bf16[32,88,128]{2,1,0:T(8,128)(2,1)S(1)} %all_to_all.77.own), channel_id=1, source_target_pairs={{0,16},{16,0},{1,17},{17,1},{2,18},{18,2},{3,19},{19,3},{4,20},{20... | collective-permute-start | bytes 2162696 | tf_op jit(solution)/shard_map/ppermute | solution.py:1081

commit v5 on v4

--- a/solution.py
+++ b/solution.py
@@ -409,6 +409,111 @@
     return down(mm(jnp.concatenate(lines, axis=0).astype(BF16), w))
 
 
+def through_nt(sums, w):
+    high = sums.astype(BF16)
+    rest = sums - high.astype(F32)
+    mid = rest.astype(BF16)
+    low = (rest - mid.astype(F32)).astype(BF16)
+    lines = [v.astype(F32) for v in (high, mid, low)]
+    lines.append(jnp.zeros((5, sums.shape[1]), F32))
+    return down(mm_nt(jnp.concatenate(lines, axis=0).astype(BF16), w))
+
+
+def put_split(send, at, values):
+    rows = values.shape[0]
+    high = values.astype(BF16)
+    rest = (values - high.astype(F32)).astype(BF16)
+    for k, part in enumerate((high, rest)):
+        send[:, at + rows * k : at + rows * (k + 1), :] = jnp.broadcast_to(
+            part[None], (send.shape[0], rows, LANES)
+        )
+
+
+def get_split(got, at, rows):
+    return got[:, at : at + rows, :].astype(F32) + got[:, at + rows : at + 2 * rows, :].astype(F32)
+
+
+def over_group(values, marks, label):
+    return jnp.sum(values * (marks == label).astype(F32), axis=0)
+
+
+def stack(rows):
+    return jnp.concatenate(rows, axis=0)
+
+
+def pair_products(tab, z, norm, keeps, act, act_sum, slope, both, centred):
+    rows = z.shape[0]
+    label = entry(tab, OWN)
+    mean, rstd = keeps[0:1, :], keeps[1:2, :]
+    scale = rstd * gain_of(norm, label)
+    bias = 0.5 * (shift_of(norm, label) - mean * scale)
+    scale = 0.5 * scale
+    keep = valid_cols(LANES) & chan_mask(tab)
+    middle = act_sum * (1.0 / (rows * (COLS - 4)))
+
+    def put(i, carry):
+        zz = z[i]
+        s = jnp.where(keep, slope_of_half(zz * scale + bias), 0.0)
+        sx = s * ((zz - mean) * rstd)
+        slope[i] = s
+        both[i, :, 0:LANES] = s.astype(BF16)
+        both[i, :, LANES:] = sx.astype(BF16)
+        centred[i] = (act[i].astype(F32) - middle).astype(BF16)
+        return carry[0] + fold(s), carry[1] + fold(sx)
+
+    sums = lax.fori_loop(0, rows, put, (zeros8(LANES), zeros8(LANES)), unroll=4)
+    return mm_tn(flat(centred[...]), flat(both[...])), stack([down(v) for v in sums])
+
+
+def put_pair(send, at, share, product, sums):
+    devices, n = send.shape[0], LANES
+    missing = devices * share - n
+    for h in (0, 1):
+        values = product[:, n * h : n * (h + 1)]
+        if missing:
+            values = stack([values, jnp.zeros((missing, n), F32)])
+        first = at + share * h
+        send[:, first : first + share, :] = values.reshape(devices, share, n).astype(BF16)
+    put_split(send, at + 2 * share, sums)
+
+
+def pass_pair(send, at, got, got_at, share, marks, groups):
+    rows = got[:, got_at : got_at + 2 * share, :].astype(F32)
+    out = None
+    for g in range(groups):
+        same = (marks == float(g)).astype(F32)
+        term = jnp.sum(rows * same, axis=0)[None] * same
+        out = term if out is None else out + term
+    send[:, at : at + 2 * share, :] = out.astype(BF16)
+
+
+def pair_solve(tab, marks, outer, inner, sums, w, act_sums, q_rows, p_rows, pixels):
+    label, n = entry(tab, OWN), LANES
+    (norm_o, keeps_o), (norm_i, keeps_i) = outer, inner
+    shift_o, gain_o, shift_i, gain_i = sums
+    images = group_count(marks, label)
+    count, count_o = images * pixels, tiled(images, norm_o.shape[2]) * pixels
+    rstd_o = keeps_o[1:2, :]
+    a_o = rstd_o * gain_of(norm_o, label)
+    b_o, c_o = -(a_o * rstd_o) * gain_o / count_o, -a_o * shift_o / count_o
+    m = mm_nt((w[...].astype(F32) * b_o).astype(BF16), w[...]).astype(BF16)
+    e = through_nt(c_o, w[...])
+    same = (marks == label).astype(F32)
+    middle = jnp.sum(act_sums * same, axis=0) / count
+    spread_out = ((act_sums * (1.0 / pixels) - middle[None]) * same).reshape(-1, n).astype(BF16)
+    share = p_rows.shape[1] // 2
+    found = []
+    for h, start in enumerate((shift_i, gain_i)):
+        q = q_rows[:, h : h + 1, :]
+        p = p_rows[:, share * h : share * (h + 1), :].reshape(-1, n)[0:n]
+        p = p + mm_tn(spread_out, q.reshape(-1, n).astype(BF16))
+        found.append(start + down(m.astype(F32) * p) + e * jnp.sum(q * same, axis=0))
+    rstd_i = keeps_i[1:2, :]
+    a = rstd_i * gain_of(norm_i, label)
+    coefs = a, -(a * rstd_i) * found[1] / count, -a * found[0] / count
+    return m, e - through(middle, m), coefs, found
+
+
 def expanded_moments(got, labels, tab, w, pixels):
     label = entry(tab, OWN)
     total = group_sum(got, labels, label)
@@ -437,8 +542,9 @@
     return down(lax.fori_loop(0, rows, put, zeros8(LANES), unroll=7))
 
 
-def f3(tab, got, labels, z_in, norm, w, w_p, act, z, send, keeps, keeps_p):
+def f3(tab, got, labels, z_in, norm, w, w_p, act, z, send, keeps, keeps_p, act_sum):
     sums = activate(tab, got, labels, z_in, norm, act, keeps)
+    act_sum[...] = sums
     expand(act, w, z, send, sums)
     marks, label = labels[...], entry(tab, OWN)
     total = group_sum(got, marks, label)
@@ -450,7 +556,7 @@
     keeps_p[1:2, :] = rstd
 
 
-def f4(tab, got, labels, zc, zp, norm_c, norm_p, keeps_p, w_c, w, joined, slope, z, send, keeps):
+def f4(tab, got, labels, zc, zp, norm_c, norm_p, keeps_p, w_c, w, joined, slope, z, stats, keeps):
     rows, chans = zc.shape[0], zc.shape[2]
     pixels = 1.0 * rows * (COLS - 4)
     mean_c, rstd_c = expanded_moments(got, labels[...], tab, w_c, pixels)
@@ -483,7 +589,14 @@
         parts = values.reshape(-1, 8, LANES)
         sums = sums + jnp.sum(parts, axis=0)
         squares = squares + jnp.sum(parts * parts, axis=0)
-    spread(send, [down(sums), down(squares)])
+    stats[0:1, :] = down(sums)
+    stats[1:2, :] = down(squares)
+
+
+def pair_1(tab, stats, z, norm, keeps, act, act_sum, send, slope, both, centred, *, share):
+    product, sums = pair_products(tab, z, norm, keeps, act, act_sum[...], slope, both, centred)
+    put_split(send, 0, stats[...])
+    put_pair(send, 4, share, product, sums)
 
 
 def put_shares(xz, send, part):
@@ -499,7 +612,10 @@
 def f5(tab, got, labels, z_in, norm, w_two, w_last, xz, x3, z, send, keeps):
     rows = z_in.shape[0]
     pixels = 1.0 * rows * (COLS - 4)
-    mean, rstd, gain, shift, _ = scale_shift(got, labels[...], tab, norm, pixels)
+    marks, label = labels[...], entry(tab, OWN)
+    total = over_group(get_split(got, 0, 2), marks, label)
+    mean, rstd = moments(total[0:1], total[1:2], group_count(marks, label) * pixels)
+    gain, shift = gain_of(norm, label), shift_of(norm, label)
     keeps[0:1, :] = mean
     keeps[1:2, :] = rstd
     scale = rstd * gain
@@ -560,27 +676,36 @@
     spread(send, [down(sums) * gate, down(products) * rstd * gate])
 
 
-def backward_norm(tab, got, labels, norm, keeps, pixels, grad_norm):
-    marks = labels[...]
-    chans = norm.shape[2]
-    own_shift = jnp.zeros((1, chans), F32)
-    own_gain = jnp.zeros((1, chans), F32)
-    group = entry(tab, OWN)
-    for g in range(norm.shape[0]):
-        total = group_sum(got.at[:, :, 0 : 2 * LANES], marks, float(g))
-        shift_sum, gain_sum = row(total, 0), row(total, 1)
+def lane_sums(got, marks, channels):
+    def sums_of(g):
+        total = group_sum(got, marks, float(g))
+        return row(total, 0), row(total, 1)
+
+    return sums_of
+
+
+def row_sums(got, marks):
+    def sums_of(g):
+        total = over_group(get_split(got, 0, 2), marks, float(g))
+        return total[0:1], total[1:2]
+
+    return sums_of
+
+
+def backward_norm(tab, sums_of, marks, norm, keeps, pixels, grad_norm):
+    group, chans = entry(tab, OWN), norm.shape[2]
+    sums = [sums_of(g) for g in range(norm.shape[0])]
+    for g, (shift_sum, gain_sum) in enumerate(sums):
         grad_norm[g, 0:1, :] = gain_sum
         grad_norm[g, 1:2, :] = shift_sum
-        mine = tiled(group, chans) == float(g)
-        own_shift = jnp.where(mine, shift_sum, own_shift)
-        own_gain = jnp.where(mine, gain_sum, own_gain)
     count = tiled(group_count(marks, group), chans) * pixels
+    own_shift, own_gain = (own_of([v[k] for v in sums], group) for k in (0, 1))
     mean, rstd = keeps[0:1, :], keeps[1:2, :]
     a = rstd * gain_of(norm, group)
     return mean, a, -(a * rstd) * own_gain / count, -a * own_shift / count
 
 
-def slope_sums(tab, d, z_in, norm, keeps, dout, send):
+def slope_sums(tab, d, z_in, norm, keeps, dout):
     rows = z_in.shape[0]
     mean, rstd = keeps[0:1, :], keeps[1:2, :]
     group = entry(tab, OWN)
@@ -599,7 +724,7 @@
     sums, products = lax.fori_loop(
         0, rows, put, (zeros8(LANES), zeros8(LANES)), unroll=4
     )
-    spread(send, [down(sums), down(products) * rstd])
+    return down(sums), down(products) * rstd
 
 
 def b8(
@@ -608,7 +733,9 @@
 ):
     rows, chans = z.shape[0], z.shape[2]
     pixels = 1.0 * rows * (COLS - 4)
-    mean, a, b, c = backward_norm(tab, got, labels, norm, keeps, pixels, grad_norm)
+    marks = labels[...]
+    sums_of = lane_sums(got, marks, chans)
+    mean, a, b, c = backward_norm(tab, sums_of, marks, norm, keeps, pixels, grad_norm)
     a = a * (0.25 * tiled(entry(tab, GATE), norm.shape[2]))
     keep = valid_cols(chans)
 
@@ -619,17 +746,20 @@
 
     lax.fori_loop(0, rows, put, 0, unroll=2)
     d[...] = mm_nt(flat(dz[...]), w[...]).reshape(d.shape)
-    slope_sums(tab, d, z_in, norm_in, keeps_in, dout, send.at[:, :, 0 : 2 * LANES])
+    sums = slope_sums(tab, d, z_in, norm_in, keeps_in, dout)
+    spread(send.at[:, :, 0 : 2 * LANES], sums)
     put_shares(xz, send, 1)
 
 
 def b9(
-    tab, got, labels, dout_in, z, norm, keeps, b_two, b_last, z_in, norm_in, keeps_in, x_sum,
-    dz, dout, send, grad_norm, d3, d,
+    tab, got, labels, dout_in, z, norm, keeps, b_two, b_last, z_in, norm_in, keeps_in, x_sum, pair_got,
+    dz, dout, send, grad_norm, d3, d, *, share,
 ):
     rows = z.shape[0]
     pixels = 1.0 * rows * (COLS - 4)
-    mean, a, b, c = backward_norm(tab, got, labels, norm, keeps, pixels, grad_norm)
+    marks = labels[...]
+    sums_of = lane_sums(got.at[:, :, 0 : 2 * LANES], marks, LANES)
+    mean, a, b, c = backward_norm(tab, sums_of, marks, norm, keeps, pixels, grad_norm)
     keep = valid_cols(LANES)
     n = LANES
     d3[0] = jnp.zeros(d3.shape[1:], BF16)
@@ -652,33 +782,31 @@
         value = mm_nt(flat(d3[step * k + 2 : step * (k + 1) + 2]), b_last[...])
         value = value + both[COLS:, 0:n] + both[0 : step * COLS, n : 2 * n]
         d[step * k : step * (k + 1)] = value.reshape(step, COLS, LANES)
-    slope_sums(tab, d, z_in, norm_in, keeps_in, dout, send.at[:, :, 0 : 2 * n])
-    turned = join([jnp.transpose(x_sum[lanes, :])[0:1] for lanes in columns(x_sum.shape[0])])
-    spread(send.at[:, :, 2 * n :], [turned[:, lanes] for lanes in columns(x_sum.shape[0])])
+    put_split(send, 0, stack(slope_sums(tab, d, z_in, norm_in, keeps_in, dout)))
+    blocks = columns(x_sum.shape[0])
+    put_split(send, 4, stack([jnp.transpose(x_sum[lanes, :])[0:1] for lanes in blocks]))
+    pass_pair(send, 4 + 2 * len(blocks), pair_got, 4, share, marks, norm.shape[0])
 
 
 def b10(
     tab, got, labels, dout_in, z, norm, keeps, w, grad_pre, slope, zc, zp, keeps_cp,
-    dz, grad_pre_2, send, grad_norm, sums_p, d,
+    norm_c, w_c, slope_in, z_in, keeps_in,
+    dz, grad_pre_2, send, grad_norm, d_in, d, low,
 ):
     rows, chans = zc.shape[0], zc.shape[2]
     pixels = 1.0 * rows * (COLS - 4)
-    mean, a, b, c = backward_norm(tab, got, labels, norm, keeps, pixels, grad_norm)
-    keep = valid_cols(LANES)
-
-    def put(i, carry):
-        v = a * dout_in[i] + b * (z[i] - mean) + c
-        dz[i] = jnp.where(keep, v, 0.0).astype(BF16)
-        return carry
-
-    lax.fori_loop(0, rows, put, 0, unroll=4)
+    marks = labels[...]
+    coefs = backward_norm(tab, row_sums(got, marks), marks, norm, keeps, pixels, grad_norm)
+    normed_grad(dz, dout_in, z, *coefs)
     d[...] = mm_nt(flat(dz[...]), w[...]).reshape(d.shape)
     mean_c, rstd_c, mean_p, rstd_p = (keeps_cp[k : k + 1, :] for k in range(4))
+    a_c = rstd_c * gain_of(norm_c, entry(tab, OWN))
 
     def sum_up(i, carry):
         sums, prod_c, prod_p = carry
         g = (grad_pre[i] + d[i]).astype(BF16).astype(F32) * slope[i]
         grad_pre_2[i] = g
+        low[i] = (a_c * g).astype(BF16)
         return (
             sums + fold(g),
             prod_c + fold(g * (zc[i] - mean_c)),
@@ -687,22 +815,33 @@
 
     start = zeros8(chans)
     sums, prod_c, prod_p = lax.fori_loop(0, rows, sum_up, (start, start, start), unroll=2)
-    spread(send, [down(sums), down(prod_c) * rstd_c])
-    sums_p[0:1, :] = down(sums)
-    sums_p[1:2, :] = down(prod_p) * rstd_p
-
-
-def b11(
-    tab, got, labels, grad_pre_2, zc, norm, keeps, w, z_in, norm_in, keeps_in, sums_p,
-    dz, dout, send, grad_norm, d,
-):
-    pixels = 1.0 * zc.shape[0] * (COLS - 4)
-    mean, a, b, c = backward_norm(tab, got, labels, norm, keeps.at[0:2], pixels, grad_norm)
-    normed_grad(dz, grad_pre_2, zc, mean, a, b, c)
-    d[...] = mm_nt(flat(dz[...]), w[...]).reshape(d.shape)
-    slope_sums(tab, d, z_in, norm_in, keeps_in, dout, send.at[:, :, 0 : 2 * LANES])
-    products = sums_p[1:2, :]
-    spread(send.at[:, :, 2 * LANES :], [products[:, lanes] for lanes in columns(zc.shape[2])])
+    wide = [down(sums), down(prod_c) * rstd_c, down(prod_p) * rstd_p]
+    inner = inner_sums(low, w_c, slope_in, z_in, keeps_in, d_in)
+    parts = [stack([v[:, 0 : chans // 2], v[:, chans // 2 :]]) for v in wide]
+    values = join([*parts, stack(inner)])
+    send[...] = jnp.broadcast_to(values[None], send.shape)
+
+
+def inner_sums(low, w, slope, z, keeps, d_in):
+    d_in[...] = mm_nt(flat(low[...]), w[...]).reshape(d_in.shape)
+    mean, rstd = keeps[0:1, :], keeps[1:2, :]
+
+    def add(i, carry):
+        g = slope[i] * d_in[i]
+        return carry[0] + fold(g), carry[1] + fold(g * (z[i] - mean))
+
+    sums = lax.fori_loop(0, z.shape[0], add, (zeros8(LANES), zeros8(LANES)), unroll=7)
+    return down(sums[0]), down(sums[1]) * rstd
+
+
+def inner_grad(act, m, line, slope, d_in, d):
+    d[...] = mm(flat(act[...]), m).reshape(d.shape)
+
+    def put(i, carry):
+        d[i] = slope[i] * (d_in[i] + d[i] + line)
+        return carry
+
+    lax.fori_loop(0, d.shape[0], put, 0, unroll=7)
 
 
 def normed_grad(dz, dout, z, mean, a, b, c):
@@ -716,32 +855,30 @@
     lax.fori_loop(0, z.shape[0], put, 0, unroll=2)
 
 
-def joined_norm(tab, got_c, got_p, labels, norm, keeps, pixels, grad_norm):
-    marks, group, chans = labels[...], entry(tab, OWN), norm.shape[2]
-    sums = []
-    for g in range(norm.shape[0]):
-        shift_sum = row(group_sum(got_c.at[:, :, 0:LANES], marks, float(g)), 0)
-        gain_sum = group_sum(got_p.at[:, :, 2 * LANES :], marks, float(g))
-        grad_norm[g, 0:1, :] = gain_sum
-        grad_norm[g, 1:2, :] = shift_sum
-        sums.append((gain_sum, shift_sum))
-    count = tiled(group_count(marks, group), chans) * pixels
-    own_gain, own_shift = (own_of([v[k] for v in sums], group) for k in (0, 1))
-    mean, rstd = keeps[0:1, :], keeps[1:2, :]
-    a = rstd * gain_of(norm, group)
-    return mean, a, -(a * rstd) * own_gain / count, -a * own_shift / count
-
-
-def b12(tab, got, labels, dout_in, z, norm, keeps, xs, d2, kept, sent, grad_norm, dz, packed):
+def b12(
+    tab, own10, labels, norm_c, keeps_c, w_c, got_act, got_q, got_p, act, slope, d_in,
+    z, norm, keeps, xs, d2, kept, sent, own_sums, dz, packed, dout, *, share, q_at, p_at,
+):
     rows = z.shape[0]
     pixels = 1.0 * rows * (COLS - 4)
-    mean, a, b, c = backward_norm(tab, got, labels, norm, keeps, pixels, grad_norm)
+    outer, n = norm_c.shape[2], LANES
+    marks = labels[...]
+    total = own10[...]
+    cuts = (0, outer, 2 * outer, 2 * outer + n, 2 * outer + 2 * n)
+    m, line, (a, b, c), found = pair_solve(
+        tab, marks, (norm_c, keeps_c.at[0:2]), (norm, keeps),
+        [total[:, u:v] for u, v in zip(cuts, cuts[1:])], w_c, got_act[:, :, 0:n],
+        get_split(got_q, q_at, 2), got_p[:, p_at : p_at + 2 * share, :].astype(F32), pixels,
+    )
+    own_sums[0:1, :] = found[0]
+    own_sums[1:2, :] = found[1]
+    inner_grad(act, m, line, slope, d_in, dout)
+    mean = keeps[0:1, :]
     keep = valid_cols(LANES)
-    n = LANES
     d2[rows] = jnp.zeros(d2.shape[1:], BF16)
 
     def put(i, carry):
-        v = a * dout_in[i] + b * (z[i] - mean) + c
+        v = a * dout[i] + b * (z[i] - mean) + c
         v = jnp.where(keep, v, 0.0)
         low = v.astype(BF16)
         dz[i] = low
@@ -804,7 +941,7 @@
     tab, got, labels, norm, keeps, w, z_own, z_for, dn_own, dn_for, gs_own, gs_for, *rest, at, held
 ):
     finished, outs = rest[:held], rest[held : 2 * held]
-    grad, grad_norm, dz, wide, grad_v, norm_v, sems = rest[2 * held :]
+    grad, grad_norm, grad_inner, dz, wide, grad_v, norm_v, inner_v, sems = rest[2 * held :]
     copies = [
         pltpu.make_async_copy(a, b, sems.at[k]) for k, (a, b) in enumerate(zip(finished, outs))
     ]
@@ -818,8 +955,14 @@
     for g in range(norm.shape[0]):
         norm_v[g, 0:1, :] = totals[g][1]
         norm_v[g, 1:2, :] = totals[g][0]
-    copies.append(pltpu.make_async_copy(norm_v, grad_norm, sems.at[held]))
-    copies[-1].start()
+    found = get_split(got, at + 4, 2)
+    for g in range(norm.shape[0]):
+        total = over_group(found, marks, float(g)) / group_count(marks, float(g))
+        inner_v[g, 0:1, :] = total[1:2]
+        inner_v[g, 1:2, :] = total[0:1]
+    for k, (value, out) in enumerate(((norm_v, grad_norm), (inner_v, grad_inner))):
+        copies.append(pltpu.make_async_copy(value, out, sems.at[held + k]))
+        copies[-1].start()
     keep = lax.broadcasted_iota(jnp.int32, (z_own.shape[1], LANES), 0) < cols
     for k, (z, dn, gs) in enumerate(((z_own, dn_own, gs_own), (z_for, dn_for, gs_for))):
         group = entry(tab, OWN if k == 0 else OTHER)
@@ -858,7 +1001,7 @@
             part = pl.ds(step * q, step)
             copies.append(
                 pltpu.make_async_copy(
-                    grad_v.at[place, part], grad.at[place, part], sems.at[held + 1 + 2 * k + q]
+                    grad_v.at[place, part], grad.at[place, part], sems.at[held + 2 + 2 * k + q]
                 )
             )
             copies[-1].start()
@@ -891,13 +1034,34 @@
 
 
 def g_most(
-    tab, act_2b, dz_2c, x3, dz_2b, joined, dz_2a, act_1b, dz_1c, xee, w_p,
-    got_c, got_p, labels, norm, keeps, grad_pre_2, zp,
-    kept, sent, gs_own, gs_oth, grad_norm, packed, dz_p,
+    tab, act_2b, dz_2c, x3, dz_2b, joined, dz_2a, act_1b, xee, w_p,
+    got, labels, norm_c, norm_p, keeps, grad_pre_2, zc, zp,
+    kept, sent, gs_own, gs_oth, grad_norm_c, grad_norm_p, own10, packed, dz_1c, dz_p,
 ):
-    rows = dz_2b.shape[0]
+    rows, outer = dz_2b.shape[0], zc.shape[2]
     pixels = 1.0 * rows * (COLS - 4)
-    coefs = joined_norm(tab, got_c, got_p, labels, norm, keeps.at[2:4], pixels, grad_norm)
+    marks = labels[...]
+
+    totals = [group_sum(got, marks, float(g)) for g in range(norm_c.shape[0])]
+    side = outer // 2
+
+    def line(total, k):
+        return join([total[h : h + 1, side * k : side * (k + 1)] for h in (0, 1)])
+
+    lines = [[line(total, k) for k in range(3)] for total in totals]
+    label = entry(tab, OWN)
+    for k in range(2):
+        own10[:, outer * k : outer * (k + 1)] = own_of([v[k] for v in lines], label)
+        inner = [total[k : k + 1, 3 * side :] for total in totals]
+        at = 2 * outer + LANES * k
+        own10[:, at : at + LANES] = own_of(inner, label)
+    coefs = backward_norm(
+        tab, lambda g: (lines[g][0], lines[g][1]), marks, norm_c, keeps.at[0:2], pixels, grad_norm_c
+    )
+    normed_grad(dz_1c, grad_pre_2, zc, *coefs)
+    coefs = backward_norm(
+        tab, lambda g: (lines[g][0], lines[g][2]), marks, norm_p, keeps.at[2:4], pixels, grad_norm_p
+    )
     normed_grad(dz_p, grad_pre_2, zp, *coefs)
     at = put_rows(packed, 0, mm_tn(flat(act_2b[...]), flat(dz_2c[...])))
     low = flat(dz_2b[...])
@@ -957,7 +1121,8 @@
         term = mm_tn(flat(x[...]), flat(low[...]))
         value = term if value is None else value + term
     marks, label = labels[...], entry(tab, OWN)
-    total = group_sum(got_x.at[:, :, 2 * n :], marks, label)
+    total = over_group(get_split(got_x, 4, x_sum.shape[0] // n), marks, label)
+    total = join([total[k : k + 1] for k in range(total.shape[0])])
     total = total / tiled(group_count(marks, label), total.shape[1])
     total = jnp.broadcast_to(total, (8, total.shape[1]))
     means = jnp.concatenate(
@@ -970,7 +1135,7 @@
         out[at:, :] = jnp.zeros((out.shape[0] - at, n), BF16)
 
 
-def pack_last(tall, sums, kept, got, kept_1b, got_1b, send, *, stats_at):
+def pack_last(tall, sums, found, kept, got, kept_1b, got_1b, send, *, stats_at):
     n = LANES
     devices = send.shape[0]
     piece, share = kept.shape[1], tall.shape[0] // devices
@@ -981,10 +1146,8 @@
     if second < devices:
         send[second:, 0:piece, :] = jnp.zeros((devices - second, piece, n), BF16)
     send[:, piece : piece + share, :] = tall[...].reshape(devices, share, n)
-    high = sums[...].astype(BF16)
-    rest = (sums[...] - high.astype(F32)).astype(BF16)
-    for k, v in enumerate((high, rest)):
-        send[:, stats_at + 2 * k : stats_at + 2 * k + 2, :] = jnp.broadcast_to(v[None], (devices, 2, n))
+    put_split(send, stats_at, sums[...])
+    put_split(send, stats_at + 4, found[...])
 
 
 def last_sums(stats, marks, groups):
@@ -1145,15 +1308,23 @@
          ((m, 1, n), F32), mean_scale(n, 2), mean_scale(n, norm_1a.shape[0]), wide_z],
     )(tab, g1, z_own, x_oth, w_1a, norm_1a, w_even, w_odd, stats_1p)
     g2 = gather(s2)
-    act_1b, z_1c, s3, k_1b, k_p = stage(
-        f3, [maps(n, BF16), maps(outer), send(1 + outer // n), mean_scale(n), mean_scale(outer)]
+    act_1b, z_1c, s3, k_1b, k_p, sum_1b = stage(
+        f3,
+        [maps(n, BF16), maps(outer), send(1 + outer // n), mean_scale(n), mean_scale(outer),
+         ((1, n), F32)],
     )(tab, g2, labels, z_1b, norm_1b, w_1c, w_1p)
     g3 = gather(s3)
-    joined, slope, z_2a, s4, k_cp = stage(
-        f4, [maps(outer, BF16), maps(outer), maps(n), send(2), mean_scale(outer, 2)]
+    joined, slope, z_2a, stats_2a, k_cp = stage(
+        f4, [maps(outer, BF16), maps(outer), maps(n), ((2, n), F32), mean_scale(outer, 2)]
     )(tab, g3, labels, z_1c, z_1p, norm_1c, norm_1p, k_p, w_1c, w_2a)
     share = -(-inputs // devices)
     half_in = ((rows, cols_in, n), BF16)
+    share_1 = -(-n // devices)
+    high = -(-(8 + 2 * share_1) // 16) * 16
+    s4, slope_1b = stage(
+        functools.partial(pair_1, share=share_1), [((devices, high, n), BF16), maps(n)],
+        [scratch(2 * n, BF16), scratch(n, BF16)],
+    )(tab, stats_2a, z_1b, norm_1b, k_1b, act_1b, sum_1b)
     s4, k_1a = tie(s4, k_1a)
     xz, x_sum = stage(
         g_xz, [((devices * share, n), F32), ((inputs, n), F32)],
@@ -1179,20 +1350,18 @@
     )(tab, g7, labels, grad_pre, z_2c, norm_2c, k_2c, w_2c, z_2b, norm_2b, k_2b, xz)
     g8 = gather(s8)
     dz_2b, dout_2a, s9, grad_norm_2b = stage(
-        b9, [maps(n, BF16), maps(n), send(2 + inputs // n), *params(norm_2b)],
+        functools.partial(b9, share=share_1),
+        [maps(n, BF16), maps(n), ((devices, high, n), BF16), *params(norm_2b)],
         [pltpu.VMEM((rows + 2, COLS, 3 * n), BF16), scratch(n)],
-    )(tab, g8, labels, dout_2b, z_2b, norm_2b, k_2b, b_two, b_last, z_2a, norm_2a, k_2a, x_sum)
+    )(tab, g8, labels, dout_2b, z_2b, norm_2b, k_2b, b_two, b_last, z_2a, norm_2a, k_2a, x_sum, g4)
     g9 = gather(s9)
-    dz_2a, grad_pre_2, s10, grad_norm_2a, sums_p = stage(
+    dz_2a, grad_pre_2, s10, grad_norm_2a, d_1b = stage(
         b10,
-        [maps(n, BF16), maps(outer), send(2, outer), *params(norm_2a), mean_scale(outer)],
-        [scratch(outer)],
-    )(tab, g9, labels, dout_2a, z_2a, norm_2a, k_2a, w_2a, grad_pre, slope, z_1c, z_1p, k_cp)
+        [maps(n, BF16), maps(outer), ((devices, 2, 3 * outer // 2 + n), F32), *params(norm_2a), maps(n)],
+        [scratch(outer), scratch(outer, BF16)],
+    )(tab, g9, labels, dout_2a, z_2a, norm_2a, k_2a, w_2a, grad_pre, slope, z_1c, z_1p, k_cp,
+      norm_1c, w_1c, slope_1b, z_1b, k_1b)
     g10 = gather(s10)
-    dz_1c, dout_1b, s11, grad_norm_1c = stage(
-        b11, [maps(outer, BF16), maps(n), send(2 + outer // n), *params(norm_1c)], [scratch(n)]
-    )(tab, g10, labels, grad_pre_2, z_1c, norm_1c, k_cp, w_1c, z_1b, norm_1b, k_1b, sums_p)
-    g11 = gather(s11)
     half_map = ((rows // 2, COLS, inputs), BF16)
     most_rows = sum(v.size for v in (w_2c, w_2b, w_2a, w_1c, w_1p)) // n
     rows_1b = w_1b.size // n
@@ -1201,17 +1370,20 @@
         piece += 16
     first, second = -(-most_rows // (2 * piece)), -(-rows_1b // (2 * piece))
     part, part_1b = ((first, piece, n), BF16), ((second, piece, n), BF16)
-    kept, sent, gs_own, gs_send, grad_norm_1p = stage(
-        g_most, [part, part, half_map, half_map, *params(norm_1p)],
-        [pltpu.VMEM((2 * first * piece, n), BF16), scratch(outer, BF16)],
-    )(tab, act_2b, dz_2c, x3, dz_2b, joined, dz_2a, act_1b, dz_1c, xee, w_1p,
-      g10, g11, labels, norm_1p, k_cp, grad_pre_2, z_1p)
+    kept, sent, gs_own, gs_send, grad_norm_1c, grad_norm_1p, own10 = stage(
+        g_most,
+        [part, part, half_map, half_map, *params(norm_1c, norm_1p), ((1, 2 * outer + 2 * n), F32)],
+        [pltpu.VMEM((2 * first * piece, n), BF16), scratch(outer, BF16), scratch(outer, BF16)],
+    )(tab, act_2b, dz_2c, x3, dz_2b, joined, dz_2a, act_1b, xee, w_1p,
+      g10, labels, norm_1c, norm_1p, k_cp, grad_pre_2, z_1c, z_1p)
     got, gs_for = swap(sent), swap(gs_send)
-    g11, _ = tie(g11, sent)
-    d2, kept_1b, sent_1b, grad_norm_1b = stage(
-        b12, [((rows + 1, COLS, 2 * n), BF16), part_1b, part_1b, *params(norm_1b)],
-        [scratch(n, BF16), pltpu.VMEM((2 * second * piece, n), BF16)],
-    )(tab, g11, labels, dout_1b, z_1b, norm_1b, k_1b, xs)
+    half_in = ((rows, cols_in, n), BF16)
+    d2, kept_1b, sent_1b, found_1b = stage(
+        functools.partial(b12, share=share_1, q_at=4 + 2 * share_1, p_at=4 + 2 * (inputs // n)),
+        [((rows + 1, COLS, 2 * n), BF16), part_1b, part_1b, ((2, n), F32)],
+        [scratch(n, BF16), pltpu.VMEM((2 * second * piece, n), BF16), scratch(n)],
+    )(tab, own10, labels, norm_1c, k_cp, w_1c, g3, g4, g9, act_1b, slope_1b, d_1b,
+      z_1b, norm_1b, k_1b, xs)
     got_1b = swap(sent_1b)
     sides = []
     for own, z in ((False, z_oth), (True, z_own)):
@@ -1227,14 +1399,14 @@
             d2, _ = tie(d2, sides[0][0])
     (dn_send, sums_send), (dn_own, sums_own) = sides
     stats_at = piece + -(-share // 8) * 8
-    high = -(-(stats_at + 4) // 16) * 16
+    high = -(-(stats_at + 8) // 16) * 16
     tall, sums_1a = stage(
         g_xd, [((devices * share, n), BF16), ((2, n), F32)], [pltpu.VMEM(half_in[0], BF16)]
     )(tab, sums_own, sums_send, norm_1a, k_1a, x_sum, g9, labels, x_own, x_oth, dn_own, dn_send)
     tall, gs_for, dn_for = tie(tall, gs_for, dn_for)
     (s12,) = stage(
         functools.partial(pack_last, stats_at=stats_at), [((devices, high, n), BF16)]
-    )(tall, sums_1a, kept, got, kept_1b, got_1b)
+    )(tall, sums_1a, found_1b, kept, got, kept_1b, got_1b)
     g12 = gather(s12)
     pixels = 4.0 * images.shape[1] * images.shape[1]
     (mine,) = stage(
@@ -1242,18 +1414,18 @@
         [((devices, piece + share, n), BF16)],
     )(g12, labels, norm_1a, k_all, g5, g8)
     finished = (
-        result, grad_norm_1b, grad_norm_1c, grad_norm_1p, grad_norm_2a, grad_norm_2b, grad_norm_2c
+        result, grad_norm_1c, grad_norm_1p, grad_norm_2a, grad_norm_2b, grad_norm_2c
     )
     held = len(finished)
-    *finished, grad_images, grad_norm_1a = stage(
+    *finished, grad_images, grad_norm_1a, grad_norm_1b = stage(
         functools.partial(b13, at=stats_at, held=held),
-        [*((v.shape, v.dtype) for v in finished), (images.shape, BF16), *params(norm_1a)],
+        [*((v.shape, v.dtype) for v in finished), (images.shape, BF16), *params(norm_1a, norm_1b)],
         [pltpu.VMEM(half_in[0], BF16), pltpu.VMEM((inputs // n, rows, cols_in, n), F32),
-         pltpu.VMEM(images.shape, BF16), pltpu.VMEM(norm_1a.shape, F32),
-         pltpu.SemaphoreType.DMA((held + 5,))],
-        hbm_out=range(held + 2),
+         pltpu.VMEM(images.shape, BF16), *(pltpu.VMEM(norm_1a.shape, F32) for _ in range(2)),
+         pltpu.SemaphoreType.DMA((held + 6,))],
+        hbm_out=range(held + 3),
     )(tab, g12, labels, norm_1a, k_1a, w_1a, z_own, z_for, dn_own, dn_for, gs_own, gs_for, *finished)
-    result, grad_norm_1b, grad_norm_1c, grad_norm_1p, grad_norm_2a, grad_norm_2b, grad_norm_2c = finished
+    result, grad_norm_1c, grad_norm_1p, grad_norm_2a, grad_norm_2b, grad_norm_2c = finished
     whole = gather(mine)
     weights = (w_1a, w_1b.reshape(-1, n), w_2c, w_2b.reshape(-1, n), w_2a, w_1c, w_1p)
     totals = stage(

time: 188 us -> 184 us (0.979)
  blocking collectives: 155 us -> 150 us
  Pallas kernels: 29.1 us -> 31.1 us
    all_to_all x13 -> x12, blocking collectives: 155 us -> 150 us  [gather(): return lax.all_to_all(send, AXES, 0, 0)]
    pallas_call x23, Pallas kernels: 29.1 us -> 31.1 us  [call(): pl.pallas_call(kernel, out_shape=tuple((jax.ShapeDtypeStruct(s, d) for s,...]
where the time goes in v5:
time: 184 us
  blocking collectives  150 us (82%)
  Pallas kernels  31.1 us (17%)
    all_to_all x12, blocking collectives, gather(): return lax.all_to_all(send, AXES, 0, 0)  150 us
    pallas_call x23, Pallas kernels, call(): pl.pallas_call(kernel, out_shape=tuple((jax.ShapeDtypeStruct(s, d) for s,...  31.1 us
  transfers between devices with their start and end apart: 6, of which 0 were waited for; matrix products, arithmetic and copies ran while one was open for 0% of the time, Pallas kernels for 4%

profile of v5, /device:TPU:0, one launch (start us, length us, event | category | flops | bytes accessed | tf_op | source)
XLA Modules:
  0.0 184.0 jit_solution(9665742339698817788)
XLA Ops:
  0.7 2.3 %f1.1 = (f32[8,128]{1,0:T(8,128)S(1)}, bf16[28,64,256]{2,1,0:T(8,128)(2,1)S(1)}, bf16[28,64,256]{2,1,0:T(8,128)(2,1)S(1)}, f32[28,64,128]{2,1,0:T(8,128)S(1)}, f...) custom-call(s32[1]{0:T(128)} %bitcast.half_at, s32[2]{0:T(128)} %group_at.1, s32[3]{0:T(128)} %width_at.1, s32[3]{0:T(128)} %gate_at.1, ...), custom_call_target="tpu_custom_call" | custom-call | tf_op jit(solution)/shard_map/f1/pallas_call | solution.py:32
  3.8 14.2 %all_to_all.60.got = f32[32,1,640]{2,1,0:T(1,128)S(1)} all-to-all(f32[32,1,640]{2,1,0:T(1,128)S(1)} %get-tuple-element.151), channel_id=1, replica_groups=mesh['rows'=2,'batch'=16] {'rows','batch'}, dimensions={0} | all-to-all | bytes 163840 | tf_op jit(solution)/shard_map/all_to_all | solution.py:1236
  18.0 0.9 f1_strided.1
  19.0 1.9 %f2.1 = (bf16[29,32,768]{2,1,0:T(8,128)(2,1)S(1)}, f32[28,32,128]{2,1,0:T(8,128)S(1)}, f32[32,1,1024]{2,1,0:T(1,128)S(1)}, f32[32,1,128]{2,1,0:T(1,128)S(1)}, f3...) custom-call(f32[8,128]{1,0:T(8,128)S(1)} %get-tuple-element.137.tab, ...), custom_call_target="tpu_custom_call" | custom-call | tf_op jit(solution)/shard_map/f2/pallas_call | solution.py:32
  20.8 9.6 %all_to_all.61.got = f32[32,1,1024]{2,1,0:T(1,128)S(1)} all-to-all(f32[32,1,1024]{2,1,0:T(1,128)S(1)} %get-tuple-element.160), channel_id=1, replica_groups=mesh['rows'=2,'batch'=16] {'rows','batch'}, dimensions={0} | all-to-all | bytes 262144 | tf_op jit(solution)/shard_map/all_to_all | solution.py:1236
  30.5 0.7 f3.1
  31.1 9.4 %all_to_all.62.got.got_act = f32[32,1,640]{2,1,0:T(1,128)S(1)} all-to-all(f32[32,1,640]{2,1,0:T(1,128)S(1)} %get-tuple-element.163), channel_id=1, replica_groups=mesh['rows'=2,'batch'=16] {'rows','batch'}, dimensions={0} | all-to-all | bytes 163840 | tf_op jit(solution)/shard_map/all_to_all | solution.py:1236
  40.6 1.4 f4.1
  41.9 0.6 pair_1.1
  42.6 1.1 g_xz.1
  43.7 9.7 %all_to_all.63.got.pair_got.got_q = bf16[32,16,128]{2,1,0:T(8,128)(2,1)S(1)} all-to-all(bf16[32,16,128]{2,1,0:T(8,128)(2,1)S(1)} %get-tuple-element.178), channel_id=1, replica_groups=mesh['rows'=2,'batch'=16] {'rows','batch'}, dimensions={0} | all-to-all | bytes 262144 | tf_op jit(solution)/shard_map/all_to_all | solution.py:1236
  53.5 1.1 f5.1
  54.5 9.6 %all_to_all.64.got.got_a = f32[32,1,768]{2,1,0:T(1,128)S(1)} all-to-all(f32[32,1,768]{2,1,0:T(1,128)S(1)} %get-tuple-element.183), channel_id=1, replica_groups=mesh['rows'=2,'batch'=16] {'rows','batch'}, dimensions={0} | all-to-all | bytes 196608 | tf_op jit(solution)/shard_map/all_to_all | solution.py:1236
  64.1 0.7 f6.1
  64.8 9.2 %all_to_all.65.got = f32[32,1,640]{2,1,0:T(1,128)S(1)} all-to-all(f32[32,1,640]{2,1,0:T(1,128)S(1)} %get-tuple-element.186), channel_id=1, replica_groups=mesh['rows'=2,'batch'=16] {'rows','batch'}, dimensions={0} | all-to-all | bytes 163840 | tf_op jit(solution)/shard_map/all_to_all | solution.py:1236
  74.0 1.8 b7.1
  75.8 9.6 %all_to_all.66.got = f32[32,4,256]{2,1,0:T(4,128)S(1)} all-to-all(f32[32,4,256]{2,1,0:T(4,128)S(1)} %get-tuple-element.189), channel_id=1, replica_groups=mesh['rows'=2,'batch'=16] {'rows','batch'}, dimensions={0} | all-to-all | bytes 262144 | tf_op jit(solution)/shard_map/all_to_all | solution.py:1236
  85.4 1.4 b8.1
  86.7 9.6 %all_to_all.67.got.got_b = f32[32,1,768]{2,1,0:T(1,128)S(1)} all-to-all(f32[32,1,768]{2,1,0:T(1,128)S(1)} %get-tuple-element.195), channel_id=1, replica_groups=mesh['rows'=2,'batch'=16] {'rows','batch'}, dimensions={0} | all-to-all | bytes 196608 | tf_op jit(solution)/shard_map/all_to_all | solution.py:1236
  96.3 1.7 b9.1
  98.0 9.6 %all_to_all.68.got.got_p.got_x = bf16[32,16,128]{2,1,0:T(8,128)(2,1)S(1)} all-to-all(bf16[32,16,128]{2,1,0:T(8,128)(2,1)S(1)} %get-tuple-element.202), channel_id=1, replica_groups=mesh['rows'=2,'batch'=16] {'rows','batch'}, dimensions={0} | all-to-all | bytes 262144 | tf_op jit(solution)/shard_map/all_to_all | solution.py:1236
  107.6 2.6 %b10.1 = (bf16[28,32,128]{2,1,0:T(8,128)(2,1)S(1)}, f32[28,32,512]{2,1,0:T(8,128)S(1)}, f32[32,2,896]{2,1,0:T(2,128)S(1)}, f32[3,2,128]{2,1,0:T(2,128)S(1)}, f32[28,32,128]{2,1,0:T(8,128)S(1)}) custom-call(f32[8,128]{1,0:T(8,128)S(1)} %get-tuple-element.137.tab, bf16[32,16,128]{2,1,0:T(8,128)(2,1)S(1)} %all_to_all.68.got.got_p.got_x, ...), custom_call_target="tpu_custom_call" | custom-call | tf_op jit(solution)/shard_map/b10/pallas_call | solution.py:32
  110.2 12.4 %all_to_all.69.got = f32[32,2,896]{2,1,0:T(2,128)S(1)} all-to-all(f32[32,2,896]{2,1,0:T(2,128)S(1)} %get-tuple-element.209), channel_id=1, replica_groups=mesh['rows'=2,'batch'=16] {'rows','batch'}, dimensions={0} | all-to-all | bytes 458752 | tf_op jit(solution)/shard_map/all_to_all | solution.py:1236
  122.6 3.1 %g_most.1 = (bf16[24,80,128]{2,1,0:T(8,128)(2,1)S(1)}, bf16[24,80,128]{2,1,0:T(8,128)(2,1)S(1)}, bf16[14,32,256]{2,1,0:T(8,128)(2,1)S(1)}, bf16[14,32,256]{2,1,0...) custom-call(f32[8,128]{1,0:T(8,128)S(1)} %get-tuple-element.137.tab, ...), custom_call_target="tpu_custom_call" | custom-call | tf_op jit(solution)/shard_map/g_most/pallas_call | solution.py:32
  125.8 1.5 b12.1
  127.4 1.1 b12_images.2
  129.5 1.1 b12_images.3
  130.6 1.1 g_xd.1
  132.0 24.2 %all_to_all.70.got = bf16[32,96,128]{2,1,0:T(8,128)(2,1)S(1)} all-to-all(bf16[32,96,128]{2,1,0:T(8,128)(2,1)S(1)} %pack_last.1), channel_id=1, replica_groups=mesh['rows'=2,'batch'=16] {'rows','batch'}, dimensions={0} | all-to-all | bytes 1572864 | tf_op jit(solution)/shard_map/all_to_all | solution.py:1236
  156.8 22.8 %all_to_all.71.own = bf16[32,88,128]{2,1,0:T(8,128)(2,1)S(1)} all-to-all(bf16[32,88,128]{2,1,0:T(8,128)(2,1)S(1)} %add_all.1), channel_id=1, replica_groups=mesh['rows'=2,'batch'=16] {'rows','batch'}, dimensions={0} | all-to-all | bytes 1441792 | tf_op jit(solution)/shard_map/all_to_all | solution.py:1236
  179.6 2.5 %b13.1 = (bf16[28,28,512]{2,1,0:T(8,128)(2,1)}, f32[3,2,512]{2,1,0:T(2,128)}, f32[3,2,512]{2,1,0:T(2,128)}, f32[3,2,128]{2,1,0:T(2,128)}, f32[3,2,128]{2,1,0:T(2...) custom-call(f32[8,128]{1,0:T(8,128)S(1)} %get-tuple-element.137.tab,, ...), custom_call_target="tpu_custom_call" | custom-call | tf_op jit(solution)/shard_map/b13/pallas_call | solution.py:32
  182.1 1.7 unpack.1
  (45 shorter events, 2.7 us)
Async XLA Ops:
  0.6 2.4 %copy-start.7 = (bf16[3,3,128,128]{3,2,1,0:T(8,128)(2,1)S(1)}, bf16[3,3,128,128]{3,2,1,0:T(8,128)(2,1)}, u32[]{:S(2)}) copy-start(bf16[3,3,128,128]{3,2,1,0:T(8,128)(2,1)} %w2b) | copy-start | bytes 884740
  0.7 2.4 %copy-start.6 = (bf16[3,3,128,128]{3,2,1,0:T(8,128)(2,1)S(1)}, bf16[3,3,128,128]{3,2,1,0:T(8,128)(2,1)}, u32[]{:S(2)}) copy-start(bf16[3,3,128,128]{3,2,1,0:T(8,128)(2,1)} %w1b) | copy-start | bytes 884740
  0.7 17.4 %copy-start = (bf16[256,512]{1,0:T(8,128)(2,1)S(1)}, bf16[256,512]{1,0:T(8,128)(2,1)}, u32[]{:S(2)}) copy-start(bf16[256,512]{1,0:T(8,128)(2,1)} %w_p.3) | copy-start | bytes 786436
  3.0 15.9 %copy-start.4 = (bf16[256,128]{1,0:T(8,128)(2,1)S(1)}, bf16[256,128]{1,0:T(8,128)(2,1)}, u32[]{:S(2)}) copy-start(bf16[256,128]{1,0:T(8,128)(2,1)} %w.17) | copy-start | bytes 196612
  3.0 15.9 %copy-start.9 = (f32[2,3,128]{2,0,1:T(2,128)S(1)}, f32[2,3,128]{2,0,1:T(2,128)}, u32[]{:S(2)}) copy-start(f32[2,3,128]{2,0,1:T(2,128)} %param.27) | copy-start | bytes 9220
  3.3 14.8 %collective-permute-start = (bf16[28,64,256]{2,1,0:T(8,128)(2,1)S(1)}, bf16[28,64,256]{2,1,0:T(8,128)(2,1)S(1)}, u32[]{:S(2)}, u32[]{:S(2)}) collective-permute-start(bf16[28,64,256]{2,1,0:T(8,128)(2,1)S(1)} %get-tuple-element.152), channel_id=1, source_target_pairs={{0,16},{16,0},{1,17},{17,1},{2,18},{18,2},{3,19},{19,3},{4,20},{20... | collective-permute-start | bytes 2752520 | tf_op jit(solution)/shard_map/ppermute | solution.py:1244
  18.0 12.4 %copy-start.1 = (bf16[128,512]{1,0:T(8,128)(2,1)S(1)}, bf16[128,512]{1,0:T(8,128)(2,1)}, u32[]{:S(2)}) copy-start(bf16[128,512]{1,0:T(8,128)(2,1)} %w_c.5) | copy-start | bytes 393220
  18.0 12.4 %copy-start.12 = (f32[2,3,128]{2,0,1:T(2,128)S(1)}, f32[2,3,128]{2,0,1:T(2,128)}, u32[]{:S(2)}) copy-start(f32[2,3,128]{2,0,1:T(2,128)} %param.28) | copy-start | bytes 9220
  18.9 21.6 %copy-start.5 = (bf16[512,128]{1,0:T(8,128)(2,1)S(1)}, bf16[512,128]{1,0:T(8,128)(2,1)}, u32[]{:S(2)}) copy-start(bf16[512,128]{1,0:T(8,128)(2,1)} %w.16) | copy-start | bytes 393220
  18.9 21.6 %copy-start.8 = (f32[2,3,512]{2,0,1:T(2,128)S(1)}, f32[2,3,512]{2,0,1:T(2,128)}, u32[]{:S(2)}) copy-start(f32[2,3,512]{2,0,1:T(2,128)} %param.29) | copy-start | bytes 36868
  19.0 21.6 %copy-start.11 = (f32[2,3,512]{2,0,1:T(2,128)S(1)}, f32[2,3,512]{2,0,1:T(2,128)}, u32[]{:S(2)}) copy-start(f32[2,3,512]{2,0,1:T(2,128)} %param.30) | copy-start | bytes 36868
  42.6 10.9 %copy-start.14 = (f32[2,3,128]{2,0,1:T(2,128)S(1)}, f32[2,3,128]{2,0,1:T(2,128)}, u32[]{:S(2)}) copy-start(f32[2,3,128]{2,0,1:T(2,128)} %param.31) | copy-start | bytes 9220
  42.6 21.5 %copy-start.2 = (bf16[128,512]{1,0:T(8,128)(2,1)S(1)}, bf16[128,512]{1,0:T(8,128)(2,1)}, u32[]{:S(2)}) copy-start(bf16[128,512]{1,0:T(8,128)(2,1)} %w.15) | copy-start | bytes 393220
  42.6 21.5 %copy-start.13 = (f32[2,3,128]{2,0,1:T(2,128)S(1)}, f32[2,3,128]{2,0,1:T(2,128)}, u32[]{:S(2)}) copy-start(f32[2,3,128]{2,0,1:T(2,128)} %param.32) | copy-start | bytes 9220
  43.7 30.3 %copy-start.3 = (bf16[1,28,28,512]{3,2,1,0:T(8,128)(2,1)S(1)}, bf16[1,28,28,512]{3,2,1,0:T(8,128)(2,1)}, u32[]{:S(2)}) copy-start(bf16[1,28,28,512]{3,2,1,0:T(8,128)(2,1)} %param.34) | copy-start | bytes 2408452
  43.7 30.3 %copy-start.10 = (f32[2,3,512]{2,0,1:T(2,128)S(1)}, f32[2,3,512]{2,0,1:T(2,128)}, u32[]{:S(2)}) copy-start(f32[2,3,512]{2,0,1:T(2,128)} %param.33) | copy-start | bytes 36868
  125.8 6.1 %collective-permute-start.3 = (bf16[24,80,128]{2,1,0:T(8,128)(2,1)S(1)}, bf16[24,80,128]{2,1,0:T(8,128)(2,1)S(1)}, u32[]{:S(2)}, u32[]{:S(2)}) collective-permute-start(bf16[24,80,128]{2,1,0:T(8,128)(2,1)S(1)} %get-tuple-element.228), channel_id=1, source_target_pairs={{0,16},{16,0},{1,17},{17,1},{2,18},{18,2},{3,19},{19,3},{4,20},{20... | collective-permute-start | bytes 1474568 | tf_op jit(solution)/shard_map/ppermute | solution.py:1244
  128.5 3.3 %collective-permute-start.2 = (bf16[28,64,128]{2,1,0:T(8,128)(2,1)S(1)}, bf16[28,64,128]{2,1,0:T(8,128)(2,1)S(1)}, u32[]{:S(2)}, u32[]{:S(2)}) collective-permute-start(bf16[28,64,128]{2,1,0:T(8,128)(2,1)S(1)} %get-tuple-element.217.dn_oth), channel_id=1, source_target_pairs={{0,16},{16,0},{1,17},{17,1},{2,18},{18,2},{3,19},{19,3},{4,20},{20... | collective-permute-start | bytes 1376264 | tf_op jit(solution)/shard_map/ppermute | solution.py:1244
  129.0 2.8 %collective-permute-start.1 = (bf16[14,32,256]{2,1,0:T(8,128)(2,1)S(1)}, bf16[14,32,256]{2,1,0:T(8,128)(2,1)S(1)}, u32[]{:S(2)}, u32[]{:S(2)}) collective-permute-start(bf16[14,32,256]{2,1,0:T(8,128)(2,1)S(1)} %get-tuple-element.223), channel_id=1, source_target_pairs={{0,16},{16,0},{1,17},{17,1},{2,18},{18,2},{3,19},{19,3},{4,20},{20... | collective-permute-start | bytes 688136 | tf_op jit(solution)/shard_map/ppermute | solution.py:1244
  129.1 2.7 %collective-permute-start.4 = (bf16[8,80,128]{2,1,0:T(8,128)(2,1)S(1)}, bf16[8,80,128]{2,1,0:T(8,128)(2,1)S(1)}, u32[]{:S(2)}, u32[]{:S(2)}) collective-permute-start(bf16[8,80,128]{2,1,0:T(8,128)(2,1)S(1)} %get-tuple-element.230), channel_id=1, source_target_pairs={{0,16},{16,0},{1,17},{17,1},{2,18},{18,2},{3,19},{19,3},{4,20},{20... | collective-permute-start | bytes 491528 | tf_op jit(solution)/shard_map/ppermute | solution.py:1244
  179.6 2.5 %collective-permute-start.5 = (bf16[32,88,128]{2,1,0:T(8,128)(2,1)S(1)}, bf16[32,88,128]{2,1,0:T(8,128)(2,1)S(1)}, u32[]{:S(2)}, u32[]{:S(2)}) collective-permute-start(bf16[32,88,128]{2,1,0:T(8,128)(2,1)S(1)} %all_to_all.71.own), channel_id=1, source_target_pairs={{0,16},{16,0},{1,17},{17,1},{2,18},{18,2},{3,19},{19,3},{4,20},{20... | collective-permute-start | bytes 2162696 | tf_op jit(solution)/shard_map/ppermute | solution.py:1244

commit v6 on v5

--- a/solution.py
+++ b/solution.py
@@ -14,6 +14,7 @@
 VMEM_LIMIT = 14 * 1024 * 1024
 LANES = 128
 COLS = 32
+NEAR = 4
 
 
 def full(memory=pltpu.VMEM):
@@ -151,15 +152,15 @@
     return jnp.sum(x, axis=0, keepdims=True)
 
 
-OWN, OTHER, HALF, LIMIT, GATE = range(5)
+OWN, OTHER, HALF, LIMIT, GATE, MINOR = range(6)
 
 
 def entry(tab, k):
     return tab[k : k + 1, :]
 
 
-def half_of(tab):
-    return (jnp.sum(entry(tab, HALF)) * (1.0 / LANES)).astype(jnp.int32)
+def half_of(tab, k=HALF):
+    return (jnp.sum(entry(tab, k)) * (1.0 / LANES)).astype(jnp.int32)
 
 
 def prepare(w1b, w2b, w_even, w_odd, w_two, w_last, b_even, b_odd, b_two, b_last):
@@ -215,11 +216,11 @@
 
 
 def f1(
-    half_at, group_at, width_at, gate_at, images, w_at, tab, x_own, x_for, z_own, z_for, send,
-    half_ref, group, width, gate, raw, w, found, sems,
+    place_at, group_at, width_at, gate_at, images, w_at, tab, x_own, x_for, z_own, z_for, send,
+    place_ref, group, width, gate, raw, w, found, sems, *, batch,
 ):
     pairs = (
-        (half_at, half_ref), (group_at, group), (width_at, width), (gate_at, gate), (w_at, w),
+        (place_at, place_ref), (group_at, group), (width_at, width), (gate_at, gate), (w_at, w),
         (images.at[0], raw.at[0]), (images.at[1], raw.at[1]),
     )
     copies = [pltpu.make_async_copy(a, b, sems.at[k]) for k, (a, b) in enumerate(pairs)]
@@ -227,7 +228,7 @@
         copies[k].start()
     for k in (0, 4, 5):
         copies[k].wait()
-    half = half_ref[0]
+    half = lax.div(place_ref[0], batch)
     sides = ((x_own, z_own), (x_for, z_for))
 
     def one(k):
@@ -250,7 +251,8 @@
     rows = [found[k : k + 1, :] for k in range(4)]
     own, other = group[half], group[1 - half]
     values = {
-        OWN: own, OTHER: other, HALF: half, LIMIT: w.shape[1] // 4 * width[own], GATE: gate[own]
+        OWN: own, OTHER: other, HALF: half, LIMIT: w.shape[1] // 4 * width[own], GATE: gate[own],
+        MINOR: lax.rem(lax.rem(place_ref[0], batch), NEAR),
     }
     tab[...] = jnp.zeros(tab.shape, F32)
     for k, v in values.items():
@@ -1164,7 +1166,7 @@
     half = devices // 2
     split = got_a.shape[2] // n - 2
     share = split + got_b.shape[2] // n - 2
-    piece = out.shape[1] - share
+    piece = (out.shape[1] - share) // 2
     marks = labels[...]
     value = jnp.sum(got[:, piece : piece + share, :].astype(F32), axis=0)
     sums = last_sums(got.at[:, at : at + 4, :], marks, norm.shape[0])
@@ -1181,53 +1183,56 @@
         value = value + jnp.concatenate(rows, axis=0) * b
     for k in (0, 1):
         total = jnp.sum(got[half * k : half * (k + 1), 0:piece, :].astype(F32), axis=0).astype(BF16)
-        out[half * k : half * (k + 1), 0:piece, :] = jnp.broadcast_to(total[None], (half, piece, n))
-    out[:, piece:, :] = jnp.broadcast_to(value.astype(BF16)[None], (devices, share, n))
-
-
-def unpack(
-    tab, own, other, o_1a, o_1b, o_2c, o_2b, o_2a, o_1c, o_1p,
-    w_1a, w_1b, w_2c, w_2b, w_2a, w_1c, w_1p, tall, sems, *, first, second, piece,
-):
-    half = half_of(tab)
-    copies = []
-
-    def leave(value, out):
-        copies.append(pltpu.make_async_copy(value, out, sems.at[len(copies)]))
-        return copies[-1]
-
-    weights = ((w_2c, o_2c), (w_2b, o_2b), (w_2a, o_2a), (w_1c, o_1c), (w_1p, o_1p))
-    leaving = [leave(*v) for v in (*weights, (w_1b, o_1b), (w_1a, o_1a))]
-    for place in (0, 1):
-
-        @pl.when(half == place)
-        def _():
-            halves = (own, other) if place == 0 else (other, own)
-            most = [flat(v[0:first, 0:piece, :]) for v in halves]
-            last = [flat(v[first : first + second, 0:piece, :]) for v in halves]
-            size = first * piece
-
-            def source(at, rows):
-                pieces = []
-                if at < size:
-                    pieces.append(most[0][at : min(at + rows, size)])
-                if at + rows > size:
-                    pieces.append(most[1][max(at - size, 0) : at + rows - size])
-                pieces = [v.astype(F32) for v in pieces]
-                return pieces[0] if len(pieces) == 1 else jnp.concatenate(pieces, axis=0)
-
-            at = 0
-            for k, (value, _) in enumerate(weights):
-                at = take_rows(source, at, value)
-                leaving[k].start()
-            size = second * piece
-            w_1b[0:size] = last[0].astype(F32)
-            w_1b[size:] = last[1][0 : w_1b.shape[0] - size].astype(F32)
-            leaving[5].start()
-
-    tall[...] = own[:, piece:, :].astype(F32).reshape(tall.shape)
-    w_1a[...] = tall[0 : w_1a.shape[0], :]
-    leaving[6].start()
+        out[:, piece * k : piece * (k + 1), :] = jnp.broadcast_to(
+            total[None], (out.shape[0], piece, n)
+        )
+    out[:, 2 * piece :, :] = jnp.broadcast_to(value.astype(BF16)[None], (out.shape[0], share, n))
+
+
+def unpack(tab, *refs, first, second, piece):
+    parts, outs, values = refs[: 2 * NEAR], refs[2 * NEAR : 2 * NEAR + 7], refs[2 * NEAR + 7 :]
+    *values, tall, packed, sems = values
+    half, minor = half_of(tab), half_of(tab, MINOR)
+    far = parts[0].shape[0]
+    for k, part in enumerate(parts):
+        core = half if k < NEAR else 1 - half
+        base = core * (far * NEAR) + lax.bitwise_xor(minor, jnp.int32(k % NEAR))
+
+        def place(z, carry, part=part, base=base):
+            owner = base + NEAR * z
+            for h in (0, 1):
+                packed[h, owner] = part[z, piece * h : piece * (h + 1), :]
+            tall[owner] = part[z, 2 * piece :, :].astype(F32)
+            return carry
+
+        lax.fori_loop(0, far, place, 0, unroll=min(far, 4))
+    copies = [
+        pltpu.make_async_copy(value, out, sems.at[k]) for k, (value, out) in enumerate(zip(values, outs))
+    ]
+    most = [flat(packed[h, 0:first]) for h in (0, 1)]
+    last = [flat(packed[h, first : first + second]) for h in (0, 1)]
+    size = first * piece
+
+    def source(at, rows):
+        pieces = []
+        if at < size:
+            pieces.append(most[0][at : min(at + rows, size)])
+        if at + rows > size:
+            pieces.append(most[1][max(at - size, 0) : at + rows - size])
+        pieces = [v.astype(F32) for v in pieces]
+        return pieces[0] if len(pieces) == 1 else stack(pieces)
+
+    at = 0
+    for k, value in enumerate(values[0:5]):
+        at = take_rows(source, at, value)
+        copies[k].start()
+    w_1b, w_1a = values[5:7]
+    size = second * piece
+    w_1b[0:size] = last[0].astype(F32)
+    w_1b[size:] = last[1][0 : w_1b.shape[0] - size].astype(F32)
+    copies[5].start()
+    w_1a[...] = flat(tall[...])[0 : w_1a.shape[0]]
+    copies[6].start()
     for copy in copies:
         copy.wait()
 
@@ -1250,7 +1255,7 @@
     cotangent, group, width, gate,
 ):
     devices = lax.axis_size("rows") * lax.axis_size("batch")
-    half = lax.axis_index("rows").astype(jnp.int32).reshape(1)
+    place = lax.axis_index(AXES).astype(jnp.int32).reshape(1)
     norms = (norm_1a, norm_1b, norm_1c, norm_1p, norm_2a, norm_2b, norm_2c)
     norm_1a, norm_1b, norm_1c, norm_1p, norm_2a, norm_2b, norm_2c = (
         v.transpose(1, 0, 2) for v in norms
@@ -1279,12 +1284,12 @@
     wide_z = ((rows, cols_in, n), F32)
     raw = images.shape
     tab, x_own, x_for, z_own, z_for, s1 = stage(
-        f1, [((8, n), F32), wide_in, wide_in, wide_z, wide_z, send(5)],
-        [*(pltpu.SMEM(v.shape, jnp.int32) for v in (half, group, width, gate)),
+        functools.partial(f1, batch=devices // 2), [((8, n), F32), wide_in, wide_in, wide_z, wide_z, send(5)],
+        [*(pltpu.SMEM(v.shape, jnp.int32) for v in (place, group, width, gate)),
          pltpu.VMEM(raw, BF16), pltpu.VMEM(w_1a.shape, BF16), pltpu.VMEM((8, n), F32),
          pltpu.SemaphoreType.DMA((7,))],
         hbm=(0, 1, 2, 3, 4, 5),
-    )(half, group, width, gate, images, w_1a)
+    )(place, group, width, gate, images, w_1a)
     s1, v_1b, v_2b = tie(s1, w_1b, w_2b)
     built = stage(
         prepare,
@@ -1409,10 +1414,17 @@
     )(tall, sums_1a, found_1b, kept, got, kept_1b, got_1b)
     g12 = gather(s12)
     pixels = 4.0 * images.shape[1] * images.shape[1]
+    batch = devices // 2
+    far = batch // NEAR
     (mine,) = stage(
         functools.partial(add_all, at=stats_at, pixels=pixels),
-        [((devices, piece + share, n), BF16)],
+        [((far, 2 * piece + share, n), BF16)],
     )(g12, labels, norm_1a, k_all, g5, g8)
+    columns_of = [[k + NEAR * z for z in range(far)] for k in range(NEAR)]
+    along = lax.all_to_all(mine, "batch", 0, 0, axis_index_groups=columns_of)
+    near = [
+        lax.ppermute(along, "batch", [(i, i ^ k) for i in range(batch)]) for k in range(1, NEAR)
+    ]
     finished = (
         result, grad_norm_1c, grad_norm_1p, grad_norm_2a, grad_norm_2b, grad_norm_2c
     )
@@ -1426,16 +1438,16 @@
         hbm_out=range(held + 3),
     )(tab, g12, labels, norm_1a, k_1a, w_1a, z_own, z_for, dn_own, dn_for, gs_own, gs_for, *finished)
     result, grad_norm_1c, grad_norm_1p, grad_norm_2a, grad_norm_2b, grad_norm_2c = finished
-    whole = gather(mine)
-    weights = (w_1a, w_1b.reshape(-1, n), w_2c, w_2b.reshape(-1, n), w_2a, w_1c, w_1p)
-    totals = stage(
+    *near, grad_images = tie(*near, grad_images)
+    parts = [along, *near]
+    weights = (w_2c, w_2b.reshape(-1, n), w_2a, w_1c, w_1p, w_1b.reshape(-1, n), w_1a)
+    t_2c, t_2b, t_2a, t_1c, t_1p, t_1b, t_1a = stage(
         functools.partial(unpack, first=first, second=second, piece=piece),
         [(v.shape, F32) for v in weights],
-        [*(pltpu.VMEM(v.shape, F32) for v in weights),
-         pltpu.VMEM((devices * share, n), F32), pltpu.SemaphoreType.DMA((7,))],
+        [*(pltpu.VMEM(v.shape, F32) for v in weights), pltpu.VMEM((devices, share, n), F32),
+         pltpu.VMEM((2, devices, piece, n), BF16), pltpu.SemaphoreType.DMA((7,))],
         hbm_out=range(7),
-    )(tab, whole, swap(whole))
-    t_1a, t_1b, t_2c, t_2b, t_2a, t_1c, t_1p = totals
+    )(tab, *parts, *(swap(v) for v in parts))
     grads = (
         grad_norm_1a, grad_norm_1b, grad_norm_1c, grad_norm_1p,
         grad_norm_2a, grad_norm_2b, grad_norm_2c,

time: 184 us -> 179 us (0.973)
  blocking collectives: 150 us -> 137 us
  waiting for transfers between devices: 0.02 us -> 4.1 us
  starting transfers between devices: 1.66 us -> 5.73 us
    all_to_all x12 -> x11, blocking collectives: 150 us -> 127 us  [gather(): return lax.all_to_all(send, AXES, 0, 0)]
    all_to_all x0 -> x1, blocking collectives: none -> 9.42 us  [body(): along = lax.all_to_all(mine, 'batch', 0, 0, axis_index_groups=columns_of)]
    ppermute x0 -> x3, starting transfers between devices: none -> 3.49 us  [body(): lax.ppermute(along, 'batch', [(i, i ^ k) for i in range(batch)])]
    ppermute x0 -> x3, waiting for transfers between devices: none -> 2.69 us  [body(): lax.ppermute(along, 'batch', [(i, i ^ k) for i in range(batch)])]
  transfers between devices with their start and end apart: 6 -> 12, of which waited for: 0 -> 5; matrix products, arithmetic and copies ran while one was open for 0% -> 0% of each run, Pallas kernels for 4% -> 4%
where the time goes in v6:
time: 179 us
  blocking collectives  137 us (77%)
  Pallas kernels  31.2 us (17%)
  starting transfers between devices  5.73 us (3%)
  waiting for transfers between devices  4.1 us (2%)
    all_to_all x11, blocking collectives, gather(): return lax.all_to_all(send, AXES, 0, 0)  127 us
    pallas_call x23, Pallas kernels, call(): pl.pallas_call(kernel, out_shape=tuple((jax.ShapeDtypeStruct(s, d) for s,...  31.2 us
    all_to_all x1, blocking collectives, body(): along = lax.all_to_all(mine, 'batch', 0, 0, axis_index_groups=columns_of)  9.42 us
  transfers between devices with their start and end apart: 12, of which 5 were waited for; matrix products, arithmetic and copies ran while one was open for 0% of the time, Pallas kernels for 4%

profile of v6, /device:TPU:0, one launch (start us, length us, event | category | flops | bytes accessed | tf_op | source)
XLA Modules:
  0.0 178.9 jit_solution(13540998168229128322)
XLA Ops:
  0.7 2.3 %f1.1 = (f32[8,128]{1,0:T(8,128)S(1)}, bf16[28,64,256]{2,1,0:T(8,128)(2,1)S(1)}, bf16[28,64,256]{2,1,0:T(8,128)(2,1)S(1)}, f32[28,64,128]{2,1,0:T(8,128)S(1)}, f...) custom-call(s32[1]{0:T(128)} %bitcast.place_at, s32[2]{0:T(128)} %group_at.1, s32[3]{0:T(128)} %width_at.1, ...), custom_call_target="tpu_custom_call" | custom-call | tf_op jit(solution)/shard_map/f1/pallas_call | solution.py:33
  3.8 14.2 %all_to_all.60.got = f32[32,1,640]{2,1,0:T(1,128)S(1)} all-to-all(f32[32,1,640]{2,1,0:T(1,128)S(1)} %get-tuple-element.155), channel_id=1, replica_groups=mesh['rows'=2,'batch'=16] {'rows','batch'}, dimensions={0} | all-to-all | bytes 163840 | tf_op jit(solution)/shard_map/all_to_all | solution.py:1241
  19.0 1.9 %f2.1 = (bf16[29,32,768]{2,1,0:T(8,128)(2,1)S(1)}, f32[28,32,128]{2,1,0:T(8,128)S(1)}, f32[32,1,1024]{2,1,0:T(1,128)S(1)}, f32[32,1,128]{2,1,0:T(1,128)S(1)}, f3...) custom-call(f32[8,128]{1,0:T(8,128)S(1)} %get-tuple-element.141.tab, ...), custom_call_target="tpu_custom_call" | custom-call | tf_op jit(solution)/shard_map/f2/pallas_call | solution.py:33
  20.8 9.6 %all_to_all.61.got = f32[32,1,1024]{2,1,0:T(1,128)S(1)} all-to-all(f32[32,1,1024]{2,1,0:T(1,128)S(1)} %get-tuple-element.164), channel_id=1, replica_groups=mesh['rows'=2,'batch'=16] {'rows','batch'}, dimensions={0} | all-to-all | bytes 262144 | tf_op jit(solution)/shard_map/all_to_all | solution.py:1241
  31.1 9.4 %all_to_all.62.got.got_act = f32[32,1,640]{2,1,0:T(1,128)S(1)} all-to-all(f32[32,1,640]{2,1,0:T(1,128)S(1)} %get-tuple-element.167), channel_id=1, replica_groups=mesh['rows'=2,'batch'=16] {'rows','batch'}, dimensions={0} | all-to-all | bytes 163840 | tf_op jit(solution)/shard_map/all_to_all | solution.py:1241
  40.6 1.4 f4.1
  42.6 1.1 g_xz.1
  43.7 9.7 %all_to_all.63.got.pair_got.got_q = bf16[32,16,128]{2,1,0:T(8,128)(2,1)S(1)} all-to-all(bf16[32,16,128]{2,1,0:T(8,128)(2,1)S(1)} %get-tuple-element.182), channel_id=1, replica_groups=mesh['rows'=2,'batch'=16] {'rows','batch'}, dimensions={0} | all-to-all | bytes 262144 | tf_op jit(solution)/shard_map/all_to_all | solution.py:1241
  53.5 1.1 f5.1
  54.5 9.6 %all_to_all.64.got.got_a = f32[32,1,768]{2,1,0:T(1,128)S(1)} all-to-all(f32[32,1,768]{2,1,0:T(1,128)S(1)} %get-tuple-element.187), channel_id=1, replica_groups=mesh['rows'=2,'batch'=16] {'rows','batch'}, dimensions={0} | all-to-all | bytes 196608 | tf_op jit(solution)/shard_map/all_to_all | solution.py:1241
  64.8 9.2 %all_to_all.65.got = f32[32,1,640]{2,1,0:T(1,128)S(1)} all-to-all(f32[32,1,640]{2,1,0:T(1,128)S(1)} %get-tuple-element.190), channel_id=1, replica_groups=mesh['rows'=2,'batch'=16] {'rows','batch'}, dimensions={0} | all-to-all | bytes 163840 | tf_op jit(solution)/shard_map/all_to_all | solution.py:1241
  74.0 1.8 %b7.1 = (bf16[28,28,512]{2,1,0:T(8,128)(2,1)S(1)}, f32[28,32,512]{2,1,0:T(8,128)S(1)}, f32[32,4,256]{2,1,0:T(4,128)S(1)}, f32[2,512]{1,0:T(2,128)S(1)}) custom-call(f32[8,128]{1,0:T(8,128)S(1)} %get-tuple-element.141.tab, f32[32,1,640]{2,1,0:T(1,128)S(1)} %all_to_all.65.got, f32[32,1,128]{2,1,0:T(1,128)S(1)} %get-tuple-element.165.labels, ...), custom_call_target="tpu_custom_call" | custom-call | tf_op jit(solution)/shard_map/b7/pallas_call | solution.py:33
  75.8 9.6 %all_to_all.66.got = f32[32,4,256]{2,1,0:T(4,128)S(1)} all-to-all(f32[32,4,256]{2,1,0:T(4,128)S(1)} %get-tuple-element.193), channel_id=1, replica_groups=mesh['rows'=2,'batch'=16] {'rows','batch'}, dimensions={0} | all-to-all | bytes 262144 | tf_op jit(solution)/shard_map/all_to_all | solution.py:1241
  85.4 1.4 b8.1
  86.8 9.6 %all_to_all.67.got.got_b = f32[32,1,768]{2,1,0:T(1,128)S(1)} all-to-all(f32[32,1,768]{2,1,0:T(1,128)S(1)} %get-tuple-element.199), channel_id=1, replica_groups=mesh['rows'=2,'batch'=16] {'rows','batch'}, dimensions={0} | all-to-all | bytes 196608 | tf_op jit(solution)/shard_map/all_to_all | solution.py:1241
  96.3 1.7 b9.1
  98.0 9.6 %all_to_all.68.got.got_p.got_x = bf16[32,16,128]{2,1,0:T(8,128)(2,1)S(1)} all-to-all(bf16[32,16,128]{2,1,0:T(8,128)(2,1)S(1)} %get-tuple-element.206), channel_id=1, replica_groups=mesh['rows'=2,'batch'=16] {'rows','batch'}, dimensions={0} | all-to-all | bytes 262144 | tf_op jit(solution)/shard_map/all_to_all | solution.py:1241
  107.6 2.6 %b10.1 = (bf16[28,32,128]{2,1,0:T(8,128)(2,1)S(1)}, f32[28,32,512]{2,1,0:T(8,128)S(1)}, f32[32,2,896]{2,1,0:T(2,128)S(1)}, f32[3,2,128]{2,1,0:T(2,128)S(1)}, f32[28,32,128]{2,1,0:T(8,128)S(1)}) custom-call(f32[8,128]{1,0:T(8,128)S(1)} %get-tuple-element.141.tab, bf16[32,16,128]{2,1,0:T(8,128)(2,1)S(1)} %all_to_all.68.got.got_p.got_x, ...), custom_call_target="tpu_custom_call" | custom-call | tf_op jit(solution)/shard_map/b10/pallas_call | solution.py:33
  110.2 12.4 %all_to_all.69.got = f32[32,2,896]{2,1,0:T(2,128)S(1)} all-to-all(f32[32,2,896]{2,1,0:T(2,128)S(1)} %get-tuple-element.213), channel_id=1, replica_groups=mesh['rows'=2,'batch'=16] {'rows','batch'}, dimensions={0} | all-to-all | bytes 458752 | tf_op jit(solution)/shard_map/all_to_all | solution.py:1241
  122.6 3.1 %g_most.1 = (bf16[24,80,128]{2,1,0:T(8,128)(2,1)S(1)}, bf16[24,80,128]{2,1,0:T(8,128)(2,1)S(1)}, bf16[14,32,256]{2,1,0:T(8,128)(2,1)S(1)}, bf16[14,32,256]{2,1,0...) custom-call(f32[8,128]{1,0:T(8,128)S(1)} %get-tuple-element.141.tab, ...), custom_call_target="tpu_custom_call" | custom-call | tf_op jit(solution)/shard_map/g_most/pallas_call | solution.py:33
  125.9 1.5 b12.1
  127.4 1.1 b12_images.2
  129.6 1.1 b12_images.3
  130.6 1.1 g_xd.1
  132.0 24.2 %all_to_all.70.got = bf16[32,96,128]{2,1,0:T(8,128)(2,1)S(1)} all-to-all(bf16[32,96,128]{2,1,0:T(8,128)(2,1)S(1)} %pack_last.1), channel_id=1, replica_groups=mesh['rows'=2,'batch'=16] {'rows','batch'}, dimensions={0} | all-to-all | bytes 1572864 | tf_op jit(solution)/shard_map/all_to_all | solution.py:1241
  156.8 9.4 %all_to_all.71.refs_0_ = bf16[4,168,128]{2,1,0:T(8,128)(2,1)S(1)} all-to-all(bf16[4,168,128]{2,1,0:T(8,128)(2,1)S(1)} %add_all.1), channel_id=1, replica_groups={{0,4,8,12},{1,5,9,13},{2,6,10,14},{3,7,11,15},{16,20,24,28},{17,21,25,2..., dimensions={0} | all-to-all | bytes 344064 | tf_op jit(solution)/shard_map/all_to_all | solution.py:1424
  167.6 2.1 %collective-permute-start.5 = (bf16[4,168,128]{2,1,0:T(8,128)(2,1)S(1)}, bf16[4,168,128]{2,1,0:T(8,128)(2,1)S(1)}, u32[]{:S(2)}, u32[]{:S(2)}) collective-permute-start(bf16[4,168,128]{2,1,0:T(8,128)(2,1)S(1)} %all_to_all.71.refs_0_), channel_id=1, source_target_pairs={{0,1},{1,0},{2,3},{3,2},{4,5},{5,4},{6,7},{7,6},{8,9},{9,8},{10,11... | collective-permute-start | bytes 516104 | tf_op jit(solution)/shard_map/ppermute | solution.py:1426
  169.7 2.5 %b13.1 = (bf16[28,28,512]{2,1,0:T(8,128)(2,1)}, f32[3,2,512]{2,1,0:T(2,128)}, f32[3,2,512]{2,1,0:T(2,128)}, f32[3,2,128]{2,1,0:T(2,128)}, f32[3,2,128]{2,1,0:T(2...) custom-call(f32[8,128]{1,0:T(8,128)S(1)} %get-tuple-element.141.tab,, ...), custom_call_target="tpu_custom_call" | custom-call | tf_op jit(solution)/shard_map/b13/pallas_call | solution.py:33
  172.3 0.9 collective-permute-done.7.refs_3_
  173.3 1.7 collective-permute-done.6.refs_2_
  175.5 0.9 collective-permute-done.9.refs_5_
  176.9 1.8 %unpack.1 = (f32[128,512]{1,0:T(8,128)}, f32[1152,128]{1,0:T(8,128)}, f32[512,128]{1,0:T(8,128)}, f32[128,512]{1,0:T(8,128)}, f32[256,512]{1,0:T(8,128)}, /*index=5*/f32[1152,128]{1,0:T(8,128)}, f32[256,128]{1,0:T(8,128)}) custom-call(f32[8,128]{1,0:T(8,128)S(1)} %get-tuple-element.141.tab, bf16[4,168,128]{2,1,0:T(8,128)(2,1)S(1)} %all_to_all.71.refs_0_, ...), custom_call_target="tpu_custom_call" | custom-call | tf_op jit(solution)/shard_map/unpack/pallas_call | solution.py:33
  (57 shorter events, 8.0 us)
Async XLA Ops:
  0.6 2.4 %copy-start.7 = (bf16[3,3,128,128]{3,2,1,0:T(8,128)(2,1)S(1)}, bf16[3,3,128,128]{3,2,1,0:T(8,128)(2,1)}, u32[]{:S(2)}) copy-start(bf16[3,3,128,128]{3,2,1,0:T(8,128)(2,1)} %w2b) | copy-start | bytes 884740
  0.7 2.4 %copy-start.6 = (bf16[3,3,128,128]{3,2,1,0:T(8,128)(2,1)S(1)}, bf16[3,3,128,128]{3,2,1,0:T(8,128)(2,1)}, u32[]{:S(2)}) copy-start(bf16[3,3,128,128]{3,2,1,0:T(8,128)(2,1)} %w1b) | copy-start | bytes 884740
  0.7 17.4 %copy-start = (bf16[256,512]{1,0:T(8,128)(2,1)S(1)}, bf16[256,512]{1,0:T(8,128)(2,1)}, u32[]{:S(2)}) copy-start(bf16[256,512]{1,0:T(8,128)(2,1)} %w_p.3) | copy-start | bytes 786436
  3.0 15.9 %copy-start.4 = (bf16[256,128]{1,0:T(8,128)(2,1)S(1)}, bf16[256,128]{1,0:T(8,128)(2,1)}, u32[]{:S(2)}) copy-start(bf16[256,128]{1,0:T(8,128)(2,1)} %w.17) | copy-start | bytes 196612
  3.0 15.9 %copy-start.9 = (f32[2,3,128]{2,0,1:T(2,128)S(1)}, f32[2,3,128]{2,0,1:T(2,128)}, u32[]{:S(2)}) copy-start(f32[2,3,128]{2,0,1:T(2,128)} %param.27) | copy-start | bytes 9220
  3.3 14.8 %collective-permute-start = (bf16[28,64,256]{2,1,0:T(8,128)(2,1)S(1)}, bf16[28,64,256]{2,1,0:T(8,128)(2,1)S(1)}, u32[]{:S(2)}, u32[]{:S(2)}) collective-permute-start(bf16[28,64,256]{2,1,0:T(8,128)(2,1)S(1)} %get-tuple-element.156), channel_id=1, source_target_pairs={{0,16},{16,0},{1,17},{17,1},{2,18},{18,2},{3,19},{19,3},{4,20},{20... | collective-permute-start | bytes 2752520 | tf_op jit(solution)/shard_map/ppermute | solution.py:1249
  18.0 12.4 %copy-start.1 = (bf16[128,512]{1,0:T(8,128)(2,1)S(1)}, bf16[128,512]{1,0:T(8,128)(2,1)}, u32[]{:S(2)}) copy-start(bf16[128,512]{1,0:T(8,128)(2,1)} %w_c.5) | copy-start | bytes 393220
  18.0 12.4 %copy-start.12 = (f32[2,3,128]{2,0,1:T(2,128)S(1)}, f32[2,3,128]{2,0,1:T(2,128)}, u32[]{:S(2)}) copy-start(f32[2,3,128]{2,0,1:T(2,128)} %param.28) | copy-start | bytes 9220
  18.9 21.6 %copy-start.5 = (bf16[512,128]{1,0:T(8,128)(2,1)S(1)}, bf16[512,128]{1,0:T(8,128)(2,1)}, u32[]{:S(2)}) copy-start(bf16[512,128]{1,0:T(8,128)(2,1)} %w.16) | copy-start | bytes 393220
  19.0 21.6 %copy-start.8 = (f32[2,3,512]{2,0,1:T(2,128)S(1)}, f32[2,3,512]{2,0,1:T(2,128)}, u32[]{:S(2)}) copy-start(f32[2,3,512]{2,0,1:T(2,128)} %param.29) | copy-start | bytes 36868
  19.0 21.6 %copy-start.11 = (f32[2,3,512]{2,0,1:T(2,128)S(1)}, f32[2,3,512]{2,0,1:T(2,128)}, u32[]{:S(2)}) copy-start(f32[2,3,512]{2,0,1:T(2,128)} %param.30) | copy-start | bytes 36868
  42.6 10.9 %copy-start.14 = (f32[2,3,128]{2,0,1:T(2,128)S(1)}, f32[2,3,128]{2,0,1:T(2,128)}, u32[]{:S(2)}) copy-start(f32[2,3,128]{2,0,1:T(2,128)} %param.31) | copy-start | bytes 9220
  42.6 21.5 %copy-start.2 = (bf16[128,512]{1,0:T(8,128)(2,1)S(1)}, bf16[128,512]{1,0:T(8,128)(2,1)}, u32[]{:S(2)}) copy-start(bf16[128,512]{1,0:T(8,128)(2,1)} %w.15) | copy-start | bytes 393220
  42.6 21.5 %copy-start.13 = (f32[2,3,128]{2,0,1:T(2,128)S(1)}, f32[2,3,128]{2,0,1:T(2,128)}, u32[]{:S(2)}) copy-start(f32[2,3,128]{2,0,1:T(2,128)} %param.32) | copy-start | bytes 9220
  43.7 30.3 %copy-start.3 = (bf16[1,28,28,512]{3,2,1,0:T(8,128)(2,1)S(1)}, bf16[1,28,28,512]{3,2,1,0:T(8,128)(2,1)}, u32[]{:S(2)}) copy-start(bf16[1,28,28,512]{3,2,1,0:T(8,128)(2,1)} %param.34) | copy-start | bytes 2408452
  43.7 30.3 %copy-start.10 = (f32[2,3,512]{2,0,1:T(2,128)S(1)}, f32[2,3,512]{2,0,1:T(2,128)}, u32[]{:S(2)}) copy-start(f32[2,3,512]{2,0,1:T(2,128)} %param.33) | copy-start | bytes 36868
  125.8 6.1 %collective-permute-start.3 = (bf16[24,80,128]{2,1,0:T(8,128)(2,1)S(1)}, bf16[24,80,128]{2,1,0:T(8,128)(2,1)S(1)}, u32[]{:S(2)}, u32[]{:S(2)}) collective-permute-start(bf16[24,80,128]{2,1,0:T(8,128)(2,1)S(1)} %get-tuple-element.232), channel_id=1, source_target_pairs={{0,16},{16,0},{1,17},{17,1},{2,18},{18,2},{3,19},{19,3},{4,20},{20... | collective-permute-start | bytes 1474568 | tf_op jit(solution)/shard_map/ppermute | solution.py:1249
  128.5 3.3 %collective-permute-start.2 = (bf16[28,64,128]{2,1,0:T(8,128)(2,1)S(1)}, bf16[28,64,128]{2,1,0:T(8,128)(2,1)S(1)}, u32[]{:S(2)}, u32[]{:S(2)}) collective-permute-start(bf16[28,64,128]{2,1,0:T(8,128)(2,1)S(1)} %get-tuple-element.221.dn_oth), channel_id=1, source_target_pairs={{0,16},{16,0},{1,17},{17,1},{2,18},{18,2},{3,19},{19,3},{4,20},{20... | collective-permute-start | bytes 1376264 | tf_op jit(solution)/shard_map/ppermute | solution.py:1249
  129.0 2.8 %collective-permute-start.1 = (bf16[14,32,256]{2,1,0:T(8,128)(2,1)S(1)}, bf16[14,32,256]{2,1,0:T(8,128)(2,1)S(1)}, u32[]{:S(2)}, u32[]{:S(2)}) collective-permute-start(bf16[14,32,256]{2,1,0:T(8,128)(2,1)S(1)} %get-tuple-element.227), channel_id=1, source_target_pairs={{0,16},{16,0},{1,17},{17,1},{2,18},{18,2},{3,19},{19,3},{4,20},{20... | collective-permute-start | bytes 688136 | tf_op jit(solution)/shard_map/ppermute | solution.py:1249
  129.1 2.7 %collective-permute-start.4 = (bf16[8,80,128]{2,1,0:T(8,128)(2,1)S(1)}, bf16[8,80,128]{2,1,0:T(8,128)(2,1)S(1)}, u32[]{:S(2)}, u32[]{:S(2)}) collective-permute-start(bf16[8,80,128]{2,1,0:T(8,128)(2,1)S(1)} %get-tuple-element.234), channel_id=1, source_target_pairs={{0,16},{16,0},{1,17},{17,1},{2,18},{18,2},{3,19},{19,3},{4,20},{20... | collective-permute-start | bytes 491528 | tf_op jit(solution)/shard_map/ppermute | solution.py:1249
  166.2 7.0 %collective-permute-start.7 = (bf16[4,168,128]{2,1,0:T(8,128)(2,1)S(1)}, bf16[4,168,128]{2,1,0:T(8,128)(2,1)S(1)}, u32[]{:S(2)}, u32[]{:S(2)}) collective-permute-start(bf16[4,168,128]{2,1,0:T(8,128)(2,1)S(1)} %all_to_all.71.refs_0_), channel_id=1, source_target_pairs={{0,3},{1,2},{2,1},{3,0},{4,7},{5,6},{6,5},{7,4},{8,11},{9,10},{10,... | collective-permute-start | bytes 516104 | tf_op jit(solution)/shard_map/ppermute | solution.py:1426
  166.9 8.1 %collective-permute-start.6 = (bf16[4,168,128]{2,1,0:T(8,128)(2,1)S(1)}, bf16[4,168,128]{2,1,0:T(8,128)(2,1)S(1)}, u32[]{:S(2)}, u32[]{:S(2)}) collective-permute-start(bf16[4,168,128]{2,1,0:T(8,128)(2,1)S(1)} %all_to_all.71.refs_0_), channel_id=1, source_target_pairs={{0,2},{1,3},{2,0},{3,1},{4,6},{5,7},{6,4},{7,5},{8,10},{9,11},{10,... | collective-permute-start | bytes 516104 | tf_op jit(solution)/shard_map/ppermute | solution.py:1426
  167.6 7.4 %collective-permute-start.5 = (bf16[4,168,128]{2,1,0:T(8,128)(2,1)S(1)}, bf16[4,168,128]{2,1,0:T(8,128)(2,1)S(1)}, u32[]{:S(2)}, u32[]{:S(2)}) collective-permute-start(bf16[4,168,128]{2,1,0:T(8,128)(2,1)S(1)} %all_to_all.71.refs_0_), channel_id=1, source_target_pairs={{0,1},{1,0},{2,3},{3,2},{4,5},{5,4},{6,7},{7,6},{8,9},{9,8},{10,11... | collective-permute-start | bytes 516104 | tf_op jit(solution)/shard_map/ppermute | solution.py:1426
  172.2 3.3 %collective-permute-start.8 = (bf16[4,168,128]{2,1,0:T(8,128)(2,1)S(1)}, bf16[4,168,128]{2,1,0:T(8,128)(2,1)S(1)}, u32[]{:S(2)}, u32[]{:S(2)}) collective-permute-start(bf16[4,168,128]{2,1,0:T(8,128)(2,1)S(1)} %all_to_all.71.refs_0_), channel_id=1, source_target_pairs={{0,16},{16,0},{1,17},{17,1},{2,18},{18,2},{3,19},{19,3},{4,20},{20... | collective-permute-start | bytes 516104 | tf_op jit(solution)/shard_map/ppermute | solution.py:1249
  175.0 1.4 collective-permute-start.9
  175.0 1.7 collective-permute-start.10
  175.5 1.4 collective-permute-start.11

commit v7 on v6

--- a/solution.py
+++ b/solution.py
@@ -380,7 +380,7 @@
     conv_stats(z, xs, pair, (slice(0, 3 * n), w_even[...], 1), send, extra)
 
 
-def expand(act, w, z, send, act_sum):
+def project(act, w, z):
     rows, chans = z.shape[0], z.shape[2]
     step = rows // 7
     squares = zeros8(chans)
@@ -389,8 +389,12 @@
         z[step * c : step * (c + 1)] = values.reshape(step, COLS, chans)
         parts = values.reshape(-1, 8, chans)
         squares = squares + jnp.sum(parts * parts, axis=0)
-    squares = down(squares)
-    spread(send, [act_sum, *(squares[:, lanes] for lanes in columns(chans))])
+    return down(squares)
+
+
+def expand(act, w, z, send, act_sum):
+    squares = project(act, w, z)
+    spread(send, [act_sum, *(squares[:, lanes] for lanes in columns(z.shape[2]))])
 
 
 def join(pieces):
@@ -467,7 +471,15 @@
     return mm_tn(flat(centred[...]), flat(both[...])), stack([down(v) for v in sums])
 
 
-def put_pair(send, at, share, product, sums):
+def rows_of(line):
+    return stack([line[:, lanes] for lanes in columns(line.shape[1])])
+
+
+def line_of(rows):
+    return join([rows[k : k + 1, :] for k in range(rows.shape[0])])
+
+
+def put_pair(send, at, share, product):
     devices, n = send.shape[0], LANES
     missing = devices * share - n
     for h in (0, 1):
@@ -476,7 +488,6 @@
             values = stack([values, jnp.zeros((missing, n), F32)])
         first = at + share * h
         send[:, first : first + share, :] = values.reshape(devices, share, n).astype(BF16)
-    put_split(send, at + 2 * share, sums)
 
 
 def pass_pair(send, at, got, got_at, share, marks, groups):
@@ -598,17 +609,16 @@
 def pair_1(tab, stats, z, norm, keeps, act, act_sum, send, slope, both, centred, *, share):
     product, sums = pair_products(tab, z, norm, keeps, act, act_sum[...], slope, both, centred)
     put_split(send, 0, stats[...])
-    put_pair(send, 4, share, product, sums)
-
-
-def put_shares(xz, send, part):
+    put_pair(send, 4, share, product)
+    put_split(send, 4 + 2 * share, sums)
+
+
+def put_shares(xz, send):
     n, devices = LANES, send.shape[0]
     share = xz.shape[0] // devices
     pieces = xz[...].reshape(devices, share, n)
-    first = (share + 1) // 2 * part
-    for q in range(first, (share + 1) // 2 if part == 0 else share):
-        at = n * (2 + q - first)
-        send[:, :, at : at + n] = pieces[:, q : q + 1, :]
+    for q in range(share):
+        send[:, :, n * (2 + q) : n * (3 + q)] = pieces[:, q : q + 1, :]
 
 
 def f5(tab, got, labels, z_in, norm, w_two, w_last, xz, x3, z, send, keeps):
@@ -640,26 +650,55 @@
     conv_stats(
         z, x3, (lanes, w_two[...], (0, 1)), (lanes, w_last[...], 2), send.at[:, :, 0 : 2 * n]
     )
-    put_shares(xz, send, 0)
-
-
-def f6(tab, got, labels, z_in, norm, w, act, z, send, keeps):
+    put_shares(xz, send)
+
+
+def f6(tab, got, labels, z_in, norm, w, act, z, send, keeps, slope, q, both, centred, *, share):
     sums = activate(tab, got, labels, z_in, norm, act, keeps)
-    expand(act, w, z, send, sums)
-
-
-def b7(tab, got, labels, joined, z, norm, w, cot, result, grad_pre, send, keeps, wide):
+    pixels = 1.0 * z.shape[0] * (COLS - 4)
+    squares = project(act, w, z)
+    first = through(sums, w[...])
+    second = squares - first * first / pixels
+    product, q[...] = pair_products(tab, z_in, norm, keeps, act, sums, slope, both, centred)
+    put_split(send, 0, sums)
+    low = rows_of(second).astype(BF16)
+    send[:, 2 : 2 + low.shape[0], :] = jnp.broadcast_to(low[None], (send.shape[0], *low.shape))
+    put_pair(send, 2 + low.shape[0], share, product)
+
+
+def gathered_moments(got, marks, label, w, pixels):
+    devices, chans = got.shape[0], w.shape[1]
+    low = (got[:, k : k + 1, :].astype(F32).reshape(devices, LANES).astype(BF16) for k in (0, 1))
+    means = sum(mm(v, w[...]) for v in low) * (1.0 / pixels)
+    blocks = chans // LANES
+    moments_2 = join(
+        [got[:, 2 + k : 3 + k, :].astype(F32).reshape(devices, LANES) for k in range(blocks)]
+    )
+    same = join([(marks == label).astype(F32).reshape(devices, LANES)] * blocks)
+    images = tiled(group_count(marks, label), chans)
+    mean = down(means * same) / images
+    away = means - mean
+    variance = down((moments_2 + pixels * (away * away)) * same) / (images * pixels)
+    return mean, lax.rsqrt(variance + EPSILON)
+
+
+def b7(
+    tab, got, labels, joined, z, norm, w, cot, slope_in, z_in, keeps_in, q,
+    result, grad_pre, send, keeps, d_in, wide, low, *, share, p_at,
+):
     rows, chans = z.shape[0], z.shape[2]
     cols = COLS - 4
     pixels = 1.0 * rows * cols
-    mean, rstd = expanded_moments(got, labels[...], tab, w, pixels)
-    gain, shift = gain_of(norm, entry(tab, OWN)), shift_of(norm, entry(tab, OWN))
+    marks, label = labels[...], entry(tab, OWN)
+    mean, rstd = gathered_moments(got, marks, label, w, pixels)
+    gain, shift = gain_of(norm, label), shift_of(norm, label)
     keeps[0:1, :] = mean
     keeps[1:2, :] = rstd
     gate = 0.25 * tiled(entry(tab, GATE), chans)
     scale = 0.5 * rstd * gain * gate
     bias = 0.5 * (shift - mean * rstd * gain) * gate
     wide[...] = jnp.zeros(wide.shape, F32)
+    a_gate = rstd * gain * gate
 
     def put(i, carry):
         sums, products = carry
@@ -671,11 +710,18 @@
         result[i] = (u + p)[0:cols].astype(BF16)
         g = wide[...] * ((0.5 + 0.5 * t) * (1.0 + u - p))
         grad_pre[i] = g
+        low[i] = (a_gate * g).astype(BF16)
         return sums + fold(g), products + fold(g * (zz - mean))
 
     start = zeros8(chans)
     sums, products = lax.fori_loop(0, rows, put, (start, start), unroll=2)
-    spread(send, [down(sums) * gate, down(products) * rstd * gate])
+    inner = inner_sums(low, w, slope_in, z_in, keeps_in, d_in)
+    blocks = chans // LANES
+    put_split(send, 0, rows_of(down(sums) * gate))
+    put_split(send, 2 * blocks, rows_of(down(products) * rstd * gate))
+    put_split(send, 4 * blocks, stack(inner))
+    put_split(send, 4 * blocks + 4, q[...])
+    pass_pair(send, 4 * blocks + 8, got, p_at, share, marks, norm.shape[0])
 
 
 def lane_sums(got, marks, channels):
@@ -729,46 +775,36 @@
     return down(sums), down(products) * rstd
 
 
-def b8(
-    tab, got, labels, grad_pre, z, norm, keeps, w, z_in, norm_in, keeps_in, xz,
-    dz, dout, send, grad_norm, d,
-):
-    rows, chans = z.shape[0], z.shape[2]
-    pixels = 1.0 * rows * (COLS - 4)
-    marks = labels[...]
-    sums_of = lane_sums(got, marks, chans)
-    mean, a, b, c = backward_norm(tab, sums_of, marks, norm, keeps, pixels, grad_norm)
-    a = a * (0.25 * tiled(entry(tab, GATE), norm.shape[2]))
-    keep = valid_cols(chans)
-
-    def put(i, carry):
-        v = a * grad_pre[i] + b * (z[i] - mean) + c
-        dz[i] = jnp.where(keep, v, 0.0).astype(BF16)
-        return carry
-
-    lax.fori_loop(0, rows, put, 0, unroll=2)
-    d[...] = mm_nt(flat(dz[...]), w[...]).reshape(d.shape)
-    sums = slope_sums(tab, d, z_in, norm_in, keeps_in, dout)
-    spread(send.at[:, :, 0 : 2 * LANES], sums)
-    put_shares(xz, send, 1)
-
-
 def b9(
-    tab, got, labels, dout_in, z, norm, keeps, b_two, b_last, z_in, norm_in, keeps_in, x_sum, pair_got,
-    dz, dout, send, grad_norm, d3, d, *, share,
+    tab, got, labels, norm_c, keeps_c, w_c, got_act, act, slope, d_in, z, norm, keeps,
+    b_two, b_last, z_in, norm_in, keeps_in, x_sum, pair_got,
+    dz, dout, send, own_sums, d3, d, *, share,
 ):
     rows = z.shape[0]
     pixels = 1.0 * rows * (COLS - 4)
-    marks = labels[...]
-    sums_of = lane_sums(got.at[:, :, 0 : 2 * LANES], marks, LANES)
-    mean, a, b, c = backward_norm(tab, sums_of, marks, norm, keeps, pixels, grad_norm)
+    marks, label = labels[...], entry(tab, OWN)
+    blocks = norm_c.shape[2] // LANES
+    at = 4 * blocks
+    wide = [
+        line_of(over_group(get_split(got, 2 * blocks * k, blocks), marks, label)) for k in (0, 1)
+    ]
+    inner = over_group(get_split(got, at, 2), marks, label)
+    m, line, (a, b, c), found = pair_solve(
+        tab, marks, (norm_c, keeps_c), (norm, keeps), [*wide, inner[0:1], inner[1:2]], w_c,
+        get_split(got_act, 0, 1), get_split(got, at + 4, 2),
+        got[:, at + 8 : at + 8 + 2 * share, :].astype(F32), pixels,
+    )
+    own_sums[0:1, :] = found[0]
+    own_sums[1:2, :] = found[1]
+    inner_grad(act, m, line, slope, d_in, d)
+    mean = keeps[0:1, :]
     keep = valid_cols(LANES)
     n = LANES
     d3[0] = jnp.zeros(d3.shape[1:], BF16)
     d3[rows + 1] = jnp.zeros(d3.shape[1:], BF16)
 
     def put(i, carry):
-        v = a * dout_in[i] + b * (z[i] - mean) + c
+        v = a * d[i] + b * (z[i] - mean) + c
         v = jnp.where(keep, v, 0.0)
         d3[i + 1, :, 0:n] = pltpu.roll(v, COLS - 1, 0).astype(BF16)
         low = v.astype(BF16)
@@ -806,7 +842,7 @@
 
     def sum_up(i, carry):
         sums, prod_c, prod_p = carry
-        g = (grad_pre[i] + d[i]).astype(BF16).astype(F32) * slope[i]
+        g = (grad_pre[i] + d[i]) * slope[i]
         grad_pre_2[i] = g
         low[i] = (a_c * g).astype(BF16)
         return (
@@ -819,9 +855,14 @@
     sums, prod_c, prod_p = lax.fori_loop(0, rows, sum_up, (start, start, start), unroll=2)
     wide = [down(sums), down(prod_c) * rstd_c, down(prod_p) * rstd_p]
     inner = inner_sums(low, w_c, slope_in, z_in, keeps_in, d_in)
-    parts = [stack([v[:, 0 : chans // 2], v[:, chans // 2 :]]) for v in wide]
-    values = join([*parts, stack(inner)])
-    send[...] = jnp.broadcast_to(values[None], send.shape)
+    blocks = chans // LANES
+    put_split(send, 0, rows_of(wide[0]))
+    put_split(send, 2 * blocks, rows_of(wide[1]))
+    put_split(send, 4 * blocks, stack(inner))
+    last = rows_of(wide[2]).astype(BF16)
+    send[:, 4 * blocks + 4 : 5 * blocks + 4, :] = jnp.broadcast_to(
+        last[None], (send.shape[0], *last.shape)
+    )
 
 
 def inner_sums(low, w, slope, z, keeps, d_in):
@@ -957,11 +998,7 @@
     for g in range(norm.shape[0]):
         norm_v[g, 0:1, :] = totals[g][1]
         norm_v[g, 1:2, :] = totals[g][0]
-    found = get_split(got, at + 4, 2)
-    for g in range(norm.shape[0]):
-        total = over_group(found, marks, float(g)) / group_count(marks, float(g))
-        inner_v[g, 0:1, :] = total[1:2]
-        inner_v[g, 1:2, :] = total[0:1]
+    norm_from_owners(get_split(got, at + 4, 2), marks, inner_v)
     for k, (value, out) in enumerate(((norm_v, grad_norm), (inner_v, grad_inner))):
         copies.append(pltpu.make_async_copy(value, out, sems.at[held + k]))
         copies[-1].start()
@@ -1036,27 +1073,42 @@
 
 
 def g_most(
-    tab, act_2b, dz_2c, x3, dz_2b, joined, dz_2a, act_1b, xee, w_p,
+    tab, act_2b, x3, dz_2b, joined, dz_2a, act_1b, xee, w_p,
     got, labels, norm_c, norm_p, keeps, grad_pre_2, zc, zp,
-    kept, sent, gs_own, gs_oth, grad_norm_c, grad_norm_p, own10, packed, dz_1c, dz_p,
+    got_2c, norm_2c, keeps_2c, grad_pre, z_2c,
+    kept, sent, gs_own, gs_oth, grad_norm_c, grad_norm_p, grad_norm_2c, own10, packed, dz_1c, dz_p, dz_2c,
 ):
     rows, outer = dz_2b.shape[0], zc.shape[2]
     pixels = 1.0 * rows * (COLS - 4)
     marks = labels[...]
 
-    totals = [group_sum(got, marks, float(g)) for g in range(norm_c.shape[0])]
-    side = outer // 2
-
-    def line(total, k):
-        return join([total[h : h + 1, side * k : side * (k + 1)] for h in (0, 1)])
-
-    lines = [[line(total, k) for k in range(3)] for total in totals]
+    blocks = outer // LANES
     label = entry(tab, OWN)
+
+    def wide_sums(source, count):
+        values = [get_split(source, 2 * blocks * k, blocks) for k in range(count)]
+        return [
+            [line_of(over_group(v, marks, float(g))) for v in values]
+            for g in range(norm_c.shape[0])
+        ]
+
+    lines = wide_sums(got, 2)
+    last = got[:, 4 * blocks + 4 : 5 * blocks + 4, :].astype(F32)
+    for g, line in enumerate(lines):
+        line.append(line_of(over_group(last, marks, float(g))))
     for k in range(2):
         own10[:, outer * k : outer * (k + 1)] = own_of([v[k] for v in lines], label)
-        inner = [total[k : k + 1, 3 * side :] for total in totals]
+    inner = over_group(get_split(got, 4 * blocks, 2), marks, label)
+    for k in range(2):
         at = 2 * outer + LANES * k
-        own10[:, at : at + LANES] = own_of(inner, label)
+        own10[:, at : at + LANES] = inner[k : k + 1]
+    lines_2c = wide_sums(got_2c, 2)
+    mean, a, b, c = backward_norm(
+        tab, lambda g: (lines_2c[g][0], lines_2c[g][1]), marks, norm_2c, keeps_2c, pixels,
+        grad_norm_2c,
+    )
+    gate = 0.25 * tiled(entry(tab, GATE), outer)
+    normed_grad(dz_2c, grad_pre, z_2c, mean, a * gate, b, c)
     coefs = backward_norm(
         tab, lambda g: (lines[g][0], lines[g][1]), marks, norm_c, keeps.at[0:2], pixels, grad_norm_c
     )
@@ -1161,12 +1213,11 @@
     return out
 
 
-def add_all(got, labels, norm, keeps_all, got_a, got_b, out, *, at, pixels):
+def add_all(got, labels, norm, keeps_all, xz_got, found, out, *, at, pixels):
     devices, n = got.shape[0], LANES
     half = devices // 2
-    split = got_a.shape[2] // n - 2
-    share = split + got_b.shape[2] // n - 2
-    piece = (out.shape[1] - share) // 2
+    share = xz_got.shape[2] // n - 2
+    piece = (out.shape[1] - share - 4) // 2
     marks = labels[...]
     value = jnp.sum(got[:, piece : piece + share, :].astype(F32), axis=0)
     sums = last_sums(got.at[:, at : at + 4, :], marks, norm.shape[0])
@@ -1176,9 +1227,7 @@
         b = -(rstd * rstd * norm[g, 0:1, :]) * sums[g][1] / count
         same = (marks == float(g)).astype(F32)
         rows = [
-            jnp.sum(source[:, :, n * (2 + q) : n * (3 + q)] * same, axis=0)
-            for source, count_q in ((got_a, split), (got_b, share - split))
-            for q in range(count_q)
+            jnp.sum(xz_got[:, :, n * (2 + q) : n * (3 + q)] * same, axis=0) for q in range(share)
         ]
         value = value + jnp.concatenate(rows, axis=0) * b
     for k in (0, 1):
@@ -1186,14 +1235,17 @@
         out[:, piece * k : piece * (k + 1), :] = jnp.broadcast_to(
             total[None], (out.shape[0], piece, n)
         )
-    out[:, 2 * piece :, :] = jnp.broadcast_to(value.astype(BF16)[None], (out.shape[0], share, n))
-
-
-def unpack(tab, *refs, first, second, piece):
-    parts, outs, values = refs[: 2 * NEAR], refs[2 * NEAR : 2 * NEAR + 7], refs[2 * NEAR + 7 :]
-    *values, tall, packed, sems = values
+    out[:, 2 * piece : 2 * piece + share, :] = jnp.broadcast_to(
+        value.astype(BF16)[None], (out.shape[0], share, n)
+    )
+    put_split(out, 2 * piece + share, found[...])
+
+
+def unpack(tab, labels, *refs, first, second, piece):
+    parts, outs, values = refs[: 2 * NEAR], refs[2 * NEAR : 2 * NEAR + 8], refs[2 * NEAR + 8 :]
+    *values, tall, packed, found, sems = values
     half, minor = half_of(tab), half_of(tab, MINOR)
-    far = parts[0].shape[0]
+    far, share = parts[0].shape[0], tall.shape[1]
     for k, part in enumerate(parts):
         core = half if k < NEAR else 1 - half
         base = core * (far * NEAR) + lax.bitwise_xor(minor, jnp.int32(k % NEAR))
@@ -1202,7 +1254,9 @@
             owner = base + NEAR * z
             for h in (0, 1):
                 packed[h, owner] = part[z, piece * h : piece * (h + 1), :]
-            tall[owner] = part[z, 2 * piece :, :].astype(F32)
+            tall[owner] = part[z, 2 * piece : 2 * piece + share, :].astype(F32)
+            sums = part[z, 2 * piece + share :, :].astype(F32)
+            found[owner] = sums[0:2] + sums[2:4]
             return carry
 
         lax.fori_loop(0, far, place, 0, unroll=min(far, 4))
@@ -1226,15 +1280,24 @@
     for k, value in enumerate(values[0:5]):
         at = take_rows(source, at, value)
         copies[k].start()
-    w_1b, w_1a = values[5:7]
+    w_1b, w_1a, grad_norm = values[5:8]
     size = second * piece
     w_1b[0:size] = last[0].astype(F32)
     w_1b[size:] = last[1][0 : w_1b.shape[0] - size].astype(F32)
     copies[5].start()
     w_1a[...] = flat(tall[...])[0 : w_1a.shape[0]]
     copies[6].start()
+    norm_from_owners(found[...], labels[...], grad_norm)
+    copies[7].start()
     for copy in copies:
         copy.wait()
+
+
+def norm_from_owners(found, marks, grad_norm):
+    for g in range(grad_norm.shape[0]):
+        total = over_group(found, marks, float(g)) / group_count(marks, float(g))
+        grad_norm[g, 0:1, :] = total[1:2]
+        grad_norm[g, 1:2, :] = total[0:1]
 
 
 def gather(send):
@@ -1338,31 +1401,37 @@
     s4, xz, x_sum = tie(s4, xz, x_sum)
     g4 = gather(s4)
     x3, z_2b, s5, k_2a = stage(
-        f5, [((rows + 2, COLS, 3 * n), BF16), maps(n), send(2 + (share + 1) // 2), mean_scale(n)]
+        f5, [((rows + 2, COLS, 3 * n), BF16), maps(n), send(2 + share), mean_scale(n)]
     )(tab, g4, labels, z_2a, norm_2a, w_two, w_last, xz)
     g5 = gather(s5)
-    act_2b, z_2c, s6, k_2b = stage(
-        f6, [maps(n, BF16), maps(outer), send(1 + outer // n), mean_scale(n)]
+    wide_rows = outer // n
+    p_6 = 2 + wide_rows
+    high_6 = -(-(p_6 + 2 * share_1) // 16) * 16
+    act_2b, z_2c, s6, k_2b, slope_2b, q_2b = stage(
+        functools.partial(f6, share=share_1),
+        [maps(n, BF16), maps(outer), ((devices, high_6, n), BF16), mean_scale(n), maps(n),
+         ((2, n), F32)],
+        [scratch(2 * n, BF16), scratch(n, BF16)],
     )(tab, g5, labels, z_2b, norm_2b, w_2c)
     g6 = gather(s6)
-    result, grad_pre, s7, k_2c = stage(
-        b7, [(cotangent.shape[1:], BF16), maps(outer), send(2, outer), mean_scale(outer)],
-        [pltpu.VMEM((COLS, outer), F32)],
-    )(tab, g6, labels, joined, z_2c, norm_2c, w_2c, cotangent[0])
+    high_7 = -(-(4 * wide_rows + 8 + 2 * share_1) // 16) * 16
+    result, grad_pre, s7, k_2c, d_2b = stage(
+        functools.partial(b7, share=share_1, p_at=p_6),
+        [(cotangent.shape[1:], BF16), maps(outer), ((devices, high_7, n), BF16),
+         mean_scale(outer), maps(n)],
+        [pltpu.VMEM((COLS, outer), F32), scratch(outer, BF16)],
+    )(tab, g6, labels, joined, z_2c, norm_2c, w_2c, cotangent[0], slope_2b, z_2b, k_2b, q_2b)
     g7 = gather(s7)
-    dz_2c, dout_2b, s8, grad_norm_2c = stage(
-        b8, [maps(outer, BF16), maps(n), send(2 + share // 2), *params(norm_2c)], [scratch(n)]
-    )(tab, g7, labels, grad_pre, z_2c, norm_2c, k_2c, w_2c, z_2b, norm_2b, k_2b, xz)
-    g8 = gather(s8)
-    dz_2b, dout_2a, s9, grad_norm_2b = stage(
+    dz_2b, dout_2a, s9, found_2b = stage(
         functools.partial(b9, share=share_1),
-        [maps(n, BF16), maps(n), ((devices, high, n), BF16), *params(norm_2b)],
+        [maps(n, BF16), maps(n), ((devices, high, n), BF16), ((2, n), F32)],
         [pltpu.VMEM((rows + 2, COLS, 3 * n), BF16), scratch(n)],
-    )(tab, g8, labels, dout_2b, z_2b, norm_2b, k_2b, b_two, b_last, z_2a, norm_2a, k_2a, x_sum, g4)
+    )(tab, g7, labels, norm_2c, k_2c, w_2c, g6, act_2b, slope_2b, d_2b, z_2b, norm_2b, k_2b,
+      b_two, b_last, z_2a, norm_2a, k_2a, x_sum, g4)
     g9 = gather(s9)
     dz_2a, grad_pre_2, s10, grad_norm_2a, d_1b = stage(
         b10,
-        [maps(n, BF16), maps(outer), ((devices, 2, 3 * outer // 2 + n), F32), *params(norm_2a), maps(n)],
+        [maps(n, BF16), maps(outer), ((devices, 5 * wide_rows + 4, n), BF16), *params(norm_2a), maps(n)],
         [scratch(outer), scratch(outer, BF16)],
     )(tab, g9, labels, dout_2a, z_2a, norm_2a, k_2a, w_2a, grad_pre, slope, z_1c, z_1p, k_cp,
       norm_1c, w_1c, slope_1b, z_1b, k_1b)
@@ -1375,12 +1444,14 @@
         piece += 16
     first, second = -(-most_rows // (2 * piece)), -(-rows_1b // (2 * piece))
     part, part_1b = ((first, piece, n), BF16), ((second, piece, n), BF16)
-    kept, sent, gs_own, gs_send, grad_norm_1c, grad_norm_1p, own10 = stage(
+    kept, sent, gs_own, gs_send, grad_norm_1c, grad_norm_1p, grad_norm_2c, own10 = stage(
         g_most,
-        [part, part, half_map, half_map, *params(norm_1c, norm_1p), ((1, 2 * outer + 2 * n), F32)],
-        [pltpu.VMEM((2 * first * piece, n), BF16), scratch(outer, BF16), scratch(outer, BF16)],
-    )(tab, act_2b, dz_2c, x3, dz_2b, joined, dz_2a, act_1b, xee, w_1p,
-      g10, labels, norm_1c, norm_1p, k_cp, grad_pre_2, z_1c, z_1p)
+        [part, part, half_map, half_map, *params(norm_1c, norm_1p, norm_2c),
+         ((1, 2 * outer + 2 * n), F32)],
+        [pltpu.VMEM((2 * first * piece, n), BF16), *(scratch(outer, BF16) for _ in range(3))],
+    )(tab, act_2b, x3, dz_2b, joined, dz_2a, act_1b, xee, w_1p,
+      g10, labels, norm_1c, norm_1p, k_cp, grad_pre_2, z_1c, z_1p,
+      g7, norm_2c, k_2c, grad_pre, z_2c)
     got, gs_for = swap(sent), swap(gs_send)
     half_in = ((rows, cols_in, n), BF16)
     d2, kept_1b, sent_1b, found_1b = stage(
@@ -1418,15 +1489,15 @@
     far = batch // NEAR
     (mine,) = stage(
         functools.partial(add_all, at=stats_at, pixels=pixels),
-        [((far, 2 * piece + share, n), BF16)],
-    )(g12, labels, norm_1a, k_all, g5, g8)
+        [((far, 2 * piece + share + 4, n), BF16)],
+    )(g12, labels, norm_1a, k_all, g5, found_2b)
     columns_of = [[k + NEAR * z for z in range(far)] for k in range(NEAR)]
     along = lax.all_to_all(mine, "batch", 0, 0, axis_index_groups=columns_of)
     near = [
         lax.ppermute(along, "batch", [(i, i ^ k) for i in range(batch)]) for k in range(1, NEAR)
     ]
     finished = (
-        result, grad_norm_1c, grad_norm_1p, grad_norm_2a, grad_norm_2b, grad_norm_2c
+        result, grad_norm_1c, grad_norm_1p, grad_norm_2a, grad_norm_2c
     )
     held = len(finished)
     *finished, grad_images, grad_norm_1a, grad_norm_1b = stage(
@@ -1437,17 +1508,18 @@
          pltpu.SemaphoreType.DMA((held + 6,))],
         hbm_out=range(held + 3),
     )(tab, g12, labels, norm_1a, k_1a, w_1a, z_own, z_for, dn_own, dn_for, gs_own, gs_for, *finished)
-    result, grad_norm_1c, grad_norm_1p, grad_norm_2a, grad_norm_2b, grad_norm_2c = finished
+    result, grad_norm_1c, grad_norm_1p, grad_norm_2a, grad_norm_2c = finished
     *near, grad_images = tie(*near, grad_images)
     parts = [along, *near]
     weights = (w_2c, w_2b.reshape(-1, n), w_2a, w_1c, w_1p, w_1b.reshape(-1, n), w_1a)
-    t_2c, t_2b, t_2a, t_1c, t_1p, t_1b, t_1a = stage(
+    t_2c, t_2b, t_2a, t_1c, t_1p, t_1b, t_1a, grad_norm_2b = stage(
         functools.partial(unpack, first=first, second=second, piece=piece),
-        [(v.shape, F32) for v in weights],
-        [*(pltpu.VMEM(v.shape, F32) for v in weights), pltpu.VMEM((devices, share, n), F32),
-         pltpu.VMEM((2, devices, piece, n), BF16), pltpu.SemaphoreType.DMA((7,))],
-        hbm_out=range(7),
-    )(tab, *parts, *(swap(v) for v in parts))
+        [(v.shape, F32) for v in (*weights, norm_2b)],
+        [*(pltpu.VMEM(v.shape, F32) for v in (*weights, norm_2b)),
+         pltpu.VMEM((devices, share, n), F32), pltpu.VMEM((2, devices, piece, n), BF16),
+         pltpu.VMEM((devices, 2, n), F32), pltpu.SemaphoreType.DMA((8,))],
+        hbm_out=range(8),
+    )(tab, labels, *parts, *(swap(v) for v in parts))
     grads = (
         grad_norm_1a, grad_norm_1b, grad_norm_1c, grad_norm_1p,
         grad_norm_2a, grad_norm_2b, grad_norm_2c,

time: 179 us -> 176 us (0.983)
  blocking collectives: 137 us -> 132 us
    all_to_all x11 -> x10, blocking collectives: 127 us -> 122 us  [gather(): return lax.all_to_all(send, AXES, 0, 0)]
    pallas_call x23 -> x22, Pallas kernels: 31.2 us -> 32.3 us  [call(): pl.pallas_call(kernel, out_shape=tuple((jax.ShapeDtypeStruct(s, d) for s,...]
where the time goes in v7:
time: 176 us; the launch traced here: 175 us
  blocking collectives  132 us (75%)
  Pallas kernels  32.3 us (18%)
  starting transfers between devices  5.72 us (3%)
  waiting for transfers between devices  4.39 us (2%)
    all_to_all x10, blocking collectives, gather(): return lax.all_to_all(send, AXES, 0, 0)  122 us
    pallas_call x22, Pallas kernels, call(): pl.pallas_call(kernel, out_shape=tuple((jax.ShapeDtypeStruct(s, d) for s,...  32.3 us
    all_to_all x1, blocking collectives, body(): along = lax.all_to_all(mine, 'batch', 0, 0, axis_index_groups=columns_of)  9.55 us
  transfers between devices with their start and end apart: 12, of which 5 were waited for; matrix products, arithmetic and copies ran while one was open for 0% of the time, Pallas kernels for 4%

profile of v7, /device:TPU:0, one launch (start us, length us, event | category | flops | bytes accessed | tf_op | source)
XLA Modules:
  0.0 175.3 jit_solution(2676422077251269498)
XLA Ops:
  0.7 2.3 %f1.1 = (f32[8,128]{1,0:T(8,128)S(1)}, bf16[28,64,256]{2,1,0:T(8,128)(2,1)S(1)}, bf16[28,64,256]{2,1,0:T(8,128)(2,1)S(1)}, f32[28,64,128]{2,1,0:T(8,128)S(1)}, f...) custom-call(s32[1]{0:T(128)} %bitcast.place_at, s32[2]{0:T(128)} %group_at.1, s32[3]{0:T(128)} %width_at.1, ...), custom_call_target="tpu_custom_call" | custom-call | tf_op jit(solution)/shard_map/f1/pallas_call | solution.py:33
  3.8 14.2 %all_to_all.55.got = f32[32,1,640]{2,1,0:T(1,128)S(1)} all-to-all(f32[32,1,640]{2,1,0:T(1,128)S(1)} %get-tuple-element.155), channel_id=1, replica_groups=mesh['rows'=2,'batch'=16] {'rows','batch'}, dimensions={0} | all-to-all | bytes 163840 | tf_op jit(solution)/shard_map/all_to_all | solution.py:1304
  18.0 0.9 f1_strided.1
  19.0 1.9 %f2.1 = (bf16[29,32,768]{2,1,0:T(8,128)(2,1)S(1)}, f32[28,32,128]{2,1,0:T(8,128)S(1)}, f32[32,1,1024]{2,1,0:T(1,128)S(1)}, f32[32,1,128]{2,1,0:T(1,128)S(1)}, f3...) custom-call(f32[8,128]{1,0:T(8,128)S(1)} %get-tuple-element.141.tab, ...), custom_call_target="tpu_custom_call" | custom-call | tf_op jit(solution)/shard_map/f2/pallas_call | solution.py:33
  20.8 9.6 %all_to_all.56.got = f32[32,1,1024]{2,1,0:T(1,128)S(1)} all-to-all(f32[32,1,1024]{2,1,0:T(1,128)S(1)} %get-tuple-element.164), channel_id=1, replica_groups=mesh['rows'=2,'batch'=16] {'rows','batch'}, dimensions={0} | all-to-all | bytes 262144 | tf_op jit(solution)/shard_map/all_to_all | solution.py:1304
  31.1 9.4 %all_to_all.57.got.got_act = f32[32,1,640]{2,1,0:T(1,128)S(1)} all-to-all(f32[32,1,640]{2,1,0:T(1,128)S(1)} %get-tuple-element.167), channel_id=1, replica_groups=mesh['rows'=2,'batch'=16] {'rows','batch'}, dimensions={0} | all-to-all | bytes 163840 | tf_op jit(solution)/shard_map/all_to_all | solution.py:1304
  40.6 1.4 f4.1
  42.6 1.0 g_xz.1
  43.7 9.7 %all_to_all.58.got.pair_got.got_q = bf16[32,16,128]{2,1,0:T(8,128)(2,1)S(1)} all-to-all(bf16[32,16,128]{2,1,0:T(8,128)(2,1)S(1)} %get-tuple-element.182), channel_id=1, replica_groups=mesh['rows'=2,'batch'=16] {'rows','batch'}, dimensions={0} | all-to-all | bytes 262144 | tf_op jit(solution)/shard_map/all_to_all | solution.py:1304
  53.4 1.1 f5.1
  54.5 10.7 %all_to_all.59.got.xz_got = f32[32,1,1280]{2,1,0:T(1,128)S(1)} all-to-all(f32[32,1,1280]{2,1,0:T(1,128)S(1)} %get-tuple-element.187), channel_id=1, replica_groups=mesh['rows'=2,'batch'=16] {'rows','batch'}, dimensions={0} | all-to-all | bytes 327680 | tf_op jit(solution)/shard_map/all_to_all | solution.py:1304
  65.2 1.4 f6.1
  66.6 9.7 %all_to_all.60.got.got_act = bf16[32,16,128]{2,1,0:T(8,128)(2,1)S(1)} all-to-all(bf16[32,16,128]{2,1,0:T(8,128)(2,1)S(1)} %get-tuple-element.191), channel_id=1, replica_groups=mesh['rows'=2,'batch'=16] {'rows','batch'}, dimensions={0} | all-to-all | bytes 262144 | tf_op jit(solution)/shard_map/all_to_all | solution.py:1304
  76.3 2.7 %b7.1 = (bf16[28,28,512]{2,1,0:T(8,128)(2,1)S(1)}, f32[28,32,512]{2,1,0:T(8,128)S(1)}, bf16[32,32,128]{2,1,0:T(8,128)(2,1)S(1)}, f32[2,512]{1,0:T(2,128)S(1)}, f32[28,32,128]{2,1,0:T(8,128)S(1)}) custom-call(f32[8,128]{1,0:T(8,128)S(1)} %get-tuple-element.141.tab, bf16[32,16,128]{2,1,0:T(8,128)(2,1)S(1)} %all_to_all.60.got.got_act, ...), custom_call_target="tpu_custom_call" | custom-call | tf_op jit(solution)/shard_map/b7/pallas_call | solution.py:33
  79.0 13.2 %all_to_all.61.got.got_2c = bf16[32,32,128]{2,1,0:T(8,128)(2,1)S(1)} all-to-all(bf16[32,32,128]{2,1,0:T(8,128)(2,1)S(1)} %get-tuple-element.197), channel_id=1, replica_groups=mesh['rows'=2,'batch'=16] {'rows','batch'}, dimensions={0} | all-to-all | bytes 524288 | tf_op jit(solution)/shard_map/all_to_all | solution.py:1304
  92.2 2.3 %b9.1 = (bf16[28,32,128]{2,1,0:T(8,128)(2,1)S(1)}, f32[28,32,128]{2,1,0:T(8,128)S(1)}, bf16[32,16,128]{2,1,0:T(8,128)(2,1)S(1)}, f32[2,128]{1,0:T(2,128)S(1)}) custom-call(f32[8,128]{1,0:T(8,128)S(1)} %get-tuple-element.141.tab, bf16[32,32,128]{2,1,0:T(8,128)(2,1)S(1)} %all_to_all.61.got.got_2c, f32[32,1,128]{2,1,0:T(1,128)S(1)} %get-tuple-element.165.labels, ...), custom_call_target="tpu_custom_call" | custom-call | tf_op jit(solution)/shard_map/b9/pallas_call | solution.py:33
  94.5 9.6 %all_to_all.62.got.got_p.got_x = bf16[32,16,128]{2,1,0:T(8,128)(2,1)S(1)} all-to-all(bf16[32,16,128]{2,1,0:T(8,128)(2,1)S(1)} %get-tuple-element.205), channel_id=1, replica_groups=mesh['rows'=2,'batch'=16] {'rows','batch'}, dimensions={0} | all-to-all | bytes 262144 | tf_op jit(solution)/shard_map/all_to_all | solution.py:1304
  104.1 2.5 %b10.1 = (bf16[28,32,128]{2,1,0:T(8,128)(2,1)S(1)}, f32[28,32,512]{2,1,0:T(8,128)S(1)}, bf16[32,24,128]{2,1,0:T(8,128)(2,1)S(1)}, f32[3,2,128]{2,1,0:T(2,128)S(1)}, f32[28,32,128]{2,1,0:T(8,128)S(1)}) custom-call(f32[8,128]{1,0:T(8,128)S(1)} %get-tuple-element.141.tab, bf16[32,16,128]{2,1,0:T(8,128)(2,1)S(1)} %all_to_all.62.got.got_p.got_x, ...), custom_call_target="tpu_custom_call" | custom-call | tf_op jit(solution)/shard_map/b10/pallas_call | solution.py:33
  106.6 11.7 %all_to_all.63.got = bf16[32,24,128]{2,1,0:T(8,128)(2,1)S(1)} all-to-all(bf16[32,24,128]{2,1,0:T(8,128)(2,1)S(1)} %get-tuple-element.213), channel_id=1, replica_groups=mesh['rows'=2,'batch'=16] {'rows','batch'}, dimensions={0} | all-to-all | bytes 393216 | tf_op jit(solution)/shard_map/all_to_all | solution.py:1304
  118.4 3.5 %g_most.1 = (bf16[24,80,128]{2,1,0:T(8,128)(2,1)S(1)}, bf16[24,80,128]{2,1,0:T(8,128)(2,1)S(1)}, bf16[14,32,256]{2,1,0:T(8,128)(2,1)S(1)}, bf16[14,32,256]{2,1,0...) custom-call(f32[8,128]{1,0:T(8,128)S(1)} %get-tuple-element.141.tab,, ...), custom_call_target="tpu_custom_call" | custom-call | tf_op jit(solution)/shard_map/g_most/pallas_call | solution.py:33
  121.9 1.5 b12.1
  123.5 1.1 b12_images.2
  125.6 1.1 b12_images.3
  126.6 1.1 g_xd.1
  128.0 24.2 %all_to_all.64.got = bf16[32,96,128]{2,1,0:T(8,128)(2,1)S(1)} all-to-all(bf16[32,96,128]{2,1,0:T(8,128)(2,1)S(1)} %pack_last.1), channel_id=1, replica_groups=mesh['rows'=2,'batch'=16] {'rows','batch'}, dimensions={0} | all-to-all | bytes 1572864 | tf_op jit(solution)/shard_map/all_to_all | solution.py:1304
  152.8 9.6 %all_to_all.65.refs_0_ = bf16[4,172,128]{2,1,0:T(8,128)(2,1)S(1)} all-to-all(bf16[4,172,128]{2,1,0:T(8,128)(2,1)S(1)} %add_all.1), channel_id=1, replica_groups={{0,4,8,12},{1,5,9,13},{2,6,10,14},{3,7,11,15},{16,20,24,28},{17,21,25,2..., dimensions={0} | all-to-all | bytes 352256 | tf_op jit(solution)/shard_map/all_to_all | solution.py:1495
  163.7 2.1 %collective-permute-start.5 = (bf16[4,172,128]{2,1,0:T(8,128)(2,1)S(1)}, bf16[4,172,128]{2,1,0:T(8,128)(2,1)S(1)}, u32[]{:S(2)}, u32[]{:S(2)}) collective-permute-start(bf16[4,172,128]{2,1,0:T(8,128)(2,1)S(1)} %all_to_all.65.refs_0_), channel_id=1, source_target_pairs={{0,1},{1,0},{2,3},{3,2},{4,5},{5,4},{6,7},{7,6},{8,9},{9,8},{10,11... | collective-permute-start | bytes 528392 | tf_op jit(solution)/shard_map/ppermute | solution.py:1497
  165.8 2.5 %b13.1 = (bf16[28,28,512]{2,1,0:T(8,128)(2,1)}, f32[3,2,512]{2,1,0:T(2,128)}, f32[3,2,512]{2,1,0:T(2,128)}, f32[3,2,128]{2,1,0:T(2,128)}, f32[3,2,512]{2,1,0:T(2...) custom-call(f32[8,128]{1,0:T(8,128)S(1)} %get-tuple-element.141.tab, ...), custom_call_target="tpu_custom_call" | custom-call | tf_op jit(solution)/shard_map/b13/pallas_call | solution.py:33
  168.4 1.1 collective-permute-done.7.refs_3_
  169.6 1.8 %collective-permute-done.6.refs_2_ = bf16[4,172,128]{2,1,0:T(8,128)(2,1)S(1)} collective-permute-done((bf16[4,172,128]{2,1,0:T(8,128)(2,1)S(1)}, bf16[4,172,128]{2,1,0:T(8,128)(2,1)S(1)}, u32[]{:S(2)}, u32[]{:S(2)}) %collective-permute-start.6) | collective-permute-done | bytes 176160 | tf_op jit(solution)/shard_map/ppermute | solution.py:1497
  171.9 0.9 collective-permute-done.9.refs_5_
  173.3 1.8 %unpack.1 = (f32[128,512]{1,0:T(8,128)}, f32[1152,128]{1,0:T(8,128)}, f32[512,128]{1,0:T(8,128)}, f32[128,512]{1,0:T(8,128)}, f32[256,512]{1,0:T(8,128)}, /*inde...) custom-call(f32[8,128]{1,0:T(8,128)S(1)} %get-tuple-element.141.tab, ...), custom_call_target="tpu_custom_call" | custom-call | tf_op jit(solution)/shard_map/unpack/pallas_call | solution.py:33
  (55 shorter events, 6.5 us)
Async XLA Ops:
  0.6 2.4 %copy-start.7 = (bf16[3,3,128,128]{3,2,1,0:T(8,128)(2,1)S(1)}, bf16[3,3,128,128]{3,2,1,0:T(8,128)(2,1)}, u32[]{:S(2)}) copy-start(bf16[3,3,128,128]{3,2,1,0:T(8,128)(2,1)} %w2b) | copy-start | bytes 884740
  0.7 2.4 %copy-start.6 = (bf16[3,3,128,128]{3,2,1,0:T(8,128)(2,1)S(1)}, bf16[3,3,128,128]{3,2,1,0:T(8,128)(2,1)}, u32[]{:S(2)}) copy-start(bf16[3,3,128,128]{3,2,1,0:T(8,128)(2,1)} %w1b) | copy-start | bytes 884740
  0.7 17.4 %copy-start = (bf16[256,512]{1,0:T(8,128)(2,1)S(1)}, bf16[256,512]{1,0:T(8,128)(2,1)}, u32[]{:S(2)}) copy-start(bf16[256,512]{1,0:T(8,128)(2,1)} %w_p.3) | copy-start | bytes 786436
  3.0 15.9 %copy-start.4 = (bf16[256,128]{1,0:T(8,128)(2,1)S(1)}, bf16[256,128]{1,0:T(8,128)(2,1)}, u32[]{:S(2)}) copy-start(bf16[256,128]{1,0:T(8,128)(2,1)} %w.15) | copy-start | bytes 196612
  3.0 15.9 %copy-start.10 = (f32[2,3,128]{2,0,1:T(2,128)S(1)}, f32[2,3,128]{2,0,1:T(2,128)}, u32[]{:S(2)}) copy-start(f32[2,3,128]{2,0,1:T(2,128)} %param.27) | copy-start | bytes 9220
  3.3 14.8 %collective-permute-start = (bf16[28,64,256]{2,1,0:T(8,128)(2,1)S(1)}, bf16[28,64,256]{2,1,0:T(8,128)(2,1)S(1)}, u32[]{:S(2)}, u32[]{:S(2)}) collective-permute-start(bf16[28,64,256]{2,1,0:T(8,128)(2,1)S(1)} %get-tuple-element.156), channel_id=1, source_target_pairs={{0,16},{16,0},{1,17},{17,1},{2,18},{18,2},{3,19},{19,3},{4,20},{20... | collective-permute-start | bytes 2752520 | tf_op jit(solution)/shard_map/ppermute | solution.py:1312
  18.0 12.4 %copy-start.1 = (bf16[128,512]{1,0:T(8,128)(2,1)S(1)}, bf16[128,512]{1,0:T(8,128)(2,1)}, u32[]{:S(2)}) copy-start(bf16[128,512]{1,0:T(8,128)(2,1)} %w_c.7) | copy-start | bytes 393220
  18.0 12.4 %copy-start.13 = (f32[2,3,128]{2,0,1:T(2,128)S(1)}, f32[2,3,128]{2,0,1:T(2,128)}, u32[]{:S(2)}) copy-start(f32[2,3,128]{2,0,1:T(2,128)} %param.28) | copy-start | bytes 9220
  18.9 21.6 %copy-start.5 = (bf16[512,128]{1,0:T(8,128)(2,1)S(1)}, bf16[512,128]{1,0:T(8,128)(2,1)}, u32[]{:S(2)}) copy-start(bf16[512,128]{1,0:T(8,128)(2,1)} %w.14) | copy-start | bytes 393220
  19.0 21.6 %copy-start.8 = (f32[2,3,512]{2,0,1:T(2,128)S(1)}, f32[2,3,512]{2,0,1:T(2,128)}, u32[]{:S(2)}) copy-start(f32[2,3,512]{2,0,1:T(2,128)} %param.29) | copy-start | bytes 36868
  19.0 21.6 %copy-start.11 = (f32[2,3,512]{2,0,1:T(2,128)S(1)}, f32[2,3,512]{2,0,1:T(2,128)}, u32[]{:S(2)}) copy-start(f32[2,3,512]{2,0,1:T(2,128)} %param.30) | copy-start | bytes 36868
  42.6 10.9 %copy-start.12 = (f32[2,3,128]{2,0,1:T(2,128)S(1)}, f32[2,3,128]{2,0,1:T(2,128)}, u32[]{:S(2)}) copy-start(f32[2,3,128]{2,0,1:T(2,128)} %param.31) | copy-start | bytes 9220
  42.6 22.6 %copy-start.2 = (bf16[128,512]{1,0:T(8,128)(2,1)S(1)}, bf16[128,512]{1,0:T(8,128)(2,1)}, u32[]{:S(2)}) copy-start(bf16[128,512]{1,0:T(8,128)(2,1)} %w_c.5) | copy-start | bytes 393220
  42.6 22.6 %copy-start.14 = (f32[2,3,128]{2,0,1:T(2,128)S(1)}, f32[2,3,128]{2,0,1:T(2,128)}, u32[]{:S(2)}) copy-start(f32[2,3,128]{2,0,1:T(2,128)} %param.32) | copy-start | bytes 9220
  43.7 32.7 %copy-start.3 = (bf16[1,28,28,512]{3,2,1,0:T(8,128)(2,1)S(1)}, bf16[1,28,28,512]{3,2,1,0:T(8,128)(2,1)}, u32[]{:S(2)}) copy-start(bf16[1,28,28,512]{3,2,1,0:T(8,128)(2,1)} %param.34) | copy-start | bytes 2408452
  43.7 32.7 %copy-start.9 = (f32[2,3,512]{2,0,1:T(2,128)S(1)}, f32[2,3,512]{2,0,1:T(2,128)}, u32[]{:S(2)}) copy-start(f32[2,3,512]{2,0,1:T(2,128)} %param.33) | copy-start | bytes 36868
  121.8 6.0 %collective-permute-start.3 = (bf16[24,80,128]{2,1,0:T(8,128)(2,1)S(1)}, bf16[24,80,128]{2,1,0:T(8,128)(2,1)S(1)}, u32[]{:S(2)}, u32[]{:S(2)}) collective-permute-start(bf16[24,80,128]{2,1,0:T(8,128)(2,1)S(1)} %get-tuple-element.232), channel_id=1, source_target_pairs={{0,16},{16,0},{1,17},{17,1},{2,18},{18,2},{3,19},{19,3},{4,20},{20... | collective-permute-start | bytes 1474568 | tf_op jit(solution)/shard_map/ppermute | solution.py:1312
  124.5 3.3 %collective-permute-start.2 = (bf16[28,64,128]{2,1,0:T(8,128)(2,1)S(1)}, bf16[28,64,128]{2,1,0:T(8,128)(2,1)S(1)}, u32[]{:S(2)}, u32[]{:S(2)}) collective-permute-start(bf16[28,64,128]{2,1,0:T(8,128)(2,1)S(1)} %get-tuple-element.221.dn_oth), channel_id=1, source_target_pairs={{0,16},{16,0},{1,17},{17,1},{2,18},{18,2},{3,19},{19,3},{4,20},{20... | collective-permute-start | bytes 1376264 | tf_op jit(solution)/shard_map/ppermute | solution.py:1312
  125.1 2.7 %collective-permute-start.1 = (bf16[14,32,256]{2,1,0:T(8,128)(2,1)S(1)}, bf16[14,32,256]{2,1,0:T(8,128)(2,1)S(1)}, u32[]{:S(2)}, u32[]{:S(2)}) collective-permute-start(bf16[14,32,256]{2,1,0:T(8,128)(2,1)S(1)} %get-tuple-element.227), channel_id=1, source_target_pairs={{0,16},{16,0},{1,17},{17,1},{2,18},{18,2},{3,19},{19,3},{4,20},{20... | collective-permute-start | bytes 688136 | tf_op jit(solution)/shard_map/ppermute | solution.py:1312
  125.2 2.7 %collective-permute-start.4 = (bf16[8,80,128]{2,1,0:T(8,128)(2,1)S(1)}, bf16[8,80,128]{2,1,0:T(8,128)(2,1)S(1)}, u32[]{:S(2)}, u32[]{:S(2)}) collective-permute-start(bf16[8,80,128]{2,1,0:T(8,128)(2,1)S(1)} %get-tuple-element.234), channel_id=1, source_target_pairs={{0,16},{16,0},{1,17},{17,1},{2,18},{18,2},{3,19},{19,3},{4,20},{20... | collective-permute-start | bytes 491528 | tf_op jit(solution)/shard_map/ppermute | solution.py:1312
  162.4 7.2 %collective-permute-start.7 = (bf16[4,172,128]{2,1,0:T(8,128)(2,1)S(1)}, bf16[4,172,128]{2,1,0:T(8,128)(2,1)S(1)}, u32[]{:S(2)}, u32[]{:S(2)}) collective-permute-start(bf16[4,172,128]{2,1,0:T(8,128)(2,1)S(1)} %all_to_all.65.refs_0_), channel_id=1, source_target_pairs={{0,3},{1,2},{2,1},{3,0},{4,7},{5,6},{6,5},{7,4},{8,11},{9,10},{10,... | collective-permute-start | bytes 528392 | tf_op jit(solution)/shard_map/ppermute | solution.py:1497
  163.1 8.3 %collective-permute-start.6 = (bf16[4,172,128]{2,1,0:T(8,128)(2,1)S(1)}, bf16[4,172,128]{2,1,0:T(8,128)(2,1)S(1)}, u32[]{:S(2)}, u32[]{:S(2)}) collective-permute-start(bf16[4,172,128]{2,1,0:T(8,128)(2,1)S(1)} %all_to_all.65.refs_0_), channel_id=1, source_target_pairs={{0,2},{1,3},{2,0},{3,1},{4,6},{5,7},{6,4},{7,5},{8,10},{9,11},{10,... | collective-permute-start | bytes 528392 | tf_op jit(solution)/shard_map/ppermute | solution.py:1497
  163.7 7.6 %collective-permute-start.5 = (bf16[4,172,128]{2,1,0:T(8,128)(2,1)S(1)}, bf16[4,172,128]{2,1,0:T(8,128)(2,1)S(1)}, u32[]{:S(2)}, u32[]{:S(2)}) collective-permute-start(bf16[4,172,128]{2,1,0:T(8,128)(2,1)S(1)} %all_to_all.65.refs_0_), channel_id=1, source_target_pairs={{0,1},{1,0},{2,3},{3,2},{4,5},{5,4},{6,7},{7,6},{8,9},{9,8},{10,11... | collective-permute-start | bytes 528392 | tf_op jit(solution)/shard_map/ppermute | solution.py:1497
  168.3 3.6 %collective-permute-start.8 = (bf16[4,172,128]{2,1,0:T(8,128)(2,1)S(1)}, bf16[4,172,128]{2,1,0:T(8,128)(2,1)S(1)}, u32[]{:S(2)}, u32[]{:S(2)}) collective-permute-start(bf16[4,172,128]{2,1,0:T(8,128)(2,1)S(1)} %all_to_all.65.refs_0_), channel_id=1, source_target_pairs={{0,16},{16,0},{1,17},{17,1},{2,18},{18,2},{3,19},{19,3},{4,20},{20... | collective-permute-start | bytes 528392 | tf_op jit(solution)/shard_map/ppermute | solution.py:1312
  171.4 1.4 collective-permute-start.9
  171.4 1.7 collective-permute-start.10
  171.9 1.4 collective-permute-start.11

commit v8 on v7

--- a/solution.py
+++ b/solution.py
@@ -392,11 +392,6 @@
     return down(squares)
 
 
-def expand(act, w, z, send, act_sum):
-    squares = project(act, w, z)
-    spread(send, [act_sum, *(squares[:, lanes] for lanes in columns(z.shape[2]))])
-
-
 def join(pieces):
     return pieces[0] if len(pieces) == 1 else jnp.concatenate(pieces, axis=1)
 
@@ -447,7 +442,7 @@
     return jnp.concatenate(rows, axis=0)
 
 
-def pair_products(tab, z, norm, keeps, act, act_sum, slope, both, centred):
+def pair_products(tab, z, norm, keeps, act, act_sum, slope, both):
     rows = z.shape[0]
     label = entry(tab, OWN)
     mean, rstd = keeps[0:1, :], keeps[1:2, :]
@@ -462,13 +457,18 @@
         s = jnp.where(keep, slope_of_half(zz * scale + bias), 0.0)
         sx = s * ((zz - mean) * rstd)
         slope[i] = s
-        both[i, :, 0:LANES] = s.astype(BF16)
-        both[i, :, LANES:] = sx.astype(BF16)
-        centred[i] = (act[i].astype(F32) - middle).astype(BF16)
+        for k, v in enumerate((s, sx)):
+            high = v.astype(BF16)
+            both[i, :, LANES * k : LANES * (k + 1)] = high
+            both[i, :, LANES * (k + 2) : LANES * (k + 3)] = (v - high.astype(F32)).astype(BF16)
         return carry[0] + fold(s), carry[1] + fold(sx)
 
     sums = lax.fori_loop(0, rows, put, (zeros8(LANES), zeros8(LANES)), unroll=4)
-    return mm_tn(flat(centred[...]), flat(both[...])), stack([down(v) for v in sums])
+    sums = [down(v) for v in sums]
+    product = mm_tn(flat(act[...]), flat(both[...]))
+    product = product[:, 0 : 2 * LANES] + product[:, 2 * LANES :]
+    column = jnp.transpose(jnp.broadcast_to(middle, (8, LANES)))[:, 0:1]
+    return product - column * join(sums), stack(sums)
 
 
 def rows_of(line):
@@ -479,25 +479,30 @@
     return join([rows[k : k + 1, :] for k in range(rows.shape[0])])
 
 
-def put_pair(send, at, share, product):
-    devices, n = send.shape[0], LANES
+def pair_rows(product, devices, share, high, low, own):
+    n = LANES
     missing = devices * share - n
     for h in (0, 1):
         values = product[:, n * h : n * (h + 1)]
         if missing:
             values = stack([values, jnp.zeros((missing, n), F32)])
-        first = at + share * h
-        send[:, first : first + share, :] = values.reshape(devices, share, n).astype(BF16)
-
-
-def pass_pair(send, at, got, got_at, share, marks, groups):
-    rows = got[:, got_at : got_at + 2 * share, :].astype(F32)
-    out = None
+        values = values.reshape(devices, share, n)
+        first, last = share * h, share * (h + 1)
+        top = values.astype(BF16)
+        rest = (values - top.astype(F32)).astype(BF16)
+        high[:, first:last, :] = top
+        low[:, first:last, :] = rest
+        own[:, first:last, :] = top.astype(F32) + rest.astype(F32)
+
+
+def pass_pair(send, at, high, low, marks, groups):
+    rows = high.astype(F32) + low.astype(F32)
+    out = -rows
     for g in range(groups):
         same = (marks == float(g)).astype(F32)
-        term = jnp.sum(rows * same, axis=0)[None] * same
-        out = term if out is None else out + term
-    send[:, at : at + 2 * share, :] = out.astype(BF16)
+        images = jnp.maximum(jnp.sum(same, axis=0), 1.0)
+        out = out + (jnp.sum(rows * same, axis=0) / images)[None] * same
+    send[:, at : at + rows.shape[1], :] = out.astype(BF16)
 
 
 def pair_solve(tab, marks, outer, inner, sums, w, act_sums, q_rows, p_rows, pixels):
@@ -509,30 +514,29 @@
     rstd_o = keeps_o[1:2, :]
     a_o = rstd_o * gain_of(norm_o, label)
     b_o, c_o = -(a_o * rstd_o) * gain_o / count_o, -a_o * shift_o / count_o
-    m = mm_nt((w[...].astype(F32) * b_o).astype(BF16), w[...]).astype(BF16)
+    scaled = w[...].astype(F32) * b_o
+    high = scaled.astype(BF16)
+    m = mm_nt(high, w[...]) + mm_nt((scaled - high.astype(F32)).astype(BF16), w[...])
+    m_high = m.astype(BF16)
+    m_low = (m - m_high.astype(F32)).astype(BF16)
+    m = m_high.astype(F32) + m_low.astype(F32)
     e = through_nt(c_o, w[...])
     same = (marks == label).astype(F32)
     middle = jnp.sum(act_sums * same, axis=0) / count
     spread_out = ((act_sums * (1.0 / pixels) - middle[None]) * same).reshape(-1, n).astype(BF16)
     share = p_rows.shape[1] // 2
+    p_rows = p_rows * images[None]
     found = []
     for h, start in enumerate((shift_i, gain_i)):
         q = q_rows[:, h : h + 1, :]
         p = p_rows[:, share * h : share * (h + 1), :].reshape(-1, n)[0:n]
         p = p + mm_tn(spread_out, q.reshape(-1, n).astype(BF16))
-        found.append(start + down(m.astype(F32) * p) + e * jnp.sum(q * same, axis=0))
+        found.append(start + down(m * p) + e * jnp.sum(q * same, axis=0))
     rstd_i = keeps_i[1:2, :]
     a = rstd_i * gain_of(norm_i, label)
     coefs = a, -(a * rstd_i) * found[1] / count, -a * found[0] / count
-    return m, e - through(middle, m), coefs, found
-
-
-def expanded_moments(got, labels, tab, w, pixels):
-    label = entry(tab, OWN)
-    total = group_sum(got, labels, label)
-    chans = w.shape[1]
-    count = tiled(group_count(labels, label), chans) * pixels
-    return moments(through(total[:, 0:LANES], w[...]), total[:, LANES:], count)
+    line = e - through(middle, m_high) - through(middle, m_low)
+    return join([m_high, m_low]), line, coefs, found
 
 
 def activate(tab, got, labels, z_in, norm, act, keeps):
@@ -555,10 +559,13 @@
     return down(lax.fori_loop(0, rows, put, zeros8(LANES), unroll=7))
 
 
-def f3(tab, got, labels, z_in, norm, w, w_p, act, z, send, keeps, keeps_p, act_sum):
+def f3(
+    tab, got, labels, z_in, norm, w, w_p,
+    act, z, send, keeps, keeps_p, slope, q, high, own, both, low, *, share,
+):
     sums = activate(tab, got, labels, z_in, norm, act, keeps)
-    act_sum[...] = sums
-    expand(act, w, z, send, sums)
+    at = expand_pair(tab, z_in, norm, keeps, act, sums, w, z, send, slope, q, both, high, low, own, share)
+    send[:, at : at + 2 * share, :] = low[...]
     marks, label = labels[...], entry(tab, OWN)
     total = group_sum(got, marks, label)
     outer, first = z.shape[2], 2 * LANES
@@ -569,10 +576,26 @@
     keeps_p[1:2, :] = rstd
 
 
-def f4(tab, got, labels, zc, zp, norm_c, norm_p, keeps_p, w_c, w, joined, slope, z, stats, keeps):
+def expand_pair(tab, z_in, norm, keeps, act, sums, w, z, send, slope, q, both, high, low, own, share):
+    pixels = 1.0 * z.shape[0] * (COLS - 4)
+    squares = project(act, w, z)
+    first = through(sums, w[...])
+    second = squares - first * first / pixels
+    product, q[...] = pair_products(tab, z_in, norm, keeps, act, sums, slope, both)
+    pair_rows(product, send.shape[0], share, high, low, own)
+    put_split(send, 0, sums)
+    moved = rows_of(second).astype(BF16)
+    send[:, 2 : 2 + moved.shape[0], :] = jnp.broadcast_to(moved[None], (send.shape[0], *moved.shape))
+    return 2 + moved.shape[0]
+
+
+def f4(
+    tab, got, labels, zc, zp, norm_c, norm_p, keeps_p, w_c, w, high, q,
+    joined, slope, z, send, keeps,
+):
     rows, chans = zc.shape[0], zc.shape[2]
     pixels = 1.0 * rows * (COLS - 4)
-    mean_c, rstd_c = expanded_moments(got, labels[...], tab, w_c, pixels)
+    mean_c, rstd_c = gathered_moments(got, labels[...], entry(tab, OWN), w_c, pixels)
     mean_p, rstd_p = keeps_p[0:1, :], keeps_p[1:2, :]
     for k, v in enumerate((mean_c, rstd_c, mean_p, rstd_p)):
         keeps[k : k + 1, :] = v
@@ -602,15 +625,9 @@
         parts = values.reshape(-1, 8, LANES)
         sums = sums + jnp.sum(parts, axis=0)
         squares = squares + jnp.sum(parts * parts, axis=0)
-    stats[0:1, :] = down(sums)
-    stats[1:2, :] = down(squares)
-
-
-def pair_1(tab, stats, z, norm, keeps, act, act_sum, send, slope, both, centred, *, share):
-    product, sums = pair_products(tab, z, norm, keeps, act, act_sum[...], slope, both, centred)
-    put_split(send, 0, stats[...])
-    put_pair(send, 4, share, product)
-    put_split(send, 4 + 2 * share, sums)
+    put_split(send, 0, stack([down(sums), down(squares)]))
+    send[:, 4 : 4 + high.shape[1], :] = high[...]
+    put_split(send, 4 + high.shape[1], q[...])
 
 
 def put_shares(xz, send):
@@ -653,17 +670,14 @@
     put_shares(xz, send)
 
 
-def f6(tab, got, labels, z_in, norm, w, act, z, send, keeps, slope, q, both, centred, *, share):
+def f6(
+    tab, got, labels, z_in, norm, w,
+    act, z, send, keeps, slope, q, own, both, high, low, *, share,
+):
     sums = activate(tab, got, labels, z_in, norm, act, keeps)
-    pixels = 1.0 * z.shape[0] * (COLS - 4)
-    squares = project(act, w, z)
-    first = through(sums, w[...])
-    second = squares - first * first / pixels
-    product, q[...] = pair_products(tab, z_in, norm, keeps, act, sums, slope, both, centred)
-    put_split(send, 0, sums)
-    low = rows_of(second).astype(BF16)
-    send[:, 2 : 2 + low.shape[0], :] = jnp.broadcast_to(low[None], (send.shape[0], *low.shape))
-    put_pair(send, 2 + low.shape[0], share, product)
+    at = expand_pair(tab, z_in, norm, keeps, act, sums, w, z, send, slope, q, both, high, low, own, share)
+    send[:, at : at + 2 * share, :] = high[...]
+    send[:, at + 2 * share : at + 4 * share, :] = low[...]
 
 
 def gathered_moments(got, marks, label, w, pixels):
@@ -721,7 +735,9 @@
     put_split(send, 2 * blocks, rows_of(down(products) * rstd * gate))
     put_split(send, 4 * blocks, stack(inner))
     put_split(send, 4 * blocks + 4, q[...])
-    pass_pair(send, 4 * blocks + 8, got, p_at, share, marks, norm.shape[0])
+    high = got[:, p_at : p_at + 2 * share, :]
+    low_p = got[:, p_at + 2 * share : p_at + 4 * share, :]
+    pass_pair(send, 4 * blocks + 8, high, low_p, marks, norm.shape[0])
 
 
 def lane_sums(got, marks, channels):
@@ -777,8 +793,8 @@
 
 def b9(
     tab, got, labels, norm_c, keeps_c, w_c, got_act, act, slope, d_in, z, norm, keeps,
-    b_two, b_last, z_in, norm_in, keeps_in, x_sum, pair_got,
-    dz, dout, send, own_sums, d3, d, *, share,
+    b_two, b_last, z_in, norm_in, keeps_in, x_sum, pair_high, pair_low, own_p,
+    dz, dout, send, own_sums, d3, d, *, share, p_at,
 ):
     rows = z.shape[0]
     pixels = 1.0 * rows * (COLS - 4)
@@ -792,7 +808,7 @@
     m, line, (a, b, c), found = pair_solve(
         tab, marks, (norm_c, keeps_c), (norm, keeps), [*wide, inner[0:1], inner[1:2]], w_c,
         get_split(got_act, 0, 1), get_split(got, at + 4, 2),
-        got[:, at + 8 : at + 8 + 2 * share, :].astype(F32), pixels,
+        got[:, at + 8 : at + 8 + 2 * share, :].astype(F32) + own_p[...], pixels,
     )
     own_sums[0:1, :] = found[0]
     own_sums[1:2, :] = found[1]
@@ -823,7 +839,8 @@
     put_split(send, 0, stack(slope_sums(tab, d, z_in, norm_in, keeps_in, dout)))
     blocks = columns(x_sum.shape[0])
     put_split(send, 4, stack([jnp.transpose(x_sum[lanes, :])[0:1] for lanes in blocks]))
-    pass_pair(send, 4 + 2 * len(blocks), pair_got, 4, share, marks, norm.shape[0])
+    high, low = pair_high[:, 4 : 4 + 2 * share, :], pair_low[:, p_at : p_at + 2 * share, :]
+    pass_pair(send, 4 + 2 * len(blocks), high, low, marks, norm.shape[0])
 
 
 def b10(
@@ -855,14 +872,9 @@
     sums, prod_c, prod_p = lax.fori_loop(0, rows, sum_up, (start, start, start), unroll=2)
     wide = [down(sums), down(prod_c) * rstd_c, down(prod_p) * rstd_p]
     inner = inner_sums(low, w_c, slope_in, z_in, keeps_in, d_in)
-    blocks = chans // LANES
-    put_split(send, 0, rows_of(wide[0]))
-    put_split(send, 2 * blocks, rows_of(wide[1]))
-    put_split(send, 4 * blocks, stack(inner))
-    last = rows_of(wide[2]).astype(BF16)
-    send[:, 4 * blocks + 4 : 5 * blocks + 4, :] = jnp.broadcast_to(
-        last[None], (send.shape[0], *last.shape)
-    )
+    parts = [stack([v[:, 0 : chans // 2], v[:, chans // 2 :]]) for v in wide]
+    values = join([*parts, stack(inner)])
+    send[...] = jnp.broadcast_to(values[None], send.shape)
 
 
 def inner_sums(low, w, slope, z, keeps, d_in):
@@ -878,7 +890,8 @@
 
 
 def inner_grad(act, m, line, slope, d_in, d):
-    d[...] = mm(flat(act[...]), m).reshape(d.shape)
+    both = mm(flat(act[...]), m)
+    d[...] = (both[:, 0:LANES] + both[:, LANES:]).reshape(d.shape)
 
     def put(i, carry):
         d[i] = slope[i] * (d_in[i] + d[i] + line)
@@ -899,7 +912,7 @@
 
 
 def b12(
-    tab, own10, labels, norm_c, keeps_c, w_c, got_act, got_q, got_p, act, slope, d_in,
+    tab, own10, labels, norm_c, keeps_c, w_c, got_act, got_q, got_p, own_p, act, slope, d_in,
     z, norm, keeps, xs, d2, kept, sent, own_sums, dz, packed, dout, *, share, q_at, p_at,
 ):
     rows = z.shape[0]
@@ -910,8 +923,9 @@
     cuts = (0, outer, 2 * outer, 2 * outer + n, 2 * outer + 2 * n)
     m, line, (a, b, c), found = pair_solve(
         tab, marks, (norm_c, keeps_c.at[0:2]), (norm, keeps),
-        [total[:, u:v] for u, v in zip(cuts, cuts[1:])], w_c, got_act[:, :, 0:n],
-        get_split(got_q, q_at, 2), got_p[:, p_at : p_at + 2 * share, :].astype(F32), pixels,
+        [total[:, u:v] for u, v in zip(cuts, cuts[1:])], w_c, get_split(got_act, 0, 1),
+        get_split(got_q, q_at, 2),
+        got_p[:, p_at : p_at + 2 * share, :].astype(F32) + own_p[...], pixels,
     )
     own_sums[0:1, :] = found[0]
     own_sums[1:2, :] = found[1]
@@ -1092,16 +1106,16 @@
             for g in range(norm_c.shape[0])
         ]
 
-    lines = wide_sums(got, 2)
-    last = got[:, 4 * blocks + 4 : 5 * blocks + 4, :].astype(F32)
-    for g, line in enumerate(lines):
-        line.append(line_of(over_group(last, marks, float(g))))
+    totals = [group_sum(got, marks, float(g)) for g in range(norm_c.shape[0])]
+    side = outer // 2
+    lines = [
+        [join([total[h : h + 1, side * k : side * (k + 1)] for h in (0, 1)]) for k in range(3)]
+        for total in totals
+    ]
     for k in range(2):
         own10[:, outer * k : outer * (k + 1)] = own_of([v[k] for v in lines], label)
-    inner = over_group(get_split(got, 4 * blocks, 2), marks, label)
-    for k in range(2):
         at = 2 * outer + LANES * k
-        own10[:, at : at + LANES] = inner[k : k + 1]
+        own10[:, at : at + LANES] = own_of([v[k : k + 1, 3 * side :] for v in totals], label)
     lines_2c = wide_sums(got_2c, 2)
     mean, a, b, c = backward_norm(
         tab, lambda g: (lines_2c[g][0], lines_2c[g][1]), marks, norm_2c, keeps_2c, pixels,
@@ -1156,7 +1170,7 @@
 
 def g_xd(
     tab, sums_own, sums_oth, norm, keeps, x_sum, got_x, labels, x_own, x_oth, dn_own, dn_oth,
-    out, sums, low,
+    z_own, z_oth, out, sums, low,
 ):
     rows = dn_own.shape[0]
     n = LANES
@@ -1164,11 +1178,13 @@
     sums[...] = sums_own[...] + sums_oth[...]
     a = keeps[1:2, :] * gain_of(norm, entry(tab, OWN))
     local = sums[0:1, :] / pixels
+    mean = keeps[0:1, :]
+    b = -(a * keeps[1:2, :]) * sums[1:2, :] / pixels
     value = None
-    for x, dn in ((x_own, dn_own), (x_oth, dn_oth)):
-
-        def put(i, carry, dn=dn):
-            low[i] = (a * (dn[i].astype(F32) - local)).astype(BF16)
+    for x, dn, z in ((x_own, dn_own, z_own), (x_oth, dn_oth, z_oth)):
+
+        def put(i, carry, dn=dn, z=z):
+            low[i] = (a * (dn[i].astype(F32) - local) + b * (z[i] - mean)).astype(BF16)
             return carry
 
         lax.fori_loop(0, rows, put, 0, unroll=4)
@@ -1220,16 +1236,18 @@
     piece = (out.shape[1] - share - 4) // 2
     marks = labels[...]
     value = jnp.sum(got[:, piece : piece + share, :].astype(F32), axis=0)
-    sums = last_sums(got.at[:, at : at + 4, :], marks, norm.shape[0])
+    products = get_split(got, at, 2)[:, 1:2, :]
+    lack = jnp.zeros(products.shape, F32)
     for g in range(norm.shape[0]):
         rstd = keeps_all[2 * g + 1 : 2 * g + 2, :]
-        count = group_count(marks, float(g)) * pixels
-        b = -(rstd * rstd * norm[g, 0:1, :]) * sums[g][1] / count
+        factor = -(rstd * rstd * norm[g, 0:1, :]) / pixels
         same = (marks == float(g)).astype(F32)
-        rows = [
-            jnp.sum(xz_got[:, :, n * (2 + q) : n * (3 + q)] * same, axis=0) for q in range(share)
-        ]
-        value = value + jnp.concatenate(rows, axis=0) * b
+        middle = jnp.sum(products * same, axis=0) / jnp.sum(same, axis=0)
+        lack = lack + (middle[None] - products) * (factor[None] * same)
+    rows = [
+        jnp.sum(xz_got[:, :, n * (2 + q) : n * (3 + q)] * lack, axis=0) for q in range(share)
+    ]
+    value = value + jnp.concatenate(rows, axis=0)
     for k in (0, 1):
         total = jnp.sum(got[half * k : half * (k + 1), 0:piece, :].astype(F32), axis=0).astype(BF16)
         out[:, piece * k : piece * (k + 1), :] = jnp.broadcast_to(
@@ -1376,23 +1394,27 @@
          ((m, 1, n), F32), mean_scale(n, 2), mean_scale(n, norm_1a.shape[0]), wide_z],
     )(tab, g1, z_own, x_oth, w_1a, norm_1a, w_even, w_odd, stats_1p)
     g2 = gather(s2)
-    act_1b, z_1c, s3, k_1b, k_p, sum_1b = stage(
-        f3,
-        [maps(n, BF16), maps(outer), send(1 + outer // n), mean_scale(n), mean_scale(outer),
-         ((1, n), F32)],
+    share_1 = -(-n // devices)
+    p_rows = ((devices, 2 * share_1, n), BF16)
+    own_rows = ((devices, 2 * share_1, n), F32)
+    wide_rows = outer // n
+    p_at = 2 + wide_rows
+    high_3 = -(-(p_at + 2 * share_1) // 16) * 16
+    act_1b, z_1c, s3, k_1b, k_p, slope_1b, q_1b, p_1b, own_1b = stage(
+        functools.partial(f3, share=share_1),
+        [maps(n, BF16), maps(outer), ((devices, high_3, n), BF16), mean_scale(n),
+         mean_scale(outer), maps(n), ((2, n), F32), p_rows, own_rows],
+        [scratch(4 * n, BF16), pltpu.VMEM(p_rows[0], BF16)],
     )(tab, g2, labels, z_1b, norm_1b, w_1c, w_1p)
     g3 = gather(s3)
-    joined, slope, z_2a, stats_2a, k_cp = stage(
-        f4, [maps(outer, BF16), maps(outer), maps(n), ((2, n), F32), mean_scale(outer, 2)]
-    )(tab, g3, labels, z_1c, z_1p, norm_1c, norm_1p, k_p, w_1c, w_2a)
+    high = -(-(8 + 2 * share_1) // 16) * 16
+    joined, slope, z_2a, s4, k_cp = stage(
+        f4,
+        [maps(outer, BF16), maps(outer), maps(n), ((devices, high, n), BF16),
+         mean_scale(outer, 2)],
+    )(tab, g3, labels, z_1c, z_1p, norm_1c, norm_1p, k_p, w_1c, w_2a, p_1b, q_1b)
     share = -(-inputs // devices)
     half_in = ((rows, cols_in, n), BF16)
-    share_1 = -(-n // devices)
-    high = -(-(8 + 2 * share_1) // 16) * 16
-    s4, slope_1b = stage(
-        functools.partial(pair_1, share=share_1), [((devices, high, n), BF16), maps(n)],
-        [scratch(2 * n, BF16), scratch(n, BF16)],
-    )(tab, stats_2a, z_1b, norm_1b, k_1b, act_1b, sum_1b)
     s4, k_1a = tie(s4, k_1a)
     xz, x_sum = stage(
         g_xz, [((devices * share, n), F32), ((inputs, n), F32)],
@@ -1404,34 +1426,32 @@
         f5, [((rows + 2, COLS, 3 * n), BF16), maps(n), send(2 + share), mean_scale(n)]
     )(tab, g4, labels, z_2a, norm_2a, w_two, w_last, xz)
     g5 = gather(s5)
-    wide_rows = outer // n
-    p_6 = 2 + wide_rows
-    high_6 = -(-(p_6 + 2 * share_1) // 16) * 16
-    act_2b, z_2c, s6, k_2b, slope_2b, q_2b = stage(
+    high_6 = -(-(p_at + 4 * share_1) // 8) * 8
+    act_2b, z_2c, s6, k_2b, slope_2b, q_2b, own_2b = stage(
         functools.partial(f6, share=share_1),
         [maps(n, BF16), maps(outer), ((devices, high_6, n), BF16), mean_scale(n), maps(n),
-         ((2, n), F32)],
-        [scratch(2 * n, BF16), scratch(n, BF16)],
+         ((2, n), F32), own_rows],
+        [scratch(4 * n, BF16), *(pltpu.VMEM(p_rows[0], BF16) for _ in range(2))],
     )(tab, g5, labels, z_2b, norm_2b, w_2c)
     g6 = gather(s6)
     high_7 = -(-(4 * wide_rows + 8 + 2 * share_1) // 16) * 16
     result, grad_pre, s7, k_2c, d_2b = stage(
-        functools.partial(b7, share=share_1, p_at=p_6),
+        functools.partial(b7, share=share_1, p_at=p_at),
         [(cotangent.shape[1:], BF16), maps(outer), ((devices, high_7, n), BF16),
          mean_scale(outer), maps(n)],
         [pltpu.VMEM((COLS, outer), F32), scratch(outer, BF16)],
     )(tab, g6, labels, joined, z_2c, norm_2c, w_2c, cotangent[0], slope_2b, z_2b, k_2b, q_2b)
     g7 = gather(s7)
     dz_2b, dout_2a, s9, found_2b = stage(
-        functools.partial(b9, share=share_1),
+        functools.partial(b9, share=share_1, p_at=p_at),
         [maps(n, BF16), maps(n), ((devices, high, n), BF16), ((2, n), F32)],
         [pltpu.VMEM((rows + 2, COLS, 3 * n), BF16), scratch(n)],
     )(tab, g7, labels, norm_2c, k_2c, w_2c, g6, act_2b, slope_2b, d_2b, z_2b, norm_2b, k_2b,
-      b_two, b_last, z_2a, norm_2a, k_2a, x_sum, g4)
+      b_two, b_last, z_2a, norm_2a, k_2a, x_sum, g4, g3, own_2b)
     g9 = gather(s9)
     dz_2a, grad_pre_2, s10, grad_norm_2a, d_1b = stage(
         b10,
-        [maps(n, BF16), maps(outer), ((devices, 5 * wide_rows + 4, n), BF16), *params(norm_2a), maps(n)],
+        [maps(n, BF16), maps(outer), ((devices, 2, 3 * outer // 2 + n), F32), *params(norm_2a), maps(n)],
         [scratch(outer), scratch(outer, BF16)],
     )(tab, g9, labels, dout_2a, z_2a, norm_2a, k_2a, w_2a, grad_pre, slope, z_1c, z_1p, k_cp,
       norm_1c, w_1c, slope_1b, z_1b, k_1b)
@@ -1458,7 +1478,7 @@
         functools.partial(b12, share=share_1, q_at=4 + 2 * share_1, p_at=4 + 2 * (inputs // n)),
         [((rows + 1, COLS, 2 * n), BF16), part_1b, part_1b, ((2, n), F32)],
         [scratch(n, BF16), pltpu.VMEM((2 * second * piece, n), BF16), scratch(n)],
-    )(tab, own10, labels, norm_1c, k_cp, w_1c, g3, g4, g9, act_1b, slope_1b, d_1b,
+    )(tab, own10, labels, norm_1c, k_cp, w_1c, g3, g4, g9, own_1b, act_1b, slope_1b, d_1b,
       z_1b, norm_1b, k_1b, xs)
     got_1b = swap(sent_1b)
     sides = []
@@ -1478,7 +1498,8 @@
     high = -(-(stats_at + 8) // 16) * 16
     tall, sums_1a = stage(
         g_xd, [((devices * share, n), BF16), ((2, n), F32)], [pltpu.VMEM(half_in[0], BF16)]
-    )(tab, sums_own, sums_send, norm_1a, k_1a, x_sum, g9, labels, x_own, x_oth, dn_own, dn_send)
+    )(tab, sums_own, sums_send, norm_1a, k_1a, x_sum, g9, labels, x_own, x_oth, dn_own, dn_send,
+      z_own, z_oth)
     tall, gs_for, dn_for = tie(tall, gs_for, dn_for)
     (s12,) = stage(
         functools.partial(pack_last, stats_at=stats_at), [((devices, high, n), BF16)]

time: 176 us -> 181 us (1.028)
  blocking collectives: 132 us -> 135 us
    all_to_all x10, blocking collectives: 122 us -> 125 us  [gather(): return lax.all_to_all(send, AXES, 0, 0)]
    pallas_call x22 -> x21, Pallas kernels: 32.3 us -> 34 us  [call(): pl.pallas_call(kernel, out_shape=tuple((jax.ShapeDtypeStruct(s, d) for s,...]
where the time goes in v8:
time: 181 us; the launch traced here: 180 us
  blocking collectives  135 us (75%)
  Pallas kernels  34 us (19%)
  starting transfers between devices  5.74 us (3%)
  waiting for transfers between devices  4.37 us (2%)
    all_to_all x10, blocking collectives, gather(): return lax.all_to_all(send, AXES, 0, 0)  125 us
    pallas_call x21, Pallas kernels, call(): pl.pallas_call(kernel, out_shape=tuple((jax.ShapeDtypeStruct(s, d) for s,...  34 us
    all_to_all x1, blocking collectives, body(): along = lax.all_to_all(mine, 'batch', 0, 0, axis_index_groups=columns_of)  9.55 us
  transfers between devices with their start and end apart: 12, of which 5 were waited for; matrix products, arithmetic and copies ran while one was open for 0% of the time, Pallas kernels for 4%

profile of v8, /device:TPU:0, one launch (start us, length us, event | category | flops | bytes accessed | tf_op | source)
XLA Modules:
  0.0 180.3 jit_solution(16236519094926707085)
XLA Ops:
  0.7 2.3 %f1.1 = (f32[8,128]{1,0:T(8,128)S(1)}, bf16[28,64,256]{2,1,0:T(8,128)(2,1)S(1)}, bf16[28,64,256]{2,1,0:T(8,128)(2,1)S(1)}, f32[28,64,128]{2,1,0:T(8,128)S(1)}, f...) custom-call(s32[1]{0:T(128)} %bitcast.place_at, s32[2]{0:T(128)} %group_at.1, s32[3]{0:T(128)} %width_at.1, ...), custom_call_target="tpu_custom_call" | custom-call | tf_op jit(solution)/shard_map/f1/pallas_call | solution.py:33
  3.8 14.2 %all_to_all.55.got = f32[32,1,640]{2,1,0:T(1,128)S(1)} all-to-all(f32[32,1,640]{2,1,0:T(1,128)S(1)} %get-tuple-element.157), channel_id=1, replica_groups=mesh['rows'=2,'batch'=16] {'rows','batch'}, dimensions={0} | all-to-all | bytes 163840 | tf_op jit(solution)/shard_map/all_to_all | solution.py:1322
  19.0 1.9 %f2.1 = (bf16[29,32,768]{2,1,0:T(8,128)(2,1)S(1)}, f32[28,32,128]{2,1,0:T(8,128)S(1)}, f32[32,1,1024]{2,1,0:T(1,128)S(1)}, f32[32,1,128]{2,1,0:T(1,128)S(1)}, f3...) custom-call(f32[8,128]{1,0:T(8,128)S(1)} %get-tuple-element.143.tab, ...), custom_call_target="tpu_custom_call" | custom-call | tf_op jit(solution)/shard_map/f2/pallas_call | solution.py:33
  20.8 9.6 %all_to_all.56.got = f32[32,1,1024]{2,1,0:T(1,128)S(1)} all-to-all(f32[32,1,1024]{2,1,0:T(1,128)S(1)} %get-tuple-element.166), channel_id=1, replica_groups=mesh['rows'=2,'batch'=16] {'rows','batch'}, dimensions={0} | all-to-all | bytes 262144 | tf_op jit(solution)/shard_map/all_to_all | solution.py:1322
  30.5 1.7 f3.1
  32.2 9.8 %all_to_all.57.got.pair_low.got_act = bf16[32,16,128]{2,1,0:T(8,128)(2,1)S(1)} all-to-all(bf16[32,16,128]{2,1,0:T(8,128)(2,1)S(1)} %get-tuple-element.169), channel_id=1, replica_groups=mesh['rows'=2,'batch'=16] {'rows','batch'}, dimensions={0} | all-to-all | bytes 262144 | tf_op jit(solution)/shard_map/all_to_all | solution.py:1322
  42.0 1.4 f4.1
  43.5 1.1 g_xz.1
  44.6 9.9 %all_to_all.58.got.pair_high.got_q = bf16[32,16,128]{2,1,0:T(8,128)(2,1)S(1)} all-to-all(bf16[32,16,128]{2,1,0:T(8,128)(2,1)S(1)} %get-tuple-element.182), channel_id=1, replica_groups=mesh['rows'=2,'batch'=16] {'rows','batch'}, dimensions={0} | all-to-all | bytes 262144 | tf_op jit(solution)/shard_map/all_to_all | solution.py:1322
  54.5 1.1 f5.1
  55.6 10.8 %all_to_all.59.got.xz_got = f32[32,1,1280]{2,1,0:T(1,128)S(1)} all-to-all(f32[32,1,1280]{2,1,0:T(1,128)S(1)} %get-tuple-element.187), channel_id=1, replica_groups=mesh['rows'=2,'batch'=16] {'rows','batch'}, dimensions={0} | all-to-all | bytes 327680 | tf_op jit(solution)/shard_map/all_to_all | solution.py:1322
  66.4 1.8 f6.1
  68.1 11.6 %all_to_all.60.got.got_act = bf16[32,24,128]{2,1,0:T(8,128)(2,1)S(1)} all-to-all(bf16[32,24,128]{2,1,0:T(8,128)(2,1)S(1)} %get-tuple-element.191), channel_id=1, replica_groups=mesh['rows'=2,'batch'=16] {'rows','batch'}, dimensions={0} | all-to-all | bytes 393216 | tf_op jit(solution)/shard_map/all_to_all | solution.py:1322
  79.8 2.8 %b7.1 = (bf16[28,28,512]{2,1,0:T(8,128)(2,1)S(1)}, f32[28,32,512]{2,1,0:T(8,128)S(1)}, bf16[32,32,128]{2,1,0:T(8,128)(2,1)S(1)}, f32[2,512]{1,0:T(2,128)S(1)}, f32[28,32,128]{2,1,0:T(8,128)S(1)}) custom-call(f32[8,128]{1,0:T(8,128)S(1)} %get-tuple-element.143.tab, bf16[32,24,128]{2,1,0:T(8,128)(2,1)S(1)} %all_to_all.60.got.got_act, ...), custom_call_target="tpu_custom_call" | custom-call | tf_op jit(solution)/shard_map/b7/pallas_call | solution.py:33
  82.5 12.9 %all_to_all.61.got.got_2c = bf16[32,32,128]{2,1,0:T(8,128)(2,1)S(1)} all-to-all(bf16[32,32,128]{2,1,0:T(8,128)(2,1)S(1)} %get-tuple-element.197), channel_id=1, replica_groups=mesh['rows'=2,'batch'=16] {'rows','batch'}, dimensions={0} | all-to-all | bytes 524288 | tf_op jit(solution)/shard_map/all_to_all | solution.py:1322
  95.5 2.6 %b9.1 = (bf16[28,32,128]{2,1,0:T(8,128)(2,1)S(1)}, f32[28,32,128]{2,1,0:T(8,128)S(1)}, bf16[32,16,128]{2,1,0:T(8,128)(2,1)S(1)}, f32[2,128]{1,0:T(2,128)S(1)}) custom-call(f32[8,128]{1,0:T(8,128)S(1)} %get-tuple-element.143.tab, bf16[32,32,128]{2,1,0:T(8,128)(2,1)S(1)} %all_to_all.61.got.got_2c, f32[32,1,128]{2,1,0:T(1,128)S(1)} %get-tuple-element.167.labels, ...), custom_call_target="tpu_custom_call" | custom-call | tf_op jit(solution)/shard_map/b9/pallas_call | solution.py:33
  98.1 9.8 %all_to_all.62.got.got_p.got_x = bf16[32,16,128]{2,1,0:T(8,128)(2,1)S(1)} all-to-all(bf16[32,16,128]{2,1,0:T(8,128)(2,1)S(1)} %get-tuple-element.206), channel_id=1, replica_groups=mesh['rows'=2,'batch'=16] {'rows','batch'}, dimensions={0} | all-to-all | bytes 262144 | tf_op jit(solution)/shard_map/all_to_all | solution.py:1322
  107.9 2.5 %b10.1 = (bf16[28,32,128]{2,1,0:T(8,128)(2,1)S(1)}, f32[28,32,512]{2,1,0:T(8,128)S(1)}, f32[32,2,896]{2,1,0:T(2,128)S(1)}, f32[3,2,128]{2,1,0:T(2,128)S(1)}, f32[28,32,128]{2,1,0:T(8,128)S(1)}) custom-call(f32[8,128]{1,0:T(8,128)S(1)} %get-tuple-element.143.tab, bf16[32,16,128]{2,1,0:T(8,128)(2,1)S(1)} %all_to_all.62.got.got_p.got_x, ...), custom_call_target="tpu_custom_call" | custom-call | tf_op jit(solution)/shard_map/b10/pallas_call | solution.py:33
  110.4 12.4 %all_to_all.63.got = f32[32,2,896]{2,1,0:T(2,128)S(1)} all-to-all(f32[32,2,896]{2,1,0:T(2,128)S(1)} %get-tuple-element.216), channel_id=1, replica_groups=mesh['rows'=2,'batch'=16] {'rows','batch'}, dimensions={0} | all-to-all | bytes 458752 | tf_op jit(solution)/shard_map/all_to_all | solution.py:1322
  122.8 3.6 %g_most.1 = (bf16[24,80,128]{2,1,0:T(8,128)(2,1)S(1)}, bf16[24,80,128]{2,1,0:T(8,128)(2,1)S(1)}, bf16[14,32,256]{2,1,0:T(8,128)(2,1)S(1)}, bf16[14,32,256]{2,1,0...) custom-call(f32[8,128]{1,0:T(8,128)S(1)} %get-tuple-element.143.tab,, ...), custom_call_target="tpu_custom_call" | custom-call | tf_op jit(solution)/shard_map/g_most/pallas_call | solution.py:33
  126.5 1.8 b12.1
  128.3 1.1 b12_images.2
  130.5 1.1 b12_images.3
  131.5 1.3 g_xd.1
  133.1 24.2 %all_to_all.64.got = bf16[32,96,128]{2,1,0:T(8,128)(2,1)S(1)} all-to-all(bf16[32,96,128]{2,1,0:T(8,128)(2,1)S(1)} %pack_last.1), channel_id=1, replica_groups=mesh['rows'=2,'batch'=16] {'rows','batch'}, dimensions={0} | all-to-all | bytes 1572864 | tf_op jit(solution)/shard_map/all_to_all | solution.py:1322
  157.8 9.6 %all_to_all.65.refs_0_ = bf16[4,172,128]{2,1,0:T(8,128)(2,1)S(1)} all-to-all(bf16[4,172,128]{2,1,0:T(8,128)(2,1)S(1)} %add_all.1), channel_id=1, replica_groups={{0,4,8,12},{1,5,9,13},{2,6,10,14},{3,7,11,15},{16,20,24,28},{17,21,25,2..., dimensions={0} | all-to-all | bytes 352256 | tf_op jit(solution)/shard_map/all_to_all | solution.py:1516
  168.7 2.1 %collective-permute-start.5 = (bf16[4,172,128]{2,1,0:T(8,128)(2,1)S(1)}, bf16[4,172,128]{2,1,0:T(8,128)(2,1)S(1)}, u32[]{:S(2)}, u32[]{:S(2)}) collective-permute-start(bf16[4,172,128]{2,1,0:T(8,128)(2,1)S(1)} %all_to_all.65.refs_0_), channel_id=1, source_target_pairs={{0,1},{1,0},{2,3},{3,2},{4,5},{5,4},{6,7},{7,6},{8,9},{9,8},{10,11... | collective-permute-start | bytes 528392 | tf_op jit(solution)/shard_map/ppermute | solution.py:1518
  170.8 2.5 %b13.1 = (bf16[28,28,512]{2,1,0:T(8,128)(2,1)}, f32[3,2,512]{2,1,0:T(2,128)}, f32[3,2,512]{2,1,0:T(2,128)}, f32[3,2,128]{2,1,0:T(2,128)}, f32[3,2,512]{2,1,0:T(2...) custom-call(f32[8,128]{1,0:T(8,128)S(1)} %get-tuple-element.143.tab, ...), custom_call_target="tpu_custom_call" | custom-call | tf_op jit(solution)/shard_map/b13/pallas_call | solution.py:33
  173.4 1.1 collective-permute-done.7.refs_3_
  174.5 1.8 %collective-permute-done.6.refs_2_ = bf16[4,172,128]{2,1,0:T(8,128)(2,1)S(1)} collective-permute-done((bf16[4,172,128]{2,1,0:T(8,128)(2,1)S(1)}, bf16[4,172,128]{2,1,0:T(8,128)(2,1)S(1)}, u32[]{:S(2)}, u32[]{:S(2)}) %collective-permute-start.6) | collective-permute-done | bytes 176160 | tf_op jit(solution)/shard_map/ppermute | solution.py:1518
  176.8 0.9 collective-permute-done.9.refs_5_
  178.3 1.8 %unpack.1 = (f32[128,512]{1,0:T(8,128)}, f32[1152,128]{1,0:T(8,128)}, f32[512,128]{1,0:T(8,128)}, f32[128,512]{1,0:T(8,128)}, f32[256,512]{1,0:T(8,128)}, /*inde...) custom-call(f32[8,128]{1,0:T(8,128)S(1)} %get-tuple-element.143.tab, ...), custom_call_target="tpu_custom_call" | custom-call | tf_op jit(solution)/shard_map/unpack/pallas_call | solution.py:33
  (54 shorter events, 5.9 us)
Async XLA Ops:
  0.6 2.4 %copy-start.7 = (bf16[3,3,128,128]{3,2,1,0:T(8,128)(2,1)S(1)}, bf16[3,3,128,128]{3,2,1,0:T(8,128)(2,1)}, u32[]{:S(2)}) copy-start(bf16[3,3,128,128]{3,2,1,0:T(8,128)(2,1)} %w2b) | copy-start | bytes 884740
  0.7 2.4 %copy-start.6 = (bf16[3,3,128,128]{3,2,1,0:T(8,128)(2,1)S(1)}, bf16[3,3,128,128]{3,2,1,0:T(8,128)(2,1)}, u32[]{:S(2)}) copy-start(bf16[3,3,128,128]{3,2,1,0:T(8,128)(2,1)} %w1b) | copy-start | bytes 884740
  0.7 17.4 %copy-start = (bf16[256,512]{1,0:T(8,128)(2,1)S(1)}, bf16[256,512]{1,0:T(8,128)(2,1)}, u32[]{:S(2)}) copy-start(bf16[256,512]{1,0:T(8,128)(2,1)} %w_p.3) | copy-start | bytes 786436
  3.0 15.9 %copy-start.4 = (bf16[256,128]{1,0:T(8,128)(2,1)S(1)}, bf16[256,128]{1,0:T(8,128)(2,1)}, u32[]{:S(2)}) copy-start(bf16[256,128]{1,0:T(8,128)(2,1)} %w.15) | copy-start | bytes 196612
  3.0 15.9 %copy-start.10 = (f32[2,3,128]{2,0,1:T(2,128)S(1)}, f32[2,3,128]{2,0,1:T(2,128)}, u32[]{:S(2)}) copy-start(f32[2,3,128]{2,0,1:T(2,128)} %param.27) | copy-start | bytes 9220
  3.3 14.8 %collective-permute-start = (bf16[28,64,256]{2,1,0:T(8,128)(2,1)S(1)}, bf16[28,64,256]{2,1,0:T(8,128)(2,1)S(1)}, u32[]{:S(2)}, u32[]{:S(2)}) collective-permute-start(bf16[28,64,256]{2,1,0:T(8,128)(2,1)S(1)} %get-tuple-element.158), channel_id=1, source_target_pairs={{0,16},{16,0},{1,17},{17,1},{2,18},{18,2},{3,19},{19,3},{4,20},{20... | collective-permute-start | bytes 2752520 | tf_op jit(solution)/shard_map/ppermute | solution.py:1330
  18.0 12.4 %copy-start.1 = (bf16[128,512]{1,0:T(8,128)(2,1)S(1)}, bf16[128,512]{1,0:T(8,128)(2,1)}, u32[]{:S(2)}) copy-start(bf16[128,512]{1,0:T(8,128)(2,1)} %w_c.7) | copy-start | bytes 393220
  18.0 12.4 %copy-start.14 = (f32[2,3,128]{2,0,1:T(2,128)S(1)}, f32[2,3,128]{2,0,1:T(2,128)}, u32[]{:S(2)}) copy-start(f32[2,3,128]{2,0,1:T(2,128)} %param.28) | copy-start | bytes 9220
  18.9 23.0 %copy-start.5 = (bf16[512,128]{1,0:T(8,128)(2,1)S(1)}, bf16[512,128]{1,0:T(8,128)(2,1)}, u32[]{:S(2)}) copy-start(bf16[512,128]{1,0:T(8,128)(2,1)} %w.14) | copy-start | bytes 393220
  19.0 23.0 %copy-start.8 = (f32[2,3,512]{2,0,1:T(2,128)S(1)}, f32[2,3,512]{2,0,1:T(2,128)}, u32[]{:S(2)}) copy-start(f32[2,3,512]{2,0,1:T(2,128)} %param.29) | copy-start | bytes 36868
  19.0 23.0 %copy-start.11 = (f32[2,3,512]{2,0,1:T(2,128)S(1)}, f32[2,3,512]{2,0,1:T(2,128)}, u32[]{:S(2)}) copy-start(f32[2,3,512]{2,0,1:T(2,128)} %param.30) | copy-start | bytes 36868
  43.4 11.0 %copy-start.12 = (f32[2,3,128]{2,0,1:T(2,128)S(1)}, f32[2,3,128]{2,0,1:T(2,128)}, u32[]{:S(2)}) copy-start(f32[2,3,128]{2,0,1:T(2,128)} %param.31) | copy-start | bytes 9220
  43.5 22.9 %copy-start.2 = (bf16[128,512]{1,0:T(8,128)(2,1)S(1)}, bf16[128,512]{1,0:T(8,128)(2,1)}, u32[]{:S(2)}) copy-start(bf16[128,512]{1,0:T(8,128)(2,1)} %w_c.5) | copy-start | bytes 393220
  43.5 22.9 %copy-start.13 = (f32[2,3,128]{2,0,1:T(2,128)S(1)}, f32[2,3,128]{2,0,1:T(2,128)}, u32[]{:S(2)}) copy-start(f32[2,3,128]{2,0,1:T(2,128)} %param.32) | copy-start | bytes 9220
  44.5 35.2 %copy-start.3 = (bf16[1,28,28,512]{3,2,1,0:T(8,128)(2,1)S(1)}, bf16[1,28,28,512]{3,2,1,0:T(8,128)(2,1)}, u32[]{:S(2)}) copy-start(bf16[1,28,28,512]{3,2,1,0:T(8,128)(2,1)} %param.34) | copy-start | bytes 2408452
  44.5 35.2 %copy-start.9 = (f32[2,3,512]{2,0,1:T(2,128)S(1)}, f32[2,3,512]{2,0,1:T(2,128)}, u32[]{:S(2)}) copy-start(f32[2,3,512]{2,0,1:T(2,128)} %param.33) | copy-start | bytes 36868
  126.4 6.5 %collective-permute-start.3 = (bf16[24,80,128]{2,1,0:T(8,128)(2,1)S(1)}, bf16[24,80,128]{2,1,0:T(8,128)(2,1)S(1)}, u32[]{:S(2)}, u32[]{:S(2)}) collective-permute-start(bf16[24,80,128]{2,1,0:T(8,128)(2,1)S(1)} %get-tuple-element.236), channel_id=1, source_target_pairs={{0,16},{16,0},{1,17},{17,1},{2,18},{18,2},{3,19},{19,3},{4,20},{20... | collective-permute-start | bytes 1474568 | tf_op jit(solution)/shard_map/ppermute | solution.py:1330
  129.4 3.5 %collective-permute-start.2 = (bf16[28,64,128]{2,1,0:T(8,128)(2,1)S(1)}, bf16[28,64,128]{2,1,0:T(8,128)(2,1)S(1)}, u32[]{:S(2)}, u32[]{:S(2)}) collective-permute-start(bf16[28,64,128]{2,1,0:T(8,128)(2,1)S(1)} %get-tuple-element.225.dn_oth), channel_id=1, source_target_pairs={{0,16},{16,0},{1,17},{17,1},{2,18},{18,2},{3,19},{19,3},{4,20},{20... | collective-permute-start | bytes 1376264 | tf_op jit(solution)/shard_map/ppermute | solution.py:1330
  130.0 2.9 %collective-permute-start.1 = (bf16[14,32,256]{2,1,0:T(8,128)(2,1)S(1)}, bf16[14,32,256]{2,1,0:T(8,128)(2,1)S(1)}, u32[]{:S(2)}, u32[]{:S(2)}) collective-permute-start(bf16[14,32,256]{2,1,0:T(8,128)(2,1)S(1)} %get-tuple-element.231), channel_id=1, source_target_pairs={{0,16},{16,0},{1,17},{17,1},{2,18},{18,2},{3,19},{19,3},{4,20},{20... | collective-permute-start | bytes 688136 | tf_op jit(solution)/shard_map/ppermute | solution.py:1330
  130.0 2.9 %collective-permute-start.4 = (bf16[8,80,128]{2,1,0:T(8,128)(2,1)S(1)}, bf16[8,80,128]{2,1,0:T(8,128)(2,1)S(1)}, u32[]{:S(2)}, u32[]{:S(2)}) collective-permute-start(bf16[8,80,128]{2,1,0:T(8,128)(2,1)S(1)} %get-tuple-element.238), channel_id=1, source_target_pairs={{0,16},{16,0},{1,17},{17,1},{2,18},{18,2},{3,19},{19,3},{4,20},{20... | collective-permute-start | bytes 491528 | tf_op jit(solution)/shard_map/ppermute | solution.py:1330
  167.3 7.2 %collective-permute-start.7 = (bf16[4,172,128]{2,1,0:T(8,128)(2,1)S(1)}, bf16[4,172,128]{2,1,0:T(8,128)(2,1)S(1)}, u32[]{:S(2)}, u32[]{:S(2)}) collective-permute-start(bf16[4,172,128]{2,1,0:T(8,128)(2,1)S(1)} %all_to_all.65.refs_0_), channel_id=1, source_target_pairs={{0,3},{1,2},{2,1},{3,0},{4,7},{5,6},{6,5},{7,4},{8,11},{9,10},{10,... | collective-permute-start | bytes 528392 | tf_op jit(solution)/shard_map/ppermute | solution.py:1518
  168.1 8.3 %collective-permute-start.6 = (bf16[4,172,128]{2,1,0:T(8,128)(2,1)S(1)}, bf16[4,172,128]{2,1,0:T(8,128)(2,1)S(1)}, u32[]{:S(2)}, u32[]{:S(2)}) collective-permute-start(bf16[4,172,128]{2,1,0:T(8,128)(2,1)S(1)} %all_to_all.65.refs_0_), channel_id=1, source_target_pairs={{0,2},{1,3},{2,0},{3,1},{4,6},{5,7},{6,4},{7,5},{8,10},{9,11},{10,... | collective-permute-start | bytes 528392 | tf_op jit(solution)/shard_map/ppermute | solution.py:1518
  168.7 7.6 %collective-permute-start.5 = (bf16[4,172,128]{2,1,0:T(8,128)(2,1)S(1)}, bf16[4,172,128]{2,1,0:T(8,128)(2,1)S(1)}, u32[]{:S(2)}, u32[]{:S(2)}) collective-permute-start(bf16[4,172,128]{2,1,0:T(8,128)(2,1)S(1)} %all_to_all.65.refs_0_), channel_id=1, source_target_pairs={{0,1},{1,0},{2,3},{3,2},{4,5},{5,4},{6,7},{7,6},{8,9},{9,8},{10,11... | collective-permute-start | bytes 528392 | tf_op jit(solution)/shard_map/ppermute | solution.py:1518
  173.3 3.5 %collective-permute-start.8 = (bf16[4,172,128]{2,1,0:T(8,128)(2,1)S(1)}, bf16[4,172,128]{2,1,0:T(8,128)(2,1)S(1)}, u32[]{:S(2)}, u32[]{:S(2)}) collective-permute-start(bf16[4,172,128]{2,1,0:T(8,128)(2,1)S(1)} %all_to_all.65.refs_0_), channel_id=1, source_target_pairs={{0,16},{16,0},{1,17},{17,1},{2,18},{18,2},{3,19},{19,3},{4,20},{20... | collective-permute-start | bytes 528392 | tf_op jit(solution)/shard_map/ppermute | solution.py:1330
  176.3 1.4 collective-permute-start.9
  176.3 1.7 collective-permute-start.10
  176.8 1.4 collective-permute-start.11

commit v9 on v8

--- a/solution.py
+++ b/solution.py
@@ -400,24 +400,18 @@
     return [slice(LANES * j, LANES * (j + 1)) for j in range(channels // LANES)]
 
 
-def through(sums, w):
+def three_parts(sums):
     high = sums.astype(BF16)
     rest = sums - high.astype(F32)
     mid = rest.astype(BF16)
     low = (rest - mid.astype(F32)).astype(BF16)
     lines = [v.astype(F32) for v in (high, mid, low)]
-    lines.append(jnp.zeros((5, sums.shape[1]), F32))
-    return down(mm(jnp.concatenate(lines, axis=0).astype(BF16), w))
-
-
-def through_nt(sums, w):
-    high = sums.astype(BF16)
-    rest = sums - high.astype(F32)
-    mid = rest.astype(BF16)
-    low = (rest - mid.astype(F32)).astype(BF16)
-    lines = [v.astype(F32) for v in (high, mid, low)]
-    lines.append(jnp.zeros((5, sums.shape[1]), F32))
-    return down(mm_nt(jnp.concatenate(lines, axis=0).astype(BF16), w))
+    lines.append(jnp.zeros((13, sums.shape[1]), F32))
+    return jnp.concatenate(lines, axis=0).astype(BF16)
+
+
+def through(sums, w):
+    return down(mm(three_parts(sums), w))
 
 
 def put_split(send, at, values):
@@ -477,6 +471,12 @@
 
 def line_of(rows):
     return join([rows[k : k + 1, :] for k in range(rows.shape[0])])
+
+
+def put_part(send, at, rows, part):
+    first, last = part
+    if last > first:
+        send[:, at : at + last - first, :] = rows[:, first:last, :]
 
 
 def pair_rows(product, devices, share, high, low, own):
@@ -516,27 +516,31 @@
     b_o, c_o = -(a_o * rstd_o) * gain_o / count_o, -a_o * shift_o / count_o
     scaled = w[...].astype(F32) * b_o
     high = scaled.astype(BF16)
-    m = mm_nt(high, w[...]) + mm_nt((scaled - high.astype(F32)).astype(BF16), w[...])
+    low = (scaled - high.astype(F32)).astype(BF16)
+    got = mm_nt(jnp.concatenate([high, low, three_parts(c_o)], axis=0), w[...])
+    m, e = got[0:n] + got[n : 2 * n], down(got[2 * n :])
     m_high = m.astype(BF16)
     m_low = (m - m_high.astype(F32)).astype(BF16)
     m = m_high.astype(F32) + m_low.astype(F32)
-    e = through_nt(c_o, w[...])
     same = (marks == label).astype(F32)
     middle = jnp.sum(act_sums * same, axis=0) / count
     spread_out = ((act_sums * (1.0 / pixels) - middle[None]) * same).reshape(-1, n).astype(BF16)
     share = p_rows.shape[1] // 2
     p_rows = p_rows * images[None]
     found = []
+    q = join([q_rows[:, h : h + 1, :].reshape(-1, n) for h in (0, 1)])
+    away = mm_tn(spread_out, q.astype(BF16))
+    q = down(q * join([same.reshape(-1, n)] * 2))
     for h, start in enumerate((shift_i, gain_i)):
-        q = q_rows[:, h : h + 1, :]
-        p = p_rows[:, share * h : share * (h + 1), :].reshape(-1, n)[0:n]
-        p = p + mm_tn(spread_out, q.reshape(-1, n).astype(BF16))
-        found.append(start + down(m * p) + e * jnp.sum(q * same, axis=0))
+        lanes = slice(n * h, n * (h + 1))
+        p = p_rows[:, share * h : share * (h + 1), :].reshape(-1, n)[0:n] + away[:, lanes]
+        found.append(start + down(m * p) + e * q[:, lanes])
     rstd_i = keeps_i[1:2, :]
     a = rstd_i * gain_of(norm_i, label)
     coefs = a, -(a * rstd_i) * found[1] / count, -a * found[0] / count
-    line = e - through(middle, m_high) - through(middle, m_low)
-    return join([m_high, m_low]), line, coefs, found
+    both = join([m_high, m_low])
+    line = through(middle, both)
+    return both, e - line[:, 0:n] - line[:, n:], coefs, found
 
 
 def activate(tab, got, labels, z_in, norm, act, keeps):
@@ -560,12 +564,13 @@
 
 
 def f3(
-    tab, got, labels, z_in, norm, w, w_p,
-    act, z, send, keeps, keeps_p, slope, q, high, own, both, low, *, share,
+    tab, got, labels, z_in, norm, w, w_p, xz,
+    act, z, send, keeps, keeps_p, slope, q, high, own, both, low, *, share, part,
 ):
     sums = activate(tab, got, labels, z_in, norm, act, keeps)
     at = expand_pair(tab, z_in, norm, keeps, act, sums, w, z, send, slope, q, both, high, low, own, share)
     send[:, at : at + 2 * share, :] = low[...]
+    put_part(send, at + 2 * share, xz, part)
     marks, label = labels[...], entry(tab, OWN)
     total = group_sum(got, marks, label)
     outer, first = z.shape[2], 2 * LANES
@@ -630,15 +635,7 @@
     put_split(send, 4 + high.shape[1], q[...])
 
 
-def put_shares(xz, send):
-    n, devices = LANES, send.shape[0]
-    share = xz.shape[0] // devices
-    pieces = xz[...].reshape(devices, share, n)
-    for q in range(share):
-        send[:, :, n * (2 + q) : n * (3 + q)] = pieces[:, q : q + 1, :]
-
-
-def f5(tab, got, labels, z_in, norm, w_two, w_last, xz, x3, z, send, keeps):
+def f5(tab, got, labels, z_in, norm, w_two, w_last, x3, z, send, keeps):
     rows = z_in.shape[0]
     pixels = 1.0 * rows * (COLS - 4)
     marks, label = labels[...], entry(tab, OWN)
@@ -665,25 +662,26 @@
     lax.fori_loop(0, rows, put, 0, unroll=2)
     lanes = slice(0, 3 * n)
     conv_stats(
-        z, x3, (lanes, w_two[...], (0, 1)), (lanes, w_last[...], 2), send.at[:, :, 0 : 2 * n]
+        z, x3, (lanes, w_two[...], (0, 1)), (lanes, w_last[...], 2), send
     )
-    put_shares(xz, send)
 
 
 def f6(
-    tab, got, labels, z_in, norm, w,
-    act, z, send, keeps, slope, q, own, both, high, low, *, share,
+    tab, got, labels, z_in, norm, w, xz,
+    act, z, send, keeps, slope, q, own, both, high, low, *, share, part,
 ):
     sums = activate(tab, got, labels, z_in, norm, act, keeps)
     at = expand_pair(tab, z_in, norm, keeps, act, sums, w, z, send, slope, q, both, high, low, own, share)
     send[:, at : at + 2 * share, :] = high[...]
     send[:, at + 2 * share : at + 4 * share, :] = low[...]
+    put_part(send, at + 4 * share, xz, part)
 
 
 def gathered_moments(got, marks, label, w, pixels):
     devices, chans = got.shape[0], w.shape[1]
-    low = (got[:, k : k + 1, :].astype(F32).reshape(devices, LANES).astype(BF16) for k in (0, 1))
-    means = sum(mm(v, w[...]) for v in low) * (1.0 / pixels)
+    low = stack([got[:, k : k + 1, :].astype(F32).reshape(devices, LANES) for k in (0, 1)])
+    means = mm(low.astype(BF16), w[...]) * (1.0 / pixels)
+    means = means[0:devices] + means[devices:]
     blocks = chans // LANES
     moments_2 = join(
         [got[:, 2 + k : 3 + k, :].astype(F32).reshape(devices, LANES) for k in range(blocks)]
@@ -998,7 +996,7 @@
     tab, got, labels, norm, keeps, w, z_own, z_for, dn_own, dn_for, gs_own, gs_for, *rest, at, held
 ):
     finished, outs = rest[:held], rest[held : 2 * held]
-    grad, grad_norm, grad_inner, dz, wide, grad_v, norm_v, inner_v, sems = rest[2 * held :]
+    grad, grad_norm, dz, wide, grad_v, norm_v, sems = rest[2 * held :]
     copies = [
         pltpu.make_async_copy(a, b, sems.at[k]) for k, (a, b) in enumerate(zip(finished, outs))
     ]
@@ -1012,10 +1010,8 @@
     for g in range(norm.shape[0]):
         norm_v[g, 0:1, :] = totals[g][1]
         norm_v[g, 1:2, :] = totals[g][0]
-    norm_from_owners(get_split(got, at + 4, 2), marks, inner_v)
-    for k, (value, out) in enumerate(((norm_v, grad_norm), (inner_v, grad_inner))):
-        copies.append(pltpu.make_async_copy(value, out, sems.at[held + k]))
-        copies[-1].start()
+    copies.append(pltpu.make_async_copy(norm_v, grad_norm, sems.at[held]))
+    copies[-1].start()
     keep = lax.broadcasted_iota(jnp.int32, (z_own.shape[1], LANES), 0) < cols
     for k, (z, dn, gs) in enumerate(((z_own, dn_own, gs_own), (z_for, dn_for, gs_for))):
         group = entry(tab, OWN if k == 0 else OTHER)
@@ -1054,7 +1050,7 @@
             part = pl.ds(step * q, step)
             copies.append(
                 pltpu.make_async_copy(
-                    grad_v.at[place, part], grad.at[place, part], sems.at[held + 2 + 2 * k + q]
+                    grad_v.at[place, part], grad.at[place, part], sems.at[held + 1 + 2 * k + q]
                 )
             )
             copies[-1].start()
@@ -1147,7 +1143,7 @@
         gs[...] = got.reshape(gs.shape).astype(BF16)
 
 
-def g_xz(keeps, x_own, x_oth, z_own, z_oth, out, x_sum, low):
+def g_xz(keeps, x_own, x_oth, z_own, z_oth, out, x_sum, low, tall):
     rows, n = z_own.shape[0], LANES
     mean = keeps[0:1, :]
     low[:, :, n : 2 * n] = jnp.ones((rows, z_own.shape[1], n), BF16)
@@ -1162,9 +1158,10 @@
         term = mm_tn(flat(x[...]), flat(low[...]))
         value = term if value is None else value + term
     at = value.shape[0]
-    out[0:at, :] = value[:, 0:n]
-    if at < out.shape[0]:
-        out[at:, :] = jnp.zeros((out.shape[0] - at, n), F32)
+    tall[0:at, :] = value[:, 0:n]
+    if at < tall.shape[0]:
+        tall[at:, :] = jnp.zeros((tall.shape[0] - at, n), F32)
+    out[...] = tall[...].reshape(out.shape).astype(BF16)
     x_sum[...] = value[:, n : 2 * n]
 
 
@@ -1205,7 +1202,7 @@
         out[at:, :] = jnp.zeros((out.shape[0] - at, n), BF16)
 
 
-def pack_last(tall, sums, found, kept, got, kept_1b, got_1b, send, *, stats_at):
+def pack_last(tall, sums, kept, got, kept_1b, got_1b, xz, send, *, stats_at, part):
     n = LANES
     devices = send.shape[0]
     piece, share = kept.shape[1], tall.shape[0] // devices
@@ -1217,7 +1214,7 @@
         send[second:, 0:piece, :] = jnp.zeros((devices - second, piece, n), BF16)
     send[:, piece : piece + share, :] = tall[...].reshape(devices, share, n)
     put_split(send, stats_at, sums[...])
-    put_split(send, stats_at + 4, found[...])
+    put_part(send, stats_at + 4, xz, part)
 
 
 def last_sums(stats, marks, groups):
@@ -1229,11 +1226,13 @@
     return out
 
 
-def add_all(got, labels, norm, keeps_all, xz_got, found, out, *, at, pixels):
+def add_all(
+    got, labels, norm, keeps_all, got_a, got_b, found_2b, found_1b, out, *, at, pixels, parts
+):
     devices, n = got.shape[0], LANES
     half = devices // 2
-    share = xz_got.shape[2] // n - 2
-    piece = (out.shape[1] - share - 4) // 2
+    share = parts[-1][2]
+    piece = (out.shape[1] - share - 8) // 2
     marks = labels[...]
     value = jnp.sum(got[:, piece : piece + share, :].astype(F32), axis=0)
     products = get_split(got, at, 2)[:, 1:2, :]
@@ -1245,7 +1244,9 @@
         middle = jnp.sum(products * same, axis=0) / jnp.sum(same, axis=0)
         lack = lack + (middle[None] - products) * (factor[None] * same)
     rows = [
-        jnp.sum(xz_got[:, :, n * (2 + q) : n * (3 + q)] * lack, axis=0) for q in range(share)
+        jnp.sum(source[:, start : start + last - first, :].astype(F32) * lack, axis=0)
+        for source, (start, first, last) in zip((got_a, got_b, got), parts)
+        if last > first
     ]
     value = value + jnp.concatenate(rows, axis=0)
     for k in (0, 1):
@@ -1256,17 +1257,13 @@
     out[:, 2 * piece : 2 * piece + share, :] = jnp.broadcast_to(
         value.astype(BF16)[None], (out.shape[0], share, n)
     )
-    put_split(out, 2 * piece + share, found[...])
-
-
-def unpack(tab, labels, *refs, first, second, piece):
-    parts, outs, values = refs[: 2 * NEAR], refs[2 * NEAR : 2 * NEAR + 8], refs[2 * NEAR + 8 :]
-    *values, tall, packed, found, sems = values
-    half, minor = half_of(tab), half_of(tab, MINOR)
+    put_split(out, 2 * piece + share, stack([found_2b[...], found_1b[...]]))
+
+
+def place_parts(minor, parts, packed, tall, found, piece):
     far, share = parts[0].shape[0], tall.shape[1]
     for k, part in enumerate(parts):
-        core = half if k < NEAR else 1 - half
-        base = core * (far * NEAR) + lax.bitwise_xor(minor, jnp.int32(k % NEAR))
+        base = lax.bitwise_xor(minor, jnp.int32(k))
 
         def place(z, carry, part=part, base=base):
             owner = base + NEAR * z
@@ -1274,39 +1271,78 @@
                 packed[h, owner] = part[z, piece * h : piece * (h + 1), :]
             tall[owner] = part[z, 2 * piece : 2 * piece + share, :].astype(F32)
             sums = part[z, 2 * piece + share :, :].astype(F32)
-            found[owner] = sums[0:2] + sums[2:4]
+            found[owner] = sums[0:4] + sums[4:8]
             return carry
 
         lax.fori_loop(0, far, place, 0, unroll=min(far, 4))
+
+
+def unpack_own(tab, *refs, piece):
+    place_parts(half_of(tab, MINOR), refs[:NEAR], *refs[NEAR:], piece)
+
+
+def unpack(tab, labels, packed_own, tall_own, found_own, *refs, first, second, piece):
+    parts, outs, values = refs[:NEAR], refs[NEAR : NEAR + 9], refs[NEAR + 9 :]
+    *values, packed_oth, tall_oth, found_oth, sems = values
+    place_parts(half_of(tab, MINOR), parts, packed_oth, tall_oth, found_oth, piece)
+    half = half_of(tab)
     copies = [
         pltpu.make_async_copy(value, out, sems.at[k]) for k, (value, out) in enumerate(zip(values, outs))
     ]
-    most = [flat(packed[h, 0:first]) for h in (0, 1)]
-    last = [flat(packed[h, first : first + second]) for h in (0, 1)]
-    size = first * piece
-
-    def source(at, rows):
-        pieces = []
-        if at < size:
-            pieces.append(most[0][at : min(at + rows, size)])
-        if at + rows > size:
-            pieces.append(most[1][max(at - size, 0) : at + rows - size])
-        pieces = [v.astype(F32) for v in pieces]
-        return pieces[0] if len(pieces) == 1 else stack(pieces)
-
-    at = 0
-    for k, value in enumerate(values[0:5]):
-        at = take_rows(source, at, value)
-        copies[k].start()
-    w_1b, w_1a, grad_norm = values[5:8]
-    size = second * piece
-    w_1b[0:size] = last[0].astype(F32)
-    w_1b[size:] = last[1][0 : w_1b.shape[0] - size].astype(F32)
-    copies[5].start()
-    w_1a[...] = flat(tall[...])[0 : w_1a.shape[0]]
-    copies[6].start()
-    norm_from_owners(found[...], labels[...], grad_norm)
-    copies[7].start()
+    w_1b, w_1a, *grad_norms = values[5:9]
+    own, oth = (packed_own, tall_own, found_own), (packed_oth, tall_oth, found_oth)
+    for core in (0, 1):
+
+        @pl.when(half == core)
+        def _():
+            packed, tall, found = zip(*((own, oth) if core == 0 else (oth, own)))
+            most, last = [], []
+            for h in (0, 1):
+                pieces = [flat(v[h]) for v in packed]
+                middle = pieces[0].shape[0]
+                cut = first * piece
+                most.append((pieces, middle))
+                last.append((cut, pieces, middle))
+
+            def span(pieces, middle, at, rows):
+                found_rows = []
+                if at < middle:
+                    found_rows.append(pieces[0][at : min(at + rows, middle)])
+                if at + rows > middle:
+                    found_rows.append(pieces[1][max(at - middle, 0) : at + rows - middle])
+                return [v.astype(F32) for v in found_rows]
+
+            size = first * piece
+
+            def source(at, rows):
+                out = []
+                if at < size:
+                    out += span(*most[0], at, min(rows, size - at))
+                if at + rows > size:
+                    start = max(at - size, 0)
+                    out += span(*most[1], start, at + rows - size - start)
+                return out[0] if len(out) == 1 else stack(out)
+
+            at = 0
+            for k, value in enumerate(values[0:5]):
+                at = take_rows(source, at, value)
+                copies[k].start()
+            left = w_1b.shape[0]
+            for k, (cut, pieces, middle) in enumerate(last):
+                rows = min(second * piece, left)
+                lines = span(pieces, middle, cut, rows)
+                start = second * piece * k
+                w_1b[start : start + rows, :] = lines[0] if len(lines) == 1 else stack(lines)
+                left -= rows
+            copies[5].start()
+            lines = stack([flat(v[...]) for v in tall])
+            w_1a[...] = lines[0 : w_1a.shape[0]]
+            copies[6].start()
+            sums = jnp.concatenate([v[...] for v in found], axis=0)
+            for k, grad_norm in enumerate(grad_norms):
+                norm_from_owners(sums[:, 2 * k : 2 * k + 2, :], labels[...], grad_norm)
+                copies[7 + k].start()
+
     for copy in copies:
         copy.wait()
 
@@ -1393,19 +1429,31 @@
         [((rows + 1, COLS, 6 * n), BF16), maps(n), send(2 + (inputs + outer) // n),
          ((m, 1, n), F32), mean_scale(n, 2), mean_scale(n, norm_1a.shape[0]), wide_z],
     )(tab, g1, z_own, x_oth, w_1a, norm_1a, w_even, w_odd, stats_1p)
+    share = -(-inputs // devices)
+    half_in = ((rows, cols_in, n), BF16)
+    xz, x_sum = stage(
+        g_xz, [((devices, share, n), BF16), ((inputs, n), F32)],
+        [pltpu.VMEM((rows, cols_in, 2 * n), BF16), pltpu.VMEM((devices * share, n), F32)],
+    )(k_1a, x_own, x_oth, z_own, z_oth)
+    s2, xz, x_sum = tie(s2, xz, x_sum)
     g2 = gather(s2)
     share_1 = -(-n // devices)
     p_rows = ((devices, 2 * share_1, n), BF16)
     own_rows = ((devices, 2 * share_1, n), F32)
     wide_rows = outer // n
     p_at = 2 + wide_rows
-    high_3 = -(-(p_at + 2 * share_1) // 16) * 16
+    xz_3 = p_at + 2 * share_1
+    high_3 = -(-xz_3 // 16) * 16
+    xz_6 = p_at + 4 * share_1
+    high_6 = -(-xz_6 // 8) * 8
+    cut_3 = min(share, high_3 - xz_3)
+    cut_6 = min(share, cut_3 + high_6 - xz_6)
     act_1b, z_1c, s3, k_1b, k_p, slope_1b, q_1b, p_1b, own_1b = stage(
-        functools.partial(f3, share=share_1),
+        functools.partial(f3, share=share_1, part=(0, cut_3)),
         [maps(n, BF16), maps(outer), ((devices, high_3, n), BF16), mean_scale(n),
          mean_scale(outer), maps(n), ((2, n), F32), p_rows, own_rows],
         [scratch(4 * n, BF16), pltpu.VMEM(p_rows[0], BF16)],
-    )(tab, g2, labels, z_1b, norm_1b, w_1c, w_1p)
+    )(tab, g2, labels, z_1b, norm_1b, w_1c, w_1p, xz)
     g3 = gather(s3)
     high = -(-(8 + 2 * share_1) // 16) * 16
     joined, slope, z_2a, s4, k_cp = stage(
@@ -1413,26 +1461,17 @@
         [maps(outer, BF16), maps(outer), maps(n), ((devices, high, n), BF16),
          mean_scale(outer, 2)],
     )(tab, g3, labels, z_1c, z_1p, norm_1c, norm_1p, k_p, w_1c, w_2a, p_1b, q_1b)
-    share = -(-inputs // devices)
-    half_in = ((rows, cols_in, n), BF16)
-    s4, k_1a = tie(s4, k_1a)
-    xz, x_sum = stage(
-        g_xz, [((devices * share, n), F32), ((inputs, n), F32)],
-        [pltpu.VMEM((rows, cols_in, 2 * n), BF16)],
-    )(k_1a, x_own, x_oth, z_own, z_oth)
-    s4, xz, x_sum = tie(s4, xz, x_sum)
     g4 = gather(s4)
     x3, z_2b, s5, k_2a = stage(
-        f5, [((rows + 2, COLS, 3 * n), BF16), maps(n), send(2 + share), mean_scale(n)]
-    )(tab, g4, labels, z_2a, norm_2a, w_two, w_last, xz)
+        f5, [((rows + 2, COLS, 3 * n), BF16), maps(n), send(2), mean_scale(n)]
+    )(tab, g4, labels, z_2a, norm_2a, w_two, w_last)
     g5 = gather(s5)
-    high_6 = -(-(p_at + 4 * share_1) // 8) * 8
     act_2b, z_2c, s6, k_2b, slope_2b, q_2b, own_2b = stage(
-        functools.partial(f6, share=share_1),
+        functools.partial(f6, share=share_1, part=(cut_3, cut_6)),
         [maps(n, BF16), maps(outer), ((devices, high_6, n), BF16), mean_scale(n), maps(n),
          ((2, n), F32), own_rows],
         [scratch(4 * n, BF16), *(pltpu.VMEM(p_rows[0], BF16) for _ in range(2))],
-    )(tab, g5, labels, z_2b, norm_2b, w_2c)
+    )(tab, g5, labels, z_2b, norm_2b, w_2c, xz)
     g6 = gather(s6)
     high_7 = -(-(4 * wide_rows + 8 + 2 * share_1) // 16) * 16
     result, grad_pre, s7, k_2c, d_2b = stage(
@@ -1495,23 +1534,27 @@
             d2, _ = tie(d2, sides[0][0])
     (dn_send, sums_send), (dn_own, sums_own) = sides
     stats_at = piece + -(-share // 8) * 8
-    high = -(-(stats_at + 8) // 16) * 16
+    high = -(-(stats_at + 4 + share - cut_6) // 16) * 16
     tall, sums_1a = stage(
         g_xd, [((devices * share, n), BF16), ((2, n), F32)], [pltpu.VMEM(half_in[0], BF16)]
     )(tab, sums_own, sums_send, norm_1a, k_1a, x_sum, g9, labels, x_own, x_oth, dn_own, dn_send,
       z_own, z_oth)
     tall, gs_for, dn_for = tie(tall, gs_for, dn_for)
     (s12,) = stage(
-        functools.partial(pack_last, stats_at=stats_at), [((devices, high, n), BF16)]
-    )(tall, sums_1a, found_1b, kept, got, kept_1b, got_1b)
+        functools.partial(pack_last, stats_at=stats_at, part=(cut_6, share)),
+        [((devices, high, n), BF16)]
+    )(tall, sums_1a, kept, got, kept_1b, got_1b, xz)
     g12 = gather(s12)
     pixels = 4.0 * images.shape[1] * images.shape[1]
     batch = devices // 2
     far = batch // NEAR
     (mine,) = stage(
-        functools.partial(add_all, at=stats_at, pixels=pixels),
-        [((far, 2 * piece + share + 4, n), BF16)],
-    )(g12, labels, norm_1a, k_all, g5, found_2b)
+        functools.partial(
+            add_all, at=stats_at, pixels=pixels,
+            parts=((xz_3, 0, cut_3), (xz_6, cut_3, cut_6), (stats_at + 4, cut_6, share)),
+        ),
+        [((far, 2 * piece + share + 8, n), BF16)],
+    )(g12, labels, norm_1a, k_all, g3, g6, found_2b, found_1b)
     columns_of = [[k + NEAR * z for z in range(far)] for k in range(NEAR)]
     along = lax.all_to_all(mine, "batch", 0, 0, axis_index_groups=columns_of)
     near = [
@@ -1521,26 +1564,30 @@
         result, grad_norm_1c, grad_norm_1p, grad_norm_2a, grad_norm_2c
     )
     held = len(finished)
-    *finished, grad_images, grad_norm_1a, grad_norm_1b = stage(
+    *finished, grad_images, grad_norm_1a = stage(
         functools.partial(b13, at=stats_at, held=held),
-        [*((v.shape, v.dtype) for v in finished), (images.shape, BF16), *params(norm_1a, norm_1b)],
+        [*((v.shape, v.dtype) for v in finished), (images.shape, BF16), *params(norm_1a)],
         [pltpu.VMEM(half_in[0], BF16), pltpu.VMEM((inputs // n, rows, cols_in, n), F32),
-         pltpu.VMEM(images.shape, BF16), *(pltpu.VMEM(norm_1a.shape, F32) for _ in range(2)),
-         pltpu.SemaphoreType.DMA((held + 6,))],
-        hbm_out=range(held + 3),
+         pltpu.VMEM(images.shape, BF16), pltpu.VMEM(norm_1a.shape, F32),
+         pltpu.SemaphoreType.DMA((held + 5,))],
+        hbm_out=range(held + 2),
     )(tab, g12, labels, norm_1a, k_1a, w_1a, z_own, z_for, dn_own, dn_for, gs_own, gs_for, *finished)
     result, grad_norm_1c, grad_norm_1p, grad_norm_2a, grad_norm_2c = finished
     *near, grad_images = tie(*near, grad_images)
     parts = [along, *near]
     weights = (w_2c, w_2b.reshape(-1, n), w_2a, w_1c, w_1p, w_1b.reshape(-1, n), w_1a)
-    t_2c, t_2b, t_2a, t_1c, t_1p, t_1b, t_1a, grad_norm_2b = stage(
+    side = [
+        ((2, batch, piece, n), BF16), ((batch, share, n), F32), ((batch, 4, n), F32)
+    ]
+    crossed = [swap(v) for v in parts]
+    placed = stage(functools.partial(unpack_own, piece=piece), side)(tab, *parts)
+    t_2c, t_2b, t_2a, t_1c, t_1p, t_1b, t_1a, grad_norm_2b, grad_norm_1b = stage(
         functools.partial(unpack, first=first, second=second, piece=piece),
-        [(v.shape, F32) for v in (*weights, norm_2b)],
-        [*(pltpu.VMEM(v.shape, F32) for v in (*weights, norm_2b)),
-         pltpu.VMEM((devices, share, n), F32), pltpu.VMEM((2, devices, piece, n), BF16),
-         pltpu.VMEM((devices, 2, n), F32), pltpu.SemaphoreType.DMA((8,))],
-        hbm_out=range(8),
-    )(tab, labels, *parts, *(swap(v) for v in parts))
+        [(v.shape, F32) for v in (*weights, norm_2b, norm_1b)],
+        [*(pltpu.VMEM(v.shape, F32) for v in (*weights, norm_2b, norm_1b)),
+         *(pltpu.VMEM(*v) for v in side), pltpu.SemaphoreType.DMA((9,))],
+        hbm_out=range(9),
+    )(tab, labels, *placed, *crossed)
     grads = (
         grad_norm_1a, grad_norm_1b, grad_norm_1c, grad_norm_1p,
         grad_norm_2a, grad_norm_2b, grad_norm_2c,

time: 181 us -> 178 us (0.983)
  blocking collectives: 135 us -> 133 us
    all_to_all x10, blocking collectives: 125 us -> 123 us  [gather(): return lax.all_to_all(send, AXES, 0, 0)]
    pallas_call x21 -> x22, Pallas kernels: 34 us -> 33.8 us  [call(): pl.pallas_call(kernel, out_shape=tuple((jax.ShapeDtypeStruct(s, d) for s,...]
where the time goes in v9:
time: 178 us
  blocking collectives  133 us (75%)
  Pallas kernels  33.8 us (19%)
  starting transfers between devices  5.73 us (3%)
  waiting for transfers between devices  4.29 us (2%)
    all_to_all x10, blocking collectives, gather(): return lax.all_to_all(send, AXES, 0, 0)  123 us
    pallas_call x22, Pallas kernels, call(): pl.pallas_call(kernel, out_shape=tuple((jax.ShapeDtypeStruct(s, d) for s,...  33.8 us
    all_to_all x1, blocking collectives, body(): along = lax.all_to_all(mine, 'batch', 0, 0, axis_index_groups=columns_of)  9.55 us
  transfers between devices with their start and end apart: 12, of which 5 were waited for; matrix products, arithmetic and copies ran while one was open for 0% of the time, Pallas kernels for 4%

profile of v9, /device:TPU:0, one launch (start us, length us, event | category | flops | bytes accessed | tf_op | source)
XLA Modules:
  0.0 178.1 jit_solution(16463527546639031511)
XLA Ops:
  0.7 2.3 %f1.1 = (f32[8,128]{1,0:T(8,128)S(1)}, bf16[28,64,256]{2,1,0:T(8,128)(2,1)S(1)}, bf16[28,64,256]{2,1,0:T(8,128)(2,1)S(1)}, f32[28,64,128]{2,1,0:T(8,128)S(1)}, f...) custom-call(s32[1]{0:T(128)} %bitcast.place_at, s32[2]{0:T(128)} %group_at.1, s32[3]{0:T(128)} %width_at.1, ...), custom_call_target="tpu_custom_call" | custom-call | tf_op jit(solution)/shard_map/f1/pallas_call | solution.py:33
  3.8 14.2 %all_to_all.55.got = f32[32,1,640]{2,1,0:T(1,128)S(1)} all-to-all(f32[32,1,640]{2,1,0:T(1,128)S(1)} %get-tuple-element.158), channel_id=1, replica_groups=mesh['rows'=2,'batch'=16] {'rows','batch'}, dimensions={0} | all-to-all | bytes 163840 | tf_op jit(solution)/shard_map/all_to_all | solution.py:1358
  18.0 0.9 f1_strided.1
  18.9 1.9 %f2.1 = (bf16[29,32,768]{2,1,0:T(8,128)(2,1)S(1)}, f32[28,32,128]{2,1,0:T(8,128)S(1)}, f32[32,1,1024]{2,1,0:T(1,128)S(1)}, f32[32,1,128]{2,1,0:T(1,128)S(1)}, f3...) custom-call(f32[8,128]{1,0:T(8,128)S(1)} %get-tuple-element.144.tab, ...), custom_call_target="tpu_custom_call" | custom-call | tf_op jit(solution)/shard_map/f2/pallas_call | solution.py:33
  20.8 1.0 g_xz.1
  21.9 9.6 %all_to_all.56.got = f32[32,1,1024]{2,1,0:T(1,128)S(1)} all-to-all(f32[32,1,1024]{2,1,0:T(1,128)S(1)} %get-tuple-element.172), channel_id=1, replica_groups=mesh['rows'=2,'batch'=16] {'rows','batch'}, dimensions={0} | all-to-all | bytes 262144 | tf_op jit(solution)/shard_map/all_to_all | solution.py:1358
  31.5 1.7 f3.1
  33.2 9.8 %all_to_all.57.got.pair_low.got_act.got_a = bf16[32,16,128]{2,1,0:T(8,128)(2,1)S(1)} all-to-all(bf16[32,16,128]{2,1,0:T(8,128)(2,1)S(1)} %get-tuple-element.176), channel_id=1, replica_groups=mesh['rows'=2,'batch'=16] {'rows','batch'}, dimensions={0} | all-to-all | bytes 262144 | tf_op jit(solution)/shard_map/all_to_all | solution.py:1358
  43.1 1.4 f4.1
  44.6 9.9 %all_to_all.58.got.pair_high.got_q = bf16[32,16,128]{2,1,0:T(8,128)(2,1)S(1)} all-to-all(bf16[32,16,128]{2,1,0:T(8,128)(2,1)S(1)} %get-tuple-element.182), channel_id=1, replica_groups=mesh['rows'=2,'batch'=16] {'rows','batch'}, dimensions={0} | all-to-all | bytes 262144 | tf_op jit(solution)/shard_map/all_to_all | solution.py:1358
  54.5 1.1 f5.1
  55.6 9.2 %all_to_all.59.got = f32[32,1,256]{2,1,0:T(1,128)S(1)} all-to-all(f32[32,1,256]{2,1,0:T(1,128)S(1)} %get-tuple-element.186), channel_id=1, replica_groups=mesh['rows'=2,'batch'=16] {'rows','batch'}, dimensions={0} | all-to-all | bytes 65536 | tf_op jit(solution)/shard_map/all_to_all | solution.py:1358
  64.8 1.8 f6.1
  66.6 11.5 %all_to_all.60.got.got_act.got_b = bf16[32,24,128]{2,1,0:T(8,128)(2,1)S(1)} all-to-all(bf16[32,24,128]{2,1,0:T(8,128)(2,1)S(1)} %get-tuple-element.190), channel_id=1, replica_groups=mesh['rows'=2,'batch'=16] {'rows','batch'}, dimensions={0} | all-to-all | bytes 393216 | tf_op jit(solution)/shard_map/all_to_all | solution.py:1358
  78.1 2.8 %b7.1 = (bf16[28,28,512]{2,1,0:T(8,128)(2,1)S(1)}, f32[28,32,512]{2,1,0:T(8,128)S(1)}, bf16[32,32,128]{2,1,0:T(8,128)(2,1)S(1)}, f32[2,512]{1,0:T(2,128)S(1)}, f32[28,32,128]{2,1,0:T(8,128)S(1)}) custom-call(f32[8,128]{1,0:T(8,128)S(1)} %get-tuple-element.144.tab, bf16[32,24,128]{2,1,0:T(8,128)(2,1)S(1)} %all_to_all.60.got.got_act.got_b, ...), custom_call_target="tpu_custom_call" | custom-call | tf_op jit(solution)/shard_map/b7/pallas_call | solution.py:33
  80.9 12.9 %all_to_all.61.got.got_2c = bf16[32,32,128]{2,1,0:T(8,128)(2,1)S(1)} all-to-all(bf16[32,32,128]{2,1,0:T(8,128)(2,1)S(1)} %get-tuple-element.196), channel_id=1, replica_groups=mesh['rows'=2,'batch'=16] {'rows','batch'}, dimensions={0} | all-to-all | bytes 524288 | tf_op jit(solution)/shard_map/all_to_all | solution.py:1358
  93.8 2.5 %b9.1 = (bf16[28,32,128]{2,1,0:T(8,128)(2,1)S(1)}, f32[28,32,128]{2,1,0:T(8,128)S(1)}, bf16[32,16,128]{2,1,0:T(8,128)(2,1)S(1)}, f32[2,128]{1,0:T(2,128)S(1)}) custom-call(f32[8,128]{1,0:T(8,128)S(1)} %get-tuple-element.144.tab, bf16[32,32,128]{2,1,0:T(8,128)(2,1)S(1)} %all_to_all.61.got.got_2c, f32[32,1,128]{2,1,0:T(1,128)S(1)} %get-tuple-element.173.labels, ...), custom_call_target="tpu_custom_call" | custom-call | tf_op jit(solution)/shard_map/b9/pallas_call | solution.py:33
  96.3 9.6 %all_to_all.62.got.got_p.got_x = bf16[32,16,128]{2,1,0:T(8,128)(2,1)S(1)} all-to-all(bf16[32,16,128]{2,1,0:T(8,128)(2,1)S(1)} %get-tuple-element.205), channel_id=1, replica_groups=mesh['rows'=2,'batch'=16] {'rows','batch'}, dimensions={0} | all-to-all | bytes 262144 | tf_op jit(solution)/shard_map/all_to_all | solution.py:1358
  105.9 2.5 %b10.1 = (bf16[28,32,128]{2,1,0:T(8,128)(2,1)S(1)}, f32[28,32,512]{2,1,0:T(8,128)S(1)}, f32[32,2,896]{2,1,0:T(2,128)S(1)}, f32[3,2,128]{2,1,0:T(2,128)S(1)}, f32[28,32,128]{2,1,0:T(8,128)S(1)}) custom-call(f32[8,128]{1,0:T(8,128)S(1)} %get-tuple-element.144.tab, bf16[32,16,128]{2,1,0:T(8,128)(2,1)S(1)} %all_to_all.62.got.got_p.got_x, ...), custom_call_target="tpu_custom_call" | custom-call | tf_op jit(solution)/shard_map/b10/pallas_call | solution.py:33
  108.4 12.4 %all_to_all.63.got = f32[32,2,896]{2,1,0:T(2,128)S(1)} all-to-all(f32[32,2,896]{2,1,0:T(2,128)S(1)} %get-tuple-element.215), channel_id=1, replica_groups=mesh['rows'=2,'batch'=16] {'rows','batch'}, dimensions={0} | all-to-all | bytes 458752 | tf_op jit(solution)/shard_map/all_to_all | solution.py:1358
  120.8 3.6 %g_most.1 = (bf16[24,80,128]{2,1,0:T(8,128)(2,1)S(1)}, bf16[24,80,128]{2,1,0:T(8,128)(2,1)S(1)}, bf16[14,32,256]{2,1,0:T(8,128)(2,1)S(1)}, bf16[14,32,256]{2,1,0...) custom-call(f32[8,128]{1,0:T(8,128)S(1)} %get-tuple-element.144.tab,, ...), custom_call_target="tpu_custom_call" | custom-call | tf_op jit(solution)/shard_map/g_most/pallas_call | solution.py:33
  124.5 1.8 b12.1
  126.3 1.1 b12_images.2
  128.4 1.1 b12_images.3
  129.5 1.3 g_xd.1
  131.1 24.2 %all_to_all.64.got = bf16[32,96,128]{2,1,0:T(8,128)(2,1)S(1)} all-to-all(bf16[32,96,128]{2,1,0:T(8,128)(2,1)S(1)} %pack_last.1), channel_id=1, replica_groups=mesh['rows'=2,'batch'=16] {'rows','batch'}, dimensions={0} | all-to-all | bytes 1572864 | tf_op jit(solution)/shard_map/all_to_all | solution.py:1358
  155.6 9.6 %all_to_all.65.refs_0_ = bf16[4,176,128]{2,1,0:T(8,128)(2,1)S(1)} all-to-all(bf16[4,176,128]{2,1,0:T(8,128)(2,1)S(1)} %add_all.1), channel_id=1, replica_groups={{0,4,8,12},{1,5,9,13},{2,6,10,14},{3,7,11,15},{16,20,24,28},{17,21,25,2..., dimensions={0} | all-to-all | bytes 360448 | tf_op jit(solution)/shard_map/all_to_all | solution.py:1559
  166.6 2.1 %collective-permute-start.5 = (bf16[4,176,128]{2,1,0:T(8,128)(2,1)S(1)}, bf16[4,176,128]{2,1,0:T(8,128)(2,1)S(1)}, u32[]{:S(2)}, u32[]{:S(2)}) collective-permute-start(bf16[4,176,128]{2,1,0:T(8,128)(2,1)S(1)} %all_to_all.65.refs_0_), channel_id=1, source_target_pairs={{0,1},{1,0},{2,3},{3,2},{4,5},{5,4},{6,7},{7,6},{8,9},{9,8},{10,11... | collective-permute-start | bytes 540680 | tf_op jit(solution)/shard_map/ppermute | solution.py:1561
  168.7 2.4 %b13.1 = (bf16[28,28,512]{2,1,0:T(8,128)(2,1)}, f32[3,2,512]{2,1,0:T(2,128)}, f32[3,2,512]{2,1,0:T(2,128)}, f32[3,2,128]{2,1,0:T(2,128)}, f32[3,2,512]{2,1,0:T(2...) custom-call(f32[8,128]{1,0:T(8,128)S(1)} %get-tuple-element.144.tab, ...), custom_call_target="tpu_custom_call" | custom-call | tf_op jit(solution)/shard_map/b13/pallas_call | solution.py:33
  171.2 1.2 collective-permute-done.7.refs_3_
  172.4 1.8 %collective-permute-done.6.refs_2_ = bf16[4,176,128]{2,1,0:T(8,128)(2,1)S(1)} collective-permute-done((bf16[4,176,128]{2,1,0:T(8,128)(2,1)S(1)}, bf16[4,176,128]{2,1,0:T(8,128)(2,1)S(1)}, u32[]{:S(2)}, u32[]{:S(2)}) %collective-permute-start.6) | collective-permute-done | bytes 180256 | tf_op jit(solution)/shard_map/ppermute | solution.py:1561
  176.2 1.8 unpack.1
  (55 shorter events, 5.9 us)
Async XLA Ops:
  0.6 2.4 %copy-start.7 = (bf16[3,3,128,128]{3,2,1,0:T(8,128)(2,1)S(1)}, bf16[3,3,128,128]{3,2,1,0:T(8,128)(2,1)}, u32[]{:S(2)}) copy-start(bf16[3,3,128,128]{3,2,1,0:T(8,128)(2,1)} %w2b) | copy-start | bytes 884740
  0.7 2.4 %copy-start.6 = (bf16[3,3,128,128]{3,2,1,0:T(8,128)(2,1)S(1)}, bf16[3,3,128,128]{3,2,1,0:T(8,128)(2,1)}, u32[]{:S(2)}) copy-start(bf16[3,3,128,128]{3,2,1,0:T(8,128)(2,1)} %w1b) | copy-start | bytes 884740
  0.7 17.4 %copy-start = (bf16[256,512]{1,0:T(8,128)(2,1)S(1)}, bf16[256,512]{1,0:T(8,128)(2,1)}, u32[]{:S(2)}) copy-start(bf16[256,512]{1,0:T(8,128)(2,1)} %w_p.3) | copy-start | bytes 786436
  3.0 15.9 %copy-start.4 = (bf16[256,128]{1,0:T(8,128)(2,1)S(1)}, bf16[256,128]{1,0:T(8,128)(2,1)}, u32[]{:S(2)}) copy-start(bf16[256,128]{1,0:T(8,128)(2,1)} %w.15) | copy-start | bytes 196612
  3.0 15.9 %copy-start.10 = (f32[2,3,128]{2,0,1:T(2,128)S(1)}, f32[2,3,128]{2,0,1:T(2,128)}, u32[]{:S(2)}) copy-start(f32[2,3,128]{2,0,1:T(2,128)} %param.27) | copy-start | bytes 9220
  3.3 14.8 %collective-permute-start = (bf16[28,64,256]{2,1,0:T(8,128)(2,1)S(1)}, bf16[28,64,256]{2,1,0:T(8,128)(2,1)S(1)}, u32[]{:S(2)}, u32[]{:S(2)}) collective-permute-start(bf16[28,64,256]{2,1,0:T(8,128)(2,1)S(1)} %get-tuple-element.159), channel_id=1, source_target_pairs={{0,16},{16,0},{1,17},{17,1},{2,18},{18,2},{3,19},{19,3},{4,20},{20... | collective-permute-start | bytes 2752520 | tf_op jit(solution)/shard_map/ppermute | solution.py:1366
  20.8 10.7 %copy-start.1 = (bf16[128,512]{1,0:T(8,128)(2,1)S(1)}, bf16[128,512]{1,0:T(8,128)(2,1)}, u32[]{:S(2)}) copy-start(bf16[128,512]{1,0:T(8,128)(2,1)} %w_c.7) | copy-start | bytes 393220
  20.8 10.7 %copy-start.14 = (f32[2,3,128]{2,0,1:T(2,128)S(1)}, f32[2,3,128]{2,0,1:T(2,128)}, u32[]{:S(2)}) copy-start(f32[2,3,128]{2,0,1:T(2,128)} %param.28) | copy-start | bytes 9220
  20.8 22.3 %copy-start.5 = (bf16[512,128]{1,0:T(8,128)(2,1)S(1)}, bf16[512,128]{1,0:T(8,128)(2,1)}, u32[]{:S(2)}) copy-start(bf16[512,128]{1,0:T(8,128)(2,1)} %w.14) | copy-start | bytes 393220
  20.8 22.3 %copy-start.8 = (f32[2,3,512]{2,0,1:T(2,128)S(1)}, f32[2,3,512]{2,0,1:T(2,128)}, u32[]{:S(2)}) copy-start(f32[2,3,512]{2,0,1:T(2,128)} %param.29) | copy-start | bytes 36868
  20.8 22.2 %copy-start.11 = (f32[2,3,512]{2,0,1:T(2,128)S(1)}, f32[2,3,512]{2,0,1:T(2,128)}, u32[]{:S(2)}) copy-start(f32[2,3,512]{2,0,1:T(2,128)} %param.30) | copy-start | bytes 36868
  43.1 11.4 %copy-start.12 = (f32[2,3,128]{2,0,1:T(2,128)S(1)}, f32[2,3,128]{2,0,1:T(2,128)}, u32[]{:S(2)}) copy-start(f32[2,3,128]{2,0,1:T(2,128)} %param.31) | copy-start | bytes 9220
  43.1 21.7 %copy-start.2 = (bf16[128,512]{1,0:T(8,128)(2,1)S(1)}, bf16[128,512]{1,0:T(8,128)(2,1)}, u32[]{:S(2)}) copy-start(bf16[128,512]{1,0:T(8,128)(2,1)} %w_c.5) | copy-start | bytes 393220
  43.1 21.7 %copy-start.13 = (f32[2,3,128]{2,0,1:T(2,128)S(1)}, f32[2,3,128]{2,0,1:T(2,128)}, u32[]{:S(2)}) copy-start(f32[2,3,128]{2,0,1:T(2,128)} %param.32) | copy-start | bytes 9220
  44.6 33.5 %copy-start.3 = (bf16[1,28,28,512]{3,2,1,0:T(8,128)(2,1)S(1)}, bf16[1,28,28,512]{3,2,1,0:T(8,128)(2,1)}, u32[]{:S(2)}) copy-start(bf16[1,28,28,512]{3,2,1,0:T(8,128)(2,1)} %param.34) | copy-start | bytes 2408452
  44.6 33.5 %copy-start.9 = (f32[2,3,512]{2,0,1:T(2,128)S(1)}, f32[2,3,512]{2,0,1:T(2,128)}, u32[]{:S(2)}) copy-start(f32[2,3,512]{2,0,1:T(2,128)} %param.33) | copy-start | bytes 36868
  124.5 6.4 %collective-permute-start.3 = (bf16[24,80,128]{2,1,0:T(8,128)(2,1)S(1)}, bf16[24,80,128]{2,1,0:T(8,128)(2,1)S(1)}, u32[]{:S(2)}, u32[]{:S(2)}) collective-permute-start(bf16[24,80,128]{2,1,0:T(8,128)(2,1)S(1)} %get-tuple-element.234), channel_id=1, source_target_pairs={{0,16},{16,0},{1,17},{17,1},{2,18},{18,2},{3,19},{19,3},{4,20},{20... | collective-permute-start | bytes 1474568 | tf_op jit(solution)/shard_map/ppermute | solution.py:1366
  127.4 3.5 %collective-permute-start.2 = (bf16[28,64,128]{2,1,0:T(8,128)(2,1)S(1)}, bf16[28,64,128]{2,1,0:T(8,128)(2,1)S(1)}, u32[]{:S(2)}, u32[]{:S(2)}) collective-permute-start(bf16[28,64,128]{2,1,0:T(8,128)(2,1)S(1)} %get-tuple-element.224.dn_oth), channel_id=1, source_target_pairs={{0,16},{16,0},{1,17},{17,1},{2,18},{18,2},{3,19},{19,3},{4,20},{20... | collective-permute-start | bytes 1376264 | tf_op jit(solution)/shard_map/ppermute | solution.py:1366
  127.9 2.9 %collective-permute-start.1 = (bf16[14,32,256]{2,1,0:T(8,128)(2,1)S(1)}, bf16[14,32,256]{2,1,0:T(8,128)(2,1)S(1)}, u32[]{:S(2)}, u32[]{:S(2)}) collective-permute-start(bf16[14,32,256]{2,1,0:T(8,128)(2,1)S(1)} %get-tuple-element.230), channel_id=1, source_target_pairs={{0,16},{16,0},{1,17},{17,1},{2,18},{18,2},{3,19},{19,3},{4,20},{20... | collective-permute-start | bytes 688136 | tf_op jit(solution)/shard_map/ppermute | solution.py:1366
  128.0 2.9 %collective-permute-start.4 = (bf16[8,80,128]{2,1,0:T(8,128)(2,1)S(1)}, bf16[8,80,128]{2,1,0:T(8,128)(2,1)S(1)}, u32[]{:S(2)}, u32[]{:S(2)}) collective-permute-start(bf16[8,80,128]{2,1,0:T(8,128)(2,1)S(1)} %get-tuple-element.236), channel_id=1, source_target_pairs={{0,16},{16,0},{1,17},{17,1},{2,18},{18,2},{3,19},{19,3},{4,20},{20... | collective-permute-start | bytes 491528 | tf_op jit(solution)/shard_map/ppermute | solution.py:1366
  165.2 7.2 %collective-permute-start.7 = (bf16[4,176,128]{2,1,0:T(8,128)(2,1)S(1)}, bf16[4,176,128]{2,1,0:T(8,128)(2,1)S(1)}, u32[]{:S(2)}, u32[]{:S(2)}) collective-permute-start(bf16[4,176,128]{2,1,0:T(8,128)(2,1)S(1)} %all_to_all.65.refs_0_), channel_id=1, source_target_pairs={{0,3},{1,2},{2,1},{3,0},{4,7},{5,6},{6,5},{7,4},{8,11},{9,10},{10,... | collective-permute-start | bytes 540680 | tf_op jit(solution)/shard_map/ppermute | solution.py:1561
  165.9 8.3 %collective-permute-start.6 = (bf16[4,176,128]{2,1,0:T(8,128)(2,1)S(1)}, bf16[4,176,128]{2,1,0:T(8,128)(2,1)S(1)}, u32[]{:S(2)}, u32[]{:S(2)}) collective-permute-start(bf16[4,176,128]{2,1,0:T(8,128)(2,1)S(1)} %all_to_all.65.refs_0_), channel_id=1, source_target_pairs={{0,2},{1,3},{2,0},{3,1},{4,6},{5,7},{6,4},{7,5},{8,10},{9,11},{10,... | collective-permute-start | bytes 540680 | tf_op jit(solution)/shard_map/ppermute | solution.py:1561
  166.6 7.6 %collective-permute-start.5 = (bf16[4,176,128]{2,1,0:T(8,128)(2,1)S(1)}, bf16[4,176,128]{2,1,0:T(8,128)(2,1)S(1)}, u32[]{:S(2)}, u32[]{:S(2)}) collective-permute-start(bf16[4,176,128]{2,1,0:T(8,128)(2,1)S(1)} %all_to_all.65.refs_0_), channel_id=1, source_target_pairs={{0,1},{1,0},{2,3},{3,2},{4,5},{5,4},{6,7},{7,6},{8,9},{9,8},{10,11... | collective-permute-start | bytes 540680 | tf_op jit(solution)/shard_map/ppermute | solution.py:1561
  171.1 3.9 %collective-permute-start.8 = (bf16[4,176,128]{2,1,0:T(8,128)(2,1)S(1)}, bf16[4,176,128]{2,1,0:T(8,128)(2,1)S(1)}, u32[]{:S(2)}, u32[]{:S(2)}) collective-permute-start(bf16[4,176,128]{2,1,0:T(8,128)(2,1)S(1)} %all_to_all.65.refs_0_), channel_id=1, source_target_pairs={{0,16},{16,0},{1,17},{17,1},{2,18},{18,2},{3,19},{19,3},{4,20},{20... | collective-permute-start | bytes 540680 | tf_op jit(solution)/shard_map/ppermute | solution.py:1366
  174.2 1.4 collective-permute-start.9
  174.2 1.7 collective-permute-start.10
  174.7 1.4 collective-permute-start.11

commit v10 on v9

--- a/solution.py
+++ b/solution.py
@@ -273,7 +273,7 @@
                 xee[first + i, :, lanes] = wide[b, pl.ds(0, COLS, stride=2), :].astype(BF16)
             return carry
 
-        lax.fori_loop(0, rows, put, 0, unroll=2)
+        lax.fori_loop(0, rows, put, 0, unroll=4)
     total = 2 * rows
     step = total // 7
     chans = z.shape[2]
@@ -374,7 +374,7 @@
                         lane += n
             return carry
 
-        lax.fori_loop(0, rows // 2, put, 0, unroll=2)
+        lax.fori_loop(0, rows // 2, put, 0, unroll=4)
     extra = [stats_p[:, lanes] for lanes in columns(stats_p.shape[1])]
     pair = (slice(3 * n, 6 * n), w_odd[...], (1, 0))
     conv_stats(z, xs, pair, (slice(0, 3 * n), w_even[...], 1), send, extra)
@@ -436,33 +436,40 @@
     return jnp.concatenate(rows, axis=0)
 
 
-def pair_products(tab, z, norm, keeps, act, act_sum, slope, both):
+def activate_pair(tab, got, labels, z, norm, act, keeps, slope, both):
     rows = z.shape[0]
-    label = entry(tab, OWN)
-    mean, rstd = keeps[0:1, :], keeps[1:2, :]
-    scale = rstd * gain_of(norm, label)
-    bias = 0.5 * (shift_of(norm, label) - mean * scale)
+    pixels = 1.0 * rows * (COLS - 4)
+    mean, rstd, gain, shift, _ = scale_shift(got, labels[...], tab, norm, pixels)
+    keeps[0:1, :] = mean
+    keeps[1:2, :] = rstd
+    scale = rstd * gain
+    bias = 0.5 * (shift - mean * scale)
     scale = 0.5 * scale
     keep = valid_cols(LANES) & chan_mask(tab)
-    middle = act_sum * (1.0 / (rows * (COLS - 4)))
 
     def put(i, carry):
         zz = z[i]
-        s = jnp.where(keep, slope_of_half(zz * scale + bias), 0.0)
+        u = zz * scale + bias
+        t = jnp.tanh(u)
+        p = u * t
+        low = jnp.where(keep, u + p, 0.0).astype(BF16)
+        act[i] = low
+        s = jnp.where(keep, (0.5 + 0.5 * t) * (1.0 + u - p), 0.0)
         sx = s * ((zz - mean) * rstd)
         slope[i] = s
         for k, v in enumerate((s, sx)):
             high = v.astype(BF16)
             both[i, :, LANES * k : LANES * (k + 1)] = high
             both[i, :, LANES * (k + 2) : LANES * (k + 3)] = (v - high.astype(F32)).astype(BF16)
-        return carry[0] + fold(s), carry[1] + fold(sx)
-
-    sums = lax.fori_loop(0, rows, put, (zeros8(LANES), zeros8(LANES)), unroll=4)
-    sums = [down(v) for v in sums]
+        return carry[0] + fold(low.astype(F32)), carry[1] + fold(s), carry[2] + fold(sx)
+
+    start = zeros8(LANES)
+    sums = lax.fori_loop(0, rows, put, (start, start, start), unroll=4)
+    act_sum, *sums = [down(v) for v in sums]
     product = mm_tn(flat(act[...]), flat(both[...]))
     product = product[:, 0 : 2 * LANES] + product[:, 2 * LANES :]
-    column = jnp.transpose(jnp.broadcast_to(middle, (8, LANES)))[:, 0:1]
-    return product - column * join(sums), stack(sums)
+    middle = jnp.broadcast_to(act_sum * (1.0 / pixels), (8, LANES))
+    return act_sum, product - jnp.transpose(middle)[:, 0:1] * join(sums), stack(sums)
 
 
 def rows_of(line):
@@ -543,32 +550,13 @@
     return both, e - line[:, 0:n] - line[:, n:], coefs, found
 
 
-def activate(tab, got, labels, z_in, norm, act, keeps):
-    got = got.at[:, :, 0 : 2 * LANES]
-    rows = z_in.shape[0]
-    pixels = 1.0 * rows * (COLS - 4)
-    mean, rstd, gain, shift, _ = scale_shift(got, labels[...], tab, norm, pixels)
-    keeps[0:1, :] = mean
-    keeps[1:2, :] = rstd
-    scale = rstd * gain
-    bias = 0.5 * (shift - mean * scale)
-    scale = 0.5 * scale
-    keep = valid_cols(LANES) & chan_mask(tab)
-
-    def put(i, sums):
-        low = jnp.where(keep, silu_of_half(z_in[i] * scale + bias), 0.0).astype(BF16)
-        act[i] = low
-        return sums + fold(low.astype(F32))
-
-    return down(lax.fori_loop(0, rows, put, zeros8(LANES), unroll=7))
-
-
 def f3(
     tab, got, labels, z_in, norm, w, w_p, xz,
     act, z, send, keeps, keeps_p, slope, q, high, own, both, low, *, share, part,
 ):
-    sums = activate(tab, got, labels, z_in, norm, act, keeps)
-    at = expand_pair(tab, z_in, norm, keeps, act, sums, w, z, send, slope, q, both, high, low, own, share)
+    got_1 = got.at[:, :, 0 : 2 * LANES]
+    found = activate_pair(tab, got_1, labels, z_in, norm, act, keeps, slope, both)
+    at = expand_pair(found, act, w, z, send, q, high, low, own, share)
     send[:, at : at + 2 * share, :] = low[...]
     put_part(send, at + 2 * share, xz, part)
     marks, label = labels[...], entry(tab, OWN)
@@ -581,12 +569,12 @@
     keeps_p[1:2, :] = rstd
 
 
-def expand_pair(tab, z_in, norm, keeps, act, sums, w, z, send, slope, q, both, high, low, own, share):
+def expand_pair(found, act, w, z, send, q, high, low, own, share):
+    sums, product, q[...] = found
     pixels = 1.0 * z.shape[0] * (COLS - 4)
     squares = project(act, w, z)
     first = through(sums, w[...])
     second = squares - first * first / pixels
-    product, q[...] = pair_products(tab, z_in, norm, keeps, act, sums, slope, both)
     pair_rows(product, send.shape[0], share, high, low, own)
     put_split(send, 0, sums)
     moved = rows_of(second).astype(BF16)
@@ -659,7 +647,7 @@
         x3[i + 1, :, 2 * n : 3 * n] = pltpu.roll(act, COLS - 1, 0).astype(BF16)
         return carry
 
-    lax.fori_loop(0, rows, put, 0, unroll=2)
+    lax.fori_loop(0, rows, put, 0, unroll=4)
     lanes = slice(0, 3 * n)
     conv_stats(
         z, x3, (lanes, w_two[...], (0, 1)), (lanes, w_last[...], 2), send
@@ -670,8 +658,9 @@
     tab, got, labels, z_in, norm, w, xz,
     act, z, send, keeps, slope, q, own, both, high, low, *, share, part,
 ):
-    sums = activate(tab, got, labels, z_in, norm, act, keeps)
-    at = expand_pair(tab, z_in, norm, keeps, act, sums, w, z, send, slope, q, both, high, low, own, share)
+    got_1 = got.at[:, :, 0 : 2 * LANES]
+    found = activate_pair(tab, got_1, labels, z_in, norm, act, keeps, slope, both)
+    at = expand_pair(found, act, w, z, send, q, high, low, own, share)
     send[:, at : at + 2 * share, :] = high[...]
     send[:, at + 2 * share : at + 4 * share, :] = low[...]
     put_part(send, at + 4 * share, xz, part)
@@ -726,7 +715,7 @@
         return sums + fold(g), products + fold(g * (zz - mean))
 
     start = zeros8(chans)
-    sums, products = lax.fori_loop(0, rows, put, (start, start), unroll=2)
+    sums, products = lax.fori_loop(0, rows, put, (start, start), unroll=4)
     inner = inner_sums(low, w, slope_in, z_in, keeps_in, d_in)
     blocks = chans // LANES
     put_split(send, 0, rows_of(down(sums) * gate))
@@ -738,33 +727,39 @@
     pass_pair(send, 4 * blocks + 8, high, low_p, marks, norm.shape[0])
 
 
-def lane_sums(got, marks, channels):
-    def sums_of(g):
-        total = group_sum(got, marks, float(g))
-        return row(total, 0), row(total, 1)
-
-    return sums_of
-
-
-def row_sums(got, marks):
-    def sums_of(g):
-        total = over_group(get_split(got, 0, 2), marks, float(g))
-        return total[0:1], total[1:2]
-
-    return sums_of
-
-
-def backward_norm(tab, sums_of, marks, norm, keeps, pixels, grad_norm):
-    group, chans = entry(tab, OWN), norm.shape[2]
-    sums = [sums_of(g) for g in range(norm.shape[0])]
-    for g, (shift_sum, gain_sum) in enumerate(sums):
-        grad_norm[g, 0:1, :] = gain_sum
-        grad_norm[g, 1:2, :] = shift_sum
-    count = tiled(group_count(marks, group), chans) * pixels
-    own_shift, own_gain = (own_of([v[k] for v in sums], group) for k in (0, 1))
+def own_coefs(tab, marks, norm, keeps, pixels, shift_sum, gain_sum):
+    group = entry(tab, OWN)
+    count = tiled(group_count(marks, group), norm.shape[2]) * pixels
     mean, rstd = keeps[0:1, :], keeps[1:2, :]
     a = rstd * gain_of(norm, group)
-    return mean, a, -(a * rstd) * own_gain / count, -a * own_shift / count
+    return mean, a, -(a * rstd) * gain_sum / count, -a * shift_sum / count
+
+
+def wide_lines(total, outer):
+    side = outer // 2
+    return [join([total[h : h + 1, side * k : side * (k + 1)] for h in (0, 1)]) for k in range(3)]
+
+
+def norm_tail(labels, got_2c, got_2a, got_1, grad_2c, grad_2a, grad_1c, grad_1p):
+    marks = labels[...]
+    outer = grad_2c.shape[2]
+    blocks = outer // LANES
+    for g in range(grad_2c.shape[0]):
+        label = float(g)
+        rows = [
+            line_of(over_group(get_split(got_2c, 2 * blocks * k, blocks), marks, label))
+            for k in (0, 1)
+        ]
+        pair = over_group(get_split(got_2a, 0, 2), marks, label)
+        lines = wide_lines(group_sum(got_1, marks, label), outer)
+        for out, shift_sum, gain_sum in (
+            (grad_2c, rows[0], rows[1]),
+            (grad_2a, pair[0:1], pair[1:2]),
+            (grad_1c, lines[0], lines[1]),
+            (grad_1p, lines[0], lines[2]),
+        ):
+            out[g, 0:1, :] = gain_sum
+            out[g, 1:2, :] = shift_sum
 
 
 def slope_sums(tab, d, z_in, norm, keeps, dout):
@@ -827,7 +822,7 @@
         d3[i + 1, :, 2 * n : 3 * n] = pltpu.roll(v, 1, 0).astype(BF16)
         return carry
 
-    lax.fori_loop(0, rows, put, 0, unroll=2)
+    lax.fori_loop(0, rows, put, 0, unroll=4)
     step = rows // 4
     for k in range(4):
         both = mm_nt(flat(d3[step * k : step * (k + 1) + 1]), b_two[...])
@@ -844,12 +839,13 @@
 def b10(
     tab, got, labels, dout_in, z, norm, keeps, w, grad_pre, slope, zc, zp, keeps_cp,
     norm_c, w_c, slope_in, z_in, keeps_in,
-    dz, grad_pre_2, send, grad_norm, d_in, d, low,
+    dz, grad_pre_2, send, d_in, d, low,
 ):
     rows, chans = zc.shape[0], zc.shape[2]
     pixels = 1.0 * rows * (COLS - 4)
     marks = labels[...]
-    coefs = backward_norm(tab, row_sums(got, marks), marks, norm, keeps, pixels, grad_norm)
+    total = over_group(get_split(got, 0, 2), marks, entry(tab, OWN))
+    coefs = own_coefs(tab, marks, norm, keeps, pixels, total[0:1], total[1:2])
     normed_grad(dz, dout_in, z, *coefs)
     d[...] = mm_nt(flat(dz[...]), w[...]).reshape(d.shape)
     mean_c, rstd_c, mean_p, rstd_p = (keeps_cp[k : k + 1, :] for k in range(4))
@@ -867,7 +863,7 @@
         )
 
     start = zeros8(chans)
-    sums, prod_c, prod_p = lax.fori_loop(0, rows, sum_up, (start, start, start), unroll=2)
+    sums, prod_c, prod_p = lax.fori_loop(0, rows, sum_up, (start, start, start), unroll=4)
     wide = [down(sums), down(prod_c) * rstd_c, down(prod_p) * rstd_p]
     inner = inner_sums(low, w_c, slope_in, z_in, keeps_in, d_in)
     parts = [stack([v[:, 0 : chans // 2], v[:, chans // 2 :]]) for v in wide]
@@ -906,7 +902,7 @@
         dz[i] = jnp.where(keep, v, 0.0).astype(BF16)
         return carry
 
-    lax.fori_loop(0, z.shape[0], put, 0, unroll=2)
+    lax.fori_loop(0, z.shape[0], put, 0, unroll=4)
 
 
 def b12(
@@ -987,7 +983,7 @@
             dn[2 * i + ra] = wide[ra].astype(BF16)
         return sums, products
 
-    totals = lax.fori_loop(0, rows, emit, (zeros8(n), zeros8(n)), unroll=2)
+    totals = lax.fori_loop(0, rows, emit, (zeros8(n), zeros8(n)), unroll=4)
     sums_out[0:1, :] = down(totals[0])
     sums_out[1:2, :] = down(totals[1]) * rstd_1
 
@@ -1083,49 +1079,30 @@
 
 
 def g_most(
-    tab, act_2b, x3, dz_2b, joined, dz_2a, act_1b, xee, w_p,
+    tab, act_2b, x3, dz_2b, joined, dz_2a, act_1b, xee,
     got, labels, norm_c, norm_p, keeps, grad_pre_2, zc, zp,
     got_2c, norm_2c, keeps_2c, grad_pre, z_2c,
-    kept, sent, gs_own, gs_oth, grad_norm_c, grad_norm_p, grad_norm_2c, own10, packed, dz_1c, dz_p, dz_2c,
+    kept, sent, dz_p, own10, packed, dz_1c, dz_2c,
 ):
     rows, outer = dz_2b.shape[0], zc.shape[2]
     pixels = 1.0 * rows * (COLS - 4)
-    marks = labels[...]
-
+    marks, label = labels[...], entry(tab, OWN)
     blocks = outer // LANES
-    label = entry(tab, OWN)
-
-    def wide_sums(source, count):
-        values = [get_split(source, 2 * blocks * k, blocks) for k in range(count)]
-        return [
-            [line_of(over_group(v, marks, float(g))) for v in values]
-            for g in range(norm_c.shape[0])
-        ]
-
-    totals = [group_sum(got, marks, float(g)) for g in range(norm_c.shape[0])]
-    side = outer // 2
-    lines = [
-        [join([total[h : h + 1, side * k : side * (k + 1)] for h in (0, 1)]) for k in range(3)]
-        for total in totals
+    total = group_sum(got, marks, label)
+    lines = wide_lines(total, outer)
+    for k in range(2):
+        own10[:, outer * k : outer * (k + 1)] = lines[k]
+        at = 2 * outer + LANES * k
+        own10[:, at : at + LANES] = total[k : k + 1, 3 * outer // 2 :]
+    wide = [
+        line_of(over_group(get_split(got_2c, 2 * blocks * k, blocks), marks, label)) for k in (0, 1)
     ]
-    for k in range(2):
-        own10[:, outer * k : outer * (k + 1)] = own_of([v[k] for v in lines], label)
-        at = 2 * outer + LANES * k
-        own10[:, at : at + LANES] = own_of([v[k : k + 1, 3 * side :] for v in totals], label)
-    lines_2c = wide_sums(got_2c, 2)
-    mean, a, b, c = backward_norm(
-        tab, lambda g: (lines_2c[g][0], lines_2c[g][1]), marks, norm_2c, keeps_2c, pixels,
-        grad_norm_2c,
-    )
+    mean, a, b, c = own_coefs(tab, marks, norm_2c, keeps_2c, pixels, *wide)
     gate = 0.25 * tiled(entry(tab, GATE), outer)
     normed_grad(dz_2c, grad_pre, z_2c, mean, a * gate, b, c)
-    coefs = backward_norm(
-        tab, lambda g: (lines[g][0], lines[g][1]), marks, norm_c, keeps.at[0:2], pixels, grad_norm_c
-    )
+    coefs = own_coefs(tab, marks, norm_c, keeps.at[0:2], pixels, lines[0], lines[1])
     normed_grad(dz_1c, grad_pre_2, zc, *coefs)
-    coefs = backward_norm(
-        tab, lambda g: (lines[g][0], lines[g][2]), marks, norm_p, keeps.at[2:4], pixels, grad_norm_p
-    )
+    coefs = own_coefs(tab, marks, norm_p, keeps.at[2:4], pixels, lines[0], lines[2])
     normed_grad(dz_p, grad_pre_2, zp, *coefs)
     at = put_rows(packed, 0, mm_tn(flat(act_2b[...]), flat(dz_2c[...])))
     low = flat(dz_2b[...])
@@ -1135,6 +1112,9 @@
     at = put_rows(packed, at, mm_tn(flat(act_1b[...]), flat(dz_1c[...])))
     at = put_rows(packed, at, mm_tn(flat(xee[...]), flat(dz_p[...])))
     share_out(tab, packed, at, kept, sent)
+
+
+def strided_grad(tab, dz_p, w_p, gs_own, gs_oth):
     half = half_of(tab)
     count = gs_own.shape[0]
     for k, gs in enumerate((gs_own, gs_oth)):
@@ -1185,8 +1165,9 @@
             return carry
 
         lax.fori_loop(0, rows, put, 0, unroll=4)
-        term = mm_tn(flat(x[...]), flat(low[...]))
+        term = mm_tn(flat(low[...]), flat(x[...]))
         value = term if value is None else value + term
+    value = stack([jnp.transpose(value[:, lanes]) for lanes in columns(value.shape[1])])
     marks, label = labels[...], entry(tab, OWN)
     total = over_group(get_split(got_x, 4, x_sum.shape[0] // n), marks, label)
     total = join([total[k : k + 1] for k in range(total.shape[0])])
@@ -1323,9 +1304,11 @@
                     out += span(*most[1], start, at + rows - size - start)
                 return out[0] if len(out) == 1 else stack(out)
 
-            at = 0
-            for k, value in enumerate(values[0:5]):
-                at = take_rows(source, at, value)
+            starts = [0]
+            for value in values[0:4]:
+                starts.append(starts[-1] + value.shape[0] * value.shape[1] // LANES)
+            for k in (1, 4):
+                take_rows(source, starts[k], values[k])
                 copies[k].start()
             left = w_1b.shape[0]
             for k, (cut, pieces, middle) in enumerate(last):
@@ -1335,6 +1318,9 @@
                 w_1b[start : start + rows, :] = lines[0] if len(lines) == 1 else stack(lines)
                 left -= rows
             copies[5].start()
+            for k in (0, 2, 3):
+                take_rows(source, starts[k], values[k])
+                copies[k].start()
             lines = stack([flat(v[...]) for v in tall])
             w_1a[...] = lines[0 : w_1a.shape[0]]
             copies[6].start()
@@ -1488,9 +1474,9 @@
     )(tab, g7, labels, norm_2c, k_2c, w_2c, g6, act_2b, slope_2b, d_2b, z_2b, norm_2b, k_2b,
       b_two, b_last, z_2a, norm_2a, k_2a, x_sum, g4, g3, own_2b)
     g9 = gather(s9)
-    dz_2a, grad_pre_2, s10, grad_norm_2a, d_1b = stage(
+    dz_2a, grad_pre_2, s10, d_1b = stage(
         b10,
-        [maps(n, BF16), maps(outer), ((devices, 2, 3 * outer // 2 + n), F32), *params(norm_2a), maps(n)],
+        [maps(n, BF16), maps(outer), ((devices, 2, 3 * outer // 2 + n), F32), maps(n)],
         [scratch(outer), scratch(outer, BF16)],
     )(tab, g9, labels, dout_2a, z_2a, norm_2a, k_2a, w_2a, grad_pre, slope, z_1c, z_1p, k_cp,
       norm_1c, w_1c, slope_1b, z_1b, k_1b)
@@ -1503,14 +1489,14 @@
         piece += 16
     first, second = -(-most_rows // (2 * piece)), -(-rows_1b // (2 * piece))
     part, part_1b = ((first, piece, n), BF16), ((second, piece, n), BF16)
-    kept, sent, gs_own, gs_send, grad_norm_1c, grad_norm_1p, grad_norm_2c, own10 = stage(
+    kept, sent, dz_1p, own10 = stage(
         g_most,
-        [part, part, half_map, half_map, *params(norm_1c, norm_1p, norm_2c),
-         ((1, 2 * outer + 2 * n), F32)],
-        [pltpu.VMEM((2 * first * piece, n), BF16), *(scratch(outer, BF16) for _ in range(3))],
-    )(tab, act_2b, x3, dz_2b, joined, dz_2a, act_1b, xee, w_1p,
+        [part, part, maps(outer, BF16), ((1, 2 * outer + 2 * n), F32)],
+        [pltpu.VMEM((2 * first * piece, n), BF16), *(scratch(outer, BF16) for _ in range(2))],
+    )(tab, act_2b, x3, dz_2b, joined, dz_2a, act_1b, xee,
       g10, labels, norm_1c, norm_1p, k_cp, grad_pre_2, z_1c, z_1p,
       g7, norm_2c, k_2c, grad_pre, z_2c)
+    gs_own, gs_send = stage(strided_grad, [half_map, half_map])(tab, dz_1p, w_1p)
     got, gs_for = swap(sent), swap(gs_send)
     half_in = ((rows, cols_in, n), BF16)
     d2, kept_1b, sent_1b, found_1b = stage(
@@ -1560,9 +1546,9 @@
     near = [
         lax.ppermute(along, "batch", [(i, i ^ k) for i in range(batch)]) for k in range(1, NEAR)
     ]
-    finished = (
-        result, grad_norm_1c, grad_norm_1p, grad_norm_2a, grad_norm_2c
-    )
+    late, _ = tie(labels, along)
+    grad_norms = stage(norm_tail, params(norm_2c, norm_2a, norm_1c, norm_1p))(late, g7, g9, g10)
+    finished = (result, *grad_norms)
     held = len(finished)
     *finished, grad_images, grad_norm_1a = stage(
         functools.partial(b13, at=stats_at, held=held),
@@ -1572,7 +1558,7 @@
          pltpu.SemaphoreType.DMA((held + 5,))],
         hbm_out=range(held + 2),
     )(tab, g12, labels, norm_1a, k_1a, w_1a, z_own, z_for, dn_own, dn_for, gs_own, gs_for, *finished)
-    result, grad_norm_1c, grad_norm_1p, grad_norm_2a, grad_norm_2c = finished
+    result, grad_norm_2c, grad_norm_2a, grad_norm_1c, grad_norm_1p = finished
     *near, grad_images = tie(*near, grad_images)
     parts = [along, *near]
     weights = (w_2c, w_2b.reshape(-1, n), w_2a, w_1c, w_1p, w_1b.reshape(-1, n), w_1a)

time: 178 us -> 177 us (level)
    pallas_call x22 -> x24, Pallas kernels: 33.8 us -> 33.1 us  [call(): pl.pallas_call(kernel, out_shape=tuple((jax.ShapeDtypeStruct(s, d) for s,...]
  transfers between devices with their start and end apart: 12 -> 12, of which waited for: 5 -> 5; matrix products, arithmetic and copies ran while one was open for 0% -> 0% of each run, Pallas kernels for 4% -> 5%
where the time goes in v10:
time: 177 us
  blocking collectives  133 us (75%)
  Pallas kernels  33.1 us (19%)
  starting transfers between devices  5.73 us (3%)
  waiting for transfers between devices  3.69 us (2%)
    all_to_all x10, blocking collectives, gather(): return lax.all_to_all(send, AXES, 0, 0)  123 us
    pallas_call x24, Pallas kernels, call(): pl.pallas_call(kernel, out_shape=tuple((jax.ShapeDtypeStruct(s, d) for s,...  33.1 us
    all_to_all x1, blocking collectives, body(): along = lax.all_to_all(mine, 'batch', 0, 0, axis_index_groups=columns_of)  9.55 us
  transfers between devices with their start and end apart: 12, of which 5 were waited for; matrix products, arithmetic and copies ran while one was open for 0% of the time, Pallas kernels for 5%

profile of v10, /device:TPU:0, one launch (start us, length us, event | category | flops | bytes accessed | tf_op | source)
XLA Modules:
  0.0 176.7 jit_solution(17381623694448055327)
XLA Ops:
  0.7 2.3 %f1.1 = (f32[8,128]{1,0:T(8,128)S(1)}, bf16[28,64,256]{2,1,0:T(8,128)(2,1)S(1)}, bf16[28,64,256]{2,1,0:T(8,128)(2,1)S(1)}, f32[28,64,128]{2,1,0:T(8,128)S(1)}, f...) custom-call(s32[1]{0:T(128)} %bitcast.place_at, s32[2]{0:T(128)} %group_at.1, s32[3]{0:T(128)} %width_at.1, ...), custom_call_target="tpu_custom_call" | custom-call | tf_op jit(solution)/shard_map/f1/pallas_call | solution.py:33
  3.8 14.2 %all_to_all.55.got = f32[32,1,640]{2,1,0:T(1,128)S(1)} all-to-all(f32[32,1,640]{2,1,0:T(1,128)S(1)} %get-tuple-element.160), channel_id=1, replica_groups=mesh['rows'=2,'batch'=16] {'rows','batch'}, dimensions={0} | all-to-all | bytes 163840 | tf_op jit(solution)/shard_map/all_to_all | solution.py:1344
  18.0 0.9 f1_strided.1
  18.9 1.8 %f2.1 = (bf16[29,32,768]{2,1,0:T(8,128)(2,1)S(1)}, f32[28,32,128]{2,1,0:T(8,128)S(1)}, f32[32,1,1024]{2,1,0:T(1,128)S(1)}, f32[32,1,128]{2,1,0:T(1,128)S(1)}, f3...) custom-call(f32[8,128]{1,0:T(8,128)S(1)} %get-tuple-element.146.tab, ...), custom_call_target="tpu_custom_call" | custom-call | tf_op jit(solution)/shard_map/f2/pallas_call | solution.py:33
  20.8 1.1 g_xz.1
  21.9 9.6 %all_to_all.56.got = f32[32,1,1024]{2,1,0:T(1,128)S(1)} all-to-all(f32[32,1,1024]{2,1,0:T(1,128)S(1)} %get-tuple-element.174), channel_id=1, replica_groups=mesh['rows'=2,'batch'=16] {'rows','batch'}, dimensions={0} | all-to-all | bytes 262144 | tf_op jit(solution)/shard_map/all_to_all | solution.py:1344
  31.5 1.4 f3.1
  32.9 9.8 %all_to_all.57.got.pair_low.got_act.got_a = bf16[32,16,128]{2,1,0:T(8,128)(2,1)S(1)} all-to-all(bf16[32,16,128]{2,1,0:T(8,128)(2,1)S(1)} %get-tuple-element.178), channel_id=1, replica_groups=mesh['rows'=2,'batch'=16] {'rows','batch'}, dimensions={0} | all-to-all | bytes 262144 | tf_op jit(solution)/shard_map/all_to_all | solution.py:1344
  42.8 1.4 f4.1
  44.2 9.9 %all_to_all.58.got.pair_high.got_q = bf16[32,16,128]{2,1,0:T(8,128)(2,1)S(1)} all-to-all(bf16[32,16,128]{2,1,0:T(8,128)(2,1)S(1)} %get-tuple-element.184), channel_id=1, replica_groups=mesh['rows'=2,'batch'=16] {'rows','batch'}, dimensions={0} | all-to-all | bytes 262144 | tf_op jit(solution)/shard_map/all_to_all | solution.py:1344
  54.1 1.0 f5.1
  55.1 9.2 %all_to_all.59.got = f32[32,1,256]{2,1,0:T(1,128)S(1)} all-to-all(f32[32,1,256]{2,1,0:T(1,128)S(1)} %get-tuple-element.188), channel_id=1, replica_groups=mesh['rows'=2,'batch'=16] {'rows','batch'}, dimensions={0} | all-to-all | bytes 65536 | tf_op jit(solution)/shard_map/all_to_all | solution.py:1344
  64.3 1.3 f6.1
  65.6 11.5 %all_to_all.60.got.got_act.got_b = bf16[32,24,128]{2,1,0:T(8,128)(2,1)S(1)} all-to-all(bf16[32,24,128]{2,1,0:T(8,128)(2,1)S(1)} %get-tuple-element.192), channel_id=1, replica_groups=mesh['rows'=2,'batch'=16] {'rows','batch'}, dimensions={0} | all-to-all | bytes 393216 | tf_op jit(solution)/shard_map/all_to_all | solution.py:1344
  77.1 2.7 %b7.1 = (bf16[28,28,512]{2,1,0:T(8,128)(2,1)S(1)}, f32[28,32,512]{2,1,0:T(8,128)S(1)}, bf16[32,32,128]{2,1,0:T(8,128)(2,1)S(1)}, f32[2,512]{1,0:T(2,128)S(1)}, f32[28,32,128]{2,1,0:T(8,128)S(1)}) custom-call(f32[8,128]{1,0:T(8,128)S(1)} %get-tuple-element.146.tab, bf16[32,24,128]{2,1,0:T(8,128)(2,1)S(1)} %all_to_all.60.got.got_act.got_b, ...), custom_call_target="tpu_custom_call" | custom-call | tf_op jit(solution)/shard_map/b7/pallas_call | solution.py:33
  79.8 12.9 %all_to_all.61.got.got_2c = bf16[32,32,128]{2,1,0:T(8,128)(2,1)S(1)} all-to-all(bf16[32,32,128]{2,1,0:T(8,128)(2,1)S(1)} %get-tuple-element.198), channel_id=1, replica_groups=mesh['rows'=2,'batch'=16] {'rows','batch'}, dimensions={0} | all-to-all | bytes 524288 | tf_op jit(solution)/shard_map/all_to_all | solution.py:1344
  92.8 2.5 %b9.1 = (bf16[28,32,128]{2,1,0:T(8,128)(2,1)S(1)}, f32[28,32,128]{2,1,0:T(8,128)S(1)}, bf16[32,16,128]{2,1,0:T(8,128)(2,1)S(1)}, f32[2,128]{1,0:T(2,128)S(1)}) custom-call(f32[8,128]{1,0:T(8,128)S(1)} %get-tuple-element.146.tab, bf16[32,32,128]{2,1,0:T(8,128)(2,1)S(1)} %all_to_all.61.got.got_2c, f32[32,1,128]{2,1,0:T(1,128)S(1)} %get-tuple-element.248.labels, ...), custom_call_target="tpu_custom_call" | custom-call | tf_op jit(solution)/shard_map/b9/pallas_call | solution.py:33
  95.2 9.6 %all_to_all.62.got.got_p.got_x.got_2a = bf16[32,16,128]{2,1,0:T(8,128)(2,1)S(1)} all-to-all(bf16[32,16,128]{2,1,0:T(8,128)(2,1)S(1)} %get-tuple-element.207), channel_id=1, replica_groups=mesh['rows'=2,'batch'=16] {'rows','batch'}, dimensions={0} | all-to-all | bytes 262144 | tf_op jit(solution)/shard_map/all_to_all | solution.py:1344
  104.9 2.5 %b10.1 = (bf16[28,32,128]{2,1,0:T(8,128)(2,1)S(1)}, f32[28,32,512]{2,1,0:T(8,128)S(1)}, f32[32,2,896]{2,1,0:T(2,128)S(1)}, f32[28,32,128]{2,1,0:T(8,128)S(1)}) custom-call(f32[8,128]{1,0:T(8,128)S(1)} %get-tuple-element.146.tab, bf16[32,16,128]{2,1,0:T(8,128)(2,1)S(1)} %all_to_all.62.got.got_p.got_x.got_2a, f32[32,1,128]{2,1,0:T(1,128)S(1)} %get-tuple-element.248.labels, ...), custom_call_target="tpu_custom_call" | custom-call | tf_op jit(solution)/shard_map/b10/pallas_call | solution.py:33
  107.3 12.4 %all_to_all.63.got.got_1 = f32[32,2,896]{2,1,0:T(2,128)S(1)} all-to-all(f32[32,2,896]{2,1,0:T(2,128)S(1)} %get-tuple-element.217), channel_id=1, replica_groups=mesh['rows'=2,'batch'=16] {'rows','batch'}, dimensions={0} | all-to-all | bytes 458752 | tf_op jit(solution)/shard_map/all_to_all | solution.py:1344
  119.8 3.0 %g_most.1 = (bf16[24,80,128]{2,1,0:T(8,128)(2,1)S(1)}, bf16[24,80,128]{2,1,0:T(8,128)(2,1)S(1)}, bf16[28,32,512]{2,1,0:T(8,128)(2,1)S(1)}, f32[1,1280]{1,0:T(1,128)S(1)}) custom-call(f32[8,128]{1,0:T(8,128)S(1)} %get-tuple-element.146.tab, bf16[28,32,128]{2,1,0:T(8,128)(2,1)S(1)} %get-tuple-element.190.act.act_2b, ...), custom_call_target="tpu_custom_call" | custom-call | tf_op jit(solution)/shard_map/g_most/pallas_call | solution.py:33
  122.8 1.8 b12.1
  124.6 1.1 b12_images.2
  127.3 1.0 b12_images.3
  128.3 1.2 g_xd.1
  129.7 24.2 %all_to_all.64.got = bf16[32,96,128]{2,1,0:T(8,128)(2,1)S(1)} all-to-all(bf16[32,96,128]{2,1,0:T(8,128)(2,1)S(1)} %pack_last.1), channel_id=1, replica_groups=mesh['rows'=2,'batch'=16] {'rows','batch'}, dimensions={0} | all-to-all | bytes 1572864 | tf_op jit(solution)/shard_map/all_to_all | solution.py:1344
  154.3 9.6 %all_to_all.65.refs_0_ = bf16[4,176,128]{2,1,0:T(8,128)(2,1)S(1)} all-to-all(bf16[4,176,128]{2,1,0:T(8,128)(2,1)S(1)} %add_all.1), channel_id=1, replica_groups={{0,4,8,12},{1,5,9,13},{2,6,10,14},{3,7,11,15},{16,20,24,28},{17,21,25,2..., dimensions={0} | all-to-all | bytes 360448 | tf_op jit(solution)/shard_map/all_to_all | solution.py:1545
  163.8 0.8 collective-permute-start.7
  165.2 2.1 %collective-permute-start.5 = (bf16[4,176,128]{2,1,0:T(8,128)(2,1)S(1)}, bf16[4,176,128]{2,1,0:T(8,128)(2,1)S(1)}, u32[]{:S(2)}, u32[]{:S(2)}) collective-permute-start(bf16[4,176,128]{2,1,0:T(8,128)(2,1)S(1)} %all_to_all.65.refs_0_), channel_id=1, source_target_pairs={{0,1},{1,0},{2,3},{3,2},{4,5},{5,4},{6,7},{7,6},{8,9},{9,8},{10,11... | collective-permute-start | bytes 540680 | tf_op jit(solution)/shard_map/ppermute | solution.py:1547
  168.0 2.4 %b13.1 = (bf16[28,28,512]{2,1,0:T(8,128)(2,1)}, f32[3,2,512]{2,1,0:T(2,128)}, f32[3,2,128]{2,1,0:T(2,128)}, f32[3,2,512]{2,1,0:T(2,128)}, f32[3,2,512]{2,1,0:T(2...) custom-call(f32[8,128]{1,0:T(8,128)S(1)} %get-tuple-element.146.tab, ...), custom_call_target="tpu_custom_call" | custom-call | tf_op jit(solution)/shard_map/b13/pallas_call | solution.py:33
  171.0 1.8 %collective-permute-done.6.refs_2_ = bf16[4,176,128]{2,1,0:T(8,128)(2,1)S(1)} collective-permute-done((bf16[4,176,128]{2,1,0:T(8,128)(2,1)S(1)}, bf16[4,176,128]{2,1,0:T(8,128)(2,1)S(1)}, u32[]{:S(2)}, u32[]{:S(2)}) %collective-permute-start.6) | collective-permute-done | bytes 180256 | tf_op jit(solution)/shard_map/ppermute | solution.py:1547
  174.8 1.8 %unpack.1 = (f32[128,512]{1,0:T(8,128)}, f32[1152,128]{1,0:T(8,128)}, f32[512,128]{1,0:T(8,128)}, f32[128,512]{1,0:T(8,128)}, f32[256,512]{1,0:T(8,128)}, /*inde...) custom-call(f32[8,128]{1,0:T(8,128)S(1)} %get-tuple-element.146.tab, ...), custom_call_target="tpu_custom_call" | custom-call | tf_op jit(solution)/shard_map/unpack/pallas_call | solution.py:33
  (57 shorter events, 6.9 us)
Async XLA Ops:
  0.6 2.4 %copy-start.7 = (bf16[3,3,128,128]{3,2,1,0:T(8,128)(2,1)S(1)}, bf16[3,3,128,128]{3,2,1,0:T(8,128)(2,1)}, u32[]{:S(2)}) copy-start(bf16[3,3,128,128]{3,2,1,0:T(8,128)(2,1)} %w2b) | copy-start | bytes 884740
  0.7 2.4 %copy-start.6 = (bf16[3,3,128,128]{3,2,1,0:T(8,128)(2,1)S(1)}, bf16[3,3,128,128]{3,2,1,0:T(8,128)(2,1)}, u32[]{:S(2)}) copy-start(bf16[3,3,128,128]{3,2,1,0:T(8,128)(2,1)} %w1b) | copy-start | bytes 884740
  0.7 17.4 %copy-start = (bf16[256,512]{1,0:T(8,128)(2,1)S(1)}, bf16[256,512]{1,0:T(8,128)(2,1)}, u32[]{:S(2)}) copy-start(bf16[256,512]{1,0:T(8,128)(2,1)} %w_p.3) | copy-start | bytes 786436
  3.0 15.9 %copy-start.4 = (bf16[256,128]{1,0:T(8,128)(2,1)S(1)}, bf16[256,128]{1,0:T(8,128)(2,1)}, u32[]{:S(2)}) copy-start(bf16[256,128]{1,0:T(8,128)(2,1)} %w.15) | copy-start | bytes 196612
  3.0 15.9 %copy-start.10 = (f32[2,3,128]{2,0,1:T(2,128)S(1)}, f32[2,3,128]{2,0,1:T(2,128)}, u32[]{:S(2)}) copy-start(f32[2,3,128]{2,0,1:T(2,128)} %param.27) | copy-start | bytes 9220
  3.3 14.8 %collective-permute-start = (bf16[28,64,256]{2,1,0:T(8,128)(2,1)S(1)}, bf16[28,64,256]{2,1,0:T(8,128)(2,1)S(1)}, u32[]{:S(2)}, u32[]{:S(2)}) collective-permute-start(bf16[28,64,256]{2,1,0:T(8,128)(2,1)S(1)} %get-tuple-element.161), channel_id=1, source_target_pairs={{0,16},{16,0},{1,17},{17,1},{2,18},{18,2},{3,19},{19,3},{4,20},{20... | collective-permute-start | bytes 2752520 | tf_op jit(solution)/shard_map/ppermute | solution.py:1352
  20.8 10.8 %copy-start.1 = (bf16[128,512]{1,0:T(8,128)(2,1)S(1)}, bf16[128,512]{1,0:T(8,128)(2,1)}, u32[]{:S(2)}) copy-start(bf16[128,512]{1,0:T(8,128)(2,1)} %w_c.7) | copy-start | bytes 393220
  20.8 10.7 %copy-start.14 = (f32[2,3,128]{2,0,1:T(2,128)S(1)}, f32[2,3,128]{2,0,1:T(2,128)}, u32[]{:S(2)}) copy-start(f32[2,3,128]{2,0,1:T(2,128)} %param.28) | copy-start | bytes 9220
  20.8 21.9 %copy-start.5 = (bf16[512,128]{1,0:T(8,128)(2,1)S(1)}, bf16[512,128]{1,0:T(8,128)(2,1)}, u32[]{:S(2)}) copy-start(bf16[512,128]{1,0:T(8,128)(2,1)} %w.14) | copy-start | bytes 393220
  20.8 21.9 %copy-start.8 = (f32[2,3,512]{2,0,1:T(2,128)S(1)}, f32[2,3,512]{2,0,1:T(2,128)}, u32[]{:S(2)}) copy-start(f32[2,3,512]{2,0,1:T(2,128)} %param.29) | copy-start | bytes 36868
  20.8 21.9 %copy-start.11 = (f32[2,3,512]{2,0,1:T(2,128)S(1)}, f32[2,3,512]{2,0,1:T(2,128)}, u32[]{:S(2)}) copy-start(f32[2,3,512]{2,0,1:T(2,128)} %param.30) | copy-start | bytes 36868
  42.7 11.4 %copy-start.12 = (f32[2,3,128]{2,0,1:T(2,128)S(1)}, f32[2,3,128]{2,0,1:T(2,128)}, u32[]{:S(2)}) copy-start(f32[2,3,128]{2,0,1:T(2,128)} %param.31) | copy-start | bytes 9220
  42.7 21.6 %copy-start.2 = (bf16[128,512]{1,0:T(8,128)(2,1)S(1)}, bf16[128,512]{1,0:T(8,128)(2,1)}, u32[]{:S(2)}) copy-start(bf16[128,512]{1,0:T(8,128)(2,1)} %w_c.5) | copy-start | bytes 393220
  42.8 21.6 %copy-start.13 = (f32[2,3,128]{2,0,1:T(2,128)S(1)}, f32[2,3,128]{2,0,1:T(2,128)}, u32[]{:S(2)}) copy-start(f32[2,3,128]{2,0,1:T(2,128)} %param.32) | copy-start | bytes 9220
  44.2 32.9 %copy-start.3 = (bf16[1,28,28,512]{3,2,1,0:T(8,128)(2,1)S(1)}, bf16[1,28,28,512]{3,2,1,0:T(8,128)(2,1)}, u32[]{:S(2)}) copy-start(bf16[1,28,28,512]{3,2,1,0:T(8,128)(2,1)} %param.34) | copy-start | bytes 2408452
  44.2 32.9 %copy-start.9 = (f32[2,3,512]{2,0,1:T(2,128)S(1)}, f32[2,3,512]{2,0,1:T(2,128)}, u32[]{:S(2)}) copy-start(f32[2,3,512]{2,0,1:T(2,128)} %param.33) | copy-start | bytes 36868
  122.7 6.8 %collective-permute-start.3 = (bf16[24,80,128]{2,1,0:T(8,128)(2,1)S(1)}, bf16[24,80,128]{2,1,0:T(8,128)(2,1)S(1)}, u32[]{:S(2)}, u32[]{:S(2)}) collective-permute-start(bf16[24,80,128]{2,1,0:T(8,128)(2,1)S(1)} %get-tuple-element.237), channel_id=1, source_target_pairs={{0,16},{16,0},{1,17},{17,1},{2,18},{18,2},{3,19},{19,3},{4,20},{20... | collective-permute-start | bytes 1474568 | tf_op jit(solution)/shard_map/ppermute | solution.py:1352
  125.6 3.9 %collective-permute-start.2 = (bf16[28,64,128]{2,1,0:T(8,128)(2,1)S(1)}, bf16[28,64,128]{2,1,0:T(8,128)(2,1)S(1)}, u32[]{:S(2)}, u32[]{:S(2)}) collective-permute-start(bf16[28,64,128]{2,1,0:T(8,128)(2,1)S(1)} %get-tuple-element.226.dn_oth), channel_id=1, source_target_pairs={{0,16},{16,0},{1,17},{17,1},{2,18},{18,2},{3,19},{19,3},{4,20},{20... | collective-permute-start | bytes 1376264 | tf_op jit(solution)/shard_map/ppermute | solution.py:1352
  126.7 2.8 %collective-permute-start.1 = (bf16[14,32,256]{2,1,0:T(8,128)(2,1)S(1)}, bf16[14,32,256]{2,1,0:T(8,128)(2,1)S(1)}, u32[]{:S(2)}, u32[]{:S(2)}) collective-permute-start(bf16[14,32,256]{2,1,0:T(8,128)(2,1)S(1)} %get-tuple-element.233), channel_id=1, source_target_pairs={{0,16},{16,0},{1,17},{17,1},{2,18},{18,2},{3,19},{19,3},{4,20},{20... | collective-permute-start | bytes 688136 | tf_op jit(solution)/shard_map/ppermute | solution.py:1352
  126.8 2.7 %collective-permute-start.4 = (bf16[8,80,128]{2,1,0:T(8,128)(2,1)S(1)}, bf16[8,80,128]{2,1,0:T(8,128)(2,1)S(1)}, u32[]{:S(2)}, u32[]{:S(2)}) collective-permute-start(bf16[8,80,128]{2,1,0:T(8,128)(2,1)S(1)} %get-tuple-element.239), channel_id=1, source_target_pairs={{0,16},{16,0},{1,17},{17,1},{2,18},{18,2},{3,19},{19,3},{4,20},{20... | collective-permute-start | bytes 491528 | tf_op jit(solution)/shard_map/ppermute | solution.py:1352
  163.8 7.2 %collective-permute-start.7 = (bf16[4,176,128]{2,1,0:T(8,128)(2,1)S(1)}, bf16[4,176,128]{2,1,0:T(8,128)(2,1)S(1)}, u32[]{:S(2)}, u32[]{:S(2)}) collective-permute-start(bf16[4,176,128]{2,1,0:T(8,128)(2,1)S(1)} %all_to_all.65.refs_0_), channel_id=1, source_target_pairs={{0,3},{1,2},{2,1},{3,0},{4,7},{5,6},{6,5},{7,4},{8,11},{9,10},{10,... | collective-permute-start | bytes 540680 | tf_op jit(solution)/shard_map/ppermute | solution.py:1547
  164.6 8.3 %collective-permute-start.6 = (bf16[4,176,128]{2,1,0:T(8,128)(2,1)S(1)}, bf16[4,176,128]{2,1,0:T(8,128)(2,1)S(1)}, u32[]{:S(2)}, u32[]{:S(2)}) collective-permute-start(bf16[4,176,128]{2,1,0:T(8,128)(2,1)S(1)} %all_to_all.65.refs_0_), channel_id=1, source_target_pairs={{0,2},{1,3},{2,0},{3,1},{4,6},{5,7},{6,4},{7,5},{8,10},{9,11},{10,... | collective-permute-start | bytes 540680 | tf_op jit(solution)/shard_map/ppermute | solution.py:1547
  165.2 7.6 %collective-permute-start.5 = (bf16[4,176,128]{2,1,0:T(8,128)(2,1)S(1)}, bf16[4,176,128]{2,1,0:T(8,128)(2,1)S(1)}, u32[]{:S(2)}, u32[]{:S(2)}) collective-permute-start(bf16[4,176,128]{2,1,0:T(8,128)(2,1)S(1)} %all_to_all.65.refs_0_), channel_id=1, source_target_pairs={{0,1},{1,0},{2,3},{3,2},{4,5},{5,4},{6,7},{7,6},{8,9},{9,8},{10,11... | collective-permute-start | bytes 540680 | tf_op jit(solution)/shard_map/ppermute | solution.py:1547
  167.3 6.2 %collective-permute-start.8 = (bf16[4,176,128]{2,1,0:T(8,128)(2,1)S(1)}, bf16[4,176,128]{2,1,0:T(8,128)(2,1)S(1)}, u32[]{:S(2)}, u32[]{:S(2)}) collective-permute-start(bf16[4,176,128]{2,1,0:T(8,128)(2,1)S(1)} %all_to_all.65.refs_0_), channel_id=1, source_target_pairs={{0,16},{16,0},{1,17},{17,1},{2,18},{18,2},{3,19},{19,3},{4,20},{20... | collective-permute-start | bytes 540680 | tf_op jit(solution)/shard_map/ppermute | solution.py:1352
  172.9 1.4 collective-permute-start.9
  172.9 1.7 collective-permute-start.10
  173.4 1.4 collective-permute-start.11

commit v11 on v10

--- a/solution.py
+++ b/solution.py
@@ -219,32 +219,41 @@
     place_at, group_at, width_at, gate_at, images, w_at, tab, x_own, x_for, z_own, z_for, send,
     place_ref, group, width, gate, raw, w, found, sems, *, batch,
 ):
+    rows = images.shape[1] // 2
+    parts = [pl.ds(rows * p, rows) for p in (0, 1)]
     pairs = (
         (place_at, place_ref), (group_at, group), (width_at, width), (gate_at, gate), (w_at, w),
-        (images.at[0], raw.at[0]), (images.at[1], raw.at[1]),
+        *((images.at[k, part], raw.at[k, part]) for k in (0, 1) for part in parts),
     )
     copies = [pltpu.make_async_copy(a, b, sems.at[k]) for k, (a, b) in enumerate(pairs)]
-    for k in (0, 4, 5, 6, 1, 2, 3):
+    for k in (0, 5, 4, 6, 7, 8, 1, 2, 3):
         copies[k].start()
-    for k in (0, 4, 5):
+    for k in (0, 4):
         copies[k].wait()
     half = lax.div(place_ref[0], batch)
     sides = ((x_own, z_own), (x_for, z_for))
 
     def one(k):
+        for p, part in enumerate(parts):
+            copies[5 + 2 * k + p].wait()
+            for place in (0, 1):
+
+                @pl.when(half == place)
+                def _():
+                    x_pad, _ = sides[k] if place == 0 else sides[1 - k]
+                    widen(raw.at[k, part], x_pad.at[part])
+
         for place in (0, 1):
 
             @pl.when(half == place)
             def _():
                 x_pad, z = sides[k] if place == 0 else sides[1 - k]
-                widen(raw.at[k], x_pad)
                 sums, squares = first_project(x_pad, w, z)
                 at = 2 * (k if place == 0 else 1 - k)
                 found[at : at + 1, :] = down(sums)
                 found[at + 1 : at + 2, :] = down(squares)
 
     one(0)
-    copies[6].wait()
     one(1)
     for k in (1, 2, 3):
         copies[k].wait()
@@ -805,7 +814,7 @@
     )
     own_sums[0:1, :] = found[0]
     own_sums[1:2, :] = found[1]
-    inner_grad(act, m, line, slope, d_in, d)
+    inner_part(act, m, d_in, d)
     mean = keeps[0:1, :]
     keep = valid_cols(LANES)
     n = LANES
@@ -813,7 +822,7 @@
     d3[rows + 1] = jnp.zeros(d3.shape[1:], BF16)
 
     def put(i, carry):
-        v = a * d[i] + b * (z[i] - mean) + c
+        v = a * (slope[i] * (d[i] + line)) + b * (z[i] - mean) + c
         v = jnp.where(keep, v, 0.0)
         d3[i + 1, :, 0:n] = pltpu.roll(v, COLS - 1, 0).astype(BF16)
         low = v.astype(BF16)
@@ -883,15 +892,9 @@
     return down(sums[0]), down(sums[1]) * rstd
 
 
-def inner_grad(act, m, line, slope, d_in, d):
+def inner_part(act, m, d_in, d):
     both = mm(flat(act[...]), m)
-    d[...] = (both[:, 0:LANES] + both[:, LANES:]).reshape(d.shape)
-
-    def put(i, carry):
-        d[i] = slope[i] * (d_in[i] + d[i] + line)
-        return carry
-
-    lax.fori_loop(0, d.shape[0], put, 0, unroll=7)
+    d[...] = d_in[...] + (both[:, 0:LANES] + both[:, LANES:]).reshape(d.shape)
 
 
 def normed_grad(dz, dout, z, mean, a, b, c):
@@ -923,13 +926,13 @@
     )
     own_sums[0:1, :] = found[0]
     own_sums[1:2, :] = found[1]
-    inner_grad(act, m, line, slope, d_in, dout)
+    inner_part(act, m, d_in, dout)
     mean = keeps[0:1, :]
     keep = valid_cols(LANES)
     d2[rows] = jnp.zeros(d2.shape[1:], BF16)
 
     def put(i, carry):
-        v = a * dout[i] + b * (z[i] - mean) + c
+        v = a * (slope[i] * (dout[i] + line)) + b * (z[i] - mean) + c
         v = jnp.where(keep, v, 0.0)
         low = v.astype(BF16)
         dz[i] = low
@@ -1390,7 +1393,7 @@
         functools.partial(f1, batch=devices // 2), [((8, n), F32), wide_in, wide_in, wide_z, wide_z, send(5)],
         [*(pltpu.SMEM(v.shape, jnp.int32) for v in (place, group, width, gate)),
          pltpu.VMEM(raw, BF16), pltpu.VMEM(w_1a.shape, BF16), pltpu.VMEM((8, n), F32),
-         pltpu.SemaphoreType.DMA((7,))],
+         pltpu.SemaphoreType.DMA((9,))],
         hbm=(0, 1, 2, 3, 4, 5),
     )(place, group, width, gate, images, w_1a)
     s1, v_1b, v_2b = tie(s1, w_1b, w_2b)

time: 177 us -> 177 us (level)
  no operation moved by 1% of the time
where the time goes in v11:
time: 177 us
  blocking collectives  133 us (75%)
  Pallas kernels  32.9 us (19%)
  starting transfers between devices  5.72 us (3%)
  waiting for transfers between devices  3.69 us (2%)
    all_to_all x10, blocking collectives, gather(): return lax.all_to_all(send, AXES, 0, 0)  123 us
    pallas_call x24, Pallas kernels, call(): pl.pallas_call(kernel, out_shape=tuple((jax.ShapeDtypeStruct(s, d) for s,...  32.9 us
    all_to_all x1, blocking collectives, body(): along = lax.all_to_all(mine, 'batch', 0, 0, axis_index_groups=columns_of)  9.55 us
  transfers between devices with their start and end apart: 12, of which 5 were waited for; matrix products, arithmetic and copies ran while one was open for 0% of the time, Pallas kernels for 5%

profile of v11, /device:TPU:0, one launch (start us, length us, event | category | flops | bytes accessed | tf_op | source)
XLA Modules:
  0.0 176.6 jit_solution(12771299987077132282)
XLA Ops:
  0.7 2.3 %f1.1 = (f32[8,128]{1,0:T(8,128)S(1)}, bf16[28,64,256]{2,1,0:T(8,128)(2,1)S(1)}, bf16[28,64,256]{2,1,0:T(8,128)(2,1)S(1)}, f32[28,64,128]{2,1,0:T(8,128)S(1)}, f...) custom-call(s32[1]{0:T(128)} %bitcast.place_at, s32[2]{0:T(128)} %group_at.1, s32[3]{0:T(128)} %width_at.1, ...), custom_call_target="tpu_custom_call" | custom-call | tf_op jit(solution)/shard_map/f1/pallas_call | solution.py:33
  3.8 14.2 %all_to_all.55.got = f32[32,1,640]{2,1,0:T(1,128)S(1)} all-to-all(f32[32,1,640]{2,1,0:T(1,128)S(1)} %get-tuple-element.160), channel_id=1, replica_groups=mesh['rows'=2,'batch'=16] {'rows','batch'}, dimensions={0} | all-to-all | bytes 163840 | tf_op jit(solution)/shard_map/all_to_all | solution.py:1347
  18.0 0.9 f1_strided.1
  18.9 1.8 %f2.1 = (bf16[29,32,768]{2,1,0:T(8,128)(2,1)S(1)}, f32[28,32,128]{2,1,0:T(8,128)S(1)}, f32[32,1,1024]{2,1,0:T(1,128)S(1)}, f32[32,1,128]{2,1,0:T(1,128)S(1)}, f3...) custom-call(f32[8,128]{1,0:T(8,128)S(1)} %get-tuple-element.146.tab, ...), custom_call_target="tpu_custom_call" | custom-call | tf_op jit(solution)/shard_map/f2/pallas_call | solution.py:33
  20.8 1.1 g_xz.1
  21.9 9.6 %all_to_all.56.got = f32[32,1,1024]{2,1,0:T(1,128)S(1)} all-to-all(f32[32,1,1024]{2,1,0:T(1,128)S(1)} %get-tuple-element.174), channel_id=1, replica_groups=mesh['rows'=2,'batch'=16] {'rows','batch'}, dimensions={0} | all-to-all | bytes 262144 | tf_op jit(solution)/shard_map/all_to_all | solution.py:1347
  31.5 1.4 f3.1
  32.9 9.8 %all_to_all.57.got.pair_low.got_act.got_a = bf16[32,16,128]{2,1,0:T(8,128)(2,1)S(1)} all-to-all(bf16[32,16,128]{2,1,0:T(8,128)(2,1)S(1)} %get-tuple-element.178), channel_id=1, replica_groups=mesh['rows'=2,'batch'=16] {'rows','batch'}, dimensions={0} | all-to-all | bytes 262144 | tf_op jit(solution)/shard_map/all_to_all | solution.py:1347
  42.8 1.4 f4.1
  44.2 9.9 %all_to_all.58.got.pair_high.got_q = bf16[32,16,128]{2,1,0:T(8,128)(2,1)S(1)} all-to-all(bf16[32,16,128]{2,1,0:T(8,128)(2,1)S(1)} %get-tuple-element.184), channel_id=1, replica_groups=mesh['rows'=2,'batch'=16] {'rows','batch'}, dimensions={0} | all-to-all | bytes 262144 | tf_op jit(solution)/shard_map/all_to_all | solution.py:1347
  54.1 1.0 f5.1
  55.1 9.2 %all_to_all.59.got = f32[32,1,256]{2,1,0:T(1,128)S(1)} all-to-all(f32[32,1,256]{2,1,0:T(1,128)S(1)} %get-tuple-element.188), channel_id=1, replica_groups=mesh['rows'=2,'batch'=16] {'rows','batch'}, dimensions={0} | all-to-all | bytes 65536 | tf_op jit(solution)/shard_map/all_to_all | solution.py:1347
  64.3 1.3 f6.1
  65.6 11.5 %all_to_all.60.got.got_act.got_b = bf16[32,24,128]{2,1,0:T(8,128)(2,1)S(1)} all-to-all(bf16[32,24,128]{2,1,0:T(8,128)(2,1)S(1)} %get-tuple-element.192), channel_id=1, replica_groups=mesh['rows'=2,'batch'=16] {'rows','batch'}, dimensions={0} | all-to-all | bytes 393216 | tf_op jit(solution)/shard_map/all_to_all | solution.py:1347
  77.1 2.7 %b7.1 = (bf16[28,28,512]{2,1,0:T(8,128)(2,1)S(1)}, f32[28,32,512]{2,1,0:T(8,128)S(1)}, bf16[32,32,128]{2,1,0:T(8,128)(2,1)S(1)}, f32[2,512]{1,0:T(2,128)S(1)}, f32[28,32,128]{2,1,0:T(8,128)S(1)}) custom-call(f32[8,128]{1,0:T(8,128)S(1)} %get-tuple-element.146.tab, bf16[32,24,128]{2,1,0:T(8,128)(2,1)S(1)} %all_to_all.60.got.got_act.got_b, ...), custom_call_target="tpu_custom_call" | custom-call | tf_op jit(solution)/shard_map/b7/pallas_call | solution.py:33
  79.8 12.9 %all_to_all.61.got.got_2c = bf16[32,32,128]{2,1,0:T(8,128)(2,1)S(1)} all-to-all(bf16[32,32,128]{2,1,0:T(8,128)(2,1)S(1)} %get-tuple-element.198), channel_id=1, replica_groups=mesh['rows'=2,'batch'=16] {'rows','batch'}, dimensions={0} | all-to-all | bytes 524288 | tf_op jit(solution)/shard_map/all_to_all | solution.py:1347
  92.8 2.4 %b9.1 = (bf16[28,32,128]{2,1,0:T(8,128)(2,1)S(1)}, f32[28,32,128]{2,1,0:T(8,128)S(1)}, bf16[32,16,128]{2,1,0:T(8,128)(2,1)S(1)}, f32[2,128]{1,0:T(2,128)S(1)}) custom-call(f32[8,128]{1,0:T(8,128)S(1)} %get-tuple-element.146.tab, bf16[32,32,128]{2,1,0:T(8,128)(2,1)S(1)} %all_to_all.61.got.got_2c, f32[32,1,128]{2,1,0:T(1,128)S(1)} %get-tuple-element.248.labels, ...), custom_call_target="tpu_custom_call" | custom-call | tf_op jit(solution)/shard_map/b9/pallas_call | solution.py:33
  95.2 9.6 %all_to_all.62.got.got_p.got_x.got_2a = bf16[32,16,128]{2,1,0:T(8,128)(2,1)S(1)} all-to-all(bf16[32,16,128]{2,1,0:T(8,128)(2,1)S(1)} %get-tuple-element.207), channel_id=1, replica_groups=mesh['rows'=2,'batch'=16] {'rows','batch'}, dimensions={0} | all-to-all | bytes 262144 | tf_op jit(solution)/shard_map/all_to_all | solution.py:1347
  104.8 2.5 %b10.1 = (bf16[28,32,128]{2,1,0:T(8,128)(2,1)S(1)}, f32[28,32,512]{2,1,0:T(8,128)S(1)}, f32[32,2,896]{2,1,0:T(2,128)S(1)}, f32[28,32,128]{2,1,0:T(8,128)S(1)}) custom-call(f32[8,128]{1,0:T(8,128)S(1)} %get-tuple-element.146.tab, bf16[32,16,128]{2,1,0:T(8,128)(2,1)S(1)} %all_to_all.62.got.got_p.got_x.got_2a, f32[32,1,128]{2,1,0:T(1,128)S(1)} %get-tuple-element.248.labels, ...), custom_call_target="tpu_custom_call" | custom-call | tf_op jit(solution)/shard_map/b10/pallas_call | solution.py:33
  107.3 12.4 %all_to_all.63.got.got_1 = f32[32,2,896]{2,1,0:T(2,128)S(1)} all-to-all(f32[32,2,896]{2,1,0:T(2,128)S(1)} %get-tuple-element.217), channel_id=1, replica_groups=mesh['rows'=2,'batch'=16] {'rows','batch'}, dimensions={0} | all-to-all | bytes 458752 | tf_op jit(solution)/shard_map/all_to_all | solution.py:1347
  119.7 3.0 %g_most.1 = (bf16[24,80,128]{2,1,0:T(8,128)(2,1)S(1)}, bf16[24,80,128]{2,1,0:T(8,128)(2,1)S(1)}, bf16[28,32,512]{2,1,0:T(8,128)(2,1)S(1)}, f32[1,1280]{1,0:T(1,128)S(1)}) custom-call(f32[8,128]{1,0:T(8,128)S(1)} %get-tuple-element.146.tab, bf16[28,32,128]{2,1,0:T(8,128)(2,1)S(1)} %get-tuple-element.190.act.act_2b, ...), custom_call_target="tpu_custom_call" | custom-call | tf_op jit(solution)/shard_map/g_most/pallas_call | solution.py:33
  122.7 1.7 b12.1
  124.4 1.1 b12_images.2
  127.1 1.0 b12_images.3
  128.2 1.2 g_xd.1
  129.6 24.2 %all_to_all.64.got = bf16[32,96,128]{2,1,0:T(8,128)(2,1)S(1)} all-to-all(bf16[32,96,128]{2,1,0:T(8,128)(2,1)S(1)} %pack_last.1), channel_id=1, replica_groups=mesh['rows'=2,'batch'=16] {'rows','batch'}, dimensions={0} | all-to-all | bytes 1572864 | tf_op jit(solution)/shard_map/all_to_all | solution.py:1347
  154.1 9.6 %all_to_all.65.refs_0_ = bf16[4,176,128]{2,1,0:T(8,128)(2,1)S(1)} all-to-all(bf16[4,176,128]{2,1,0:T(8,128)(2,1)S(1)} %add_all.1), channel_id=1, replica_groups={{0,4,8,12},{1,5,9,13},{2,6,10,14},{3,7,11,15},{16,20,24,28},{17,21,25,2..., dimensions={0} | all-to-all | bytes 360448 | tf_op jit(solution)/shard_map/all_to_all | solution.py:1548
  163.7 0.8 collective-permute-start.7
  165.1 2.1 %collective-permute-start.5 = (bf16[4,176,128]{2,1,0:T(8,128)(2,1)S(1)}, bf16[4,176,128]{2,1,0:T(8,128)(2,1)S(1)}, u32[]{:S(2)}, u32[]{:S(2)}) collective-permute-start(bf16[4,176,128]{2,1,0:T(8,128)(2,1)S(1)} %all_to_all.65.refs_0_), channel_id=1, source_target_pairs={{0,1},{1,0},{2,3},{3,2},{4,5},{5,4},{6,7},{7,6},{8,9},{9,8},{10,11... | collective-permute-start | bytes 540680 | tf_op jit(solution)/shard_map/ppermute | solution.py:1550
  167.9 2.4 %b13.1 = (bf16[28,28,512]{2,1,0:T(8,128)(2,1)}, f32[3,2,512]{2,1,0:T(2,128)}, f32[3,2,128]{2,1,0:T(2,128)}, f32[3,2,512]{2,1,0:T(2,128)}, f32[3,2,512]{2,1,0:T(2...) custom-call(f32[8,128]{1,0:T(8,128)S(1)} %get-tuple-element.146.tab, ...), custom_call_target="tpu_custom_call" | custom-call | tf_op jit(solution)/shard_map/b13/pallas_call | solution.py:33
  170.9 1.8 %collective-permute-done.6.refs_2_ = bf16[4,176,128]{2,1,0:T(8,128)(2,1)S(1)} collective-permute-done((bf16[4,176,128]{2,1,0:T(8,128)(2,1)S(1)}, bf16[4,176,128]{2,1,0:T(8,128)(2,1)S(1)}, u32[]{:S(2)}, u32[]{:S(2)}) %collective-permute-start.6) | collective-permute-done | bytes 180256 | tf_op jit(solution)/shard_map/ppermute | solution.py:1550
  174.7 1.8 %unpack.1 = (f32[128,512]{1,0:T(8,128)}, f32[1152,128]{1,0:T(8,128)}, f32[512,128]{1,0:T(8,128)}, f32[128,512]{1,0:T(8,128)}, f32[256,512]{1,0:T(8,128)}, /*inde...) custom-call(f32[8,128]{1,0:T(8,128)S(1)} %get-tuple-element.146.tab, ...), custom_call_target="tpu_custom_call" | custom-call | tf_op jit(solution)/shard_map/unpack/pallas_call | solution.py:33
  (57 shorter events, 6.9 us)
Async XLA Ops:
  0.6 2.4 %copy-start.7 = (bf16[3,3,128,128]{3,2,1,0:T(8,128)(2,1)S(1)}, bf16[3,3,128,128]{3,2,1,0:T(8,128)(2,1)}, u32[]{:S(2)}) copy-start(bf16[3,3,128,128]{3,2,1,0:T(8,128)(2,1)} %w2b) | copy-start | bytes 884740
  0.7 2.4 %copy-start.6 = (bf16[3,3,128,128]{3,2,1,0:T(8,128)(2,1)S(1)}, bf16[3,3,128,128]{3,2,1,0:T(8,128)(2,1)}, u32[]{:S(2)}) copy-start(bf16[3,3,128,128]{3,2,1,0:T(8,128)(2,1)} %w1b) | copy-start | bytes 884740
  0.7 17.4 %copy-start = (bf16[256,512]{1,0:T(8,128)(2,1)S(1)}, bf16[256,512]{1,0:T(8,128)(2,1)}, u32[]{:S(2)}) copy-start(bf16[256,512]{1,0:T(8,128)(2,1)} %w_p.3) | copy-start | bytes 786436
  3.0 15.9 %copy-start.4 = (bf16[256,128]{1,0:T(8,128)(2,1)S(1)}, bf16[256,128]{1,0:T(8,128)(2,1)}, u32[]{:S(2)}) copy-start(bf16[256,128]{1,0:T(8,128)(2,1)} %w.15) | copy-start | bytes 196612
  3.0 15.9 %copy-start.10 = (f32[2,3,128]{2,0,1:T(2,128)S(1)}, f32[2,3,128]{2,0,1:T(2,128)}, u32[]{:S(2)}) copy-start(f32[2,3,128]{2,0,1:T(2,128)} %param.27) | copy-start | bytes 9220
  3.3 14.8 %collective-permute-start = (bf16[28,64,256]{2,1,0:T(8,128)(2,1)S(1)}, bf16[28,64,256]{2,1,0:T(8,128)(2,1)S(1)}, u32[]{:S(2)}, u32[]{:S(2)}) collective-permute-start(bf16[28,64,256]{2,1,0:T(8,128)(2,1)S(1)} %get-tuple-element.161), channel_id=1, source_target_pairs={{0,16},{16,0},{1,17},{17,1},{2,18},{18,2},{3,19},{19,3},{4,20},{20... | collective-permute-start | bytes 2752520 | tf_op jit(solution)/shard_map/ppermute | solution.py:1355
  20.8 10.8 %copy-start.1 = (bf16[128,512]{1,0:T(8,128)(2,1)S(1)}, bf16[128,512]{1,0:T(8,128)(2,1)}, u32[]{:S(2)}) copy-start(bf16[128,512]{1,0:T(8,128)(2,1)} %w_c.7) | copy-start | bytes 393220
  20.8 10.7 %copy-start.14 = (f32[2,3,128]{2,0,1:T(2,128)S(1)}, f32[2,3,128]{2,0,1:T(2,128)}, u32[]{:S(2)}) copy-start(f32[2,3,128]{2,0,1:T(2,128)} %param.28) | copy-start | bytes 9220
  20.8 21.9 %copy-start.5 = (bf16[512,128]{1,0:T(8,128)(2,1)S(1)}, bf16[512,128]{1,0:T(8,128)(2,1)}, u32[]{:S(2)}) copy-start(bf16[512,128]{1,0:T(8,128)(2,1)} %w.14) | copy-start | bytes 393220
  20.8 21.9 %copy-start.8 = (f32[2,3,512]{2,0,1:T(2,128)S(1)}, f32[2,3,512]{2,0,1:T(2,128)}, u32[]{:S(2)}) copy-start(f32[2,3,512]{2,0,1:T(2,128)} %param.29) | copy-start | bytes 36868
  20.8 21.9 %copy-start.11 = (f32[2,3,512]{2,0,1:T(2,128)S(1)}, f32[2,3,512]{2,0,1:T(2,128)}, u32[]{:S(2)}) copy-start(f32[2,3,512]{2,0,1:T(2,128)} %param.30) | copy-start | bytes 36868
  42.7 11.4 %copy-start.12 = (f32[2,3,128]{2,0,1:T(2,128)S(1)}, f32[2,3,128]{2,0,1:T(2,128)}, u32[]{:S(2)}) copy-start(f32[2,3,128]{2,0,1:T(2,128)} %param.31) | copy-start | bytes 9220
  42.7 21.6 %copy-start.2 = (bf16[128,512]{1,0:T(8,128)(2,1)S(1)}, bf16[128,512]{1,0:T(8,128)(2,1)}, u32[]{:S(2)}) copy-start(bf16[128,512]{1,0:T(8,128)(2,1)} %w_c.5) | copy-start | bytes 393220
  42.7 21.6 %copy-start.13 = (f32[2,3,128]{2,0,1:T(2,128)S(1)}, f32[2,3,128]{2,0,1:T(2,128)}, u32[]{:S(2)}) copy-start(f32[2,3,128]{2,0,1:T(2,128)} %param.32) | copy-start | bytes 9220
  44.2 32.9 %copy-start.3 = (bf16[1,28,28,512]{3,2,1,0:T(8,128)(2,1)S(1)}, bf16[1,28,28,512]{3,2,1,0:T(8,128)(2,1)}, u32[]{:S(2)}) copy-start(bf16[1,28,28,512]{3,2,1,0:T(8,128)(2,1)} %param.34) | copy-start | bytes 2408452
  44.2 32.9 %copy-start.9 = (f32[2,3,512]{2,0,1:T(2,128)S(1)}, f32[2,3,512]{2,0,1:T(2,128)}, u32[]{:S(2)}) copy-start(f32[2,3,512]{2,0,1:T(2,128)} %param.33) | copy-start | bytes 36868
  122.7 6.7 %collective-permute-start.3 = (bf16[24,80,128]{2,1,0:T(8,128)(2,1)S(1)}, bf16[24,80,128]{2,1,0:T(8,128)(2,1)S(1)}, u32[]{:S(2)}, u32[]{:S(2)}) collective-permute-start(bf16[24,80,128]{2,1,0:T(8,128)(2,1)S(1)} %get-tuple-element.237), channel_id=1, source_target_pairs={{0,16},{16,0},{1,17},{17,1},{2,18},{18,2},{3,19},{19,3},{4,20},{20... | collective-permute-start | bytes 1474568 | tf_op jit(solution)/shard_map/ppermute | solution.py:1355
  125.5 3.9 %collective-permute-start.2 = (bf16[28,64,128]{2,1,0:T(8,128)(2,1)S(1)}, bf16[28,64,128]{2,1,0:T(8,128)(2,1)S(1)}, u32[]{:S(2)}, u32[]{:S(2)}) collective-permute-start(bf16[28,64,128]{2,1,0:T(8,128)(2,1)S(1)} %get-tuple-element.226.dn_oth), channel_id=1, source_target_pairs={{0,16},{16,0},{1,17},{17,1},{2,18},{18,2},{3,19},{19,3},{4,20},{20... | collective-permute-start | bytes 1376264 | tf_op jit(solution)/shard_map/ppermute | solution.py:1355
  126.6 2.8 %collective-permute-start.1 = (bf16[14,32,256]{2,1,0:T(8,128)(2,1)S(1)}, bf16[14,32,256]{2,1,0:T(8,128)(2,1)S(1)}, u32[]{:S(2)}, u32[]{:S(2)}) collective-permute-start(bf16[14,32,256]{2,1,0:T(8,128)(2,1)S(1)} %get-tuple-element.233), channel_id=1, source_target_pairs={{0,16},{16,0},{1,17},{17,1},{2,18},{18,2},{3,19},{19,3},{4,20},{20... | collective-permute-start | bytes 688136 | tf_op jit(solution)/shard_map/ppermute | solution.py:1355
  126.6 2.7 %collective-permute-start.4 = (bf16[8,80,128]{2,1,0:T(8,128)(2,1)S(1)}, bf16[8,80,128]{2,1,0:T(8,128)(2,1)S(1)}, u32[]{:S(2)}, u32[]{:S(2)}) collective-permute-start(bf16[8,80,128]{2,1,0:T(8,128)(2,1)S(1)} %get-tuple-element.239), channel_id=1, source_target_pairs={{0,16},{16,0},{1,17},{17,1},{2,18},{18,2},{3,19},{19,3},{4,20},{20... | collective-permute-start | bytes 491528 | tf_op jit(solution)/shard_map/ppermute | solution.py:1355
  163.7 7.2 %collective-permute-start.7 = (bf16[4,176,128]{2,1,0:T(8,128)(2,1)S(1)}, bf16[4,176,128]{2,1,0:T(8,128)(2,1)S(1)}, u32[]{:S(2)}, u32[]{:S(2)}) collective-permute-start(bf16[4,176,128]{2,1,0:T(8,128)(2,1)S(1)} %all_to_all.65.refs_0_), channel_id=1, source_target_pairs={{0,3},{1,2},{2,1},{3,0},{4,7},{5,6},{6,5},{7,4},{8,11},{9,10},{10,... | collective-permute-start | bytes 540680 | tf_op jit(solution)/shard_map/ppermute | solution.py:1550
  164.5 8.3 %collective-permute-start.6 = (bf16[4,176,128]{2,1,0:T(8,128)(2,1)S(1)}, bf16[4,176,128]{2,1,0:T(8,128)(2,1)S(1)}, u32[]{:S(2)}, u32[]{:S(2)}) collective-permute-start(bf16[4,176,128]{2,1,0:T(8,128)(2,1)S(1)} %all_to_all.65.refs_0_), channel_id=1, source_target_pairs={{0,2},{1,3},{2,0},{3,1},{4,6},{5,7},{6,4},{7,5},{8,10},{9,11},{10,... | collective-permute-start | bytes 540680 | tf_op jit(solution)/shard_map/ppermute | solution.py:1550
  165.1 7.6 %collective-permute-start.5 = (bf16[4,176,128]{2,1,0:T(8,128)(2,1)S(1)}, bf16[4,176,128]{2,1,0:T(8,128)(2,1)S(1)}, u32[]{:S(2)}, u32[]{:S(2)}) collective-permute-start(bf16[4,176,128]{2,1,0:T(8,128)(2,1)S(1)} %all_to_all.65.refs_0_), channel_id=1, source_target_pairs={{0,1},{1,0},{2,3},{3,2},{4,5},{5,4},{6,7},{7,6},{8,9},{9,8},{10,11... | collective-permute-start | bytes 540680 | tf_op jit(solution)/shard_map/ppermute | solution.py:1550
  167.2 6.2 %collective-permute-start.8 = (bf16[4,176,128]{2,1,0:T(8,128)(2,1)S(1)}, bf16[4,176,128]{2,1,0:T(8,128)(2,1)S(1)}, u32[]{:S(2)}, u32[]{:S(2)}) collective-permute-start(bf16[4,176,128]{2,1,0:T(8,128)(2,1)S(1)} %all_to_all.65.refs_0_), channel_id=1, source_target_pairs={{0,16},{16,0},{1,17},{17,1},{2,18},{18,2},{3,19},{19,3},{4,20},{20... | collective-permute-start | bytes 540680 | tf_op jit(solution)/shard_map/ppermute | solution.py:1355
  172.7 1.4 collective-permute-start.9
  172.7 1.7 collective-permute-start.10
  173.2 1.4 collective-permute-start.11

commit v12 on v11

--- a/solution.py
+++ b/solution.py
@@ -198,7 +198,7 @@
         x_pad[i, cols : cols + gap, :] = jnp.zeros((gap, chans), BF16)
         return carry
 
-    lax.fori_loop(0, rows, put, 0, unroll=4)
+    lax.fori_loop(0, rows, put, 0, unroll=7)
 
 
 def first_project(x_pad, w, z, stats=True):
@@ -282,7 +282,7 @@
                 xee[first + i, :, lanes] = wide[b, pl.ds(0, COLS, stride=2), :].astype(BF16)
             return carry
 
-        lax.fori_loop(0, rows, put, 0, unroll=4)
+        lax.fori_loop(0, rows, put, 0, unroll=7)
     total = 2 * rows
     step = total // 7
     chans = z.shape[2]
@@ -383,7 +383,7 @@
                         lane += n
             return carry
 
-        lax.fori_loop(0, rows // 2, put, 0, unroll=4)
+        lax.fori_loop(0, rows // 2, put, 0, unroll=7)
     extra = [stats_p[:, lanes] for lanes in columns(stats_p.shape[1])]
     pair = (slice(3 * n, 6 * n), w_odd[...], (1, 0))
     conv_stats(z, xs, pair, (slice(0, 3 * n), w_even[...], 1), send, extra)
@@ -473,7 +473,7 @@
         return carry[0] + fold(low.astype(F32)), carry[1] + fold(s), carry[2] + fold(sx)
 
     start = zeros8(LANES)
-    sums = lax.fori_loop(0, rows, put, (start, start, start), unroll=4)
+    sums = lax.fori_loop(0, rows, put, (start, start, start), unroll=7)
     act_sum, *sums = [down(v) for v in sums]
     product = mm_tn(flat(act[...]), flat(both[...]))
     product = product[:, 0 : 2 * LANES] + product[:, 2 * LANES :]
@@ -618,7 +618,7 @@
         slope[i] = (0.5 + 0.5 * t) * (1.0 + u - p)
         return carry
 
-    lax.fori_loop(0, rows, put, 0, unroll=4)
+    lax.fori_loop(0, rows, put, 0, unroll=7)
     step = rows // 4
     sums, squares = zeros8(LANES), zeros8(LANES)
     for c in range(4):
@@ -656,7 +656,7 @@
         x3[i + 1, :, 2 * n : 3 * n] = pltpu.roll(act, COLS - 1, 0).astype(BF16)
         return carry
 
-    lax.fori_loop(0, rows, put, 0, unroll=4)
+    lax.fori_loop(0, rows, put, 0, unroll=7)
     lanes = slice(0, 3 * n)
     conv_stats(
         z, x3, (lanes, w_two[...], (0, 1)), (lanes, w_last[...], 2), send
@@ -724,7 +724,7 @@
         return sums + fold(g), products + fold(g * (zz - mean))
 
     start = zeros8(chans)
-    sums, products = lax.fori_loop(0, rows, put, (start, start), unroll=4)
+    sums, products = lax.fori_loop(0, rows, put, (start, start), unroll=7)
     inner = inner_sums(low, w, slope_in, z_in, keeps_in, d_in)
     blocks = chans // LANES
     put_split(send, 0, rows_of(down(sums) * gate))
@@ -831,7 +831,7 @@
         d3[i + 1, :, 2 * n : 3 * n] = pltpu.roll(v, 1, 0).astype(BF16)
         return carry
 
-    lax.fori_loop(0, rows, put, 0, unroll=4)
+    lax.fori_loop(0, rows, put, 0, unroll=7)
     step = rows // 4
     for k in range(4):
         both = mm_nt(flat(d3[step * k : step * (k + 1) + 1]), b_two[...])
@@ -855,7 +855,7 @@
     marks = labels[...]
     total = over_group(get_split(got, 0, 2), marks, entry(tab, OWN))
     coefs = own_coefs(tab, marks, norm, keeps, pixels, total[0:1], total[1:2])
-    normed_grad(dz, dout_in, z, *coefs)
+    normed_grad(dout_in, (dz, z, *coefs))
     d[...] = mm_nt(flat(dz[...]), w[...]).reshape(d.shape)
     mean_c, rstd_c, mean_p, rstd_p = (keeps_cp[k : k + 1, :] for k in range(4))
     a_c = rstd_c * gain_of(norm_c, entry(tab, OWN))
@@ -872,7 +872,7 @@
         )
 
     start = zeros8(chans)
-    sums, prod_c, prod_p = lax.fori_loop(0, rows, sum_up, (start, start, start), unroll=4)
+    sums, prod_c, prod_p = lax.fori_loop(0, rows, sum_up, (start, start, start), unroll=7)
     wide = [down(sums), down(prod_c) * rstd_c, down(prod_p) * rstd_p]
     inner = inner_sums(low, w_c, slope_in, z_in, keeps_in, d_in)
     parts = [stack([v[:, 0 : chans // 2], v[:, chans // 2 :]]) for v in wide]
@@ -897,15 +897,17 @@
     d[...] = d_in[...] + (both[:, 0:LANES] + both[:, LANES:]).reshape(d.shape)
 
 
-def normed_grad(dz, dout, z, mean, a, b, c):
-    keep = valid_cols(z.shape[2])
+def normed_grad(dout, *parts):
+    keep = valid_cols(dout.shape[2])
 
     def put(i, carry):
-        v = a * dout[i] + b * (z[i] - mean) + c
-        dz[i] = jnp.where(keep, v, 0.0).astype(BF16)
+        g = dout[i]
+        for dz, z, mean, a, b, c in parts:
+            v = a * g + b * (z[i] - mean) + c
+            dz[i] = jnp.where(keep, v, 0.0).astype(BF16)
         return carry
 
-    lax.fori_loop(0, z.shape[0], put, 0, unroll=4)
+    lax.fori_loop(0, dout.shape[0], put, 0, unroll=7)
 
 
 def b12(
@@ -940,7 +942,7 @@
         d2[i, :, n : 2 * n] = pltpu.roll(v, COLS - 1, 0).astype(BF16)
         return carry
 
-    lax.fori_loop(0, rows, put, 0, unroll=4)
+    lax.fori_loop(0, rows, put, 0, unroll=7)
     low = flat(dz[...])
     cur = mm_side(flat(xs[1 : rows + 1]), low)
     for k, (y, x) in enumerate(((1, 1), (1, 2), (1, 0), (2, 1), (2, 2), (2, 0))):
@@ -986,7 +988,7 @@
             dn[2 * i + ra] = wide[ra].astype(BF16)
         return sums, products
 
-    totals = lax.fori_loop(0, rows, emit, (zeros8(n), zeros8(n)), unroll=4)
+    totals = lax.fori_loop(0, rows, emit, (zeros8(n), zeros8(n)), unroll=7)
     sums_out[0:1, :] = down(totals[0])
     sums_out[1:2, :] = down(totals[1]) * rstd_1
 
@@ -1027,7 +1029,7 @@
             dz[i] = jnp.where(keep, v, 0.0).astype(BF16)
             return carry
 
-        lax.fori_loop(0, rows, put, 0, unroll=4)
+        lax.fori_loop(0, rows, put, 0, unroll=7)
         place = half if k == 0 else 1 - half
         step = rows // 2
         for q in range(2):
@@ -1102,11 +1104,10 @@
     ]
     mean, a, b, c = own_coefs(tab, marks, norm_2c, keeps_2c, pixels, *wide)
     gate = 0.25 * tiled(entry(tab, GATE), outer)
-    normed_grad(dz_2c, grad_pre, z_2c, mean, a * gate, b, c)
-    coefs = own_coefs(tab, marks, norm_c, keeps.at[0:2], pixels, lines[0], lines[1])
-    normed_grad(dz_1c, grad_pre_2, zc, *coefs)
-    coefs = own_coefs(tab, marks, norm_p, keeps.at[2:4], pixels, lines[0], lines[2])
-    normed_grad(dz_p, grad_pre_2, zp, *coefs)
+    normed_grad(grad_pre, (dz_2c, z_2c, mean, a * gate, b, c))
+    coefs_c = own_coefs(tab, marks, norm_c, keeps.at[0:2], pixels, lines[0], lines[1])
+    coefs_p = own_coefs(tab, marks, norm_p, keeps.at[2:4], pixels, lines[0], lines[2])
+    normed_grad(grad_pre_2, (dz_1c, zc, *coefs_c), (dz_p, zp, *coefs_p))
     at = put_rows(packed, 0, mm_tn(flat(act_2b[...]), flat(dz_2c[...])))
     low = flat(dz_2b[...])
     for y in range(3):
@@ -1137,7 +1138,7 @@
             low[i, :, 0:n] = (z[i] - mean).astype(BF16)
             return carry
 
-        lax.fori_loop(0, rows, put, 0, unroll=4)
+        lax.fori_loop(0, rows, put, 0, unroll=7)
         term = mm_tn(flat(x[...]), flat(low[...]))
         value = term if value is None else value + term
     at = value.shape[0]
@@ -1167,7 +1168,7 @@
             low[i] = (a * (dn[i].astype(F32) - local) + b * (z[i] - mean)).astype(BF16)
             return carry
 
-        lax.fori_loop(0, rows, put, 0, unroll=4)
+        lax.fori_loop(0, rows, put, 0, unroll=7)
         term = mm_tn(flat(low[...]), flat(x[...]))
         value = term if value is None else value + term
     value = stack([jnp.transpose(value[:, lanes]) for lanes in columns(value.shape[1])])

time: 177 us -> 176 us (level)
  no operation moved by 1% of the time
where the time goes in v12:
time: 176 us
  blocking collectives  133 us (76%)
  Pallas kernels  32.4 us (18%)
  starting transfers between devices  5.72 us (3%)
  waiting for transfers between devices  3.75 us (2%)
    all_to_all x10, blocking collectives, gather(): return lax.all_to_all(send, AXES, 0, 0)  123 us
    pallas_call x24, Pallas kernels, call(): pl.pallas_call(kernel, out_shape=tuple((jax.ShapeDtypeStruct(s, d) for s,...  32.4 us
    all_to_all x1, blocking collectives, body(): along = lax.all_to_all(mine, 'batch', 0, 0, axis_index_groups=columns_of)  9.55 us
  transfers between devices with their start and end apart: 12, of which 5 were waited for; matrix products, arithmetic and copies ran while one was open for 0% of the time, Pallas kernels for 5%

profile of v12, /device:TPU:0, one launch (start us, length us, event | category | flops | bytes accessed | tf_op | source)
XLA Modules:
  0.0 176.1 jit_solution(15486236418795378901)
XLA Ops:
  0.7 2.3 %f1.1 = (f32[8,128]{1,0:T(8,128)S(1)}, bf16[28,64,256]{2,1,0:T(8,128)(2,1)S(1)}, bf16[28,64,256]{2,1,0:T(8,128)(2,1)S(1)}, f32[28,64,128]{2,1,0:T(8,128)S(1)}, f...) custom-call(s32[1]{0:T(128)} %bitcast.place_at, s32[2]{0:T(128)} %group_at.1, s32[3]{0:T(128)} %width_at.1, ...), custom_call_target="tpu_custom_call" | custom-call | tf_op jit(solution)/shard_map/f1/pallas_call | solution.py:33
  3.7 14.2 %all_to_all.55.got = f32[32,1,640]{2,1,0:T(1,128)S(1)} all-to-all(f32[32,1,640]{2,1,0:T(1,128)S(1)} %get-tuple-element.160), channel_id=1, replica_groups=mesh['rows'=2,'batch'=16] {'rows','batch'}, dimensions={0} | all-to-all | bytes 163840 | tf_op jit(solution)/shard_map/all_to_all | solution.py:1348
  18.0 0.8 f1_strided.1
  18.9 1.8 %f2.1 = (bf16[29,32,768]{2,1,0:T(8,128)(2,1)S(1)}, f32[28,32,128]{2,1,0:T(8,128)S(1)}, f32[32,1,1024]{2,1,0:T(1,128)S(1)}, f32[32,1,128]{2,1,0:T(1,128)S(1)}, f3...) custom-call(f32[8,128]{1,0:T(8,128)S(1)} %get-tuple-element.146.tab, ...), custom_call_target="tpu_custom_call" | custom-call | tf_op jit(solution)/shard_map/f2/pallas_call | solution.py:33
  20.7 1.0 g_xz.1
  21.8 9.6 %all_to_all.56.got = f32[32,1,1024]{2,1,0:T(1,128)S(1)} all-to-all(f32[32,1,1024]{2,1,0:T(1,128)S(1)} %get-tuple-element.174), channel_id=1, replica_groups=mesh['rows'=2,'batch'=16] {'rows','batch'}, dimensions={0} | all-to-all | bytes 262144 | tf_op jit(solution)/shard_map/all_to_all | solution.py:1348
  31.4 1.4 f3.1
  32.7 9.8 %all_to_all.57.got.pair_low.got_act.got_a = bf16[32,16,128]{2,1,0:T(8,128)(2,1)S(1)} all-to-all(bf16[32,16,128]{2,1,0:T(8,128)(2,1)S(1)} %get-tuple-element.178), channel_id=1, replica_groups=mesh['rows'=2,'batch'=16] {'rows','batch'}, dimensions={0} | all-to-all | bytes 262144 | tf_op jit(solution)/shard_map/all_to_all | solution.py:1348
  42.6 1.4 f4.1
  44.1 9.9 %all_to_all.58.got.pair_high.got_q = bf16[32,16,128]{2,1,0:T(8,128)(2,1)S(1)} all-to-all(bf16[32,16,128]{2,1,0:T(8,128)(2,1)S(1)} %get-tuple-element.184), channel_id=1, replica_groups=mesh['rows'=2,'batch'=16] {'rows','batch'}, dimensions={0} | all-to-all | bytes 262144 | tf_op jit(solution)/shard_map/all_to_all | solution.py:1348
  54.0 0.9 f5.1
  54.9 9.2 %all_to_all.59.got = f32[32,1,256]{2,1,0:T(1,128)S(1)} all-to-all(f32[32,1,256]{2,1,0:T(1,128)S(1)} %get-tuple-element.188), channel_id=1, replica_groups=mesh['rows'=2,'batch'=16] {'rows','batch'}, dimensions={0} | all-to-all | bytes 65536 | tf_op jit(solution)/shard_map/all_to_all | solution.py:1348
  64.1 1.2 f6.1
  65.4 11.5 %all_to_all.60.got.got_act.got_b = bf16[32,24,128]{2,1,0:T(8,128)(2,1)S(1)} all-to-all(bf16[32,24,128]{2,1,0:T(8,128)(2,1)S(1)} %get-tuple-element.192), channel_id=1, replica_groups=mesh['rows'=2,'batch'=16] {'rows','batch'}, dimensions={0} | all-to-all | bytes 393216 | tf_op jit(solution)/shard_map/all_to_all | solution.py:1348
  76.9 2.7 %b7.1 = (bf16[28,28,512]{2,1,0:T(8,128)(2,1)S(1)}, f32[28,32,512]{2,1,0:T(8,128)S(1)}, bf16[32,32,128]{2,1,0:T(8,128)(2,1)S(1)}, f32[2,512]{1,0:T(2,128)S(1)}, f32[28,32,128]{2,1,0:T(8,128)S(1)}) custom-call(f32[8,128]{1,0:T(8,128)S(1)} %get-tuple-element.146.tab, bf16[32,24,128]{2,1,0:T(8,128)(2,1)S(1)} %all_to_all.60.got.got_act.got_b, ...), custom_call_target="tpu_custom_call" | custom-call | tf_op jit(solution)/shard_map/b7/pallas_call | solution.py:33
  79.6 12.9 %all_to_all.61.got.got_2c = bf16[32,32,128]{2,1,0:T(8,128)(2,1)S(1)} all-to-all(bf16[32,32,128]{2,1,0:T(8,128)(2,1)S(1)} %get-tuple-element.198), channel_id=1, replica_groups=mesh['rows'=2,'batch'=16] {'rows','batch'}, dimensions={0} | all-to-all | bytes 524288 | tf_op jit(solution)/shard_map/all_to_all | solution.py:1348
  92.5 2.4 %b9.1 = (bf16[28,32,128]{2,1,0:T(8,128)(2,1)S(1)}, f32[28,32,128]{2,1,0:T(8,128)S(1)}, bf16[32,16,128]{2,1,0:T(8,128)(2,1)S(1)}, f32[2,128]{1,0:T(2,128)S(1)}) custom-call(f32[8,128]{1,0:T(8,128)S(1)} %get-tuple-element.146.tab, bf16[32,32,128]{2,1,0:T(8,128)(2,1)S(1)} %all_to_all.61.got.got_2c, f32[32,1,128]{2,1,0:T(1,128)S(1)} %get-tuple-element.248.labels, ...), custom_call_target="tpu_custom_call" | custom-call | tf_op jit(solution)/shard_map/b9/pallas_call | solution.py:33
  94.9 9.6 %all_to_all.62.got.got_p.got_x.got_2a = bf16[32,16,128]{2,1,0:T(8,128)(2,1)S(1)} all-to-all(bf16[32,16,128]{2,1,0:T(8,128)(2,1)S(1)} %get-tuple-element.207), channel_id=1, replica_groups=mesh['rows'=2,'batch'=16] {'rows','batch'}, dimensions={0} | all-to-all | bytes 262144 | tf_op jit(solution)/shard_map/all_to_all | solution.py:1348
  104.5 2.5 %b10.1 = (bf16[28,32,128]{2,1,0:T(8,128)(2,1)S(1)}, f32[28,32,512]{2,1,0:T(8,128)S(1)}, f32[32,2,896]{2,1,0:T(2,128)S(1)}, f32[28,32,128]{2,1,0:T(8,128)S(1)}) custom-call(f32[8,128]{1,0:T(8,128)S(1)} %get-tuple-element.146.tab, bf16[32,16,128]{2,1,0:T(8,128)(2,1)S(1)} %all_to_all.62.got.got_p.got_x.got_2a, f32[32,1,128]{2,1,0:T(1,128)S(1)} %get-tuple-element.248.labels, ...), custom_call_target="tpu_custom_call" | custom-call | tf_op jit(solution)/shard_map/b10/pallas_call | solution.py:33
  107.0 12.4 %all_to_all.63.got.got_1 = f32[32,2,896]{2,1,0:T(2,128)S(1)} all-to-all(f32[32,2,896]{2,1,0:T(2,128)S(1)} %get-tuple-element.217), channel_id=1, replica_groups=mesh['rows'=2,'batch'=16] {'rows','batch'}, dimensions={0} | all-to-all | bytes 458752 | tf_op jit(solution)/shard_map/all_to_all | solution.py:1348
  119.4 2.9 %g_most.1 = (bf16[24,80,128]{2,1,0:T(8,128)(2,1)S(1)}, bf16[24,80,128]{2,1,0:T(8,128)(2,1)S(1)}, bf16[28,32,512]{2,1,0:T(8,128)(2,1)S(1)}, f32[1,1280]{1,0:T(1,128)S(1)}) custom-call(f32[8,128]{1,0:T(8,128)S(1)} %get-tuple-element.146.tab, bf16[28,32,128]{2,1,0:T(8,128)(2,1)S(1)} %get-tuple-element.190.act.act_2b, ...), custom_call_target="tpu_custom_call" | custom-call | tf_op jit(solution)/shard_map/g_most/pallas_call | solution.py:33
  122.4 1.7 b12.1
  124.0 1.0 b12_images.2
  126.7 1.0 b12_images.3
  127.7 1.1 g_xd.1
  129.1 24.2 %all_to_all.64.got = bf16[32,96,128]{2,1,0:T(8,128)(2,1)S(1)} all-to-all(bf16[32,96,128]{2,1,0:T(8,128)(2,1)S(1)} %pack_last.1), channel_id=1, replica_groups=mesh['rows'=2,'batch'=16] {'rows','batch'}, dimensions={0} | all-to-all | bytes 1572864 | tf_op jit(solution)/shard_map/all_to_all | solution.py:1348
  153.7 9.6 %all_to_all.65.refs_0_ = bf16[4,176,128]{2,1,0:T(8,128)(2,1)S(1)} all-to-all(bf16[4,176,128]{2,1,0:T(8,128)(2,1)S(1)} %add_all.1), channel_id=1, replica_groups={{0,4,8,12},{1,5,9,13},{2,6,10,14},{3,7,11,15},{16,20,24,28},{17,21,25,2..., dimensions={0} | all-to-all | bytes 360448 | tf_op jit(solution)/shard_map/all_to_all | solution.py:1549
  163.2 0.8 collective-permute-start.7
  164.6 2.1 %collective-permute-start.5 = (bf16[4,176,128]{2,1,0:T(8,128)(2,1)S(1)}, bf16[4,176,128]{2,1,0:T(8,128)(2,1)S(1)}, u32[]{:S(2)}, u32[]{:S(2)}) collective-permute-start(bf16[4,176,128]{2,1,0:T(8,128)(2,1)S(1)} %all_to_all.65.refs_0_), channel_id=1, source_target_pairs={{0,1},{1,0},{2,3},{3,2},{4,5},{5,4},{6,7},{7,6},{8,9},{9,8},{10,11... | collective-permute-start | bytes 540680 | tf_op jit(solution)/shard_map/ppermute | solution.py:1551
  167.4 2.3 %b13.1 = (bf16[28,28,512]{2,1,0:T(8,128)(2,1)}, f32[3,2,512]{2,1,0:T(2,128)}, f32[3,2,128]{2,1,0:T(2,128)}, f32[3,2,512]{2,1,0:T(2,128)}, f32[3,2,512]{2,1,0:T(2...) custom-call(f32[8,128]{1,0:T(8,128)S(1)} %get-tuple-element.146.tab, ...), custom_call_target="tpu_custom_call" | custom-call | tf_op jit(solution)/shard_map/b13/pallas_call | solution.py:33
  170.4 1.8 %collective-permute-done.6.refs_2_ = bf16[4,176,128]{2,1,0:T(8,128)(2,1)S(1)} collective-permute-done((bf16[4,176,128]{2,1,0:T(8,128)(2,1)S(1)}, bf16[4,176,128]{2,1,0:T(8,128)(2,1)S(1)}, u32[]{:S(2)}, u32[]{:S(2)}) %collective-permute-start.6) | collective-permute-done | bytes 180256 | tf_op jit(solution)/shard_map/ppermute | solution.py:1551
  174.2 1.8 %unpack.1 = (f32[128,512]{1,0:T(8,128)}, f32[1152,128]{1,0:T(8,128)}, f32[512,128]{1,0:T(8,128)}, f32[128,512]{1,0:T(8,128)}, f32[256,512]{1,0:T(8,128)}, /*inde...) custom-call(f32[8,128]{1,0:T(8,128)S(1)} %get-tuple-element.146.tab, ...), custom_call_target="tpu_custom_call" | custom-call | tf_op jit(solution)/shard_map/unpack/pallas_call | solution.py:33
  (57 shorter events, 7.0 us)
Async XLA Ops:
  0.6 2.4 %copy-start.7 = (bf16[3,3,128,128]{3,2,1,0:T(8,128)(2,1)S(1)}, bf16[3,3,128,128]{3,2,1,0:T(8,128)(2,1)}, u32[]{:S(2)}) copy-start(bf16[3,3,128,128]{3,2,1,0:T(8,128)(2,1)} %w2b) | copy-start | bytes 884740
  0.7 2.4 %copy-start.6 = (bf16[3,3,128,128]{3,2,1,0:T(8,128)(2,1)S(1)}, bf16[3,3,128,128]{3,2,1,0:T(8,128)(2,1)}, u32[]{:S(2)}) copy-start(bf16[3,3,128,128]{3,2,1,0:T(8,128)(2,1)} %w1b) | copy-start | bytes 884740
  0.7 17.3 %copy-start = (bf16[256,512]{1,0:T(8,128)(2,1)S(1)}, bf16[256,512]{1,0:T(8,128)(2,1)}, u32[]{:S(2)}) copy-start(bf16[256,512]{1,0:T(8,128)(2,1)} %w_p.3) | copy-start | bytes 786436
  3.0 15.8 %copy-start.4 = (bf16[256,128]{1,0:T(8,128)(2,1)S(1)}, bf16[256,128]{1,0:T(8,128)(2,1)}, u32[]{:S(2)}) copy-start(bf16[256,128]{1,0:T(8,128)(2,1)} %w.15) | copy-start | bytes 196612
  3.0 15.8 %copy-start.10 = (f32[2,3,128]{2,0,1:T(2,128)S(1)}, f32[2,3,128]{2,0,1:T(2,128)}, u32[]{:S(2)}) copy-start(f32[2,3,128]{2,0,1:T(2,128)} %param.27) | copy-start | bytes 9220
  3.2 14.8 %collective-permute-start = (bf16[28,64,256]{2,1,0:T(8,128)(2,1)S(1)}, bf16[28,64,256]{2,1,0:T(8,128)(2,1)S(1)}, u32[]{:S(2)}, u32[]{:S(2)}) collective-permute-start(bf16[28,64,256]{2,1,0:T(8,128)(2,1)S(1)} %get-tuple-element.161), channel_id=1, source_target_pairs={{0,16},{16,0},{1,17},{17,1},{2,18},{18,2},{3,19},{19,3},{4,20},{20... | collective-permute-start | bytes 2752520 | tf_op jit(solution)/shard_map/ppermute | solution.py:1356
  20.7 10.7 %copy-start.1 = (bf16[128,512]{1,0:T(8,128)(2,1)S(1)}, bf16[128,512]{1,0:T(8,128)(2,1)}, u32[]{:S(2)}) copy-start(bf16[128,512]{1,0:T(8,128)(2,1)} %w_c.7) | copy-start | bytes 393220
  20.7 10.7 %copy-start.14 = (f32[2,3,128]{2,0,1:T(2,128)S(1)}, f32[2,3,128]{2,0,1:T(2,128)}, u32[]{:S(2)}) copy-start(f32[2,3,128]{2,0,1:T(2,128)} %param.28) | copy-start | bytes 9220
  20.7 21.9 %copy-start.5 = (bf16[512,128]{1,0:T(8,128)(2,1)S(1)}, bf16[512,128]{1,0:T(8,128)(2,1)}, u32[]{:S(2)}) copy-start(bf16[512,128]{1,0:T(8,128)(2,1)} %w.14) | copy-start | bytes 393220
  20.7 21.9 %copy-start.8 = (f32[2,3,512]{2,0,1:T(2,128)S(1)}, f32[2,3,512]{2,0,1:T(2,128)}, u32[]{:S(2)}) copy-start(f32[2,3,512]{2,0,1:T(2,128)} %param.29) | copy-start | bytes 36868
  20.7 21.9 %copy-start.11 = (f32[2,3,512]{2,0,1:T(2,128)S(1)}, f32[2,3,512]{2,0,1:T(2,128)}, u32[]{:S(2)}) copy-start(f32[2,3,512]{2,0,1:T(2,128)} %param.30) | copy-start | bytes 36868
  42.6 11.4 %copy-start.12 = (f32[2,3,128]{2,0,1:T(2,128)S(1)}, f32[2,3,128]{2,0,1:T(2,128)}, u32[]{:S(2)}) copy-start(f32[2,3,128]{2,0,1:T(2,128)} %param.31) | copy-start | bytes 9220
  42.6 21.5 %copy-start.2 = (bf16[128,512]{1,0:T(8,128)(2,1)S(1)}, bf16[128,512]{1,0:T(8,128)(2,1)}, u32[]{:S(2)}) copy-start(bf16[128,512]{1,0:T(8,128)(2,1)} %w_c.5) | copy-start | bytes 393220
  42.6 21.5 %copy-start.13 = (f32[2,3,128]{2,0,1:T(2,128)S(1)}, f32[2,3,128]{2,0,1:T(2,128)}, u32[]{:S(2)}) copy-start(f32[2,3,128]{2,0,1:T(2,128)} %param.32) | copy-start | bytes 9220
  44.0 32.9 %copy-start.3 = (bf16[1,28,28,512]{3,2,1,0:T(8,128)(2,1)S(1)}, bf16[1,28,28,512]{3,2,1,0:T(8,128)(2,1)}, u32[]{:S(2)}) copy-start(bf16[1,28,28,512]{3,2,1,0:T(8,128)(2,1)} %param.34) | copy-start | bytes 2408452
  44.0 32.9 %copy-start.9 = (f32[2,3,512]{2,0,1:T(2,128)S(1)}, f32[2,3,512]{2,0,1:T(2,128)}, u32[]{:S(2)}) copy-start(f32[2,3,512]{2,0,1:T(2,128)} %param.33) | copy-start | bytes 36868
  122.3 6.6 %collective-permute-start.3 = (bf16[24,80,128]{2,1,0:T(8,128)(2,1)S(1)}, bf16[24,80,128]{2,1,0:T(8,128)(2,1)S(1)}, u32[]{:S(2)}, u32[]{:S(2)}) collective-permute-start(bf16[24,80,128]{2,1,0:T(8,128)(2,1)S(1)} %get-tuple-element.237), channel_id=1, source_target_pairs={{0,16},{16,0},{1,17},{17,1},{2,18},{18,2},{3,19},{19,3},{4,20},{20... | collective-permute-start | bytes 1474568 | tf_op jit(solution)/shard_map/ppermute | solution.py:1356
  125.1 3.8 %collective-permute-start.2 = (bf16[28,64,128]{2,1,0:T(8,128)(2,1)S(1)}, bf16[28,64,128]{2,1,0:T(8,128)(2,1)S(1)}, u32[]{:S(2)}, u32[]{:S(2)}) collective-permute-start(bf16[28,64,128]{2,1,0:T(8,128)(2,1)S(1)} %get-tuple-element.226.dn_oth), channel_id=1, source_target_pairs={{0,16},{16,0},{1,17},{17,1},{2,18},{18,2},{3,19},{19,3},{4,20},{20... | collective-permute-start | bytes 1376264 | tf_op jit(solution)/shard_map/ppermute | solution.py:1356
  126.1 2.7 %collective-permute-start.1 = (bf16[14,32,256]{2,1,0:T(8,128)(2,1)S(1)}, bf16[14,32,256]{2,1,0:T(8,128)(2,1)S(1)}, u32[]{:S(2)}, u32[]{:S(2)}) collective-permute-start(bf16[14,32,256]{2,1,0:T(8,128)(2,1)S(1)} %get-tuple-element.233), channel_id=1, source_target_pairs={{0,16},{16,0},{1,17},{17,1},{2,18},{18,2},{3,19},{19,3},{4,20},{20... | collective-permute-start | bytes 688136 | tf_op jit(solution)/shard_map/ppermute | solution.py:1356
  126.2 2.7 %collective-permute-start.4 = (bf16[8,80,128]{2,1,0:T(8,128)(2,1)S(1)}, bf16[8,80,128]{2,1,0:T(8,128)(2,1)S(1)}, u32[]{:S(2)}, u32[]{:S(2)}) collective-permute-start(bf16[8,80,128]{2,1,0:T(8,128)(2,1)S(1)} %get-tuple-element.239), channel_id=1, source_target_pairs={{0,16},{16,0},{1,17},{17,1},{2,18},{18,2},{3,19},{19,3},{4,20},{20... | collective-permute-start | bytes 491528 | tf_op jit(solution)/shard_map/ppermute | solution.py:1356
  163.2 7.2 %collective-permute-start.7 = (bf16[4,176,128]{2,1,0:T(8,128)(2,1)S(1)}, bf16[4,176,128]{2,1,0:T(8,128)(2,1)S(1)}, u32[]{:S(2)}, u32[]{:S(2)}) collective-permute-start(bf16[4,176,128]{2,1,0:T(8,128)(2,1)S(1)} %all_to_all.65.refs_0_), channel_id=1, source_target_pairs={{0,3},{1,2},{2,1},{3,0},{4,7},{5,6},{6,5},{7,4},{8,11},{9,10},{10,... | collective-permute-start | bytes 540680 | tf_op jit(solution)/shard_map/ppermute | solution.py:1551
  164.0 8.3 %collective-permute-start.6 = (bf16[4,176,128]{2,1,0:T(8,128)(2,1)S(1)}, bf16[4,176,128]{2,1,0:T(8,128)(2,1)S(1)}, u32[]{:S(2)}, u32[]{:S(2)}) collective-permute-start(bf16[4,176,128]{2,1,0:T(8,128)(2,1)S(1)} %all_to_all.65.refs_0_), channel_id=1, source_target_pairs={{0,2},{1,3},{2,0},{3,1},{4,6},{5,7},{6,4},{7,5},{8,10},{9,11},{10,... | collective-permute-start | bytes 540680 | tf_op jit(solution)/shard_map/ppermute | solution.py:1551
  164.6 7.6 %collective-permute-start.5 = (bf16[4,176,128]{2,1,0:T(8,128)(2,1)S(1)}, bf16[4,176,128]{2,1,0:T(8,128)(2,1)S(1)}, u32[]{:S(2)}, u32[]{:S(2)}) collective-permute-start(bf16[4,176,128]{2,1,0:T(8,128)(2,1)S(1)} %all_to_all.65.refs_0_), channel_id=1, source_target_pairs={{0,1},{1,0},{2,3},{3,2},{4,5},{5,4},{6,7},{7,6},{8,9},{9,8},{10,11... | collective-permute-start | bytes 540680 | tf_op jit(solution)/shard_map/ppermute | solution.py:1551
  166.7 6.2 %collective-permute-start.8 = (bf16[4,176,128]{2,1,0:T(8,128)(2,1)S(1)}, bf16[4,176,128]{2,1,0:T(8,128)(2,1)S(1)}, u32[]{:S(2)}, u32[]{:S(2)}) collective-permute-start(bf16[4,176,128]{2,1,0:T(8,128)(2,1)S(1)} %all_to_all.65.refs_0_), channel_id=1, source_target_pairs={{0,16},{16,0},{1,17},{17,1},{2,18},{18,2},{3,19},{19,3},{4,20},{20... | collective-permute-start | bytes 540680 | tf_op jit(solution)/shard_map/ppermute | solution.py:1356
  172.2 1.4 collective-permute-start.9
  172.2 1.7 collective-permute-start.10
  172.8 1.4 collective-permute-start.11

commit v13 on v12

--- a/solution.py
+++ b/solution.py
@@ -152,7 +152,7 @@
     return jnp.sum(x, axis=0, keepdims=True)
 
 
-OWN, OTHER, HALF, LIMIT, GATE, MINOR = range(6)
+OWN, OTHER, HALF, LIMIT, GATE, MINOR, MAJOR = range(7)
 
 
 def entry(tab, k):
@@ -262,6 +262,7 @@
     values = {
         OWN: own, OTHER: other, HALF: half, LIMIT: w.shape[1] // 4 * width[own], GATE: gate[own],
         MINOR: lax.rem(lax.rem(place_ref[0], batch), NEAR),
+        MAJOR: lax.div(lax.rem(place_ref[0], batch), NEAR),
     }
     tab[...] = jnp.zeros(tab.shape, F32)
     for k, v in values.items():
@@ -272,17 +273,21 @@
 def f1_strided(tab, x_own, x_oth, w, xee, z, stats, wide):
     half = half_of(tab)
     rows = x_own.shape[0] // 2
+    sums = tuple(zeros8(LANES) for _ in range(wide.shape[0]))
     for k, x_pad in enumerate((x_own, x_oth)):
         first = rows * (half if k == 0 else 1 - half)
 
         def put(i, carry, x_pad=x_pad, first=first):
+            out = []
             for b in range(wide.shape[0]):
                 lanes = slice(LANES * b, LANES * (b + 1))
-                wide[b] = x_pad[2 * i, :, lanes].astype(F32)
-                xee[first + i, :, lanes] = wide[b, pl.ds(0, COLS, stride=2), :].astype(BF16)
-            return carry
-
-        lax.fori_loop(0, rows, put, 0, unroll=7)
+                wide[b, i] = x_pad[2 * i, :, lanes].astype(F32)
+                even = wide[b, i, pl.ds(0, COLS, stride=2), :]
+                xee[first + i, :, lanes] = even.astype(BF16)
+                out.append(carry[b] + fold(even))
+            return tuple(out)
+
+        sums = lax.fori_loop(0, rows, put, sums, unroll=7)
     total = 2 * rows
     step = total // 7
     chans = z.shape[2]
@@ -292,8 +297,7 @@
         z[step * c : step * (c + 1)] = values.reshape(step, COLS, chans)
         parts = values.reshape(-1, 8, chans)
         squares = squares + jnp.sum(parts * parts, axis=0)
-    ones = jnp.ones((8, total * COLS), BF16)
-    stats[:, 0 : w.shape[0]] = mm(ones, flat(xee[...]))[0:1]
+    stats[:, 0 : w.shape[0]] = join([down(v) for v in sums])
     stats[:, w.shape[0] :] = down(squares)
 
 
@@ -707,18 +711,18 @@
     gate = 0.25 * tiled(entry(tab, GATE), chans)
     scale = 0.5 * rstd * gain * gate
     bias = 0.5 * (shift - mean * rstd * gain) * gate
-    wide[...] = jnp.zeros(wide.shape, F32)
+    wide[:, cols:, :] = jnp.zeros((rows, COLS - cols, chans), F32)
     a_gate = rstd * gain * gate
 
     def put(i, carry):
         sums, products = carry
-        wide[0:cols, :] = cot[i].astype(F32)
+        wide[i, 0:cols, :] = cot[i].astype(F32)
         zz = z[i]
         u = 0.5 * joined[i].astype(F32) + zz * scale + bias
         t = jnp.tanh(u)
         p = u * t
         result[i] = (u + p)[0:cols].astype(BF16)
-        g = wide[...] * ((0.5 + 0.5 * t) * (1.0 + u - p))
+        g = wide[i] * ((0.5 + 0.5 * t) * (1.0 + u - p))
         grad_pre[i] = g
         low[i] = (a_gate * g).astype(BF16)
         return sums + fold(g), products + fold(g * (zz - mean))
@@ -984,8 +988,8 @@
                 g = jnp.where(keep, g, 0.0)
                 sums = sums + fold(g)
                 products = products + fold(g * (zv - mean_1))
-                wide[ra, pl.ds(cb, COLS, stride=2), :] = g
-            dn[2 * i + ra] = wide[ra].astype(BF16)
+                wide[2 * i + ra, pl.ds(cb, COLS, stride=2), :] = g
+            dn[2 * i + ra] = wide[2 * i + ra].astype(BF16)
         return sums, products
 
     totals = lax.fori_loop(0, rows, emit, (zeros8(n), zeros8(n)), unroll=7)
@@ -1245,13 +1249,13 @@
     put_split(out, 2 * piece + share, stack([found_2b[...], found_1b[...]]))
 
 
-def place_parts(minor, parts, packed, tall, found, piece):
+def place_parts(minor, major, parts, packed, tall, found, piece):
     far, share = parts[0].shape[0], tall.shape[1]
     for k, part in enumerate(parts):
         base = lax.bitwise_xor(minor, jnp.int32(k))
 
         def place(z, carry, part=part, base=base):
-            owner = base + NEAR * z
+            owner = base + NEAR * lax.bitwise_xor(major, jnp.int32(z))
             for h in (0, 1):
                 packed[h, owner] = part[z, piece * h : piece * (h + 1), :]
             tall[owner] = part[z, 2 * piece : 2 * piece + share, :].astype(F32)
@@ -1262,14 +1266,19 @@
         lax.fori_loop(0, far, place, 0, unroll=min(far, 4))
 
 
+def stack_parts(*refs):
+    for k, ref in enumerate(refs[:-1]):
+        refs[-1][k] = ref[0]
+
+
 def unpack_own(tab, *refs, piece):
-    place_parts(half_of(tab, MINOR), refs[:NEAR], *refs[NEAR:], piece)
+    place_parts(half_of(tab, MINOR), half_of(tab, MAJOR), refs[:NEAR], *refs[NEAR:], piece)
 
 
 def unpack(tab, labels, packed_own, tall_own, found_own, *refs, first, second, piece):
     parts, outs, values = refs[:NEAR], refs[NEAR : NEAR + 9], refs[NEAR + 9 :]
     *values, packed_oth, tall_oth, found_oth, sems = values
-    place_parts(half_of(tab, MINOR), parts, packed_oth, tall_oth, found_oth, piece)
+    place_parts(half_of(tab, MINOR), half_of(tab, MAJOR), parts, packed_oth, tall_oth, found_oth, piece)
     half = half_of(tab)
     copies = [
         pltpu.make_async_copy(value, out, sems.at[k]) for k, (value, out) in enumerate(zip(values, outs))
@@ -1412,7 +1421,7 @@
     xee, z_1p, stats_1p = stage(
         f1_strided,
         [maps(inputs, BF16), maps(outer), ((1, inputs + outer), F32)],
-        [pltpu.VMEM((inputs // n, cols_in, n), F32)],
+        [pltpu.VMEM((inputs // n, rows // 2, cols_in, n), F32)],
     )(tab, x_own, x_oth, w_1p)
     xs, z_1b, s2, labels, k_1a, k_all, z_oth = stage(
         f2,
@@ -1468,7 +1477,7 @@
         functools.partial(b7, share=share_1, p_at=p_at),
         [(cotangent.shape[1:], BF16), maps(outer), ((devices, high_7, n), BF16),
          mean_scale(outer), maps(n)],
-        [pltpu.VMEM((COLS, outer), F32), scratch(outer, BF16)],
+        [scratch(outer), scratch(outer, BF16)],
     )(tab, g6, labels, joined, z_2c, norm_2c, w_2c, cotangent[0], slope_2b, z_2b, k_2b, q_2b)
     g7 = gather(s7)
     dz_2b, dout_2a, s9, found_2b = stage(
@@ -1516,7 +1525,7 @@
             stage(
                 functools.partial(b12_images, own=own), [half_in, ((2, n), F32)],
                 [pltpu.VMEM((rows // 2, COLS, 2 * n), F32), pltpu.VMEM((rows // 2, COLS, 2 * n), F32),
-                 pltpu.VMEM((2, cols_in, n), F32)],
+                 pltpu.VMEM((rows, cols_in, n), F32)],
             )(tab, d2, b_even, b_odd, z, norm_1a, k_1a)
         )
         if not own:
@@ -1543,14 +1552,13 @@
             add_all, at=stats_at, pixels=pixels,
             parts=((xz_3, 0, cut_3), (xz_6, cut_3, cut_6), (stats_at + 4, cut_6, share)),
         ),
-        [((far, 2 * piece + share + 8, n), BF16)],
+        [((1, 2 * piece + share + 8, n), BF16)],
     )(g12, labels, norm_1a, k_all, g3, g6, found_2b, found_1b)
-    columns_of = [[k + NEAR * z for z in range(far)] for k in range(NEAR)]
-    along = lax.all_to_all(mine, "batch", 0, 0, axis_index_groups=columns_of)
-    near = [
-        lax.ppermute(along, "batch", [(i, i ^ k) for i in range(batch)]) for k in range(1, NEAR)
+    others = [
+        lax.ppermute(mine, "batch", [(i, i ^ (NEAR * k)) for i in range(batch)])
+        for k in range(1, far)
     ]
-    late, _ = tie(labels, along)
+    late, _ = tie(labels, mine)
     grad_norms = stage(norm_tail, params(norm_2c, norm_2a, norm_1c, norm_1p))(late, g7, g9, g10)
     finished = (result, *grad_norms)
     held = len(finished)
@@ -1563,7 +1571,11 @@
         hbm_out=range(held + 2),
     )(tab, g12, labels, norm_1a, k_1a, w_1a, z_own, z_for, dn_own, dn_for, gs_own, gs_for, *finished)
     result, grad_norm_2c, grad_norm_2a, grad_norm_1c, grad_norm_1p = finished
-    *near, grad_images = tie(*near, grad_images)
+    *others, grad_images = tie(*others, grad_images)
+    (along,) = stage(stack_parts, [((far, *mine.shape[1:]), BF16)])(mine, *others)
+    near = [
+        lax.ppermute(along, "batch", [(i, i ^ k) for i in range(batch)]) for k in range(1, NEAR)
+    ]
     parts = [along, *near]
     weights = (w_2c, w_2b.reshape(-1, n), w_2a, w_1c, w_1p, w_1b.reshape(-1, n), w_1a)
     side = [

time: 176 us -> 175 us (level)
  blocking collectives: 133 us -> 123 us
  starting transfers between devices: 5.72 us -> 10.2 us
  waiting for transfers between devices: 3.75 us -> 7.07 us
    all_to_all x1 -> x0, blocking collectives: 9.55 us -> none  [body(): along = lax.all_to_all(mine, 'batch', 0, 0, axis_index_groups=columns_of)]
    ppermute x0 -> x3, starting transfers between devices: none -> 4.45 us  [body(): lax.ppermute(mine, 'batch', [(i, i ^ NEAR * k) for i in range(batch)])]
    ppermute x3, waiting for transfers between devices: 2.52 us -> 6.09 us  [body(): lax.ppermute(along, 'batch', [(i, i ^ k) for i in range(batch)])]
    pallas_call x24 -> x25, Pallas kernels: 32.4 us -> 32.3 us  [call(): pl.pallas_call(kernel, out_shape=tuple((jax.ShapeDtypeStruct(s, d) for s,...]
  transfers between devices with their start and end apart: 12 -> 15, of which waited for: 5 -> 4; matrix products, arithmetic and copies ran while one was open for 0% -> 0% of each run, Pallas kernels for 5% -> 5%
where the time goes in v13:
time: 175 us; the launch traced here: 174 us
  blocking collectives  123 us (70%)
  Pallas kernels  32.3 us (18%)
  starting transfers between devices  10.2 us (6%)
  waiting for transfers between devices  7.07 us (4%)
    all_to_all x10, blocking collectives, gather(): return lax.all_to_all(send, AXES, 0, 0)  123 us
    pallas_call x25, Pallas kernels, call(): pl.pallas_call(kernel, out_shape=tuple((jax.ShapeDtypeStruct(s, d) for s,...  32.3 us
    ppermute x3, waiting for transfers between devices, body(): lax.ppermute(along, 'batch', [(i, i ^ k) for i in range(batch)])  6.09 us
    ppermute x3, starting transfers between devices, body(): lax.ppermute(mine, 'batch', [(i, i ^ NEAR * k) for i in range(batch)])  4.45 us
    ppermute x3, starting transfers between devices, body(): lax.ppermute(along, 'batch', [(i, i ^ k) for i in range(batch)])  3.55 us
  transfers between devices with their start and end apart: 15, of which 4 were waited for; matrix products, arithmetic and copies ran while one was open for 0% of the time, Pallas kernels for 5%

profile of v13, /device:TPU:0, one launch (start us, length us, event | category | flops | bytes accessed | tf_op | source)
XLA Modules:
  0.0 174.4 jit_solution(9988904319664618126)
XLA Ops:
  0.7 2.3 %f1.1 = (f32[8,128]{1,0:T(8,128)S(1)}, bf16[28,64,256]{2,1,0:T(8,128)(2,1)S(1)}, bf16[28,64,256]{2,1,0:T(8,128)(2,1)S(1)}, f32[28,64,128]{2,1,0:T(8,128)S(1)}, f...) custom-call(s32[1]{0:T(128)} %bitcast.place_at, s32[2]{0:T(128)} %group_at.1, s32[3]{0:T(128)} %width_at.1, ...), custom_call_target="tpu_custom_call" | custom-call | tf_op jit(solution)/shard_map/f1/pallas_call | solution.py:33
  3.7 14.2 %all_to_all.50.got = f32[32,1,640]{2,1,0:T(1,128)S(1)} all-to-all(f32[32,1,640]{2,1,0:T(1,128)S(1)} %get-tuple-element.160), channel_id=1, replica_groups=mesh['rows'=2,'batch'=16] {'rows','batch'}, dimensions={0} | all-to-all | bytes 163840 | tf_op jit(solution)/shard_map/all_to_all | solution.py:1357
  18.8 1.8 %f2.1 = (bf16[29,32,768]{2,1,0:T(8,128)(2,1)S(1)}, f32[28,32,128]{2,1,0:T(8,128)S(1)}, f32[32,1,1024]{2,1,0:T(1,128)S(1)}, f32[32,1,128]{2,1,0:T(1,128)S(1)}, f3...) custom-call(f32[8,128]{1,0:T(8,128)S(1)} %get-tuple-element.146.tab, ...), custom_call_target="tpu_custom_call" | custom-call | tf_op jit(solution)/shard_map/f2/pallas_call | solution.py:33
  20.7 1.0 g_xz.1
  21.7 9.6 %all_to_all.51.got = f32[32,1,1024]{2,1,0:T(1,128)S(1)} all-to-all(f32[32,1,1024]{2,1,0:T(1,128)S(1)} %get-tuple-element.174), channel_id=1, replica_groups=mesh['rows'=2,'batch'=16] {'rows','batch'}, dimensions={0} | all-to-all | bytes 262144 | tf_op jit(solution)/shard_map/all_to_all | solution.py:1357
  31.4 1.4 f3.1
  32.7 9.8 %all_to_all.52.got.pair_low.got_act.got_a = bf16[32,16,128]{2,1,0:T(8,128)(2,1)S(1)} all-to-all(bf16[32,16,128]{2,1,0:T(8,128)(2,1)S(1)} %get-tuple-element.178), channel_id=1, replica_groups=mesh['rows'=2,'batch'=16] {'rows','batch'}, dimensions={0} | all-to-all | bytes 262144 | tf_op jit(solution)/shard_map/all_to_all | solution.py:1357
  42.6 1.4 f4.1
  44.0 9.9 %all_to_all.53.got.pair_high.got_q = bf16[32,16,128]{2,1,0:T(8,128)(2,1)S(1)} all-to-all(bf16[32,16,128]{2,1,0:T(8,128)(2,1)S(1)} %get-tuple-element.184), channel_id=1, replica_groups=mesh['rows'=2,'batch'=16] {'rows','batch'}, dimensions={0} | all-to-all | bytes 262144 | tf_op jit(solution)/shard_map/all_to_all | solution.py:1357
  54.0 0.9 f5.1
  54.9 9.2 %all_to_all.54.got = f32[32,1,256]{2,1,0:T(1,128)S(1)} all-to-all(f32[32,1,256]{2,1,0:T(1,128)S(1)} %get-tuple-element.188), channel_id=1, replica_groups=mesh['rows'=2,'batch'=16] {'rows','batch'}, dimensions={0} | all-to-all | bytes 65536 | tf_op jit(solution)/shard_map/all_to_all | solution.py:1357
  64.1 1.2 f6.1
  65.4 11.5 %all_to_all.55.got.got_act.got_b = bf16[32,24,128]{2,1,0:T(8,128)(2,1)S(1)} all-to-all(bf16[32,24,128]{2,1,0:T(8,128)(2,1)S(1)} %get-tuple-element.192), channel_id=1, replica_groups=mesh['rows'=2,'batch'=16] {'rows','batch'}, dimensions={0} | all-to-all | bytes 393216 | tf_op jit(solution)/shard_map/all_to_all | solution.py:1357
  76.9 2.7 %b7.1 = (bf16[28,28,512]{2,1,0:T(8,128)(2,1)S(1)}, f32[28,32,512]{2,1,0:T(8,128)S(1)}, bf16[32,32,128]{2,1,0:T(8,128)(2,1)S(1)}, f32[2,512]{1,0:T(2,128)S(1)}, f32[28,32,128]{2,1,0:T(8,128)S(1)}) custom-call(f32[8,128]{1,0:T(8,128)S(1)} %get-tuple-element.146.tab, bf16[32,24,128]{2,1,0:T(8,128)(2,1)S(1)} %all_to_all.55.got.got_act.got_b, ...), custom_call_target="tpu_custom_call" | custom-call | tf_op jit(solution)/shard_map/b7/pallas_call | solution.py:33
  79.6 12.9 %all_to_all.56.got.got_2c = bf16[32,32,128]{2,1,0:T(8,128)(2,1)S(1)} all-to-all(bf16[32,32,128]{2,1,0:T(8,128)(2,1)S(1)} %get-tuple-element.198), channel_id=1, replica_groups=mesh['rows'=2,'batch'=16] {'rows','batch'}, dimensions={0} | all-to-all | bytes 524288 | tf_op jit(solution)/shard_map/all_to_all | solution.py:1357
  92.5 2.4 %b9.1 = (bf16[28,32,128]{2,1,0:T(8,128)(2,1)S(1)}, f32[28,32,128]{2,1,0:T(8,128)S(1)}, bf16[32,16,128]{2,1,0:T(8,128)(2,1)S(1)}, f32[2,128]{1,0:T(2,128)S(1)}) custom-call(f32[8,128]{1,0:T(8,128)S(1)} %get-tuple-element.146.tab, bf16[32,32,128]{2,1,0:T(8,128)(2,1)S(1)} %all_to_all.56.got.got_2c, f32[32,1,128]{2,1,0:T(1,128)S(1)} %get-tuple-element.248.labels, ...), custom_call_target="tpu_custom_call" | custom-call | tf_op jit(solution)/shard_map/b9/pallas_call | solution.py:33
  94.9 9.6 %all_to_all.57.got.got_p.got_x.got_2a = bf16[32,16,128]{2,1,0:T(8,128)(2,1)S(1)} all-to-all(bf16[32,16,128]{2,1,0:T(8,128)(2,1)S(1)} %get-tuple-element.207), channel_id=1, replica_groups=mesh['rows'=2,'batch'=16] {'rows','batch'}, dimensions={0} | all-to-all | bytes 262144 | tf_op jit(solution)/shard_map/all_to_all | solution.py:1357
  104.5 2.5 %b10.1 = (bf16[28,32,128]{2,1,0:T(8,128)(2,1)S(1)}, f32[28,32,512]{2,1,0:T(8,128)S(1)}, f32[32,2,896]{2,1,0:T(2,128)S(1)}, f32[28,32,128]{2,1,0:T(8,128)S(1)}) custom-call(f32[8,128]{1,0:T(8,128)S(1)} %get-tuple-element.146.tab, bf16[32,16,128]{2,1,0:T(8,128)(2,1)S(1)} %all_to_all.57.got.got_p.got_x.got_2a, f32[32,1,128]{2,1,0:T(1,128)S(1)} %get-tuple-element.248.labels, ...), custom_call_target="tpu_custom_call" | custom-call | tf_op jit(solution)/shard_map/b10/pallas_call | solution.py:33
  107.0 12.4 %all_to_all.58.got.got_1 = f32[32,2,896]{2,1,0:T(2,128)S(1)} all-to-all(f32[32,2,896]{2,1,0:T(2,128)S(1)} %get-tuple-element.217), channel_id=1, replica_groups=mesh['rows'=2,'batch'=16] {'rows','batch'}, dimensions={0} | all-to-all | bytes 458752 | tf_op jit(solution)/shard_map/all_to_all | solution.py:1357
  119.4 2.9 %g_most.1 = (bf16[24,80,128]{2,1,0:T(8,128)(2,1)S(1)}, bf16[24,80,128]{2,1,0:T(8,128)(2,1)S(1)}, bf16[28,32,512]{2,1,0:T(8,128)(2,1)S(1)}, f32[1,1280]{1,0:T(1,128)S(1)}) custom-call(f32[8,128]{1,0:T(8,128)S(1)} %get-tuple-element.146.tab, bf16[28,32,128]{2,1,0:T(8,128)(2,1)S(1)} %get-tuple-element.190.act.act_2b, ...), custom_call_target="tpu_custom_call" | custom-call | tf_op jit(solution)/shard_map/g_most/pallas_call | solution.py:33
  122.3 1.7 b12.1
  124.0 1.0 b12_images.2
  126.7 1.0 b12_images.3
  127.7 1.1 g_xd.1
  129.1 24.2 %all_to_all.59.got = bf16[32,96,128]{2,1,0:T(8,128)(2,1)S(1)} all-to-all(bf16[32,96,128]{2,1,0:T(8,128)(2,1)S(1)} %pack_last.1), channel_id=1, replica_groups=mesh['rows'=2,'batch'=16] {'rows','batch'}, dimensions={0} | all-to-all | bytes 1572864 | tf_op jit(solution)/shard_map/all_to_all | solution.py:1357
  153.6 0.8 collective-permute-start.7
  154.5 3.5 %collective-permute-start.5 = (bf16[1,176,128]{2,1,0:T(8,128)(2,1)S(1)}, bf16[1,176,128]{2,1,0:T(8,128)(2,1)S(1)}, u32[]{:S(2)}, u32[]{:S(2)}) collective-permute-start(bf16[1,176,128]{2,1,0:T(8,128)(2,1)S(1)} %add_all.1.refs_0_), channel_id=1, source_target_pairs={{0,4},{1,5},{2,6},{3,7},{4,0},{5,1},{6,2},{7,3},{8,12},{9,13},{10,... | collective-permute-start | bytes 135176 | tf_op jit(solution)/shard_map/ppermute | solution.py:1558
  158.7 2.3 %b13.1 = (bf16[28,28,512]{2,1,0:T(8,128)(2,1)}, f32[3,2,512]{2,1,0:T(2,128)}, f32[3,2,128]{2,1,0:T(2,128)}, f32[3,2,512]{2,1,0:T(2,128)}, f32[3,2,512]{2,1,0:T(2...) custom-call(f32[8,128]{1,0:T(8,128)S(1)} %get-tuple-element.146.tab, ...), custom_call_target="tpu_custom_call" | custom-call | tf_op jit(solution)/shard_map/b13/pallas_call | solution.py:33
  162.1 2.6 %collective-permute-start.8 = (bf16[4,176,128]{2,1,0:T(8,128)(2,1)S(1)}, bf16[4,176,128]{2,1,0:T(8,128)(2,1)S(1)}, u32[]{:S(2)}, u32[]{:S(2)}) collective-permute-start(bf16[4,176,128]{2,1,0:T(8,128)(2,1)S(1)} %stack_parts.1.refs_0_), channel_id=1, source_target_pairs={{0,1},{1,0},{2,3},{3,2},{4,5},{5,4},{6,7},{7,6},{8,9},{9,8},{10,11... | collective-permute-start | bytes 540680 | tf_op jit(solution)/shard_map/ppermute | solution.py:1577
  164.7 4.4 %collective-permute-done.10.refs_3_ = bf16[4,176,128]{2,1,0:T(8,128)(2,1)S(1)} collective-permute-done((bf16[4,176,128]{2,1,0:T(8,128)(2,1)S(1)}, bf16[4,176,128]{2,1,0:T(8,128)(2,1)S(1)}, u32[]{:S(2)}, u32[]{:S(2)}) %collective-permute-start.10) | collective-permute-done | bytes 180256 | tf_op jit(solution)/shard_map/ppermute | solution.py:1577
  169.2 1.6 collective-permute-done.9.refs_2_
  172.5 1.8 %unpack.1 = (f32[128,512]{1,0:T(8,128)}, f32[1152,128]{1,0:T(8,128)}, f32[512,128]{1,0:T(8,128)}, f32[128,512]{1,0:T(8,128)}, f32[256,512]{1,0:T(8,128)}, /*inde...) custom-call(f32[8,128]{1,0:T(8,128)S(1)} %get-tuple-element.146.tab, ...), custom_call_target="tpu_custom_call" | custom-call | tf_op jit(solution)/shard_map/unpack/pallas_call | solution.py:33
  (63 shorter events, 7.3 us)
Async XLA Ops:
  0.6 2.4 %copy-start.7 = (bf16[3,3,128,128]{3,2,1,0:T(8,128)(2,1)S(1)}, bf16[3,3,128,128]{3,2,1,0:T(8,128)(2,1)}, u32[]{:S(2)}) copy-start(bf16[3,3,128,128]{3,2,1,0:T(8,128)(2,1)} %w2b) | copy-start | bytes 884740
  0.7 2.4 %copy-start.6 = (bf16[3,3,128,128]{3,2,1,0:T(8,128)(2,1)S(1)}, bf16[3,3,128,128]{3,2,1,0:T(8,128)(2,1)}, u32[]{:S(2)}) copy-start(bf16[3,3,128,128]{3,2,1,0:T(8,128)(2,1)} %w1b) | copy-start | bytes 884740
  0.7 17.3 %copy-start = (bf16[256,512]{1,0:T(8,128)(2,1)S(1)}, bf16[256,512]{1,0:T(8,128)(2,1)}, u32[]{:S(2)}) copy-start(bf16[256,512]{1,0:T(8,128)(2,1)} %w_p.3) | copy-start | bytes 786436
  3.0 15.8 %copy-start.4 = (bf16[256,128]{1,0:T(8,128)(2,1)S(1)}, bf16[256,128]{1,0:T(8,128)(2,1)}, u32[]{:S(2)}) copy-start(bf16[256,128]{1,0:T(8,128)(2,1)} %w.15) | copy-start | bytes 196612
  3.0 15.8 %copy-start.10 = (f32[2,3,128]{2,0,1:T(2,128)S(1)}, f32[2,3,128]{2,0,1:T(2,128)}, u32[]{:S(2)}) copy-start(f32[2,3,128]{2,0,1:T(2,128)} %param.27) | copy-start | bytes 9220
  3.2 14.8 %collective-permute-start = (bf16[28,64,256]{2,1,0:T(8,128)(2,1)S(1)}, bf16[28,64,256]{2,1,0:T(8,128)(2,1)S(1)}, u32[]{:S(2)}, u32[]{:S(2)}) collective-permute-start(bf16[28,64,256]{2,1,0:T(8,128)(2,1)S(1)} %get-tuple-element.161), channel_id=1, source_target_pairs={{0,16},{16,0},{1,17},{17,1},{2,18},{18,2},{3,19},{19,3},{4,20},{20... | collective-permute-start | bytes 2752520 | tf_op jit(solution)/shard_map/ppermute | solution.py:1365
  20.6 10.7 %copy-start.1 = (bf16[128,512]{1,0:T(8,128)(2,1)S(1)}, bf16[128,512]{1,0:T(8,128)(2,1)}, u32[]{:S(2)}) copy-start(bf16[128,512]{1,0:T(8,128)(2,1)} %w_c.7) | copy-start | bytes 393220
  20.7 10.7 %copy-start.14 = (f32[2,3,128]{2,0,1:T(2,128)S(1)}, f32[2,3,128]{2,0,1:T(2,128)}, u32[]{:S(2)}) copy-start(f32[2,3,128]{2,0,1:T(2,128)} %param.28) | copy-start | bytes 9220
  20.7 21.9 %copy-start.5 = (bf16[512,128]{1,0:T(8,128)(2,1)S(1)}, bf16[512,128]{1,0:T(8,128)(2,1)}, u32[]{:S(2)}) copy-start(bf16[512,128]{1,0:T(8,128)(2,1)} %w.14) | copy-start | bytes 393220
  20.7 21.9 %copy-start.8 = (f32[2,3,512]{2,0,1:T(2,128)S(1)}, f32[2,3,512]{2,0,1:T(2,128)}, u32[]{:S(2)}) copy-start(f32[2,3,512]{2,0,1:T(2,128)} %param.29) | copy-start | bytes 36868
  20.7 21.9 %copy-start.11 = (f32[2,3,512]{2,0,1:T(2,128)S(1)}, f32[2,3,512]{2,0,1:T(2,128)}, u32[]{:S(2)}) copy-start(f32[2,3,512]{2,0,1:T(2,128)} %param.30) | copy-start | bytes 36868
  42.6 11.4 %copy-start.12 = (f32[2,3,128]{2,0,1:T(2,128)S(1)}, f32[2,3,128]{2,0,1:T(2,128)}, u32[]{:S(2)}) copy-start(f32[2,3,128]{2,0,1:T(2,128)} %param.31) | copy-start | bytes 9220
  42.6 21.5 %copy-start.2 = (bf16[128,512]{1,0:T(8,128)(2,1)S(1)}, bf16[128,512]{1,0:T(8,128)(2,1)}, u32[]{:S(2)}) copy-start(bf16[128,512]{1,0:T(8,128)(2,1)} %w_c.5) | copy-start | bytes 393220
  42.6 21.5 %copy-start.13 = (f32[2,3,128]{2,0,1:T(2,128)S(1)}, f32[2,3,128]{2,0,1:T(2,128)}, u32[]{:S(2)}) copy-start(f32[2,3,128]{2,0,1:T(2,128)} %param.32) | copy-start | bytes 9220
  44.0 32.9 %copy-start.3 = (bf16[1,28,28,512]{3,2,1,0:T(8,128)(2,1)S(1)}, bf16[1,28,28,512]{3,2,1,0:T(8,128)(2,1)}, u32[]{:S(2)}) copy-start(bf16[1,28,28,512]{3,2,1,0:T(8,128)(2,1)} %param.34) | copy-start | bytes 2408452
  44.0 32.9 %copy-start.9 = (f32[2,3,512]{2,0,1:T(2,128)S(1)}, f32[2,3,512]{2,0,1:T(2,128)}, u32[]{:S(2)}) copy-start(f32[2,3,512]{2,0,1:T(2,128)} %param.33) | copy-start | bytes 36868
  122.2 6.6 %collective-permute-start.3 = (bf16[24,80,128]{2,1,0:T(8,128)(2,1)S(1)}, bf16[24,80,128]{2,1,0:T(8,128)(2,1)S(1)}, u32[]{:S(2)}, u32[]{:S(2)}) collective-permute-start(bf16[24,80,128]{2,1,0:T(8,128)(2,1)S(1)} %get-tuple-element.237), channel_id=1, source_target_pairs={{0,16},{16,0},{1,17},{17,1},{2,18},{18,2},{3,19},{19,3},{4,20},{20... | collective-permute-start | bytes 1474568 | tf_op jit(solution)/shard_map/ppermute | solution.py:1365
  125.0 3.8 %collective-permute-start.2 = (bf16[28,64,128]{2,1,0:T(8,128)(2,1)S(1)}, bf16[28,64,128]{2,1,0:T(8,128)(2,1)S(1)}, u32[]{:S(2)}, u32[]{:S(2)}) collective-permute-start(bf16[28,64,128]{2,1,0:T(8,128)(2,1)S(1)} %get-tuple-element.226.dn_oth), channel_id=1, source_target_pairs={{0,16},{16,0},{1,17},{17,1},{2,18},{18,2},{3,19},{19,3},{4,20},{20... | collective-permute-start | bytes 1376264 | tf_op jit(solution)/shard_map/ppermute | solution.py:1365
  126.1 2.7 %collective-permute-start.1 = (bf16[14,32,256]{2,1,0:T(8,128)(2,1)S(1)}, bf16[14,32,256]{2,1,0:T(8,128)(2,1)S(1)}, u32[]{:S(2)}, u32[]{:S(2)}) collective-permute-start(bf16[14,32,256]{2,1,0:T(8,128)(2,1)S(1)} %get-tuple-element.233), channel_id=1, source_target_pairs={{0,16},{16,0},{1,17},{17,1},{2,18},{18,2},{3,19},{19,3},{4,20},{20... | collective-permute-start | bytes 688136 | tf_op jit(solution)/shard_map/ppermute | solution.py:1365
  126.2 2.7 %collective-permute-start.4 = (bf16[8,80,128]{2,1,0:T(8,128)(2,1)S(1)}, bf16[8,80,128]{2,1,0:T(8,128)(2,1)S(1)}, u32[]{:S(2)}, u32[]{:S(2)}) collective-permute-start(bf16[8,80,128]{2,1,0:T(8,128)(2,1)S(1)} %get-tuple-element.239), channel_id=1, source_target_pairs={{0,16},{16,0},{1,17},{17,1},{2,18},{18,2},{3,19},{19,3},{4,20},{20... | collective-permute-start | bytes 491528 | tf_op jit(solution)/shard_map/ppermute | solution.py:1365
  153.6 7.5 %collective-permute-start.7 = (bf16[1,176,128]{2,1,0:T(8,128)(2,1)S(1)}, bf16[1,176,128]{2,1,0:T(8,128)(2,1)S(1)}, u32[]{:S(2)}, u32[]{:S(2)}) collective-permute-start(bf16[1,176,128]{2,1,0:T(8,128)(2,1)S(1)} %add_all.1.refs_0_), channel_id=1, source_target_pairs={{0,12},{1,13},{2,14},{3,15},{4,8},{5,9},{6,10},{7,11},{8,4},{9,5},... | collective-permute-start | bytes 135176 | tf_op jit(solution)/shard_map/ppermute | solution.py:1558
  154.4 6.7 %collective-permute-start.6 = (bf16[1,176,128]{2,1,0:T(8,128)(2,1)S(1)}, bf16[1,176,128]{2,1,0:T(8,128)(2,1)S(1)}, u32[]{:S(2)}, u32[]{:S(2)}) collective-permute-start(bf16[1,176,128]{2,1,0:T(8,128)(2,1)S(1)} %add_all.1.refs_0_), channel_id=1, source_target_pairs={{0,8},{1,9},{2,10},{3,11},{4,12},{5,13},{6,14},{7,15},{8,0},{9,1},... | collective-permute-start | bytes 135176 | tf_op jit(solution)/shard_map/ppermute | solution.py:1558
  154.5 6.6 %collective-permute-start.5 = (bf16[1,176,128]{2,1,0:T(8,128)(2,1)S(1)}, bf16[1,176,128]{2,1,0:T(8,128)(2,1)S(1)}, u32[]{:S(2)}, u32[]{:S(2)}) collective-permute-start(bf16[1,176,128]{2,1,0:T(8,128)(2,1)S(1)} %add_all.1.refs_0_), channel_id=1, source_target_pairs={{0,4},{1,5},{2,6},{3,7},{4,0},{5,1},{6,2},{7,3},{8,12},{9,13},{10,... | collective-permute-start | bytes 135176 | tf_op jit(solution)/shard_map/ppermute | solution.py:1558
  161.1 8.0 %collective-permute-start.10 = (bf16[4,176,128]{2,1,0:T(8,128)(2,1)S(1)}, bf16[4,176,128]{2,1,0:T(8,128)(2,1)S(1)}, u32[]{:S(2)}, u32[]{:S(2)}) collective-permute-start(bf16[4,176,128]{2,1,0:T(8,128)(2,1)S(1)} %stack_parts.1.refs_0_), channel_id=1, source_target_pairs={{0,3},{1,2},{2,1},{3,0},{4,7},{5,6},{6,5},{7,4},{8,11},{9,10},{10,... | collective-permute-start | bytes 540680 | tf_op jit(solution)/shard_map/ppermute | solution.py:1577
  161.5 9.3 %collective-permute-start.9 = (bf16[4,176,128]{2,1,0:T(8,128)(2,1)S(1)}, bf16[4,176,128]{2,1,0:T(8,128)(2,1)S(1)}, u32[]{:S(2)}, u32[]{:S(2)}) collective-permute-start(bf16[4,176,128]{2,1,0:T(8,128)(2,1)S(1)} %stack_parts.1.refs_0_), channel_id=1, source_target_pairs={{0,2},{1,3},{2,0},{3,1},{4,6},{5,7},{6,4},{7,5},{8,10},{9,11},{10,... | collective-permute-start | bytes 540680 | tf_op jit(solution)/shard_map/ppermute | solution.py:1577
  162.1 8.7 %collective-permute-start.8 = (bf16[4,176,128]{2,1,0:T(8,128)(2,1)S(1)}, bf16[4,176,128]{2,1,0:T(8,128)(2,1)S(1)}, u32[]{:S(2)}, u32[]{:S(2)}) collective-permute-start(bf16[4,176,128]{2,1,0:T(8,128)(2,1)S(1)} %stack_parts.1.refs_0_), channel_id=1, source_target_pairs={{0,1},{1,0},{2,3},{3,2},{4,5},{5,4},{6,7},{7,6},{8,9},{9,8},{10,11... | collective-permute-start | bytes 540680 | tf_op jit(solution)/shard_map/ppermute | solution.py:1577
  164.7 6.8 %collective-permute-start.11 = (bf16[4,176,128]{2,1,0:T(8,128)(2,1)S(1)}, bf16[4,176,128]{2,1,0:T(8,128)(2,1)S(1)}, u32[]{:S(2)}, u32[]{:S(2)}) collective-permute-start(bf16[4,176,128]{2,1,0:T(8,128)(2,1)S(1)} %stack_parts.1.refs_0_), channel_id=1, source_target_pairs={{0,16},{16,0},{1,17},{17,1},{2,18},{18,2},{3,19},{19,3},{4,20},{20... | collective-permute-start | bytes 540680 | tf_op jit(solution)/shard_map/ppermute | solution.py:1365
  169.1 2.4 %collective-permute-start.14 = (bf16[4,176,128]{2,1,0:T(8,128)(2,1)S(1)}, bf16[4,176,128]{2,1,0:T(8,128)(2,1)S(1)}, u32[]{:S(2)}, u32[]{:S(2)}) collective-permute-start(bf16[4,176,128]{2,1,0:T(8,128)(2,1)S(1)} %collective-permute-done.10.refs_3_), channel_id=1, source_target_pairs={{0,16},{16,0},{1,17},{17,1},{2,18},{18,2},{3,19},{19,3},{4,20},{20... | collective-permute-start | bytes 540680 | tf_op jit(solution)/shard_map/ppermute | solution.py:1365
  170.8 1.4 collective-permute-start.13
  170.8 1.7 collective-permute-start.12

commit v14 on v13

--- a/solution.py
+++ b/solution.py
@@ -1558,9 +1558,7 @@
         lax.ppermute(mine, "batch", [(i, i ^ (NEAR * k)) for i in range(batch)])
         for k in range(1, far)
     ]
-    late, _ = tie(labels, mine)
-    grad_norms = stage(norm_tail, params(norm_2c, norm_2a, norm_1c, norm_1p))(late, g7, g9, g10)
-    finished = (result, *grad_norms)
+    finished = (result,)
     held = len(finished)
     *finished, grad_images, grad_norm_1a = stage(
         functools.partial(b13, at=stats_at, held=held),
@@ -1570,12 +1568,17 @@
          pltpu.SemaphoreType.DMA((held + 5,))],
         hbm_out=range(held + 2),
     )(tab, g12, labels, norm_1a, k_1a, w_1a, z_own, z_for, dn_own, dn_for, gs_own, gs_for, *finished)
-    result, grad_norm_2c, grad_norm_2a, grad_norm_1c, grad_norm_1p = finished
+    (result,) = finished
     *others, grad_images = tie(*others, grad_images)
     (along,) = stage(stack_parts, [((far, *mine.shape[1:]), BF16)])(mine, *others)
     near = [
         lax.ppermute(along, "batch", [(i, i ^ k) for i in range(batch)]) for k in range(1, NEAR)
     ]
+    late, _ = tie(labels, along)
+    grad_norms = stage(norm_tail, params(norm_2c, norm_2a, norm_1c, norm_1p))(late, g7, g9, g10)
+    grad_norm_2c, *near, grad_norm_2a, grad_norm_1c, grad_norm_1p = tie(
+        grad_norms[0], *near, *grad_norms[1:]
+    )
     parts = [along, *near]
     weights = (w_2c, w_2b.reshape(-1, n), w_2a, w_1c, w_1p, w_1b.reshape(-1, n), w_1a)
     side = [

time: 175 us -> 174 us (level)
  transfers between devices with their start and end apart: 15 -> 15, of which waited for: 4 -> 5; matrix products, arithmetic and copies ran while one was open for 0% -> 0% of each run, Pallas kernels for 5% -> 5%
where the time goes in v14:
time: 174 us
  blocking collectives  123 us (71%)
  Pallas kernels  32.9 us (19%)
  starting transfers between devices  10.2 us (6%)
  waiting for transfers between devices  6.1 us (4%)
    all_to_all x10, blocking collectives, gather(): return lax.all_to_all(send, AXES, 0, 0)  123 us
    pallas_call x25, Pallas kernels, call(): pl.pallas_call(kernel, out_shape=tuple((jax.ShapeDtypeStruct(s, d) for s,...  32.9 us
    ppermute x3, waiting for transfers between devices, body(): lax.ppermute(along, 'batch', [(i, i ^ k) for i in range(batch)])  4.85 us
    ppermute x3, starting transfers between devices, body(): lax.ppermute(mine, 'batch', [(i, i ^ NEAR * k) for i in range(batch)])  4.45 us
    ppermute x3, starting transfers between devices, body(): lax.ppermute(along, 'batch', [(i, i ^ k) for i in range(batch)])  3.55 us
  transfers between devices with their start and end apart: 15, of which 5 were waited for; matrix products, arithmetic and copies ran while one was open for 0% of the time, Pallas kernels for 5%

profile of v14, /device:TPU:0, one launch (start us, length us, event | category | flops | bytes accessed | tf_op | source)
XLA Modules:
  0.0 173.9 jit_solution(16303309288598671569)
XLA Ops:
  0.7 2.3 %f1.1 = (f32[8,128]{1,0:T(8,128)S(1)}, bf16[28,64,256]{2,1,0:T(8,128)(2,1)S(1)}, bf16[28,64,256]{2,1,0:T(8,128)(2,1)S(1)}, f32[28,64,128]{2,1,0:T(8,128)S(1)}, f...) custom-call(s32[1]{0:T(128)} %bitcast.place_at, s32[2]{0:T(128)} %group_at.1, s32[3]{0:T(128)} %width_at.1, ...), custom_call_target="tpu_custom_call" | custom-call | tf_op jit(solution)/shard_map/f1/pallas_call | solution.py:33
  3.7 14.2 %all_to_all.50.got = f32[32,1,640]{2,1,0:T(1,128)S(1)} all-to-all(f32[32,1,640]{2,1,0:T(1,128)S(1)} %get-tuple-element.163), channel_id=1, replica_groups=mesh['rows'=2,'batch'=16] {'rows','batch'}, dimensions={0} | all-to-all | bytes 163840 | tf_op jit(solution)/shard_map/all_to_all | solution.py:1357
  18.8 1.8 %f2.1 = (bf16[29,32,768]{2,1,0:T(8,128)(2,1)S(1)}, f32[28,32,128]{2,1,0:T(8,128)S(1)}, f32[32,1,1024]{2,1,0:T(1,128)S(1)}, f32[32,1,128]{2,1,0:T(1,128)S(1)}, f3...) custom-call(f32[8,128]{1,0:T(8,128)S(1)} %get-tuple-element.149.tab, ...), custom_call_target="tpu_custom_call" | custom-call | tf_op jit(solution)/shard_map/f2/pallas_call | solution.py:33
  20.7 1.0 g_xz.1
  21.7 9.6 %all_to_all.51.got = f32[32,1,1024]{2,1,0:T(1,128)S(1)} all-to-all(f32[32,1,1024]{2,1,0:T(1,128)S(1)} %get-tuple-element.177), channel_id=1, replica_groups=mesh['rows'=2,'batch'=16] {'rows','batch'}, dimensions={0} | all-to-all | bytes 262144 | tf_op jit(solution)/shard_map/all_to_all | solution.py:1357
  31.4 1.4 f3.1
  32.7 9.8 %all_to_all.52.got.pair_low.got_act.got_a = bf16[32,16,128]{2,1,0:T(8,128)(2,1)S(1)} all-to-all(bf16[32,16,128]{2,1,0:T(8,128)(2,1)S(1)} %get-tuple-element.181), channel_id=1, replica_groups=mesh['rows'=2,'batch'=16] {'rows','batch'}, dimensions={0} | all-to-all | bytes 262144 | tf_op jit(solution)/shard_map/all_to_all | solution.py:1357
  42.6 1.4 f4.1
  44.0 9.9 %all_to_all.53.got.pair_high.got_q = bf16[32,16,128]{2,1,0:T(8,128)(2,1)S(1)} all-to-all(bf16[32,16,128]{2,1,0:T(8,128)(2,1)S(1)} %get-tuple-element.187), channel_id=1, replica_groups=mesh['rows'=2,'batch'=16] {'rows','batch'}, dimensions={0} | all-to-all | bytes 262144 | tf_op jit(solution)/shard_map/all_to_all | solution.py:1357
  54.0 0.9 f5.1
  54.9 9.2 %all_to_all.54.got = f32[32,1,256]{2,1,0:T(1,128)S(1)} all-to-all(f32[32,1,256]{2,1,0:T(1,128)S(1)} %get-tuple-element.191), channel_id=1, replica_groups=mesh['rows'=2,'batch'=16] {'rows','batch'}, dimensions={0} | all-to-all | bytes 65536 | tf_op jit(solution)/shard_map/all_to_all | solution.py:1357
  64.1 1.2 f6.1
  65.4 11.5 %all_to_all.55.got.got_act.got_b = bf16[32,24,128]{2,1,0:T(8,128)(2,1)S(1)} all-to-all(bf16[32,24,128]{2,1,0:T(8,128)(2,1)S(1)} %get-tuple-element.195), channel_id=1, replica_groups=mesh['rows'=2,'batch'=16] {'rows','batch'}, dimensions={0} | all-to-all | bytes 393216 | tf_op jit(solution)/shard_map/all_to_all | solution.py:1357
  76.9 2.7 %b7.1 = (bf16[28,28,512]{2,1,0:T(8,128)(2,1)S(1)}, f32[28,32,512]{2,1,0:T(8,128)S(1)}, bf16[32,32,128]{2,1,0:T(8,128)(2,1)S(1)}, f32[2,512]{1,0:T(2,128)S(1)}, f32[28,32,128]{2,1,0:T(8,128)S(1)}) custom-call(f32[8,128]{1,0:T(8,128)S(1)} %get-tuple-element.149.tab, bf16[32,24,128]{2,1,0:T(8,128)(2,1)S(1)} %all_to_all.55.got.got_act.got_b, ...), custom_call_target="tpu_custom_call" | custom-call | tf_op jit(solution)/shard_map/b7/pallas_call | solution.py:33
  79.6 12.9 %all_to_all.56.got.got_2c = bf16[32,32,128]{2,1,0:T(8,128)(2,1)S(1)} all-to-all(bf16[32,32,128]{2,1,0:T(8,128)(2,1)S(1)} %get-tuple-element.201), channel_id=1, replica_groups=mesh['rows'=2,'batch'=16] {'rows','batch'}, dimensions={0} | all-to-all | bytes 524288 | tf_op jit(solution)/shard_map/all_to_all | solution.py:1357
  92.5 2.4 %b9.1 = (bf16[28,32,128]{2,1,0:T(8,128)(2,1)S(1)}, f32[28,32,128]{2,1,0:T(8,128)S(1)}, bf16[32,16,128]{2,1,0:T(8,128)(2,1)S(1)}, f32[2,128]{1,0:T(2,128)S(1)}) custom-call(f32[8,128]{1,0:T(8,128)S(1)} %get-tuple-element.149.tab, bf16[32,32,128]{2,1,0:T(8,128)(2,1)S(1)} %all_to_all.56.got.got_2c, f32[32,1,128]{2,1,0:T(1,128)S(1)} %get-tuple-element.257.labels, ...), custom_call_target="tpu_custom_call" | custom-call | tf_op jit(solution)/shard_map/b9/pallas_call | solution.py:33
  94.9 9.6 %all_to_all.57.got.got_p.got_x.got_2a = bf16[32,16,128]{2,1,0:T(8,128)(2,1)S(1)} all-to-all(bf16[32,16,128]{2,1,0:T(8,128)(2,1)S(1)} %get-tuple-element.210), channel_id=1, replica_groups=mesh['rows'=2,'batch'=16] {'rows','batch'}, dimensions={0} | all-to-all | bytes 262144 | tf_op jit(solution)/shard_map/all_to_all | solution.py:1357
  104.5 2.5 %b10.1 = (bf16[28,32,128]{2,1,0:T(8,128)(2,1)S(1)}, f32[28,32,512]{2,1,0:T(8,128)S(1)}, f32[32,2,896]{2,1,0:T(2,128)S(1)}, f32[28,32,128]{2,1,0:T(8,128)S(1)}) custom-call(f32[8,128]{1,0:T(8,128)S(1)} %get-tuple-element.149.tab, bf16[32,16,128]{2,1,0:T(8,128)(2,1)S(1)} %all_to_all.57.got.got_p.got_x.got_2a, f32[32,1,128]{2,1,0:T(1,128)S(1)} %get-tuple-element.257.labels, ...), custom_call_target="tpu_custom_call" | custom-call | tf_op jit(solution)/shard_map/b10/pallas_call | solution.py:33
  107.0 12.4 %all_to_all.58.got.got_1 = f32[32,2,896]{2,1,0:T(2,128)S(1)} all-to-all(f32[32,2,896]{2,1,0:T(2,128)S(1)} %get-tuple-element.220), channel_id=1, replica_groups=mesh['rows'=2,'batch'=16] {'rows','batch'}, dimensions={0} | all-to-all | bytes 458752 | tf_op jit(solution)/shard_map/all_to_all | solution.py:1357
  119.4 2.8 %g_most.1 = (bf16[24,80,128]{2,1,0:T(8,128)(2,1)S(1)}, bf16[24,80,128]{2,1,0:T(8,128)(2,1)S(1)}, bf16[28,32,512]{2,1,0:T(8,128)(2,1)S(1)}, f32[1,1280]{1,0:T(1,128)S(1)}) custom-call(f32[8,128]{1,0:T(8,128)S(1)} %get-tuple-element.149.tab, bf16[28,32,128]{2,1,0:T(8,128)(2,1)S(1)} %get-tuple-element.193.act.act_2b, ...), custom_call_target="tpu_custom_call" | custom-call | tf_op jit(solution)/shard_map/g_most/pallas_call | solution.py:33
  122.3 1.7 b12.1
  124.0 1.0 b12_images.2
  126.7 1.0 b12_images.3
  127.7 1.1 g_xd.1
  129.0 24.2 %all_to_all.59.got = bf16[32,96,128]{2,1,0:T(8,128)(2,1)S(1)} all-to-all(bf16[32,96,128]{2,1,0:T(8,128)(2,1)S(1)} %pack_last.1), channel_id=1, replica_groups=mesh['rows'=2,'batch'=16] {'rows','batch'}, dimensions={0} | all-to-all | bytes 1572864 | tf_op jit(solution)/shard_map/all_to_all | solution.py:1357
  154.5 3.5 %collective-permute-start.5 = (bf16[1,176,128]{2,1,0:T(8,128)(2,1)S(1)}, bf16[1,176,128]{2,1,0:T(8,128)(2,1)S(1)}, u32[]{:S(2)}, u32[]{:S(2)}) collective-permute-start(bf16[1,176,128]{2,1,0:T(8,128)(2,1)S(1)} %add_all.1.refs_0_), channel_id=1, source_target_pairs={{0,4},{1,5},{2,6},{3,7},{4,0},{5,1},{6,2},{7,3},{8,12},{9,13},{10,... | collective-permute-start | bytes 135176 | tf_op jit(solution)/shard_map/ppermute | solution.py:1558
  158.1 2.3 %b13.1 = (bf16[28,28,512]{2,1,0:T(8,128)(2,1)}, bf16[2,28,56,256]{3,2,1,0:T(8,128)(2,1)}, f32[3,2,128]{2,1,0:T(2,128)}) custom-call(f32[8,128]{1,0:T(8,128)S(1)} %get-tuple-element.149.tab, bf16[32,96,128]{2,1,0:T(8,128)(2,1)S(1)} %all_to_all.59.got, f32[32,1,128]{2,1,0:T(1,128)S(1)} %get-tuple-element.257.labels, f32[3,2,128]{2,1,0:T(2,128)S(1)} %bitcast.32, ...), custom_call_target="tpu_custom_call" | custom-call | tf_op jit(solution)/shard_map/b13/pallas_call | solution.py:33
  161.8 2.2 %collective-permute-start.8 = (bf16[4,176,128]{2,1,0:T(8,128)(2,1)S(1)}, bf16[4,176,128]{2,1,0:T(8,128)(2,1)S(1)}, u32[]{:S(2)}, u32[]{:S(2)}) collective-permute-start(bf16[4,176,128]{2,1,0:T(8,128)(2,1)S(1)} %stack_parts.1.refs_0_), channel_id=1, source_target_pairs={{0,1},{1,0},{2,3},{3,2},{4,5},{5,4},{6,7},{7,6},{8,9},{9,8},{10,11... | collective-permute-start | bytes 540680 | tf_op jit(solution)/shard_map/ppermute | solution.py:1575
  164.0 1.2 norm_tail.1
  165.2 3.2 %collective-permute-done.10.refs_3_ = bf16[4,176,128]{2,1,0:T(8,128)(2,1)S(1)} collective-permute-done((bf16[4,176,128]{2,1,0:T(8,128)(2,1)S(1)}, bf16[4,176,128]{2,1,0:T(8,128)(2,1)S(1)}, u32[]{:S(2)}, u32[]{:S(2)}) %collective-permute-start.10) | collective-permute-done | bytes 180256 | tf_op jit(solution)/shard_map/ppermute | solution.py:1575
  168.4 1.6 collective-permute-done.9.refs_2_
  172.0 1.8 %unpack.1 = (f32[128,512]{1,0:T(8,128)}, f32[1152,128]{1,0:T(8,128)}, f32[512,128]{1,0:T(8,128)}, f32[128,512]{1,0:T(8,128)}, f32[256,512]{1,0:T(8,128)}, /*inde...) custom-call(f32[8,128]{1,0:T(8,128)S(1)} %get-tuple-element.149.tab, ...), custom_call_target="tpu_custom_call" | custom-call | tf_op jit(solution)/shard_map/unpack/pallas_call | solution.py:33
  (63 shorter events, 8.1 us)
Async XLA Ops:
  0.6 2.4 %copy-start.7 = (bf16[3,3,128,128]{3,2,1,0:T(8,128)(2,1)S(1)}, bf16[3,3,128,128]{3,2,1,0:T(8,128)(2,1)}, u32[]{:S(2)}) copy-start(bf16[3,3,128,128]{3,2,1,0:T(8,128)(2,1)} %w2b) | copy-start | bytes 884740
  0.7 2.4 %copy-start.6 = (bf16[3,3,128,128]{3,2,1,0:T(8,128)(2,1)S(1)}, bf16[3,3,128,128]{3,2,1,0:T(8,128)(2,1)}, u32[]{:S(2)}) copy-start(bf16[3,3,128,128]{3,2,1,0:T(8,128)(2,1)} %w1b) | copy-start | bytes 884740
  0.7 17.3 %copy-start = (bf16[256,512]{1,0:T(8,128)(2,1)S(1)}, bf16[256,512]{1,0:T(8,128)(2,1)}, u32[]{:S(2)}) copy-start(bf16[256,512]{1,0:T(8,128)(2,1)} %w_p.3) | copy-start | bytes 786436
  3.0 15.8 %copy-start.4 = (bf16[256,128]{1,0:T(8,128)(2,1)S(1)}, bf16[256,128]{1,0:T(8,128)(2,1)}, u32[]{:S(2)}) copy-start(bf16[256,128]{1,0:T(8,128)(2,1)} %w.15) | copy-start | bytes 196612
  3.0 15.8 %copy-start.10 = (f32[2,3,128]{2,0,1:T(2,128)S(1)}, f32[2,3,128]{2,0,1:T(2,128)}, u32[]{:S(2)}) copy-start(f32[2,3,128]{2,0,1:T(2,128)} %param.27) | copy-start | bytes 9220
  3.2 14.8 %collective-permute-start = (bf16[28,64,256]{2,1,0:T(8,128)(2,1)S(1)}, bf16[28,64,256]{2,1,0:T(8,128)(2,1)S(1)}, u32[]{:S(2)}, u32[]{:S(2)}) collective-permute-start(bf16[28,64,256]{2,1,0:T(8,128)(2,1)S(1)} %get-tuple-element.164), channel_id=1, source_target_pairs={{0,16},{16,0},{1,17},{17,1},{2,18},{18,2},{3,19},{19,3},{4,20},{20... | collective-permute-start | bytes 2752520 | tf_op jit(solution)/shard_map/ppermute | solution.py:1365
  20.6 10.7 %copy-start.1 = (bf16[128,512]{1,0:T(8,128)(2,1)S(1)}, bf16[128,512]{1,0:T(8,128)(2,1)}, u32[]{:S(2)}) copy-start(bf16[128,512]{1,0:T(8,128)(2,1)} %w_c.7) | copy-start | bytes 393220
  20.7 10.7 %copy-start.14 = (f32[2,3,128]{2,0,1:T(2,128)S(1)}, f32[2,3,128]{2,0,1:T(2,128)}, u32[]{:S(2)}) copy-start(f32[2,3,128]{2,0,1:T(2,128)} %param.28) | copy-start | bytes 9220
  20.7 21.9 %copy-start.5 = (bf16[512,128]{1,0:T(8,128)(2,1)S(1)}, bf16[512,128]{1,0:T(8,128)(2,1)}, u32[]{:S(2)}) copy-start(bf16[512,128]{1,0:T(8,128)(2,1)} %w.14) | copy-start | bytes 393220
  20.7 21.9 %copy-start.8 = (f32[2,3,512]{2,0,1:T(2,128)S(1)}, f32[2,3,512]{2,0,1:T(2,128)}, u32[]{:S(2)}) copy-start(f32[2,3,512]{2,0,1:T(2,128)} %param.29) | copy-start | bytes 36868
  20.7 21.9 %copy-start.11 = (f32[2,3,512]{2,0,1:T(2,128)S(1)}, f32[2,3,512]{2,0,1:T(2,128)}, u32[]{:S(2)}) copy-start(f32[2,3,512]{2,0,1:T(2,128)} %param.30) | copy-start | bytes 36868
  42.6 11.4 %copy-start.12 = (f32[2,3,128]{2,0,1:T(2,128)S(1)}, f32[2,3,128]{2,0,1:T(2,128)}, u32[]{:S(2)}) copy-start(f32[2,3,128]{2,0,1:T(2,128)} %param.31) | copy-start | bytes 9220
  42.6 21.5 %copy-start.2 = (bf16[128,512]{1,0:T(8,128)(2,1)S(1)}, bf16[128,512]{1,0:T(8,128)(2,1)}, u32[]{:S(2)}) copy-start(bf16[128,512]{1,0:T(8,128)(2,1)} %w_c.5) | copy-start | bytes 393220
  42.6 21.5 %copy-start.13 = (f32[2,3,128]{2,0,1:T(2,128)S(1)}, f32[2,3,128]{2,0,1:T(2,128)}, u32[]{:S(2)}) copy-start(f32[2,3,128]{2,0,1:T(2,128)} %param.32) | copy-start | bytes 9220
  44.0 32.9 %copy-start.3 = (bf16[1,28,28,512]{3,2,1,0:T(8,128)(2,1)S(1)}, bf16[1,28,28,512]{3,2,1,0:T(8,128)(2,1)}, u32[]{:S(2)}) copy-start(bf16[1,28,28,512]{3,2,1,0:T(8,128)(2,1)} %param.34) | copy-start | bytes 2408452
  44.0 32.9 %copy-start.9 = (f32[2,3,512]{2,0,1:T(2,128)S(1)}, f32[2,3,512]{2,0,1:T(2,128)}, u32[]{:S(2)}) copy-start(f32[2,3,512]{2,0,1:T(2,128)} %param.33) | copy-start | bytes 36868
  122.2 6.6 %collective-permute-start.3 = (bf16[24,80,128]{2,1,0:T(8,128)(2,1)S(1)}, bf16[24,80,128]{2,1,0:T(8,128)(2,1)S(1)}, u32[]{:S(2)}, u32[]{:S(2)}) collective-permute-start(bf16[24,80,128]{2,1,0:T(8,128)(2,1)S(1)} %get-tuple-element.240), channel_id=1, source_target_pairs={{0,16},{16,0},{1,17},{17,1},{2,18},{18,2},{3,19},{19,3},{4,20},{20... | collective-permute-start | bytes 1474568 | tf_op jit(solution)/shard_map/ppermute | solution.py:1365
  125.0 3.8 %collective-permute-start.2 = (bf16[28,64,128]{2,1,0:T(8,128)(2,1)S(1)}, bf16[28,64,128]{2,1,0:T(8,128)(2,1)S(1)}, u32[]{:S(2)}, u32[]{:S(2)}) collective-permute-start(bf16[28,64,128]{2,1,0:T(8,128)(2,1)S(1)} %get-tuple-element.229.dn_oth), channel_id=1, source_target_pairs={{0,16},{16,0},{1,17},{17,1},{2,18},{18,2},{3,19},{19,3},{4,20},{20... | collective-permute-start | bytes 1376264 | tf_op jit(solution)/shard_map/ppermute | solution.py:1365
  126.1 2.7 %collective-permute-start.1 = (bf16[14,32,256]{2,1,0:T(8,128)(2,1)S(1)}, bf16[14,32,256]{2,1,0:T(8,128)(2,1)S(1)}, u32[]{:S(2)}, u32[]{:S(2)}) collective-permute-start(bf16[14,32,256]{2,1,0:T(8,128)(2,1)S(1)} %get-tuple-element.236), channel_id=1, source_target_pairs={{0,16},{16,0},{1,17},{17,1},{2,18},{18,2},{3,19},{19,3},{4,20},{20... | collective-permute-start | bytes 688136 | tf_op jit(solution)/shard_map/ppermute | solution.py:1365
  126.2 2.7 %collective-permute-start.4 = (bf16[8,80,128]{2,1,0:T(8,128)(2,1)S(1)}, bf16[8,80,128]{2,1,0:T(8,128)(2,1)S(1)}, u32[]{:S(2)}, u32[]{:S(2)}) collective-permute-start(bf16[8,80,128]{2,1,0:T(8,128)(2,1)S(1)} %get-tuple-element.242), channel_id=1, source_target_pairs={{0,16},{16,0},{1,17},{17,1},{2,18},{18,2},{3,19},{19,3},{4,20},{20... | collective-permute-start | bytes 491528 | tf_op jit(solution)/shard_map/ppermute | solution.py:1365
  153.6 6.8 %collective-permute-start.7 = (bf16[1,176,128]{2,1,0:T(8,128)(2,1)S(1)}, bf16[1,176,128]{2,1,0:T(8,128)(2,1)S(1)}, u32[]{:S(2)}, u32[]{:S(2)}) collective-permute-start(bf16[1,176,128]{2,1,0:T(8,128)(2,1)S(1)} %add_all.1.refs_0_), channel_id=1, source_target_pairs={{0,12},{1,13},{2,14},{3,15},{4,8},{5,9},{6,10},{7,11},{8,4},{9,5},... | collective-permute-start | bytes 135176 | tf_op jit(solution)/shard_map/ppermute | solution.py:1558
  154.4 5.9 %collective-permute-start.6 = (bf16[1,176,128]{2,1,0:T(8,128)(2,1)S(1)}, bf16[1,176,128]{2,1,0:T(8,128)(2,1)S(1)}, u32[]{:S(2)}, u32[]{:S(2)}) collective-permute-start(bf16[1,176,128]{2,1,0:T(8,128)(2,1)S(1)} %add_all.1.refs_0_), channel_id=1, source_target_pairs={{0,8},{1,9},{2,10},{3,11},{4,12},{5,13},{6,14},{7,15},{8,0},{9,1},... | collective-permute-start | bytes 135176 | tf_op jit(solution)/shard_map/ppermute | solution.py:1558
  154.5 5.9 %collective-permute-start.5 = (bf16[1,176,128]{2,1,0:T(8,128)(2,1)S(1)}, bf16[1,176,128]{2,1,0:T(8,128)(2,1)S(1)}, u32[]{:S(2)}, u32[]{:S(2)}) collective-permute-start(bf16[1,176,128]{2,1,0:T(8,128)(2,1)S(1)} %add_all.1.refs_0_), channel_id=1, source_target_pairs={{0,4},{1,5},{2,6},{3,7},{4,0},{5,1},{6,2},{7,3},{8,12},{9,13},{10,... | collective-permute-start | bytes 135176 | tf_op jit(solution)/shard_map/ppermute | solution.py:1558
  160.4 8.0 %collective-permute-start.10 = (bf16[4,176,128]{2,1,0:T(8,128)(2,1)S(1)}, bf16[4,176,128]{2,1,0:T(8,128)(2,1)S(1)}, u32[]{:S(2)}, u32[]{:S(2)}) collective-permute-start(bf16[4,176,128]{2,1,0:T(8,128)(2,1)S(1)} %stack_parts.1.refs_0_), channel_id=1, source_target_pairs={{0,3},{1,2},{2,1},{3,0},{4,7},{5,6},{6,5},{7,4},{8,11},{9,10},{10,... | collective-permute-start | bytes 540680 | tf_op jit(solution)/shard_map/ppermute | solution.py:1575
  160.9 9.1 %collective-permute-start.9 = (bf16[4,176,128]{2,1,0:T(8,128)(2,1)S(1)}, bf16[4,176,128]{2,1,0:T(8,128)(2,1)S(1)}, u32[]{:S(2)}, u32[]{:S(2)}) collective-permute-start(bf16[4,176,128]{2,1,0:T(8,128)(2,1)S(1)} %stack_parts.1.refs_0_), channel_id=1, source_target_pairs={{0,2},{1,3},{2,0},{3,1},{4,6},{5,7},{6,4},{7,5},{8,10},{9,11},{10,... | collective-permute-start | bytes 540680 | tf_op jit(solution)/shard_map/ppermute | solution.py:1575
  161.8 8.3 %collective-permute-start.8 = (bf16[4,176,128]{2,1,0:T(8,128)(2,1)S(1)}, bf16[4,176,128]{2,1,0:T(8,128)(2,1)S(1)}, u32[]{:S(2)}, u32[]{:S(2)}) collective-permute-start(bf16[4,176,128]{2,1,0:T(8,128)(2,1)S(1)} %stack_parts.1.refs_0_), channel_id=1, source_target_pairs={{0,1},{1,0},{2,3},{3,2},{4,5},{5,4},{6,7},{7,6},{8,9},{9,8},{10,11... | collective-permute-start | bytes 540680 | tf_op jit(solution)/shard_map/ppermute | solution.py:1575
  164.0 6.8 %collective-permute-start.11 = (bf16[4,176,128]{2,1,0:T(8,128)(2,1)S(1)}, bf16[4,176,128]{2,1,0:T(8,128)(2,1)S(1)}, u32[]{:S(2)}, u32[]{:S(2)}) collective-permute-start(bf16[4,176,128]{2,1,0:T(8,128)(2,1)S(1)} %stack_parts.1.refs_0_), channel_id=1, source_target_pairs={{0,16},{16,0},{1,17},{17,1},{2,18},{18,2},{3,19},{19,3},{4,20},{20... | collective-permute-start | bytes 540680 | tf_op jit(solution)/shard_map/ppermute | solution.py:1365
  170.1 1.4 collective-permute-start.12
  170.1 1.7 collective-permute-start.13
  170.6 1.4 collective-permute-start.14
